TPU v7x, 32 devices: a whole 2x2x4 slice. The times are simulated.
32 devices in a mesh: dp: 8 (over z, y), blk: 4 (over x, core).
Axes of the slice: x: 2, y: 2, z: 4, core: 2. Of those that a mesh axis runs over, the one named last changes fastest.
Arguments:
- hidden: bfloat16 [1024, 16, 768], P('blk', 'dp'), may hold values from -6 to 6
- side_state: bfloat16 [1024, 16, 96], P('blk', 'dp'), may hold values from -6 to 6
- doc_lengths: int32 [16, 8], P('dp'), may hold values from 1 to 832, 1024 in all within a row
- norm_in: bfloat16 [768], replicated, may hold values from 0.099609375 to 1.8984375
- w_query: bfloat16 [768, 768], replicated, may hold values from -0.21875 to 0.21875
- w_key: bfloat16 [768, 768], replicated, may hold values from -0.21875 to 0.21875
- w_value: bfloat16 [768, 768], replicated, may hold values from -0.21875 to 0.21875
- w_out: bfloat16 [768, 768], replicated, may hold values from -0.875 to 0.875
- norm_mid: bfloat16 [768], replicated, may hold values from 0.099609375 to 1.8984375
- w_inner: bfloat16 [768, 3072], replicated, may hold values from -0.21875 to 0.21875
- w_outer: bfloat16 [3072, 768], replicated, may hold values from -0.109375 to 0.109375
- w_down: bfloat16 [768, 96], replicated, may hold values from -0.21875 to 0.21875
- gate: float32 [96], replicated, may hold values from -4 to 4
- side_norm_in: float32 [96], replicated, may hold values from 0.1 to 1.9
- s_query: bfloat16 [96, 96], replicated, may hold values from -0.625 to 0.625
- s_key: bfloat16 [96, 96], replicated, may hold values from -0.625 to 0.625
- s_value: bfloat16 [96, 96], replicated, may hold values from -0.625 to 0.625
- s_out: bfloat16 [96, 96], replicated, may hold values from -1.75 to 1.75
- side_norm_mid: float32 [96], replicated, may hold values from 0.1 to 1.9
- s_inner: bfloat16 [96, 384], replicated, may hold values from -0.625 to 0.625
- s_outer: bfloat16 [384, 96], replicated, may hold values from -0.3125 to 0.3125
- cotangent: bfloat16 [1024, 16, 96], P('blk', 'dp'), may hold values from -6 to 6
Outputs:
- backbone_out: bfloat16 [1024, 16, 768], P('blk', 'dp')
- side_out: bfloat16 [1024, 16, 96], P('blk', 'dp')
- state_grad: float32 [1024, 16, 96], P('blk', 'dp')
- grad_down: float32 [768, 96], replicated
- grad_gate: float32 [96], replicated
- grad_norm_in: float32 [96], replicated
- grad_query: float32 [96, 96], replicated
- grad_key: float32 [96, 96], replicated
- grad_value: float32 [96, 96], replicated
- grad_out: float32 [96, 96], replicated
- grad_norm_mid: float32 [96], replicated
- grad_inner: float32 [96, 384], replicated
- grad_outer: float32 [384, 96], replicated
Inputs may be any that keep to these rules, and one draw needn't show every extreme that they name: `doc_lengths`: each row's 8 lengths sum to 1024, and each row has one document of exactly 832 tokens.
All inputs are finite; a program needn't handle non-finite values.
Results may differ from a plain program's by a relative error of at most 0.034.
Values may be sent and summed in bfloat16 or wider, within the bound.
No kernel may reach another device: no remote copies, remote signals or barrier semaphores. Data moves between devices by JAX's collectives and lax.ppermute only.
A program may use at most 128 MiB of HBM per device.

v0:
```python
from functools import partial

import jax
import jax.numpy as jnp
from jax import lax
from jax.sharding import PartitionSpec as P

HEADS = 12
SHEADS = 12


eps_value = 1e-06
neg_fill = -1e30


def product(left_mat, right_mat):
    return jnp.dot(left_mat, right_mat, preferred_element_type=jnp.float32)


def over_tokens(left_mat, right_mat):
    return lax.dot_general(
        left_mat, right_mat, (((0,), (0,)), ((), ())), preferred_element_type=jnp.float32
    )


def times_transposed(left_mat, right_mat):
    return lax.dot_general(
        left_mat, right_mat, (((1,), (1,)), ((), ())), preferred_element_type=jnp.float32
    )


def norm_rows(vector, gain_vec):
    return (
        vector * lax.rsqrt(jnp.mean(vector * vector, axis=-1, keepdims=True) + eps_value) * gain_vec
    )


def doc_ids(lengths, first_pos, span_len):
    doc_ends = jnp.cumsum(lengths, axis=1, dtype=jnp.int32)
    positions = first_pos + jnp.arange(span_len, dtype=jnp.int32)
    return jnp.sum(
        (positions[None, :, None] >= doc_ends[:, None, :]).astype(jnp.int32),
        axis=2,
        dtype=jnp.int32,
    )


def per_device(
    hidden,
    side_state,
    doc_lengths,
    norm_in,
    w_query,
    w_key,
    w_value,
    w_out,
    norm_mid,
    w_inner,
    w_outer,
    w_down,
    gate,
    side_norm_in,
    s_query,
    s_key,
    s_value,
    s_out,
    side_norm_mid,
    s_inner,
    s_outer,
    cotangent,
):
    shard_len, row_count, model_width = hidden.shape
    side_width = side_state.shape[2]
    tokens = shard_len * row_count
    first_pos = lax.axis_index("blk") * shard_len
    doc_here = doc_ids(doc_lengths, first_pos, shard_len)
    inputs_flat = hidden.reshape(tokens, model_width).astype(jnp.float32)
    normed = norm_rows(inputs_flat, norm_in.astype(jnp.float32)).astype(jnp.bfloat16)
    queries = product(normed, w_query).astype(jnp.bfloat16).reshape(shard_len, row_count, HEADS, -1)
    score_scale = queries.shape[-1] ** (-0.5)
    key_local = (
        product(normed, w_key).astype(jnp.bfloat16).reshape(shard_len, row_count, model_width)
    )
    value_local = (
        product(normed, w_value).astype(jnp.bfloat16).reshape(shard_len, row_count, model_width)
    )
    key_rows = lax.all_gather(key_local, "blk", axis=0, tiled=True)
    span_len = key_rows.shape[0]
    key_heads = key_rows.reshape(span_len, row_count, HEADS, -1)
    value_heads = lax.all_gather(value_local, "blk", axis=0, tiled=True).reshape(
        span_len, row_count, HEADS, -1
    )
    doc_there = doc_ids(doc_lengths, jnp.int32(0), span_len)
    same_doc = doc_here[:, None, :, None] == doc_there[:, None, None, :]
    scores = (
        jnp.einsum("qrhe,krhe->rhqk", queries, key_heads, preferred_element_type=jnp.float32)
        * score_scale
    )
    scores = jnp.where(same_doc, scores, neg_fill)
    max_old = jnp.full((row_count, HEADS, shard_len), neg_fill, jnp.float32)
    max_new = jnp.maximum(max_old, jnp.max(scores, axis=-1))
    weights_exp = jnp.where(same_doc, jnp.exp(scores - max_new[..., None]), 0.0)
    total_new = jnp.sum(weights_exp, axis=-1)
    accum_new = jnp.einsum(
        "rhqk,krhe->rhqe",
        weights_exp.astype(jnp.bfloat16),
        value_heads,
        preferred_element_type=jnp.float32,
    )
    attended = accum_new / total_new[..., None]
    attended = (
        jnp.transpose(attended, (2, 0, 1, 3)).reshape(tokens, model_width).astype(jnp.bfloat16)
    )
    after_attn = inputs_flat + product(attended, w_out)
    mid_normed = norm_rows(after_attn, norm_mid.astype(jnp.float32)).astype(jnp.bfloat16)
    inner_act = jax.nn.gelu(product(mid_normed, w_inner), approximate=False).astype(jnp.bfloat16)
    backbone_flat = (after_attn + product(inner_act, w_outer)).astype(jnp.bfloat16)
    downed = product(backbone_flat, w_down)
    gate_open = jax.nn.sigmoid(gate)
    state_flat = side_state.reshape(tokens, side_width).astype(jnp.float32)
    mixed = gate_open * downed + (1.0 - gate_open) * state_flat
    side_normed = norm_rows(mixed, side_norm_in).astype(jnp.bfloat16)
    side_query = product(side_normed, s_query).astype(jnp.bfloat16)
    side_key = product(side_normed, s_key).astype(jnp.bfloat16)
    side_value = product(side_normed, s_value).astype(jnp.bfloat16)
    all_keys, all_values = (
        lax.all_gather(
            side_key.reshape(shard_len, row_count * side_width), "blk", axis=0, tiled=True
        ),
        lax.all_gather(
            side_value.reshape(shard_len, row_count * side_width), "blk", axis=0, tiled=True
        ),
    )
    seq_len = all_keys.shape[0]
    query_heads = side_query.reshape(shard_len, row_count, SHEADS, -1)
    key_heads = all_keys.reshape(seq_len, row_count, SHEADS, -1)
    value_heads = all_values.reshape(seq_len, row_count, SHEADS, -1)
    side_scale = query_heads.shape[-1] ** (-0.5)
    doc_all = doc_ids(doc_lengths, 0, seq_len)
    same_doc = doc_here[:, None, :, None] == doc_all[:, None, None, :]
    scores = (
        jnp.einsum("qrhe,krhe->rhqk", query_heads, key_heads, preferred_element_type=jnp.float32)
        * side_scale
    )
    scores = jnp.where(same_doc, scores, neg_fill)
    row_max = jnp.max(scores, axis=-1, keepdims=True)
    weights_exp = jnp.exp(scores - row_max)
    row_total = jnp.sum(weights_exp, axis=-1, keepdims=True)
    probs = weights_exp / row_total
    probs_low = probs.astype(jnp.bfloat16)
    side_attn = jnp.einsum(
        "rhqk,krhe->qrhe", probs_low, value_heads, preferred_element_type=jnp.float32
    )
    side_attn = side_attn.reshape(tokens, side_width).astype(jnp.bfloat16)
    side_mid = mixed + product(side_attn, s_out)
    side_mid_normed = norm_rows(side_mid, side_norm_mid).astype(jnp.bfloat16)
    inner_pre = product(side_mid_normed, s_inner)
    gelu_exact = partial(jax.nn.gelu, approximate=False)
    side_act = gelu_exact(inner_pre).astype(jnp.bfloat16)
    side_flat = side_mid + product(side_act, s_outer)
    grad_flat = cotangent.reshape(tokens, side_width).astype(jnp.float32)
    grad_low = cotangent.reshape(tokens, side_width)
    grad_outer = over_tokens(side_act, grad_low)
    grad_act = times_transposed(grad_low, s_outer)
    grad_pre = jax.vjp(gelu_exact, inner_pre)[1](grad_act)[0].astype(jnp.bfloat16)
    grad_inner = over_tokens(side_mid_normed, grad_pre)
    grad_mid_normed = times_transposed(grad_pre, s_inner)
    mid_pull = jax.vjp(norm_rows, side_mid, side_norm_mid)[1]
    grad_mid_part, grad_norm_mid = mid_pull(grad_mid_normed)
    grad_mid = grad_flat + grad_mid_part
    grad_mid_low = grad_mid.astype(jnp.bfloat16)
    grad_out = over_tokens(side_attn, grad_mid_low)
    grad_attn = (
        times_transposed(grad_mid_low, s_out)
        .astype(jnp.bfloat16)
        .reshape(shard_len, row_count, SHEADS, -1)
    )
    grad_probs = jnp.einsum(
        "qrhe,krhe->rhqk", grad_attn, value_heads, preferred_element_type=jnp.float32
    )
    row_terms = jnp.sum(probs * grad_probs, axis=-1, keepdims=True)
    grad_scores = (probs * (grad_probs - row_terms)).astype(jnp.bfloat16)
    grad_query_rows = (
        jnp.einsum("rhqk,krhe->qrhe", grad_scores, key_heads, preferred_element_type=jnp.float32)
        * side_scale
    )
    grad_query_rows = grad_query_rows.reshape(tokens, side_width).astype(jnp.bfloat16)
    grad_key_all = (
        jnp.einsum("rhqk,qrhe->krhe", grad_scores, query_heads, preferred_element_type=jnp.float32)
        * side_scale
    )
    grad_value_all = jnp.einsum(
        "rhqk,qrhe->krhe", probs_low, grad_attn, preferred_element_type=jnp.float32
    )
    stacked = jnp.concatenate(
        [
            grad_key_all.reshape(seq_len, row_count * side_width),
            grad_value_all.reshape(seq_len, row_count * side_width),
        ],
        axis=1,
    )
    mine = lax.psum_scatter(
        stacked.astype(jnp.bfloat16), "blk", scatter_dimension=0, tiled=True
    ).astype(jnp.float32)
    grad_key_rows = (
        mine[:, : row_count * side_width].reshape(tokens, side_width).astype(jnp.bfloat16)
    )
    grad_value_rows = (
        mine[:, row_count * side_width :].reshape(tokens, side_width).astype(jnp.bfloat16)
    )
    grad_query = over_tokens(side_normed, grad_query_rows)
    grad_key = over_tokens(side_normed, grad_key_rows)
    grad_value = over_tokens(side_normed, grad_value_rows)
    grad_normed = (
        times_transposed(grad_query_rows, s_query)
        + times_transposed(grad_key_rows, s_key)
        + times_transposed(grad_value_rows, s_value)
    )
    in_pull = jax.vjp(norm_rows, mixed, side_norm_in)[1]
    grad_mixed_part, grad_norm_in = in_pull(grad_normed)
    grad_mixed = grad_mid + grad_mixed_part
    state_grad = (1.0 - gate_open) * grad_mixed
    grad_downed = (gate_open * grad_mixed).astype(jnp.bfloat16)
    grad_down = over_tokens(backbone_flat, grad_downed)
    grad_gate = jnp.sum(grad_mixed * (downed - state_flat), axis=0) * gate_open * (1.0 - gate_open)
    summed = lax.psum(
        (
            grad_down,
            grad_gate,
            grad_norm_in,
            grad_query,
            grad_key,
            grad_value,
            grad_out,
            grad_norm_mid,
            grad_inner,
            grad_outer,
        ),
        ("dp", "blk"),
    )
    backbone_out = backbone_flat.reshape(shard_len, row_count, model_width)
    side_out = side_flat.astype(jnp.bfloat16).reshape(shard_len, row_count, side_width)
    state_out = state_grad.reshape(shard_len, row_count, side_width)
    return (
        backbone_out,
        side_out,
        state_out,
        summed[0],
        summed[1],
        summed[2],
        summed[3],
        summed[4],
        summed[5],
        summed[6],
        summed[7],
        summed[8],
        summed[9],
    )


def solution(mesh):
    return jax.shard_map(
        per_device,
        mesh=mesh,
        in_specs=(
            P("blk", "dp", None),
            P("blk", "dp", None),
            P("dp", None),
            P(),
            P(),
            P(),
            P(),
            P(),
            P(),
            P(),
            P(),
            P(),
            P(),
            P(),
            P(),
            P(),
            P(),
            P(),
            P(),
            P(),
            P(),
            P("blk", "dp", None),
        ),
        out_specs=(
            P("blk", "dp", None),
            P("blk", "dp", None),
            P("blk", "dp", None),
            P(),
            P(),
            P(),
            P(),
            P(),
            P(),
            P(),
            P(),
            P(),
            P(),
        ),
        check_vma=False,
    )
```

profile of v0, /device:TPU:0, one launch (start us, length us, event | category | flops | bytes accessed | tf_op | source)
XLA Modules:
  0.0 568.8 jit_solution(10199471442847628743)
XLA Ops:
  7.2 2.3 reshape.204
  9.5 2.0 multiply_reduce_fusion.2
  13.5 2.0 convolution_convert_fusion.1
  16.8 2.3 convolution_convert_fusion
  20.6 2.3 convolution_convert_fusion.2
  22.9 2.2 reshape.187
  29.6 18.6 %all-gather.3.cloned.1.call-done = bf16[1024,2,768]{2,1,0:T(2,128)(2,1)} async-done(((bf16[256,2,768]{2,1,0:T(2,128)(2,1)}), bf16[1024,2,768]{2,1,0:T(2,128)(2,1)}) %all-gather.3.cloned.1.call-update) | async-done | bytes 3145744 | tf_op jit(solution)/shard_map/all_gather | solution.py:87
  48.1 8.7 %copy.100 = bf16[1024,2,768]{0,2,1:T(8,128)(2,1)} copy(bf16[1024,2,768]{2,1,0:T(2,128)(2,1)} %all-gather.3.cloned.1.call-done) | data formatting | bytes 6291456 | tf_op jit(solution)/shard_map/all_gather | solution.py:87
  56.9 13.9 %fusion.1 = (f32[2,12,256]{2,1,0:T(8,128)S(1)}, f32[2,12,256,1024]{3,2,1,0:T(8,128)}) fusion(pred[2,256,1024]{2,1,0:T(8,128)(4,1)S(1)} %broadcast_compare_fusion, bf16[1024,2,12,64]{0,3,2,1:T(8,128)(2,1)} %bitcast.82, bf16[256,2,12,64]{3,2,1,0:T(8,128)(2,1)} %reshape.187), kind=kOutput, calls=%fused_computation.7 | convolution fusion | flops 824174592 | bytes 29646848 | tf_op jit(solution)/shard_map/qrhe,krhe->rhqk/dot_general | solution.py:96
  70.8 12.7 %fusion.3 = f32[2,12,256]{2,1,0:T(8,128)S(1)} fusion(f32[2,12,256,1024]{3,2,1,0:T(8,128)} %get-tuple-element.90, f32[2,12,256]{2,1,0:T(8,128)S(1)} %broadcast_maximum_fusion, pred[2,256,1024]{2,1,0:T(8,128)(4,1)S(1)} %broadcast_compare_fusion), kind=kLoop, calls=%fused_computation.9 | loop fusion | flops 31451136 | bytes 25739264 | tf_op jit(solution)/shard_map/reduce_sum | solution.py:103
  83.5 8.7 %copy.102 = bf16[1024,2,768]{0,2,1:T(8,128)(2,1)} copy(bf16[1024,2,768]{2,1,0:T(2,128)(2,1)} %all-gather.5.cloned.1.call-done) | data formatting | bytes 6291456 | tf_op jit(solution)/shard_map/all_gather | solution.py:90
  92.2 13.2 %fusion.29 = bf16[256,2,12,64]{0,3,2,1:T(8,128)(2,1)} fusion(bf16[1024,2,12,64]{0,3,2,1:T(8,128)(2,1)} %bitcast.83, f32[2,12,256,1024]{3,2,1,0:T(8,128)} %get-tuple-element.90, f32[2,12,256]{2,1,0:T(8,128)S(1)} %broadcast_maximum_fusion, pred[2,256,1024]{2,1,0:T(8,128)(4,1)S(1)} %broadcast_compare_fusion, f32[256,2,12]{0,2,1:T(8,128)S(1)} %bitcast.96), kind=kOutput, calls=%fused_computation.43 | convolution fusion | flops 837550080 | bytes 29671424 | tf_op jit(solution)/shard_map/rhqk,krhe->rhqe/dot_general | solution.py:104
  105.3 4.7 copy.103
  110.0 4.3 convert_element_type.140
  114.3 3.1 multiply_reduce_fusion.1
  117.4 21.6 %add_convert_fusion = bf16[512,768]{1,0:T(8,128)(2,1)S(1)} fusion(f32[512,768]{1,0:T(8,128)} %get-tuple-element.92, bf16[3072,768]{1,0:T(8,128)(2,1)} %param.32, bf16[768,3072]{1,0:T(8,128)(2,1)} %param.31, f32[768]{0:T(1024)S(1)} %convert_element_type.141, f32[512]{0:T(512)S(1)} %add_rsqrt_fusion.1), kind=kOutput, calls=%fused_computation.46 | convolution fusion | flops 4936040448 | bytes 11801600 | tf_op jit(solution)/shard_map/dot_general | solution.py:17
  141.2 2.9 reshape.195
  144.0 2.4 copy.111
  146.9 7.2 %all_gather.15 = bf16[1024,192]{1,0:T(8,128)(2,1)S(1)} all-gather(bf16[256,192]{1,0:T(8,128)(2,1)S(1)} %reshape.196), channel_id=1, replica_groups=mesh['dp'=8,'blk'=4] {'blk'}, dimensions={0}, use_global_device_ids=true | all-gather | bytes 491520 | tf_op jit(solution)/shard_map/all_gather | solution.py:127
  154.8 7.3 %all_gather.14 = bf16[1024,192]{1,0:T(8,128)(2,1)S(1)} all-gather(bf16[256,192]{1,0:T(8,128)(2,1)S(1)} %reshape.193), channel_id=1, replica_groups=mesh['dp'=8,'blk'=4] {'blk'}, dimensions={0}, use_global_device_ids=true | all-gather | bytes 491520 | tf_op jit(solution)/shard_map/all_gather | solution.py:130
  162.3 13.4 %fusion.109 = (f32[2,12,256]{2,1,0:T(8,128)S(1)}, f32[2,12,256,1024]{3,2,1,0:T(8,128)}) fusion(pred[2,256,1024]{2,1,0:T(8,128)(4,1)S(1)} %broadcast_compare_fusion, bf16[256,2,12,8]{0,3,2,1:T(8,128)(2,1)S(1)} %copy.111, bf16[1024,2,12,8]{0,3,2,1:T(8,128)(2,1)S(1)} %bitcast.85), kind=kOutput, calls=%fused_computation.169 | convolution fusion | flops 125830144 | bytes 26206208 | tf_op jit(solution)/shard_map/sub | solution.py:147
  175.7 10.0 %fusion.45 = bf16[256,2,12,8]{0,3,2,1:T(8,128)(2,1)S(1)} fusion(bf16[1024,2,12,8]{0,3,2,1:T(8,128)(2,1)S(1)} %bitcast.93, f32[2,12,256,1024]{3,2,1,0:T(8,128)} %get-tuple-element.95, f32[2,12,256]{2,1,0:T(8,128)S(1)} %get-tuple-element.94), kind=kOutput, calls=%fused_computation.71 | convolution fusion | flops 113295360 | bytes 25681920 | tf_op jit(solution)/shard_map/rhqk,krhe->qrhe/dot_general | solution.py:151
  185.7 2.9 copy.112
  188.7 1.7 convert_element_type.154
  190.8 2.7 multiply_convert_fusion.8
  195.3 1.9 reshape.200
  198.5 21.0 %multiply_reduce_fusion = (f32[2,12,256]{2,1,0:T(8,128)S(1)}, f32[2,12,256,1024]{3,2,1,0:T(8,128)}) fusion(f32[2,12,256,1024]{3,2,1,0:T(8,128)} %get-tuple-element.95, f32[2,12,256]{2,1,0:T(8,128)} %copy-done.29, bf16[256,2,12,8]{0,3,2,1:T(8,128)(2,1)S(1)} %copy.117, bf16[1024,2,12,8]{0,3,2,1:T(8,128)(2,1)S(1)} %bitcast.94), kind=kOutput, calls=%fused_computation.2 | convolution fusion | flops 119531520 | bytes 50872320 | tf_op jit(solution)/shard_map/qrhe,krhe->rhqk/dot_general | solution.py:178
  219.5 9.2 %fusion.37 = bf16[2,12,8,1024]{3,2,1,0:T(8,128)(2,1)S(1)} fusion(bf16[256,2,12,8]{0,3,2,1:T(8,128)(2,1)S(1)} %copy.117, f32[2,12,256,1024]{3,2,1,0:T(8,128)} %get-tuple-element.95, f32[2,12,256]{2,1,0:T(8,128)S(1)} %copy-done.30), kind=kOutput, calls=%fused_computation.57 | convolution fusion | flops 113442816 | bytes 25681920 | tf_op jit(solution)/shard_map/rhqk,qrhe->krhe/dot_general | solution.py:192
  228.7 16.3 %multiply_convert_fusion = bf16[2,12,256,1024]{3,2,1,0:T(8,128)(2,1)S(1)} fusion(f32[2,12,256,1024]{3,2,1,0:T(8,128)} %get-tuple-element.101, f32[2,12,256]{2,1,0:T(8,128)S(1)} %get-tuple-element.100, f32[2,12,256,1024]{3,2,1,0:T(8,128)} %get-tuple-element.95, f32[2,12,256]{2,1,0:T(8,128)S(1)} %copy-done.30), kind=kLoop, calls=%fused_computation.1 | loop fusion | flops 25165824 | bytes 62963712 | tf_op jit(solution)/shard_map/convert_element_type | solution.py:182
  245.0 1.7 fusion.36
  246.7 2.8 copy-done.2
  251.2 7.9 %fusion.48 = bf16[256,2,12,8]{0,3,2,1:T(8,128)(2,1)S(1)} fusion(bf16[1024,2,12,8]{0,3,2,1:T(8,128)(2,1)S(1)} %bitcast.86, bf16[2,12,256,1024]{3,2,1,0:T(8,128)(2,1)} %copy-done.2), kind=kOutput, calls=%fused_computation.72 | convolution fusion | flops 100761600 | bytes 13074432 | tf_op jit(solution)/shard_map/rhqk,krhe->qrhe/dot_general | solution.py:184
  259.2 2.9 copy.118
  262.1 1.7 convert_element_type.165
  265.7 2.0 fusion.114
  267.8 1.9 fusion.104
  269.7 4.9 reduce-scatter.2.cloned.1.call-done
  275.8 1.7 fusion.113
  277.6 1.7 fusion.112
  279.5 1.8 multiply_reduce_fusion.4
  281.9 1.4 multiply_reduce_fusion.5
  284.7 2.2 fusion.62
  291.3 119.9 %all-reduce.5.cloned.1.call-done = (f32[96]{0:T(128)}, f32[96]{0:T(128)}, f32[96,96]{1,0:T(8,128)}, f32[96,96]{1,0:T(8,128)}, f32[96,96]{1,0:T(8,128)}, /*index=5*/f32[96,96]{1,0:T(8,128)}, f32[96]{0:T(128)}) async-done(((f32[96]{0:T(128)}, f32[96]{0:T(128)}, f32[96,96]{1,0:T(8,128)}, f32[96,96]{1,0:T(8,128)}, f32[96,96]{1,0:T(8,128)}, /*index=5*/f32[96,96]{1,0:T(8,128)}, f32[96]{0:T(128)}), (f32[96]{0:T(128)}, ...) | async-done | bytes 148624 | tf_op jit(solution)/shard_map/psum | solution.py:226
  411.1 136.7 %all-reduce.7.cloned.1.call-done = (f32[768,96]{0,1:T(8,128)}, f32[96,384]{1,0:T(8,128)}, f32[384,96]{0,1:T(8,128)}) async-done(((f32[768,96]{0,1:T(8,128)}, f32[96,384]{1,0:T(8,128)}, f32[384,96]{0,1:T(8,128)}), (f32[768,96]{0,1:T(8,128)}, f32[96,384]{1,0:T(8,128)}, f32[384,96]{0,1:T(8,128)})) %all-reduce.7.cloned.1.call-update) | async-done | bytes 589840 | tf_op jit(solution)/shard_map/psum | solution.py:226
  547.8 1.7 copy.141
  551.8 1.4 copy.144
  558.7 1.6 copy.149
  560.3 1.6 copy.150
  (156 shorter events, 35.0 us)
Async XLA Ops:
  7.2 107.1 %copy-start = (bf16[768,768]{1,0:T(8,128)(2,1)S(1)}, bf16[768,768]{1,0:T(8,128)(2,1)}, u32[]{:S(2)}) copy-start(bf16[768,768]{1,0:T(8,128)(2,1)} %param.29) | copy-start | bytes 3538948
  7.2 40.9 %all-gather.3.cloned.1.call-start = ((), (), s32[]{:S(2)}) async-start(), calls=%async_computation.1 | async-start | bytes 3932160 | tf_op jit(solution)/shard_map/all_gather | solution.py:87
  12.6 0.9 copy-start.16
  16.8 8.4 %copy-start.38 = (bf16[768]{0:T(1024)(128)(2,1)S(1)}, bf16[768]{0:T(1024)(128)(2,1)}, u32[]{:S(2)}) copy-start(bf16[768]{0:T(1024)(128)(2,1)} %param.30) | copy-start | bytes 4612
  16.8 11.4 %copy-start.39 = (s32[2,8]{1,0:T(2,128)S(1)}, s32[2,8]{1,0:T(2,128)}, u32[]{:S(2)}) copy-start(s32[2,8]{1,0:T(2,128)} %param.24) | copy-start | bytes 196
  16.8 66.7 %all-gather.5.cloned.1.call-start = ((), (), s32[]{:S(2)}) async-start(), calls=%async_computation.2 | async-start | bytes 3932160 | tf_op jit(solution)/shard_map/all_gather | solution.py:90
  20.3 254.3 %reduce-scatter.2.cloned.1.call-start = ((), (), s32[]{:S(2)}) async-start(), calls=%async_computation.3 | async-start | bytes 983040 | tf_op jit(solution)/shard_map/reduce_scatter | solution.py:202
  26.3 112.7 %copy-start.8 = (f32[512,96]{0,1:T(8,128)}, f32[512,96]{0,1:T(8,128)S(1)}, u32[]{:S(2)}) copy-start(f32[512,96]{0,1:T(8,128)S(1)} %copy.105) | copy-start | bytes 589828
  27.4 1.1 copy-start.14
  29.2 109.8 %copy-start.35 = (f32[96]{0:T(128)}, f32[96]{0:T(128)S(1)}, u32[]{:S(2)}) copy-start(f32[96]{0:T(128)S(1)} %get-tuple-element.85) | copy-start | bytes 1156
  29.2 109.8 %copy-start.37 = (f32[96]{0:T(128)}, f32[96]{0:T(128)S(1)}, u32[]{:S(2)}) copy-start(f32[96]{0:T(128)S(1)} %get-tuple-element.86) | copy-start | bytes 1156
  117.4 21.7 %copy-start.20 = (bf16[768,96]{0,1:T(8,128)(2,1)S(1)}, bf16[768,96]{0,1:T(8,128)(2,1)}, u32[]{:S(2)}) copy-start(bf16[768,96]{0,1:T(8,128)(2,1)} %param.33) | copy-start | bytes 442372
  117.4 23.3 %copy-start.34 = (f32[96]{0:T(128)S(1)}, f32[96]{0:T(128)}, u32[]{:S(2)}) copy-start(f32[96]{0:T(128)} %param.35) | copy-start | bytes 1156
  117.4 23.4 %copy-start.24 = (bf16[96,96]{1,0:T(8,128)(2,1)S(1)}, bf16[96,96]{1,0:T(8,128)(2,1)}, u32[]{:S(2)}) copy-start(bf16[96,96]{1,0:T(8,128)(2,1)} %param.36) | copy-start | bytes 55300
  139.0 36.7 %copy-start.3 = (bf16[512,768]{1,0:T(8,128)(2,1)}, bf16[512,768]{1,0:T(8,128)(2,1)S(1)}, u32[]{:S(2)}) copy-start(bf16[512,768]{1,0:T(8,128)(2,1)S(1)} %add_convert_fusion) | copy-start | bytes 2359300
  139.0 7.4 %copy-start.22 = (bf16[96,96]{1,0:T(8,128)(2,1)S(1)}, bf16[96,96]{1,0:T(8,128)(2,1)}, u32[]{:S(2)}) copy-start(bf16[96,96]{1,0:T(8,128)(2,1)} %param.37) | copy-start | bytes 55300
  139.0 15.3 %copy-start.23 = (bf16[96,96]{1,0:T(8,128)(2,1)S(1)}, bf16[96,96]{1,0:T(8,128)(2,1)}, u32[]{:S(2)}) copy-start(bf16[96,96]{1,0:T(8,128)(2,1)} %param.38) | copy-start | bytes 55300
  140.1 0.6 copy-start.31
  140.1 50.3 %copy-start.5 = (f32[512,96]{0,1:T(8,128)}, f32[512,96]{0,1:T(8,128)S(1)}, u32[]{:S(2)}) copy-start(f32[512,96]{0,1:T(8,128)S(1)} %get-tuple-element.84) | copy-start | bytes 589828
  140.8 123.1 %copy-start.6 = (bf16[512,96]{0,1:T(8,128)(2,1)}, bf16[512,96]{0,1:T(8,128)(2,1)S(1)}, u32[]{:S(2)}) copy-start(bf16[512,96]{0,1:T(8,128)(2,1)S(1)} %multiply_convert_fusion.11) | copy-start | bytes 294916
  154.3 21.4 %copy-start.9 = (bf16[1024,192]{0,1:T(8,128)(2,1)}, bf16[1024,192]{0,1:T(8,128)(2,1)S(1)}, u32[]{:S(2)}) copy-start(bf16[1024,192]{0,1:T(8,128)(2,1)S(1)} %copy.110) | copy-start | bytes 1179652
  162.3 13.4 %copy-start.17 = (bf16[1024,192]{0,1:T(8,128)(2,1)}, bf16[1024,192]{0,1:T(8,128)(2,1)S(1)}, u32[]{:S(2)}) copy-start(bf16[1024,192]{0,1:T(8,128)(2,1)S(1)} %copy.107) | copy-start | bytes 1179652
  175.7 10.0 %copy-start.29 = (f32[2,12,256]{2,1,0:T(8,128)}, f32[2,12,256]{2,1,0:T(8,128)S(1)}, u32[]{:S(2)}) copy-start(f32[2,12,256]{2,1,0:T(8,128)S(1)} %get-tuple-element.94) | copy-start | bytes 73732
  175.7 14.7 %copy-start.21 = (bf16[96,96]{1,0:T(8,128)(2,1)S(1)}, bf16[96,96]{1,0:T(8,128)(2,1)}, u32[]{:S(2)}) copy-start(bf16[96,96]{1,0:T(8,128)(2,1)} %param.39) | copy-start | bytes 55300
  175.7 15.0 %copy-start.27 = (bf16[96,384]{1,0:T(8,128)(2,1)S(1)}, bf16[96,384]{1,0:T(8,128)(2,1)}, u32[]{:S(2)}) copy-start(bf16[96,384]{1,0:T(8,128)(2,1)} %param.41) | copy-start | bytes 221188
  175.7 15.0 %copy-start.32 = (f32[96]{0:T(128)S(1)}, f32[96]{0:T(128)}, u32[]{:S(2)}) copy-start(f32[96]{0:T(128)} %param.40) | copy-start | bytes 1156
  190.4 3.0 copy-start.12
  190.7 2.7 copy-start.15
  190.7 2.7 copy-start.26
  190.7 3.2 copy-start.28
  190.8 3.2 copy-start.33
  190.8 4.1 copy-start.19
  193.5 5.0 copy-start.18
  193.9 0.9 copy-start.11
  195.0 69.9 %copy-start.7 = (f32[512,96]{0,1:T(8,128)}, f32[512,96]{0,1:T(8,128)S(1)}, u32[]{:S(2)}) copy-start(f32[512,96]{0,1:T(8,128)S(1)} %fusion.60) | copy-start | bytes 589828
  198.5 21.0 %copy-start.30 = (f32[2,12,256]{2,1,0:T(8,128)S(1)}, f32[2,12,256]{2,1,0:T(8,128)}, u32[]{:S(2)}) copy-start(f32[2,12,256]{2,1,0:T(8,128)} %copy-done.29) | copy-start | bytes 73732
  244.9 4.5 copy-start.2
  245.0 6.3 %copy-start.10 = (bf16[1024,192]{0,1:T(8,128)(2,1)S(1)}, bf16[1024,192]{0,1:T(8,128)(2,1)}, u32[]{:S(2)}) copy-start(bf16[1024,192]{0,1:T(8,128)(2,1)} %copy-done.9) | copy-start | bytes 1179652
  251.2 13.5 %copy-start.25 = (bf16[96,96]{1,0:T(8,128)(2,1)S(1)}, bf16[96,96]{1,0:T(8,128)(2,1)}, u32[]{:S(2)}) copy-start(bf16[96,96]{1,0:T(8,128)(2,1)} %param.36) | copy-start | bytes 55300
  251.2 13.7 %copy-start.13 = (bf16[512,96]{1,0:T(8,128)(2,1)S(1)}, bf16[512,96]{1,0:T(8,128)(2,1)}, u32[]{:S(2)}) copy-start(bf16[512,96]{1,0:T(8,128)(2,1)} %copy-done.12) | copy-start | bytes 294916
  251.2 159.9 %all-reduce.5.cloned.1.call-start = ((), (), s32[]{:S(2)}) async-start(), calls=%async_computation.4 | async-start | bytes 396288 | tf_op jit(solution)/shard_map/psum | solution.py:226
  263.9 24.3 %copy-start.4 = (bf16[512,768]{1,0:T(8,128)(2,1)S(1)}, bf16[512,768]{1,0:T(8,128)(2,1)}, u32[]{:S(2)}) copy-start(bf16[512,768]{1,0:T(8,128)(2,1)} %copy-done.3) | copy-start | bytes 2359300
  263.9 26.3 %copy-start.36 = (f32[96]{0:T(128)S(1)}, f32[96]{0:T(128)}, u32[]{:S(2)}) copy-start(f32[96]{0:T(128)} %copy-done.35) | copy-start | bytes 1156
  265.7 296.1 %copy-start.1 = (bf16[768,768]{1,0:T(8,128)(2,1)S(1)}, bf16[768,768]{1,0:T(8,128)(2,1)}, u32[]{:S(2)}) copy-start(bf16[768,768]{1,0:T(8,128)(2,1)} %param.29) | copy-start | bytes 3538948
  284.7 263.1 %all-reduce.7.cloned.1.call-start = ((), (), s32[]{:S(2)}) async-start(), calls=%async_computation.5 | async-start | bytes 1179648 | tf_op jit(solution)/shard_map/psum | solution.py:226
Sparse Core Ops, SparseCore 0:
  16.9 31.2 all-gather.2
  49.7 28.5 all-gather.4
  251.3 23.2 reduce-scatter.1
  284.8 126.2 all-reduce.4
  417.8 129.9 all-reduce.6
where the time goes:
time: 574 us; the launch traced here: 569 us
  waiting for transfers between devices  280 us (49%)
  matrix products  142 us (25%)
  local copies, waits for them, and re-layouts  78.5 us (14%)
  other arithmetic  38.2 us (7%)
  between operations  15 us (3%)
  blocking collectives  14.5 us (3%)
    psum x2, waiting for transfers between devices, per_device(): lax.psum((grad_down, grad_gate, grad_norm_in, grad_query, grad_key, grad_...  257 us
    dot_general x12, matrix products, product(): return jnp.dot(left_mat, right_mat, preferred_element_type=jnp.float32)  37.2 us
    unnamed x93, local copies, waits for them, and re-layouts  21.2 us
    dot_general x1, matrix products, per_device(): jnp.einsum('qrhe,krhe->rhqk', grad_attn, value_heads, preferred_element_t...  21 us
    all_gather x1, waiting for transfers between devices, per_device(): key_rows = lax.all_gather(key_local, 'blk', axis=0, tiled=True)  18.6 us
    convert_element_type x1, other arithmetic, per_device(): grad_scores = (probs * (grad_probs - row_terms)).astype(jnp.bfloat16)  16.3 us
    dot_general x1, matrix products, per_device(): jnp.einsum('qrhe,krhe->rhqk', queries, key_heads, preferred_element_type=...  13.9 us
    sub x1, matrix products, per_device(): weights_exp = jnp.exp(scores - row_max)  13.4 us
  transfers between devices with their start and end apart: 5, of which 4 were waited for; matrix products, arithmetic and copies ran while one was open for 13% of the time, Pallas kernels for 0%

commit v1 on v0

--- a/solution.py
+++ b/solution.py
@@ -43,6 +43,40 @@
         axis=2,
         dtype=jnp.int32,
     )
+
+
+def sum_everywhere(parts):
+    flat = jnp.concatenate([part.reshape(-1) for part in parts])
+    count = flat.shape[0]
+    lanes = 128
+    rows = -(-count // (lanes * 32)) * 32
+    low = jnp.pad(flat, (0, rows * lanes - count)).reshape(2, rows // 2, lanes).astype(jnp.bfloat16)
+    place = lax.axis_index("blk")
+    keep = lax.dynamic_index_in_dim(low, place % 2, 0, keepdims=False)
+    send = lax.dynamic_index_in_dim(low, 1 - place % 2, 0, keepdims=False)
+    blk_size, dp_size = lax.axis_size("blk"), lax.axis_size("dp")
+
+    def swap(value, axis, size, hop):
+        return lax.ppermute(value, axis, [(i, i ^ hop) for i in range(size)])
+
+    def add(left, right):
+        return (left.astype(jnp.float32) + right.astype(jnp.float32)).astype(jnp.bfloat16)
+
+    half = add(keep, swap(send, "blk", blk_size, 1))
+    for axis, size, start in (("blk", blk_size, 2), ("dp", dp_size, 1)):
+        hop = start
+        while hop < size:
+            half = add(half, swap(half, axis, size, hop))
+            hop *= 2
+    other = swap(half, "blk", blk_size, 1)
+    first = place % 2 == 0
+    whole = jnp.concatenate([jnp.where(first, half, other), jnp.where(first, other, half)])
+    whole = whole.reshape(-1).astype(jnp.float32)
+    out, at = [], 0
+    for part in parts:
+        out.append(whole[at : at + part.size].reshape(part.shape))
+        at += part.size
+    return out
 
 
 def per_device(
@@ -223,21 +257,19 @@
     grad_downed = (gate_open * grad_mixed).astype(jnp.bfloat16)
     grad_down = over_tokens(backbone_flat, grad_downed)
     grad_gate = jnp.sum(grad_mixed * (downed - state_flat), axis=0) * gate_open * (1.0 - gate_open)
-    summed = lax.psum(
-        (
-            grad_down,
-            grad_gate,
-            grad_norm_in,
-            grad_query,
-            grad_key,
-            grad_value,
-            grad_out,
-            grad_norm_mid,
-            grad_inner,
-            grad_outer,
-        ),
-        ("dp", "blk"),
-    )
+    parts = (
+        grad_down,
+        grad_gate,
+        grad_norm_in,
+        grad_query,
+        grad_key,
+        grad_value,
+        grad_out,
+        grad_norm_mid,
+        grad_inner,
+        grad_outer,
+    )
+    summed = sum_everywhere(parts)
     backbone_out = backbone_flat.reshape(shard_len, row_count, model_width)
     side_out = side_flat.astype(jnp.bfloat16).reshape(shard_len, row_count, side_width)
     state_out = state_grad.reshape(shard_len, row_count, side_width)

time: 574 us -> 338 us (0.59)
  waiting for transfers between devices: 280 us -> 41.6 us
  matrix products: 142 us -> 135 us
  starting transfers between devices: 0.42 us -> 6.52 us
    psum x2 -> x0, waiting for transfers between devices: 257 us -> none  [per_device(): lax.psum((grad_down, grad_gate, grad_norm_in, grad_query, grad_key, grad_...]
    ppermute x0 -> x6, waiting for transfers between devices: none -> 19.2 us  [swap(): return lax.ppermute(value, axis, [(i, i ^ hop) for i in range(size)])]
    unnamed x93 -> x73, local copies, waits for them, and re-layouts: 21.2 us -> 8.78 us
    reshape x0 -> x14, local copies, waits for them, and re-layouts: none -> 6.13 us  [the longest x7 3.73 us: sum_everywhere(): out.append(whole[at:at + part.size].reshape(part.shape))]
    ppermute x0 -> x6, starting transfers between devices: none -> 6.11 us  [swap(): return lax.ppermute(value, axis, [(i, i ^ hop) for i in range(size)])]
  transfers between devices with their start and end apart: 5 -> 9, of which waited for: 4 -> 8; matrix products, arithmetic and copies ran while one was open for 13% -> 22% of each run, Pallas kernels for 0% -> 0%
where the time goes in v1:
time: 338 us; the launch traced here: 333 us
  matrix products  135 us (40%)
  local copies, waits for them, and re-layouts  84.1 us (25%)
  waiting for transfers between devices  41.6 us (12%)
  other arithmetic  36.5 us (11%)
  between operations  14.8 us (4%)
  blocking collectives  14.5 us (4%)
  starting transfers between devices  6.52 us (2%)
    dot_general x12, matrix products, product(): return jnp.dot(left_mat, right_mat, preferred_element_type=jnp.float32)  38 us
    ppermute x6, waiting for transfers between devices, swap(): return lax.ppermute(value, axis, [(i, i ^ hop) for i in range(size)])  19.2 us
    all_gather x1, waiting for transfers between devices, per_device(): key_rows = lax.all_gather(key_local, 'blk', axis=0, tiled=True)  19.1 us
    dot_general x1, matrix products, per_device(): jnp.einsum('qrhe,krhe->rhqk', grad_attn, value_heads, preferred_element_t...  16.7 us
    convert_element_type x1, other arithmetic, per_device(): grad_scores = (probs * (grad_probs - row_terms)).astype(jnp.bfloat16)  16.2 us
    dot_general x1, matrix products, per_device(): jnp.einsum('qrhe,krhe->rhqk', queries, key_heads, preferred_element_type=...  13.9 us
    sub x1, matrix products, per_device(): weights_exp = jnp.exp(scores - row_max)  13.4 us
    dot_general x1, matrix products, per_device(): jnp.einsum('rhqk,krhe->rhqe', weights_exp.astype(jnp.bfloat16), value_hea...  13.2 us
  transfers between devices with their start and end apart: 9, of which 8 were waited for; matrix products, arithmetic and copies ran while one was open for 22% of the time, Pallas kernels for 0%

profile of v1, /device:TPU:0, one launch (start us, length us, event | category | flops | bytes accessed | tf_op | source)
XLA Modules:
  0.0 333.2 jit_solution(11343262403980587004)
XLA Ops:
  7.2 2.3 reshape.275
  9.5 2.0 multiply_reduce_fusion.2
  13.5 2.1 convolution_convert_fusion.1
  16.8 2.3 convolution_convert_fusion
  20.9 2.3 convolution_convert_fusion.2
  23.2 2.2 reshape.244
  29.1 19.1 %all-gather.3.cloned.1.call-done = bf16[1024,2,768]{2,1,0:T(2,128)(2,1)} async-done(((bf16[256,2,768]{2,1,0:T(2,128)(2,1)}), bf16[1024,2,768]{2,1,0:T(2,128)(2,1)}) %all-gather.3.cloned.1.call-update) | async-done | bytes 3145744 | tf_op jit(solution)/shard_map/all_gather | solution.py:121
  48.1 8.7 %copy.108 = bf16[1024,2,768]{0,2,1:T(8,128)(2,1)} copy(bf16[1024,2,768]{2,1,0:T(2,128)(2,1)} %all-gather.3.cloned.1.call-done) | data formatting | bytes 6291456 | tf_op jit(solution)/shard_map/all_gather | solution.py:121
  56.9 13.9 %fusion.1 = (f32[2,12,256]{2,1,0:T(8,128)S(1)}, f32[2,12,256,1024]{3,2,1,0:T(8,128)}) fusion(pred[2,256,1024]{2,1,0:T(8,128)(4,1)S(1)} %broadcast_compare_fusion, bf16[1024,2,12,64]{0,3,2,1:T(8,128)(2,1)} %bitcast.90, bf16[256,2,12,64]{3,2,1,0:T(8,128)(2,1)} %reshape.244), kind=kOutput, calls=%fused_computation.7 | convolution fusion | flops 824174592 | bytes 29646848 | tf_op jit(solution)/shard_map/qrhe,krhe->rhqk/dot_general | solution.py:130
  70.8 12.7 %fusion.3 = f32[2,12,256]{2,1,0:T(8,128)S(1)} fusion(f32[2,12,256,1024]{3,2,1,0:T(8,128)} %get-tuple-element.93, f32[2,12,256]{2,1,0:T(8,128)S(1)} %broadcast_maximum_fusion, pred[2,256,1024]{2,1,0:T(8,128)(4,1)S(1)} %broadcast_compare_fusion), kind=kLoop, calls=%fused_computation.9 | loop fusion | flops 31451136 | bytes 25739264 | tf_op jit(solution)/shard_map/reduce_sum | solution.py:137
  83.5 8.7 %copy.110 = bf16[1024,2,768]{0,2,1:T(8,128)(2,1)} copy(bf16[1024,2,768]{2,1,0:T(2,128)(2,1)} %all-gather.5.cloned.1.call-done) | data formatting | bytes 6291456 | tf_op jit(solution)/shard_map/all_gather | solution.py:124
  92.2 13.2 %fusion.29 = bf16[256,2,12,64]{0,3,2,1:T(8,128)(2,1)} fusion(bf16[1024,2,12,64]{0,3,2,1:T(8,128)(2,1)} %bitcast.91, f32[2,12,256,1024]{3,2,1,0:T(8,128)} %get-tuple-element.93, f32[2,12,256]{2,1,0:T(8,128)S(1)} %broadcast_maximum_fusion, pred[2,256,1024]{2,1,0:T(8,128)(4,1)S(1)} %broadcast_compare_fusion, f32[256,2,12]{0,2,1:T(8,128)S(1)} %bitcast.106), kind=kOutput, calls=%fused_computation.43 | convolution fusion | flops 837550080 | bytes 29671424 | tf_op jit(solution)/shard_map/rhqk,krhe->rhqe/dot_general | solution.py:138
  105.3 4.7 %copy.111 = bf16[256,2,12,64]{3,2,1,0:T(8,128)(2,1)} copy(bf16[256,2,12,64]{0,3,2,1:T(8,128)(2,1)} %fusion.29) | data formatting | bytes 1572864 | tf_op jit(solution)/shard_map/convert_element_type | solution.py:146
  110.0 4.4 %convert_element_type.200 = bf16[512,768]{1,0:T(8,128)(2,1)} reshape(bf16[256,2,12,64]{3,2,1,0:T(8,128)(2,1)} %copy.111) | data formatting | bytes 1572864 | tf_op jit(solution)/shard_map/convert_element_type | solution.py:146
  114.4 3.1 multiply_reduce_fusion.1
  117.5 21.6 %add_convert_fusion = bf16[512,768]{1,0:T(8,128)(2,1)S(1)} fusion(f32[512,768]{1,0:T(8,128)} %get-tuple-element.95, bf16[3072,768]{1,0:T(8,128)(2,1)} %param.32, bf16[768,3072]{1,0:T(8,128)(2,1)} %param.31, f32[768]{0:T(1024)S(1)} %convert_element_type.201, f32[512]{0:T(512)S(1)} %add_rsqrt_fusion.1), kind=kOutput, calls=%fused_computation.46 | convolution fusion | flops 4936040448 | bytes 11801600 | tf_op jit(solution)/shard_map/dot_general | solution.py:17
  140.7 2.9 reshape.252
  143.6 2.4 copy.119
  146.5 7.2 %all_gather.15 = bf16[1024,192]{1,0:T(8,128)(2,1)S(1)} all-gather(bf16[256,192]{1,0:T(8,128)(2,1)S(1)} %reshape.253), channel_id=1, replica_groups=mesh['dp'=8,'blk'=4] {'blk'}, dimensions={0}, use_global_device_ids=true | all-gather | bytes 491520 | tf_op jit(solution)/shard_map/all_gather | solution.py:161
  154.4 7.3 %all_gather.14 = bf16[1024,192]{1,0:T(8,128)(2,1)S(1)} all-gather(bf16[256,192]{1,0:T(8,128)(2,1)S(1)} %reshape.250), channel_id=1, replica_groups=mesh['dp'=8,'blk'=4] {'blk'}, dimensions={0}, use_global_device_ids=true | all-gather | bytes 491520 | tf_op jit(solution)/shard_map/all_gather | solution.py:164
  161.9 13.4 %fusion.111 = (f32[2,12,256]{2,1,0:T(8,128)S(1)}, f32[2,12,256,1024]{3,2,1,0:T(8,128)}) fusion(pred[2,256,1024]{2,1,0:T(8,128)(4,1)S(1)} %broadcast_compare_fusion, bf16[256,2,12,8]{0,3,2,1:T(8,128)(2,1)S(1)} %copy.119, bf16[1024,2,12,8]{0,3,2,1:T(8,128)(2,1)S(1)} %bitcast.93), kind=kOutput, calls=%fused_computation.187 | convolution fusion | flops 125830144 | bytes 26206208 | tf_op jit(solution)/shard_map/sub | solution.py:181
  175.2 10.0 %fusion.45 = bf16[256,2,12,8]{0,3,2,1:T(8,128)(2,1)S(1)} fusion(bf16[1024,2,12,8]{0,3,2,1:T(8,128)(2,1)S(1)} %bitcast.103, f32[2,12,256,1024]{3,2,1,0:T(8,128)} %get-tuple-element.98, f32[2,12,256]{2,1,0:T(8,128)S(1)} %get-tuple-element.97), kind=kOutput, calls=%fused_computation.74 | convolution fusion | flops 113295360 | bytes 25681920 | tf_op jit(solution)/shard_map/rhqk,krhe->qrhe/dot_general | solution.py:185
  185.2 2.9 copy.120
  188.2 2.4 convert_element_type.214
  191.7 3.6 %multiply_convert_fusion.8 = (bf16[512,384]{1,0:T(8,128)(2,1)}, f32[512,384]{1,0:T(8,128)S(1)}, f32[512,384]{1,0:T(8,128)S(1)}) fusion(bf16[96,384]{1,0:T(8,128)(2,1)} %param.41, f32[512,96]{0,1:T(8,128)S(1)} %get-tuple-element.100, f32[96]{0:T(128)S(1)} %copy-done.25, f32[512]{0:T(512)S(1)} %fusion.68), kind=kOutput, calls=%fused_computation.85 | convolution fusion | flops 50675712 | bytes 2238848 | tf_op jit(solution)/shard_map/dot_general | solution.py:17
  199.3 2.9 reshape.257
  202.2 2.0 copy.125
  204.2 16.7 %multiply_reduce_fusion = (f32[2,12,256]{2,1,0:T(8,128)S(1)}, f32[2,12,256,1024]{3,2,1,0:T(8,128)}) fusion(f32[2,12,256,1024]{3,2,1,0:T(8,128)} %get-tuple-element.98, f32[2,12,256]{2,1,0:T(8,128)S(1)} %get-tuple-element.97, bf16[256,2,12,8]{0,3,2,1:T(8,128)(2,1)} %copy.125, bf16[1024,2,12,8]{0,3,2,1:T(8,128)(2,1)} %bitcast.104), kind=kOutput, calls=%fused_computation.2 | convolution fusion | flops 119531520 | bytes 50872320 | tf_op jit(solution)/shard_map/qrhe,krhe->rhqk/dot_general | solution.py:212
  220.9 9.9 %fusion.37 = bf16[2,12,8,1024]{3,2,1,0:T(8,128)(2,1)} fusion(bf16[256,2,12,8]{0,3,2,1:T(8,128)(2,1)S(1)} %copy-done.16, f32[2,12,256,1024]{3,2,1,0:T(8,128)} %get-tuple-element.98, f32[2,12,256]{2,1,0:T(8,128)S(1)} %get-tuple-element.97), kind=kOutput, calls=%fused_computation.57 | convolution fusion | flops 113442816 | bytes 25681920 | tf_op jit(solution)/shard_map/rhqk,qrhe->krhe/dot_general | solution.py:226
  230.8 16.2 %multiply_convert_fusion = bf16[2,12,256,1024]{3,2,1,0:T(8,128)(2,1)S(1)} fusion(f32[2,12,256,1024]{3,2,1,0:T(8,128)} %get-tuple-element.104, f32[2,12,256]{2,1,0:T(8,128)S(1)} %get-tuple-element.103, f32[2,12,256,1024]{3,2,1,0:T(8,128)} %get-tuple-element.98, f32[2,12,256]{2,1,0:T(8,128)S(1)} %get-tuple-element.97), kind=kLoop, calls=%fused_computation.1 | loop fusion | flops 25165824 | bytes 62963712 | tf_op jit(solution)/shard_map/convert_element_type | solution.py:216
  247.1 1.7 fusion.36
  248.9 2.8 copy-done.2
  257.0 8.1 %fusion.48 = bf16[256,2,12,8]{0,3,2,1:T(8,128)(2,1)S(1)} fusion(bf16[1024,2,12,8]{0,3,2,1:T(8,128)(2,1)S(1)} %bitcast.94, bf16[2,12,256,1024]{3,2,1,0:T(8,128)(2,1)} %copy-done.2), kind=kOutput, calls=%fused_computation.75 | convolution fusion | flops 100761600 | bytes 13074432 | tf_op jit(solution)/shard_map/rhqk,krhe->qrhe/dot_general | solution.py:218
  265.1 2.9 copy.126
  268.1 2.5 convert_element_type.225
  271.8 1.3 convolution_convert_fusion.8
  274.5 3.2 reduce-scatter.2.cloned.1.call-done
  281.6 1.3 multiply_reduce_fusion.5
  285.1 4.2 %concatenate.12 = bf16[184608]{0:T(1024)(128)(2,1)S(1)} concatenate(bf16[73728]{0:T(1024)(128)(2,1)S(1)} %reshape.261, bf16[96]{0:T(256)(128)(2,1)S(1)} %multiply_convert_fusion.13, bf16[96]{0:T(256)(128)(2,1)S(1)} %get-tuple-element.67, bf16[9216]{0:T(1024)(128)(2,1)S(1)} %reshape.262, bf16[9216]{0:T(1024)(128)(2,1)S(1)} %reshape.263, bf16[9216]{0:T(1024)(128)(2,1)S(1)} %reshape.264, ...), dimensions={0} | concatenate | bytes 738432 | tf_op jit(solution)/shard_map/concatenate | solution.py:49
  289.5 1.4 collective-permute-done
  291.3 6.4 %collective-permute-done.1 = bf16[736,128]{1,0:T(8,128)(2,1)S(1)} collective-permute-done((bf16[736,128]{1,0:T(8,128)(2,1)S(1)}, bf16[736,128]{1,0:T(8,128)(2,1)S(1)}, u32[]{:S(2)}, u32[]{:S(2)}) %collective-permute-start.1) | collective-permute-done | bytes 188448 | tf_op jit(solution)/shard_map/ppermute | solution.py:60
  297.9 1.5 collective-permute-start.2
  299.4 4.5 %collective-permute-done.2 = bf16[736,128]{1,0:T(8,128)(2,1)S(1)} collective-permute-done((bf16[736,128]{1,0:T(8,128)(2,1)S(1)}, bf16[736,128]{1,0:T(8,128)(2,1)S(1)}, u32[]{:S(2)}, u32[]{:S(2)}) %collective-permute-start.2) | collective-permute-done | bytes 188448 | tf_op jit(solution)/shard_map/ppermute | solution.py:60
  303.9 1.6 collective-permute-start.3
  305.5 2.8 reshape.249
  308.3 1.2 collective-permute-done.3
  309.6 2.5 collective-permute-start.4
  313.2 5.3 %collective-permute-done.4 = bf16[736,128]{1,0:T(8,128)(2,1)S(1)} collective-permute-done((bf16[736,128]{1,0:T(8,128)(2,1)S(1)}, bf16[736,128]{1,0:T(8,128)(2,1)S(1)}, u32[]{:S(2)}, u32[]{:S(2)}) %collective-permute-start.4) | collective-permute-done | bytes 188448 | tf_op jit(solution)/shard_map/ppermute | solution.py:60
  (172 shorter events, 40.0 us)
Async XLA Ops:
  7.2 107.2 %copy-start = (bf16[768,768]{1,0:T(8,128)(2,1)S(1)}, bf16[768,768]{1,0:T(8,128)(2,1)}, u32[]{:S(2)}) copy-start(bf16[768,768]{1,0:T(8,128)(2,1)} %param.29) | copy-start | bytes 3538948
  7.2 41.0 %all-gather.3.cloned.1.call-start = ((), (), s32[]{:S(2)}) async-start(), calls=%async_computation.1 | async-start | bytes 3932160 | tf_op jit(solution)/shard_map/all_gather | solution.py:121
  12.6 0.9 copy-start.12
  13.5 7.2 %copy-start.32 = (s32[2,8]{1,0:T(2,128)S(1)}, s32[2,8]{1,0:T(2,128)}, u32[]{:S(2)}) copy-start(s32[2,8]{1,0:T(2,128)} %param.24) | copy-start | bytes 196
  16.8 8.7 %copy-start.31 = (bf16[768]{0:T(1024)(128)(2,1)S(1)}, bf16[768]{0:T(1024)(128)(2,1)}, u32[]{:S(2)}) copy-start(bf16[768]{0:T(1024)(128)(2,1)} %param.30) | copy-start | bytes 4612
  16.8 11.9 %copy-start.33 = (f32[96]{0:T(128)S(1)}, f32[96]{0:T(128)}, u32[]{:S(2)}) copy-start(f32[96]{0:T(128)} %param.34) | copy-start | bytes 1156
  16.8 66.7 %all-gather.5.cloned.1.call-start = ((), (), s32[]{:S(2)}) async-start(), calls=%async_computation.2 | async-start | bytes 3932160 | tf_op jit(solution)/shard_map/all_gather | solution.py:124
  20.3 257.4 %reduce-scatter.2.cloned.1.call-start = ((), (), s32[]{:S(2)}) async-start(), calls=%async_computation.3 | async-start | bytes 983040 | tf_op jit(solution)/shard_map/reduce_scatter | solution.py:236
  26.6 112.6 %copy-start.6 = (f32[512,96]{0,1:T(8,128)}, f32[512,96]{0,1:T(8,128)S(1)}, u32[]{:S(2)}) copy-start(f32[512,96]{0,1:T(8,128)S(1)} %copy.113) | copy-start | bytes 589828
  27.7 1.0 copy-start.10
  28.7 110.5 %copy-start.28 = (f32[96]{0:T(128)}, f32[96]{0:T(128)S(1)}, u32[]{:S(2)}) copy-start(f32[96]{0:T(128)S(1)} %get-tuple-element.75) | copy-start | bytes 1156
  28.7 110.5 %copy-start.30 = (f32[96]{0:T(128)}, f32[96]{0:T(128)S(1)}, u32[]{:S(2)}) copy-start(f32[96]{0:T(128)S(1)} %get-tuple-element.76) | copy-start | bytes 1156
  117.5 21.7 %copy-start.15 = (bf16[768,96]{0,1:T(8,128)(2,1)S(1)}, bf16[768,96]{0,1:T(8,128)(2,1)}, u32[]{:S(2)}) copy-start(bf16[768,96]{0,1:T(8,128)(2,1)} %param.33) | copy-start | bytes 442372
  117.5 22.8 %copy-start.27 = (f32[96]{0:T(128)S(1)}, f32[96]{0:T(128)}, u32[]{:S(2)}) copy-start(f32[96]{0:T(128)} %param.35) | copy-start | bytes 1156
  117.5 22.9 %copy-start.20 = (bf16[96,96]{1,0:T(8,128)(2,1)S(1)}, bf16[96,96]{1,0:T(8,128)(2,1)}, u32[]{:S(2)}) copy-start(bf16[96,96]{1,0:T(8,128)(2,1)} %param.36) | copy-start | bytes 55300
  139.1 143.8 %copy-start.3 = (bf16[512,768]{1,0:T(8,128)(2,1)}, bf16[512,768]{1,0:T(8,128)(2,1)S(1)}, u32[]{:S(2)}) copy-start(bf16[512,768]{1,0:T(8,128)(2,1)S(1)} %add_convert_fusion) | copy-start | bytes 2359300
  139.2 6.8 %copy-start.18 = (bf16[96,96]{1,0:T(8,128)(2,1)S(1)}, bf16[96,96]{1,0:T(8,128)(2,1)}, u32[]{:S(2)}) copy-start(bf16[96,96]{1,0:T(8,128)(2,1)} %param.37) | copy-start | bytes 55300
  139.2 14.7 %copy-start.19 = (bf16[96,96]{1,0:T(8,128)(2,1)S(1)}, bf16[96,96]{1,0:T(8,128)(2,1)}, u32[]{:S(2)}) copy-start(bf16[96,96]{1,0:T(8,128)(2,1)} %param.38) | copy-start | bytes 55300
  153.9 21.3 %copy-start.7 = (bf16[1024,192]{0,1:T(8,128)(2,1)}, bf16[1024,192]{0,1:T(8,128)(2,1)S(1)}, u32[]{:S(2)}) copy-start(bf16[1024,192]{0,1:T(8,128)(2,1)S(1)} %copy.118) | copy-start | bytes 1179652
  161.8 13.4 %copy-start.13 = (bf16[1024,192]{0,1:T(8,128)(2,1)}, bf16[1024,192]{0,1:T(8,128)(2,1)S(1)}, u32[]{:S(2)}) copy-start(bf16[1024,192]{0,1:T(8,128)(2,1)S(1)} %copy.115) | copy-start | bytes 1179652
  175.2 15.3 %copy-start.17 = (bf16[96,96]{1,0:T(8,128)(2,1)S(1)}, bf16[96,96]{1,0:T(8,128)(2,1)}, u32[]{:S(2)}) copy-start(bf16[96,96]{1,0:T(8,128)(2,1)} %param.39) | copy-start | bytes 55300
  175.2 16.5 %copy-start.25 = (f32[96]{0:T(128)S(1)}, f32[96]{0:T(128)}, u32[]{:S(2)}) copy-start(f32[96]{0:T(128)} %param.40) | copy-start | bytes 1156
  191.7 3.7 %copy-start.11 = (bf16[256,2,96]{2,1,0:T(2,128)(2,1)S(1)}, bf16[256,2,96]{2,1,0:T(2,128)(2,1)}, u32[]{:S(2)}) copy-start(bf16[256,2,96]{2,1,0:T(2,128)(2,1)} %copy-done.10) | copy-start | bytes 294916
  191.7 3.7 %copy-start.21 = (bf16[384,96]{0,1:T(8,128)(2,1)S(1)}, bf16[384,96]{0,1:T(8,128)(2,1)}, u32[]{:S(2)}) copy-start(bf16[384,96]{0,1:T(8,128)(2,1)} %param.42) | copy-start | bytes 221188
  191.7 5.0 %copy-start.24 = (bf16[96,384]{1,0:T(8,128)(2,1)S(1)}, bf16[96,384]{1,0:T(8,128)(2,1)}, u32[]{:S(2)}) copy-start(bf16[96,384]{1,0:T(8,128)(2,1)} %param.41) | copy-start | bytes 221188
  191.7 5.9 %copy-start.14 = (bf16[512,96]{0,1:T(8,128)(2,1)S(1)}, bf16[512,96]{0,1:T(8,128)(2,1)}, u32[]{:S(2)}) copy-start(bf16[512,96]{0,1:T(8,128)(2,1)} %copy.123) | copy-start | bytes 294916
  191.7 5.9 %copy-start.26 = (f32[96]{0:T(128)S(1)}, f32[96]{0:T(128)}, u32[]{:S(2)}) copy-start(f32[96]{0:T(128)} %param.40) | copy-start | bytes 1156
  197.8 0.7 copy-start.4
  204.2 16.7 %copy-start.16 = (bf16[256,2,12,8]{0,3,2,1:T(8,128)(2,1)S(1)}, bf16[256,2,12,8]{0,3,2,1:T(8,128)(2,1)}, u32[]{:S(2)}) copy-start(bf16[256,2,12,8]{0,3,2,1:T(8,128)(2,1)} %copy.125) | copy-start | bytes 294916
  247.1 4.5 %copy-start.2 = (bf16[2,12,256,1024]{3,2,1,0:T(8,128)(2,1)}, bf16[2,12,256,1024]{3,2,1,0:T(8,128)(2,1)S(1)}, u32[]{:S(2)}) copy-start(bf16[2,12,256,1024]{3,2,1,0:T(8,128)(2,1)S(1)} %multiply_convert_fusion) | copy-start | bytes 37748740
  247.1 7.1 %copy-start.5 = (f32[512,96]{0,1:T(8,128)S(1)}, f32[512,96]{0,1:T(8,128)}, u32[]{:S(2)}) copy-start(f32[512,96]{0,1:T(8,128)} %copy-done.4) | copy-start | bytes 589828
  247.1 9.9 %copy-start.8 = (bf16[1024,192]{0,1:T(8,128)(2,1)S(1)}, bf16[1024,192]{0,1:T(8,128)(2,1)}, u32[]{:S(2)}) copy-start(bf16[1024,192]{0,1:T(8,128)(2,1)} %copy-done.7) | copy-start | bytes 1179652
  270.6 14.5 %copy-start.23 = (bf16[9216]{0:T(1024)(128)(2,1)S(1)}, bf16[9216]{0:T(1024)(128)(2,1)}, u32[]{:S(2)}) copy-start(bf16[9216]{0:T(1024)(128)(2,1)} %reshape.265) | copy-start | bytes 55300
  273.1 39.0 %copy-start.9 = (bf16[512,384]{1,0:T(8,128)(2,1)S(1)}, bf16[512,384]{1,0:T(8,128)(2,1)}, u32[]{:S(2)}) copy-start(bf16[512,384]{1,0:T(8,128)(2,1)} %get-tuple-element.71) | copy-start | bytes 1179652
  273.1 39.0 %copy-start.22 = (bf16[384,96]{0,1:T(8,128)(2,1)S(1)}, bf16[384,96]{0,1:T(8,128)(2,1)}, u32[]{:S(2)}) copy-start(bf16[384,96]{0,1:T(8,128)(2,1)} %param.42) | copy-start | bytes 221188
  278.9 39.7 %copy-start.29 = (f32[96]{0:T(128)S(1)}, f32[96]{0:T(128)}, u32[]{:S(2)}) copy-start(f32[96]{0:T(128)} %copy-done.28) | copy-start | bytes 1156
  289.4 1.5 collective-permute-start
  291.0 6.8 %collective-permute-start.1 = (bf16[736,128]{1,0:T(8,128)(2,1)S(1)}, bf16[736,128]{1,0:T(8,128)(2,1)S(1)}, u32[]{:S(2)}, u32[]{:S(2)}) collective-permute-start(bf16[736,128]{1,0:T(8,128)(2,1)S(1)} %fusion.60), channel_id=1, source_target_pairs={{0,2},{1,3},{2,0},{3,1},{4,6},{5,7},{6,4},{7,5},{8,10},{9,11},{10,... | collective-permute-start | bytes 565256 | tf_op jit(solution)/shard_map/ppermute | solution.py:60
  297.8 28.7 %copy-start.1 = (bf16[768,768]{1,0:T(8,128)(2,1)S(1)}, bf16[768,768]{1,0:T(8,128)(2,1)}, u32[]{:S(2)}) copy-start(bf16[768,768]{1,0:T(8,128)(2,1)} %param.29) | copy-start | bytes 3538948
  297.9 6.0 %collective-permute-start.2 = (bf16[736,128]{1,0:T(8,128)(2,1)S(1)}, bf16[736,128]{1,0:T(8,128)(2,1)S(1)}, u32[]{:S(2)}, u32[]{:S(2)}) collective-permute-start(bf16[736,128]{1,0:T(8,128)(2,1)S(1)} %add_convert_fusion.5), channel_id=1, source_target_pairs={{0,4},{4,0},{8,12},{12,8},{16,20},{20,16},{24,28},{28,24},{1,5},{5... | collective-permute-start | bytes 565256 | tf_op jit(solution)/shard_map/ppermute | solution.py:60
  303.9 5.6 %collective-permute-start.3 = (bf16[736,128]{1,0:T(8,128)(2,1)S(1)}, bf16[736,128]{1,0:T(8,128)(2,1)S(1)}, u32[]{:S(2)}, u32[]{:S(2)}) collective-permute-start(bf16[736,128]{1,0:T(8,128)(2,1)S(1)} %add_convert_fusion.4), channel_id=1, source_target_pairs={{0,8},{4,12},{8,0},{12,4},{16,24},{20,28},{24,16},{28,20},{1,9},{5... | collective-permute-start | bytes 565256 | tf_op jit(solution)/shard_map/ppermute | solution.py:60
  309.6 8.9 %collective-permute-start.4 = (bf16[736,128]{1,0:T(8,128)(2,1)S(1)}, bf16[736,128]{1,0:T(8,128)(2,1)S(1)}, u32[]{:S(2)}, u32[]{:S(2)}) collective-permute-start(bf16[736,128]{1,0:T(8,128)(2,1)S(1)} %add_convert_fusion.3), channel_id=1, source_target_pairs={{0,16},{4,20},{8,24},{12,28},{16,0},{20,4},{24,8},{28,12},{1,17},{... | collective-permute-start | bytes 565256 | tf_op jit(solution)/shard_map/ppermute | solution.py:60
  318.6 1.5 collective-permute-start.5
Sparse Core Ops, SparseCore 0:
  16.9 31.2 all-gather.2
  49.7 28.5 all-gather.4
  254.4 23.3 reduce-scatter.1

commit v2 on v0

v2 whole, which is shorter than its diff:
```python
import math

import jax
import jax.numpy as jnp
from jax import lax
from jax.experimental import pallas as pl
from jax.experimental.pallas import tpu as pltpu
from jax.sharding import PartitionSpec as P

HEADS = 12
SHEADS = 12
EPS = 1e-06
LOG2E = math.log2(math.e)
FAR = 2.0**100
LOW_TOTAL, HIGH_TOTAL = 2.0**-80, 2.0**100
VMEM_BYTES = 60 * 2**20

f32, bf16, i32 = jnp.float32, jnp.bfloat16, jnp.int32


def nn(left, right):
    return jnp.dot(left, right, preferred_element_type=f32)


def nt(left, right):
    return lax.dot_general(left, right, (((1,), (1,)), ((), ())), preferred_element_type=f32)


def ones_where(condition):
    return jnp.where(condition, 1.0, 0.0).astype(bf16)


def iota(shape, dim):
    return lax.broadcasted_iota(i32, shape, dim)


def eye(size):
    return ones_where(iota((size, size), 0) == iota((size, size), 1))


def norm_lanes(value, gain):
    return value * lax.rsqrt(jnp.mean(value * value, axis=1, keepdims=True) + EPS) * gain


def gelu(value):
    return 0.5 * value * (1.0 + lax.erf(value * math.sqrt(0.5)))


def gelu_slope(value):
    bell = jnp.exp2(value * value * (-0.5 * LOG2E)) * (1.0 / math.sqrt(2.0 * math.pi))
    return 0.5 * (1.0 + lax.erf(value * math.sqrt(0.5))) + value * bell


def kernel_call(body, outs, ins, *, scratch=(), whole=(), scalars=(), cost=(0, 0, 0)):
    specs = [
        pl.BlockSpec(
            memory_space=pl.ANY if i in whole else pltpu.SMEM if i in scalars else pltpu.VMEM
        )
        for i in range(len(ins))
    ]
    return pl.pallas_call(
        body,
        out_shape=[jax.ShapeDtypeStruct(shape, kind) for shape, kind in outs],
        in_specs=specs,
        out_specs=[pl.BlockSpec(memory_space=pltpu.VMEM)] * len(outs),
        scratch_shapes=list(scratch),
        compiler_params=pltpu.CompilerParams(vmem_limit_bytes=VMEM_BYTES),
        cost_estimate=pl.CostEstimate(flops=cost[0], bytes_accessed=cost[1], transcendentals=cost[2]),
    )(*ins)


def doubled(rows, columns, feature, transposed):
    wide, thin = iota((rows, columns), 0), iota((rows, columns), 1)
    if not transposed:
        wide, thin = thin, wide
    source = (wide // (2 * feature)) * feature + wide % feature
    return ones_where(source == thin)


def prepare_body(
    w_value, w_down, s_query, s_key, s_value, s_out, s_inner, s_outer, value_t, dup, dup_t, tall_t, wide_t
):
    width, side = w_down.shape
    feature = side // SHEADS
    hidden = s_inner.shape[1]
    value_t[...] = nt(eye(width), w_value[...]).astype(bf16)
    spread = doubled(side, dup.shape[1], feature, False)
    dup[0:side] = nn(s_key[...], spread).astype(bf16)
    dup[side : 2 * side] = nn(s_value[...], spread).astype(bf16)
    spread_t = doubled(2 * side, side, feature, True)
    for i, weight in enumerate((s_query, s_key, s_value)):
        dup_t[2 * side * i : 2 * side * (i + 1)] = nt(spread_t, weight[...]).astype(bf16)
    one = eye(side)
    tall_t[0:side] = nt(one, s_out[...]).astype(bf16)
    tall_t[side : side + hidden] = nt(eye(hidden), s_inner[...]).astype(bf16)
    wide_t[:, 0:hidden] = nt(one, s_outer[...]).astype(bf16)
    wide_t[:, hidden : hidden + width] = nt(one, w_down[...]).astype(bf16)


def project(tokens, gain, w_query, w_key, value_t, scale, queries):
    normed = norm_lanes(tokens.astype(f32), gain.astype(f32)).astype(bf16)
    query = (nn(normed[0:queries], w_query[...]) * scale).astype(bf16)
    return query, nn(normed, w_key[...]).astype(bf16), nt(value_t[...], normed).astype(bf16)


def first_body(own, mate, norm_in, w_query, w_key, value_t, query, key, value):
    span, width = own.shape
    scale = LOG2E * (width // HEADS) ** -0.5
    tokens = jnp.concatenate([own[...], mate[...]], axis=0)
    query[...], key[...], value[...] = project(
        tokens, norm_in[...], w_query, w_key, value_t, scale, span
    )


def bounds(doc_lengths, row):
    starts, ends, at = [], [], jnp.int32(0)
    for d in range(doc_lengths.shape[1]):
        starts.append(at)
        at = at + doc_lengths[row, d]
        ends.append(at)
    return starts, ends


def in_doc(doc_lengths, row, blocks, span, shape, token_dim):
    starts, ends = bounds(doc_lengths, row)
    parts = []
    part_shape = list(shape)
    part_shape[token_dim] = span
    number = iota(tuple(part_shape), 1 - token_dim)
    first = jnp.zeros(tuple(part_shape), i32)
    last = first
    for d, (start, end) in enumerate(zip(starts, ends)):
        first = jnp.where(number == d, start, first)
        last = jnp.where(number == d, end, last)
    for block in blocks:
        position = iota(tuple(part_shape), token_dim) + block * span
        parts.append(jnp.where((position >= first) & (position < last), 1.0, 0.0))
    return jnp.concatenate(parts, axis=token_dim)


def out_of_range(totals):
    lowest, highest = jnp.min(totals), jnp.max(totals)
    return jnp.logical_not((lowest > LOW_TOTAL) & (highest < HIGH_TOTAL))


def backbone_body(
    doc_lengths,
    own,
    far,
    far_mate,
    query_own,
    key_near,
    value_near,
    norm_in,
    w_query,
    w_key,
    value_t,
    norm_mid,
    wide_t,
    columns,
    state_own,
    side_far,
    w_out_hbm,
    w_inner_hbm,
    w_outer_hbm,
    out_own,
    out_far,
    sn_rows,
    sn_t,
    mixed_t,
    lead_t,
    query,
    key,
    value,
    key_doc,
    query_doc,
    totals,
    attended,
    after,
    w_out,
    w_inner,
    w_outer,
    sems,
):
    copies = [
        pltpu.make_async_copy(source, target, sems.at[i])
        for i, (source, target) in enumerate(
            ((w_out_hbm, w_out), (w_inner_hbm, w_inner), (w_outer_hbm, w_outer))
        )
    ]
    for copy in copies:
        copy.start()
    span, width = own.shape
    head = width // HEADS
    stride = value.shape[0] // HEADS
    place = lax.axis_index("blk")
    half = lax.axis_size("blk") // 2
    row = place // half
    near, opposite = place ^ 1, place ^ half
    opposite_near = opposite ^ 1

    tokens = jnp.concatenate([far[...], far_mate[...]], axis=0)
    query_far, key_far, value_far = project(
        tokens, norm_in[...], w_query, w_key, value_t, LOG2E * head**-0.5, span
    )
    query[0:span] = query_own[...]
    query[span : 2 * span] = query_far
    key[0 : 2 * span] = key_near[...]
    key[2 * span : 4 * span] = key_far
    for h in range(HEADS):
        base = h * stride
        value[base : base + head, 0 : 2 * span] = value_near[h * head : (h + 1) * head]
        value[base : base + head, 2 * span : 4 * span] = value_far[h * head : (h + 1) * head]
        value[base + head : base + stride] = jnp.ones((stride - head, 4 * span), bf16)
    keys_in = in_doc(doc_lengths, row, (place, near, opposite, opposite_near), span, (4 * span, 128), 0)
    key_doc[...] = (keys_in - 1.0).astype(bf16)
    query_doc[...] = (
        in_doc(doc_lengths, row, (place, opposite), span, (2 * span, 128), 0) * FAR
    ).astype(bf16)

    def attend(shifted):
        def pair(j, carry):
            lanes = pl.ds(pl.multiple_of(j * 128, 128), 128)
            keys = jnp.concatenate([key[:, lanes], key_doc[...]], axis=1)
            results = []
            for side in range(128 // head):
                mine = ones_where(iota((1, 128), 1) // head == side)
                queries = jnp.concatenate([query[:, lanes] * mine, query_doc[...]], axis=1)
                scores = nt(keys, queries)
                if shifted:
                    scores = scores - jnp.max(scores, axis=0, keepdims=True)
                weights = jnp.exp2(scores).astype(bf16)
                at = (j * (128 // head) + side) * stride
                summed = nn(value[pl.ds(pl.multiple_of(at, 16), stride), :], weights)
                total = summed[head : head + 1]
                slot = pl.multiple_of((j * (128 // head) + side) * 8, 8)
                totals[pl.ds(slot, 8), :] = summed[head : head + 8]
                results.append(summed[0:head] * (1.0 / total))
            joined = jnp.concatenate(results, axis=0)
            attended[:, lanes] = joined.T.astype(bf16)
            return carry

        lax.fori_loop(0, width // 128, pair, 0)

    attend(False)

    @pl.when(out_of_range(totals[...]))
    def _():
        attend(True)

    copies[0].wait()
    after[0:span] = own[...].astype(f32) + nn(attended[0:span], w_out[...])
    after[span : 2 * span] = far[...].astype(f32) + nn(attended[span : 2 * span], w_out[...])
    middle = norm_lanes(after[...], norm_mid[...].astype(f32)).astype(bf16)
    copies[1].wait()
    copies[2].wait()
    hidden = w_inner.shape[1]
    step = width
    result = after[...]
    for at in range(0, hidden, step):
        act = gelu(nn(middle, w_inner[:, at : at + step])).astype(bf16)
        result = result + nn(act, w_outer[at : at + step, :])
    out = result.astype(bf16)
    out_own[...] = out[0:span]
    out_far[...] = out[span : 2 * span]

    side = state_own.shape[1]
    skip = wide_t.shape[1] - width
    down_t = nt(wide_t[:, skip : skip + width], out)
    state_t = jnp.concatenate(
        [
            nt(eye(side), state_own[...]),
            nt(ones_where(iota((side, 2 * side), 0) == iota((side, 2 * side), 1)), side_far[...]),
        ],
        axis=1,
    )
    gate_open = jax.nn.sigmoid(columns[:, 0:1])
    mixed = gate_open * down_t + (1.0 - gate_open) * state_t
    normed = (
        mixed * lax.rsqrt(jnp.mean(mixed * mixed, axis=0, keepdims=True) + EPS) * columns[:, 1:2]
    )
    mixed_t[...] = mixed
    lead_t[...] = down_t - state_t
    sn_t[...] = normed.astype(bf16)
    sn_rows[...] = normed.T.astype(bf16)


def side_body(
    doc_lengths,
    sn_own,
    sn_mate,
    mixed_t,
    cot_own,
    side_far,
    dup,
    dup_t,
    tall_t,
    wide_t,
    s_out,
    s_inner,
    s_outer,
    columns,
    out_own,
    out_far,
    dquery,
    dkv_own,
    dkv_mate,
    dmid_t,
    early,
    weights,
    keys,
    values,
    key_t,
    value_t,
    query_t,
    query_s,
    query_h,
    attn_t,
    inverse,
    totals,
    dattn_s,
    dterm_s,
    dattn_h,
    dkv_t,
):
    tokens, side = sn_own.shape
    span = tokens // 2
    feature = side // SHEADS
    hidden = s_inner.shape[1]
    wide = 2 * side
    place = lax.axis_index("blk")
    half = lax.axis_size("blk") // 2
    row = place // half
    near, opposite = place ^ 1, place ^ half
    opposite_near = opposite ^ 1
    scale = feature**-0.5

    sn = jnp.concatenate([sn_own[...], sn_mate[...]], axis=0)
    lane = iota((2 * tokens, keys.shape[1]), 1)
    docs = in_doc(
        doc_lengths, row, (place, opposite, near, opposite_near), span, (2 * tokens, 128), 0
    )
    shift = wide % 128
    docs = pltpu.roll(docs, shift, 1)
    projected = nn(sn, dup[0:side]).astype(bf16)
    low_lane = iota((2 * tokens, 128), 1) < shift
    keys[:, 0:128] = projected[:, 0:128]
    keys[:, 128:256] = jnp.where(low_lane, projected[:, 128:256].astype(f32), docs - 1.0).astype(bf16)
    projected = nn(sn, dup[side : 2 * side]).astype(bf16)
    values[:, 0:128] = projected[:, 0:128]
    values[:, 128:256] = jnp.where(low_lane, projected[:, 128:256].astype(f32), 1.0).astype(bf16)
    key_t[...] = nt(dup_t[wide : 2 * wide], sn).astype(bf16)
    second = iota((wide, 2 * tokens), 0) % (2 * feature) >= feature
    value_t[...] = jnp.where(second, 1.0, nt(dup_t[2 * wide : 3 * wide], sn)).astype(bf16)
    query = nt(dup_t[0:wide], sn_own[...]).astype(bf16)
    query_t[...] = query
    scaled = query.astype(f32) * (scale * LOG2E)
    high = scaled.astype(bf16).astype(f32)
    second = iota((wide, tokens), 0) % (2 * feature) >= feature
    query_s[...] = jnp.where(second, scaled - high, high).astype(bf16)
    query_docs = in_doc(doc_lengths, row, (place, opposite), span, (16, tokens), 1) * FAR
    for i in range(2):
        query_h[i] = jnp.zeros(query_h.shape[1:], bf16)
        query_h[i, wide : wide + 16] = query_docs.astype(bf16)

    def attend(shifted):
        def pair(j, carry):
            for i in range(2):
                h = 2 * j + i
                rows = pl.ds(pl.multiple_of(h * 16, 16), 16)
                eight = pl.ds(pl.multiple_of(h * 8, 8), 8)
                query_h[i, rows, :] = query_s[rows, :]
                scores = nn(keys[...], query_h[i])
                query_h[i, rows, :] = jnp.zeros((16, tokens), bf16)
                if shifted:
                    scores = scores - jnp.max(scores, axis=0, keepdims=True)
                weight = jnp.exp2(scores).astype(bf16)
                weights[h] = weight
                summed = nn(value_t[rows, :], weight)
                total = summed[feature : 2 * feature]
                totals[eight, :] = total
                invert = 1.0 / total
                inverse[eight, :] = invert
                attn_t[eight, :] = summed[0:feature] * invert
            return carry

        lax.fori_loop(0, SHEADS // 2, pair, 0)

    attend(False)

    @pl.when(out_of_range(totals[...]))
    def _():
        attend(True)

    attn = attn_t[...]
    attn_low = attn.astype(bf16)
    mid = mixed_t[...] + nn(tall_t[0:side], attn_low)
    mid_scale = lax.rsqrt(jnp.mean(mid * mid, axis=0, keepdims=True) + EPS)
    gain = columns[:, 2:3]
    unit = mid * mid_scale
    normed = (unit * gain).astype(bf16)
    inner = nn(tall_t[side : side + hidden], normed)
    act = gelu(inner).astype(bf16)
    out = (mid + nn(wide_t[:, 0:hidden], act)).T.astype(bf16)
    out_own[...] = out[0:span]
    out_far[...] = out[span : 2 * span]

    pick = ones_where(iota((side, 2 * side), 0) + side == iota((side, 2 * side), 1))
    dy = jnp.concatenate([nt(eye(side), cot_own[...]), nt(pick, side_far[...])], axis=1)
    dy_low = dy.astype(bf16)
    early[:, hidden : 2 * hidden] = nt(dy_low, act)
    dinner = (gelu_slope(inner) * nn(s_outer[...], dy_low)).astype(bf16)
    early[:, 0:hidden] = nt(normed, dinner)
    dnormed = nn(s_inner[...], dinner)
    grad_gain = jnp.sum(dnormed * unit, axis=1, keepdims=True)
    scaled = dnormed * gain
    dmid = dy + mid_scale * (scaled - unit * jnp.mean(scaled * unit, axis=0, keepdims=True))
    dmid_t[...] = dmid
    dmid_low = dmid.astype(bf16)
    last = jnp.concatenate(
        [nt(attn_low, dmid_low), jnp.zeros((side, 128 - side), f32)], axis=1
    )
    early[:, 2 * hidden : 2 * hidden + 128] = jnp.where(
        iota((side, 128), 1) == side, grad_gain, last
    )
    dattn = nn(s_out[...], dmid_low).astype(bf16).astype(f32)

    number = iota((feature, tokens), 0)
    for h in range(SHEADS):
        eight = slice(h * feature, (h + 1) * feature)
        invert = inverse[eight, :]
        part = dattn[eight] * invert
        high = part.astype(bf16).astype(f32)
        dattn_s[h * 16 : (h + 1) * 16] = jnp.concatenate([high, part - high], axis=0).astype(bf16)
        term = -jnp.sum(dattn[eight] * attn[eight], axis=0, keepdims=True) * invert
        first = term.astype(bf16).astype(f32)
        rest = term - first
        middle = rest.astype(bf16).astype(f32)
        piece = jnp.where(
            number == 0, first, jnp.where(number == 1, middle, jnp.where(number == 2, rest - middle, 0.0))
        )
        dterm_s[h * 16 : (h + 1) * 16] = jnp.concatenate(
            [piece, jnp.zeros_like(piece)], axis=0
        ).astype(bf16)
    for i in range(2):
        dattn_h[i] = jnp.zeros(dattn_h.shape[1:], bf16)

    def back(j, carry):
        for i in range(2):
            h = 2 * j + i
            rows = pl.ds(pl.multiple_of(h * 16, 16), 16)
            eight = pl.ds(pl.multiple_of(h * 8, 8), 8)
            eight_v = pl.ds(pl.multiple_of(side + h * 8, 8), 8)
            dattn_h[i, rows, :] = dattn_s[rows, :]
            dattn_h[i, wide : wide + 16] = dterm_s[rows, :]
            slope = nn(values[...], dattn_h[i])
            dattn_h[i, rows, :] = jnp.zeros((16, tokens), bf16)
            weight = weights[h]
            dscores = (weight.astype(f32) * slope).astype(bf16)
            dquery[eight, :] = nn(key_t[rows, :], dscores)[0:feature] * scale
            dkv_t[eight, :] = nt(query_t[rows, :], dscores)[0:feature] * scale
            both = nt(dattn_s[rows, :], weight)
            dkv_t[eight_v, :] = both[0:feature] + both[feature : 2 * feature]
        return carry

    lax.fori_loop(0, SHEADS // 2, back, 0)
    dkv_own[...] = dkv_t[:, 0:tokens]
    dkv_mate[...] = dkv_t[:, tokens : 2 * tokens].astype(bf16)


def last_body(
    dquery,
    dkv_own,
    dkv_back,
    sn_t,
    dmid_t,
    mixed_t,
    lead_t,
    out_own,
    out_far,
    s_query,
    s_key,
    s_value,
    columns,
    early,
    state_own,
    state_far,
    keep,
    send,
    pack,
):
    side, tokens = sn_t.shape
    span = tokens // 2
    width = out_own.shape[1]
    dq = dquery[...].astype(bf16)
    dkv = (dkv_own[...].astype(bf16).astype(f32) + dkv_back[...].astype(f32)).astype(bf16)
    dk, dv = dkv[0:side], dkv[side : 2 * side]
    sn = sn_t[...]
    dnormed = nn(s_query[...], dq) + nn(s_key[...], dk) + nn(s_value[...], dv)
    mixed = mixed_t[...]
    mixed_scale = lax.rsqrt(jnp.mean(mixed * mixed, axis=0, keepdims=True) + EPS)
    unit = mixed * mixed_scale
    scaled = dnormed * columns[:, 1:2]
    dmixed = dmid_t[...] + mixed_scale * (
        scaled - unit * jnp.mean(scaled * unit, axis=0, keepdims=True)
    )
    gate_open = jax.nn.sigmoid(columns[:, 0:1])
    grad_gain = jnp.sum(dnormed * unit, axis=1, keepdims=True)
    grad_gate = jnp.sum(dmixed * lead_t[...], axis=1, keepdims=True) * gate_open * (1.0 - gate_open)
    state = ((1.0 - gate_open) * dmixed).T
    state_own[...] = state[0:span]
    state_far[...] = state[span : 2 * span]
    ddown = (gate_open * dmixed).astype(bf16)
    pack[:, 0:width] = nn(ddown[:, 0:span], out_own[...]) + nn(ddown[:, span:tokens], out_far[...])
    at = width
    blank = jnp.zeros((side, 128 - side), f32)
    for grad in (dq, dk, dv):
        pack[:, at : at + 128] = jnp.concatenate([nt(sn, grad), blank], axis=1)
        at += 128
    lane = iota((side, 128), 1)
    inner = early.shape[1] - 128
    vectors = early[:, inner : inner + 128]
    vectors = jnp.where(lane == side + 1, grad_gain, vectors)
    pack[:, at : at + 128] = jnp.where(lane == side + 2, grad_gate, vectors)
    pack[:, at + 128 : at + 128 + inner] = early[:, 0:inner]
    size = keep.shape[1]
    core = lax.axis_index("blk") % 2
    keep[...] = pack[:, pl.ds(pl.multiple_of(core * size, 128), size)].astype(bf16)
    send[...] = pack[:, pl.ds(pl.multiple_of((1 - core) * size, 128), size)].astype(bf16)


def spread_body(
    half, other, grad_down, grad_gate, gain_in, grad_query, grad_key, grad_value, grad_out, gain_mid, grad_inner, grad_outer
):
    side = grad_query.shape[0]
    width = grad_down.shape[0]
    hidden = grad_inner.shape[1]
    even = lax.axis_index("blk") % 2 == 0
    first = jnp.where(even, half[...].astype(f32), other[...].astype(f32))
    second = jnp.where(even, other[...].astype(f32), half[...].astype(f32))
    whole = jnp.concatenate([first, second], axis=1)
    grad_down[...] = whole[:, 0:width].T
    at = width
    for target in (grad_query, grad_key, grad_value):
        target[...] = whole[:, at : at + side]
        at += 128
    block = whole[:, at : at + 128]
    grad_out[...] = block[:, 0:side]
    rows = block.T
    gain_mid[...] = rows[side : side + 1]
    gain_in[...] = rows[side + 1 : side + 2]
    grad_gate[...] = rows[side + 2 : side + 3]
    at += 128
    grad_inner[...] = whole[:, at : at + hidden]
    grad_outer[...] = whole[:, at + hidden : at + 2 * hidden].T


def per_device(
    hidden,
    side_state,
    doc_lengths,
    norm_in,
    w_query,
    w_key,
    w_value,
    w_out,
    norm_mid,
    w_inner,
    w_outer,
    w_down,
    gate,
    side_norm_in,
    s_query,
    s_key,
    s_value,
    s_out,
    side_norm_mid,
    s_inner,
    s_outer,
    cotangent,
):
    span, rows, width = hidden.shape
    side = side_state.shape[2]
    ff = w_inner.shape[1]
    sff = s_inner.shape[1]
    tokens = 2 * span
    blk_size, dp_size = lax.axis_size("blk"), lax.axis_size("dp")
    half = blk_size // 2
    place = lax.axis_index("blk")
    row = place // half

    def swap(value, axis, size, hop):
        return lax.ppermute(value, axis, [(i, i ^ hop) for i in range(size)])

    def across(value):
        return swap(value, "blk", blk_size, half)

    def beside(value):
        return swap(value, "blk", blk_size, 1)

    def of_row(array, which):
        return lax.dynamic_index_in_dim(array, which, 1, keepdims=False)

    hidden_far = across(of_row(hidden, 1 - row))
    side_far = across(
        jnp.concatenate([of_row(side_state, 1 - row), of_row(cotangent, 1 - row)], axis=1)
    )
    hidden_own = of_row(hidden, row)
    hidden_mate = beside(hidden_own)
    state_own, cot_own = of_row(side_state, row), of_row(cotangent, row)
    columns = jnp.stack([gate, side_norm_in, side_norm_mid], axis=1)
    gain_in, gain_mid = norm_in.reshape(1, width), norm_mid.reshape(1, width)

    value_t, dup, dup_t, tall_t, wide_t = kernel_call(
        prepare_body,
        [
            ((width, width), bf16),
            ((2 * side, 256), bf16),
            ((6 * side, side), bf16),
            ((side + sff, side), bf16),
            ((side, sff + width), bf16),
        ],
        [w_value, w_down, s_query, s_key, s_value, s_out, s_inner, s_outer],
        cost=(2 * width**3, 4 * width * width, 0),
    )
    query_own, key_near, value_near = kernel_call(
        first_body,
        [((span, width), bf16), ((tokens, width), bf16), ((width, tokens), bf16)],
        [hidden_own, hidden_mate, gain_in, w_query, w_key, value_t],
        cost=(5 * tokens * width * width, 8 * width * width, 0),
    )
    far_mate = beside(hidden_far)
    stride = width // HEADS + 16
    out_own, out_far, sn_rows, sn_t, mixed_t, lead_t = kernel_call(
        backbone_body,
        [
            ((span, width), bf16),
            ((span, width), bf16),
            ((tokens, side), bf16),
            ((side, tokens), bf16),
            ((side, tokens), f32),
            ((side, tokens), f32),
        ],
        [
            doc_lengths,
            hidden_own,
            hidden_far,
            far_mate,
            query_own,
            key_near,
            value_near,
            gain_in,
            w_query,
            w_key,
            value_t,
            gain_mid,
            wide_t,
            columns,
            state_own,
            side_far,
            w_out,
            w_inner,
            w_outer,
        ],
        scalars=(0,),
        whole=(16, 17, 18),
        scratch=[
            pltpu.VMEM((tokens, width), bf16),
            pltpu.VMEM((2 * tokens, width), bf16),
            pltpu.VMEM((HEADS * stride, 2 * tokens), bf16),
            pltpu.VMEM((2 * tokens, 128), bf16),
            pltpu.VMEM((tokens, 128), bf16),
            pltpu.VMEM((HEADS * 8, tokens), f32),
            pltpu.VMEM((tokens, width), bf16),
            pltpu.VMEM((tokens, width), f32),
            pltpu.VMEM((width, width), bf16),
            pltpu.VMEM((width, ff), bf16),
            pltpu.VMEM((ff, width), bf16),
            pltpu.SemaphoreType.DMA((3,)),
        ],
        cost=(20 * 10**9, 16 * 10**6, 0),
    )
    sn_mate = beside(sn_rows)
    side_own, side_back, dquery, dkv_own, dkv_mate, dmid_t, early = kernel_call(
        side_body,
        [
            ((span, side), bf16),
            ((span, side), bf16),
            ((side, tokens), f32),
            ((2 * side, tokens), f32),
            ((2 * side, tokens), bf16),
            ((side, tokens), f32),
            ((side, 2 * sff + 128), f32),
        ],
        [
            doc_lengths,
            sn_rows,
            sn_mate,
            mixed_t,
            cot_own,
            side_far,
            dup,
            dup_t,
            tall_t,
            wide_t,
            s_out,
            s_inner,
            s_outer,
            columns,
        ],
        scalars=(0,),
        scratch=[
            pltpu.VMEM((SHEADS, 2 * tokens, tokens), bf16),
            pltpu.VMEM((2 * tokens, 256), bf16),
            pltpu.VMEM((2 * tokens, 256), bf16),
            pltpu.VMEM((2 * side, 2 * tokens), bf16),
            pltpu.VMEM((2 * side, 2 * tokens), bf16),
            pltpu.VMEM((2 * side, tokens), bf16),
            pltpu.VMEM((2 * side, tokens), bf16),
            pltpu.VMEM((2, 256, tokens), bf16),
            pltpu.VMEM((side, tokens), f32),
            pltpu.VMEM((side, tokens), f32),
            pltpu.VMEM((side, tokens), f32),
            pltpu.VMEM((2 * side, tokens), bf16),
            pltpu.VMEM((2 * side, tokens), bf16),
            pltpu.VMEM((2, 256, tokens), bf16),
            pltpu.VMEM((2 * side, 2 * tokens), f32),
        ],
        cost=(30 * 10**9, 3 * 10**6, 0),
    )
    dkv_back = beside(dkv_mate)
    packed = width + 4 * 128 + 2 * sff
    grad_own, grad_far, keep, send = kernel_call(
        last_body,
        [
            ((span, side), f32),
            ((span, side), f32),
            ((side, packed // 2), bf16),
            ((side, packed // 2), bf16),
        ],
        [
            dquery,
            dkv_own,
            dkv_back,
            sn_t,
            dmid_t,
            mixed_t,
            lead_t,
            out_own,
            out_far,
            s_query,
            s_key,
            s_value,
            columns,
            early,
        ],
        scratch=[pltpu.VMEM((side, packed), f32)],
        cost=(10**9, 3 * 10**6, 0),
    )

    def add(left, right):
        return (left.astype(f32) + right.astype(f32)).astype(bf16)

    total = add(keep, beside(send))
    for axis, size, hop in (("blk", blk_size, 2), ("dp", dp_size, 1)):
        while hop < size:
            total = add(total, swap(total, axis, size, hop))
            hop *= 2
    other = beside(total)
    vector = ((1, side), f32)
    square = ((side, side), f32)
    grads = kernel_call(
        spread_body,
        [
            ((width, side), f32),
            vector,
            vector,
            square,
            square,
            square,
            square,
            vector,
            ((side, sff), f32),
            ((sff, side), f32),
        ],
        [total, other],
        cost=(0, 2 * 10**6, 0),
    )
    grads = [grad.reshape(side) if grad.shape[0] == 1 else grad for grad in grads]

    def both_rows(own, far):
        first = jnp.where(row == 0, own, far)
        second = jnp.where(row == 0, far, own)
        return jnp.stack([first, second], axis=1)

    return (
        both_rows(out_own, across(out_far)),
        both_rows(side_own, across(side_back)),
        both_rows(grad_own, across(grad_far)),
        *grads,
    )


def solution(mesh):
    split = P("blk", "dp", None)
    return jax.shard_map(
        per_device,
        mesh=mesh,
        in_specs=(split, split, P("dp", None)) + (P(),) * 18 + (split,),
        out_specs=(split,) * 3 + (P(),) * 10,
        check_vma=False,
    )
```

time: 574 us -> 131 us (0.23)
  waiting for transfers between devices: 280 us -> 36.7 us
  matrix products: 142 us -> 0 us
  local copies, waits for them, and re-layouts: 78.5 us -> 18.7 us
  Pallas kernels: 0 us -> 57.9 us
  other arithmetic: 38.2 us -> 1.55 us
  blocking collectives: 14.5 us -> 0 us
  starting transfers between devices: 0.42 us -> 14.7 us
  between operations: 15 us -> 0.97 us
    psum x2 -> x0, waiting for transfers between devices: 257 us -> none  [per_device(): lax.psum((grad_down, grad_gate, grad_norm_in, grad_query, grad_key, grad_...]
    dot_general x32 -> x0, matrix products: 129 us -> none  [the longest x12 37.2 us: product(): return jnp.dot(left_mat, right_mat, preferred_element_type=jnp.float32)]
    pallas_call x0 -> x6, Pallas kernels: none -> 57.9 us  [kernel_call(): pl.pallas_call(body, out_shape=[jax.ShapeDtypeStruct(shape, kind) for sha...]
    ppermute x0 -> x15, waiting for transfers between devices: none -> 36.7 us  [swap(): return lax.ppermute(value, axis, [(i, i ^ hop) for i in range(size)])]
    convert_element_type x16 -> x0, local copies, waits for them, and re-layouts: 22.6 us -> none  [the longest x2 8.94 us: per_device(): jnp.transpose(attended, (2, 0, 1, 3)).reshape(tokens, model_width)]
    all_gather x2 -> x0, waiting for transfers between devices: 18.6 us -> none  [the longest x1 18.6 us: per_device(): key_rows = lax.all_gather(key_local, 'blk', axis=0, tiled=True)]
    all_gather x4 -> x0, local copies, waits for them, and re-layouts: 17.8 us -> none  [the longest x1 8.71 us: per_device(): key_rows = lax.all_gather(key_local, 'blk', axis=0, tiled=True)]
    reduce_sum x5 -> x0, other arithmetic: 16.3 us -> none  [the longest x1 12.7 us: per_device(): total_new = jnp.sum(weights_exp, axis=-1)]
  transfers between devices with their start and end apart: 5 -> 15, of which waited for: 4 -> 8; matrix products, arithmetic and copies ran while one was open for 13% -> 7% of each run, Pallas kernels for 0% -> 7%
where the time goes in v2:
time: 131 us
  Pallas kernels  57.9 us (44%)
  waiting for transfers between devices  36.7 us (28%)
  local copies, waits for them, and re-layouts  18.7 us (14%)
  starting transfers between devices  14.7 us (11%)
  other arithmetic  1.55 us (1%)
    pallas_call x6, Pallas kernels, kernel_call(): pl.pallas_call(body, out_shape=[jax.ShapeDtypeStruct(shape, kind) for sha...  57.9 us
    ppermute x15, waiting for transfers between devices, swap(): return lax.ppermute(value, axis, [(i, i ^ hop) for i in range(size)])  36.7 us
    ppermute x15, starting transfers between devices, swap(): return lax.ppermute(value, axis, [(i, i ^ hop) for i in range(size)])  14.7 us
    unnamed x57, local copies, waits for them, and re-layouts  12.1 us
    dynamic_slice x6, local copies, waits for them, and re-layouts, of_row(): return lax.dynamic_index_in_dim(array, which, 1, keepdims=False)  4.75 us
  transfers between devices with their start and end apart: 15, of which 8 were waited for; matrix products, arithmetic and copies ran while one was open for 7% of the time, Pallas kernels for 7%

profile of v2, /device:TPU:0, one launch (start us, length us, event | category | flops | bytes accessed | tf_op | source)
XLA Modules:
  0.0 130.6 jit_solution(18124164507282410449)
XLA Ops:
  0.7 3.1 %constant_dynamic-slice_fusion.4 = (bf16[256,1,768]{2,1,0:T(2,128)(2,1)S(1)}, bf16[256,1,768]{2,1,0:T(2,128)(2,1)S(1)}) fusion(bf16[256,2,768]{2,1,0:T(2,128)(2,1)} %param.22, s32[]{:T(128)S(6)} %select_n.54, s32[]{:T(128)S(6)} %select_n.53), kind=kLoop, calls=%fused_computation.22 | loop fusion | bytes 1572872 | tf_op jit(solution)/shard_map/jit(dynamic_index_in_dim)/dynamic_slice | solution.py:602
  3.8 3.0 %collective-permute-start = (bf16[256,768]{1,0:T(8,128)(2,1)S(1)}, bf16[256,768]{1,0:T(8,128)(2,1)S(1)}, u32[]{:S(2)}, u32[]{:S(2)}) collective-permute-start(bf16[256,768]{1,0:T(8,128)(2,1)S(1)} %bitcast.31), channel_id=1, source_target_pairs={{0,2},{1,3},{2,0},{3,1},{4,6},{5,7},{6,4},{7,5},{8,10},{9,11},{10,... | collective-permute-start | bytes 1179656 | tf_op jit(solution)/shard_map/ppermute | solution.py:593
  7.1 0.1 copy.72
  7.2 0.1 copy.73
  7.3 8.7 %collective-permute-done.far = bf16[256,768]{1,0:T(8,128)(2,1)S(1)} collective-permute-done((bf16[256,768]{1,0:T(8,128)(2,1)S(1)}, bf16[256,768]{1,0:T(8,128)(2,1)S(1)}, u32[]{:S(2)}, u32[]{:S(2)}) %collective-permute-start) | collective-permute-done | bytes 393248 | tf_op jit(solution)/shard_map/ppermute | solution.py:593
  16.1 1.8 %collective-permute-start.3 = (bf16[256,192]{1,0:T(8,128)(2,1)S(1)}, bf16[256,192]{1,0:T(8,128)(2,1)S(1)}, u32[]{:S(2)}, u32[]{:S(2)}) collective-permute-start(bf16[256,192]{1,0:T(8,128)(2,1)S(1)} %pad_maximum_fusion.2), channel_id=1, source_target_pairs={{0,2},{1,3},{2,0},{3,1},{4,6},{5,7},{6,4},{7,5},{8,10},{9,11},{10,... | collective-permute-start | bytes 294920 | tf_op jit(solution)/shard_map/ppermute | solution.py:593
  17.9 0.8 copy.70.s_outer
  18.6 0.8 copy.69.w_down
  19.4 0.6 reshape.41.norm_in
  20.0 0.7 copy.71
  20.8 0.7 copy.74.columns
  21.5 0.6 reshape.42.norm_mid
  22.1 3.9 %shard_map.309 = (bf16[768,768]{1,0:T(8,128)(2,1)}, bf16[192,256]{1,0:T(8,128)(2,1)}, bf16[576,96]{1,0:T(8,128)(2,1)}, bf16[480,96]{1,0:T(8,128)(2,1)}, bf16[96,1152]{1,0:T(8,128)(2,1)}) custom-call(bf16[768,768]{1,0:T(8,128)(2,1)} %w_value.1, bf16[768,96]{1,0:T(8,128)(2,1)} %copy.69.w_down, bf16[96,96]{1,0:T(8,128)(2,1)} %s_query.3, bf16[96,96]{1,0:T(8,128)(2,1)} %s_key.3, ...), custom_call_target="tpu_custom_call" | custom-call | flops 905969664 | bytes 2359296 | tf_op jit(solution)/shard_map/pallas_call | solution.py:61
  26.0 0.8 copy-done.17
  26.8 4.9 %shard_map.310 = (bf16[256,768]{1,0:T(8,128)(2,1)}, bf16[512,768]{1,0:T(8,128)(2,1)}, bf16[768,512]{1,0:T(8,128)(2,1)}) custom-call(bf16[256,768]{1,0:T(8,128)(2,1)} %bitcast.29, bf16[256,768]{1,0:T(8,128)(2,1)} %copy-done.17, bf16[1,768]{1,0:T(2,128)(2,1)} %reshape.41.norm_in, bf16[768,768]{1,0:T(8,128)(2,1)} %w_query.3, bf16[768,768]{1,0:T(8,128)(2,1)} %w_key.3, ...), custom_call_target="tpu_custom_call" | custom-call | flops 1509949440 | bytes 4718592 | tf_op jit(solution)/shard_map/pallas_call | solution.py:61
  31.7 0.6 copy-done.21
  32.4 0.1 copy-done.18
  32.5 20.3 %shard_map.311 = (bf16[256,768]{1,0:T(8,128)(2,1)}, bf16[256,768]{1,0:T(8,128)(2,1)}, bf16[512,96]{1,0:T(8,128)(2,1)}, bf16[96,512]{1,0:T(8,128)(2,1)}, f32[96,512]{1,0:T(8,128)}, /*index=5*/f32[96,512]{1,0:T(8,128)}) custom-call(s32[2,8]{1,0:T(2,128)} %doc_lengths.3, bf16[256,768]{1,0:T(8,128)(2,1)} %bitcast.30, bf16[256,768]{1,0:T(8,128)(2,1)} %copy-done.16, ...), custom_call_target="tpu_custom_call" | custom-call | flops 20000000000 | bytes 16000000 | tf_op jit(solution)/shard_map/pallas_call | solution.py:61
  52.8 0.3 collective-permute-start.5
  53.0 0.7 copy.75
  53.8 0.6 collective-permute-done.5.sn_mate
  54.4 0.7 copy-done.22
  55.0 23.6 %shard_map.312 = (bf16[256,96]{1,0:T(8,128)(2,1)}, bf16[256,96]{1,0:T(8,128)(2,1)}, f32[96,512]{1,0:T(8,128)}, f32[192,512]{1,0:T(8,128)}, bf16[192,512]{1,0:T(8...) custom-call(s32[2,8]{1,0:T(2,128)} %doc_lengths.3, bf16[512,96]{1,0:T(8,128)(2,1)} %get-tuple-element.55.sn_own, ...), custom_call_target="tpu_custom_call" | custom-call | flops 30000001024 | bytes 3000000 | tf_op jit(solution)/shard_map/pallas_call | solution.py:61
  78.6 0.2 collective-permute-start.7
  78.9 1.4 %collective-permute-done.7.dkv_back = bf16[192,512]{1,0:T(8,128)(2,1)S(1)} collective-permute-done((bf16[192,512]{1,0:T(8,128)(2,1)}, bf16[192,512]{1,0:T(8,128)(2,1)S(1)}, u32[]{:S(2)}, u32[]{:S(2)}) %collective-permute-start.7) | collective-permute-done | bytes 196640 | tf_op jit(solution)/shard_map/ppermute | solution.py:593
  80.3 0.7 copy-done.19
  81.0 3.2 %shard_map.313 = (f32[256,96]{1,0:T(8,128)}, f32[256,96]{1,0:T(8,128)}, bf16[96,1024]{1,0:T(8,128)(2,1)}, bf16[96,1024]{1,0:T(8,128)(2,1)}) custom-call(f32[96,512]{1,0:T(8,128)} %get-tuple-element.62.dquery, f32[192,512]{1,0:T(8,128)} %get-tuple-element.63.dkv_own, bf16[192,512]{1,0:T(8,128)(2,1)} %copy-done.19, bf16[96,512]{1,0:T(8,128)(2,1)} %get-tuple-element.65.sn_t, ...), custom_call_target="tpu_custom_call" | custom-call | flops 1000000000 | bytes 3000000 | tf_op jit(solution)/shard_map/pallas_call | solution.py:61
  84.2 0.3 collective-permute-start.9
  84.5 1.4 %collective-permute-done.9 = bf16[96,1024]{1,0:T(8,128)(2,1)S(1)} collective-permute-done((bf16[96,1024]{1,0:T(8,128)(2,1)}, bf16[96,1024]{1,0:T(8,128)(2,1)S(1)}, u32[]{:S(2)}, u32[]{:S(2)}) %collective-permute-start.9) | collective-permute-done | bytes 196640 | tf_op jit(solution)/shard_map/ppermute | solution.py:593
  85.9 1.0 add_convert_fusion.4
  86.9 0.3 collective-permute-start.10
  87.3 1.7 %collective-permute-start.4 = (bf16[256,768]{1,0:T(8,128)(2,1)S(1)}, bf16[256,768]{1,0:T(8,128)(2,1)S(1)}, u32[]{:S(2)}, u32[]{:S(2)}) collective-permute-start(bf16[256,768]{1,0:T(8,128)(2,1)S(1)} %copy-done.15), channel_id=1, source_target_pairs={{0,2},{1,3},{2,0},{3,1},{4,6},{5,7},{6,4},{7,5},{8,10},{9,11},{10,... | collective-permute-start | bytes 1179656 | tf_op jit(solution)/shard_map/ppermute | solution.py:593
  89.0 0.3 collective-permute-start.6
  89.3 5.4 %collective-permute-done.10 = bf16[96,1024]{1,0:T(8,128)(2,1)S(1)} collective-permute-done((bf16[96,1024]{1,0:T(8,128)(2,1)S(1)}, bf16[96,1024]{1,0:T(8,128)(2,1)S(1)}, u32[]{:S(2)}, u32[]{:S(2)}) %collective-permute-start.10) | collective-permute-done | bytes 196640 | tf_op jit(solution)/shard_map/ppermute | solution.py:593
  94.8 1.6 %collective-permute-start.11 = (bf16[96,1024]{1,0:T(8,128)(2,1)S(1)}, bf16[96,1024]{1,0:T(8,128)(2,1)S(1)}, u32[]{:S(2)}, u32[]{:S(2)}) collective-permute-start(bf16[96,1024]{1,0:T(8,128)(2,1)S(1)} %add_convert_fusion.3), channel_id=1, source_target_pairs={{0,4},{4,0},{8,12},{12,8},{16,20},{20,16},{24,28},{28,24},{1,5},{5... | collective-permute-start | bytes 589832 | tf_op jit(solution)/shard_map/ppermute | solution.py:593
  96.4 7.5 %collective-permute-done.6 = bf16[256,96]{1,0:T(8,128)(2,1)S(1)} collective-permute-done((bf16[256,96]{1,0:T(8,128)(2,1)S(1)}, bf16[256,96]{1,0:T(8,128)(2,1)S(1)}, u32[]{:S(2)}, u32[]{:S(2)}) %collective-permute-start.6) | collective-permute-done | bytes 49184 | tf_op jit(solution)/shard_map/ppermute | solution.py:593
  103.9 0.7 copy.80
  104.7 0.3 collective-permute-start.8
  105.0 1.9 %collective-permute-start.12 = (bf16[96,1024]{1,0:T(8,128)(2,1)S(1)}, bf16[96,1024]{1,0:T(8,128)(2,1)S(1)}, u32[]{:S(2)}, u32[]{:S(2)}) collective-permute-start(bf16[96,1024]{1,0:T(8,128)(2,1)S(1)} %add_convert_fusion.2), channel_id=1, source_target_pairs={{0,8},{4,12},{8,0},{12,4},{16,24},{20,28},{24,16},{28,20},{1,9},{5... | collective-permute-start | bytes 589832 | tf_op jit(solution)/shard_map/ppermute | solution.py:593
  107.0 4.1 %collective-permute-done.12 = bf16[96,1024]{1,0:T(8,128)(2,1)S(1)} collective-permute-done((bf16[96,1024]{1,0:T(8,128)(2,1)S(1)}, bf16[96,1024]{1,0:T(8,128)(2,1)S(1)}, u32[]{:S(2)}, u32[]{:S(2)}) %collective-permute-start.12) | collective-permute-done | bytes 196640 | tf_op jit(solution)/shard_map/ppermute | solution.py:593
  111.2 2.8 %collective-permute-start.13 = (bf16[96,1024]{1,0:T(8,128)(2,1)S(1)}, bf16[96,1024]{1,0:T(8,128)(2,1)S(1)}, u32[]{:S(2)}, u32[]{:S(2)}) collective-permute-start(bf16[96,1024]{1,0:T(8,128)(2,1)S(1)} %add_convert_fusion.1), channel_id=1, source_target_pairs={{0,16},{4,20},{8,24},{12,28},{16,0},{20,4},{24,8},{28,12},{1,17},{... | collective-permute-start | bytes 589832 | tf_op jit(solution)/shard_map/ppermute | solution.py:593
  114.0 7.5 %collective-permute-done.13 = bf16[96,1024]{1,0:T(8,128)(2,1)S(1)} collective-permute-done((bf16[96,1024]{1,0:T(8,128)(2,1)S(1)}, bf16[96,1024]{1,0:T(8,128)(2,1)S(1)}, u32[]{:S(2)}, u32[]{:S(2)}) %collective-permute-start.13) | collective-permute-done | bytes 196640 | tf_op jit(solution)/shard_map/ppermute | solution.py:593
  121.7 0.8 copy.81
  122.6 1.7 %copy.79 = bf16[256,2,768]{2,1,0:T(2,128)(2,1)} copy(bf16[256,2,768]{2,0,1:T(8,128)(2,1)S(1)} %pad_maximum_fusion) | data formatting | bytes 1572864
  124.2 0.7 copy-done.3
  124.9 2.1 %shard_map.314 = (f32[768,96]{1,0:T(8,128)}, f32[1,96]{1,0:T(1,128)}, f32[1,96]{1,0:T(1,128)}, f32[96,96]{1,0:T(8,128)}, f32[96,96]{1,0:T(8,128)}, /*index=5*/f3...) custom-call(bf16[96,1024]{1,0:T(8,128)(2,1)} %copy-done, ...), custom_call_target="tpu_custom_call" | custom-call | bytes 2000000 | tf_op jit(solution)/shard_map/pallas_call | solution.py:61
  127.0 1.9 %copy.82 = f32[768,96]{0,1:T(8,128)} copy(f32[768,96]{1,0:T(8,128)} %get-tuple-element.112) | data formatting | bytes 589824
  128.8 1.7 %copy.83 = f32[384,96]{0,1:T(8,128)} copy(f32[384,96]{1,0:T(8,128)} %get-tuple-element.121) | data formatting | bytes 294912
  (67 shorter events, 0.9 us)
Async XLA Ops:
  3.7 3.3 %copy-start.6 = (bf16[256,2,96]{0,2,1:T(8,128)(2,1)S(1)}, bf16[256,2,96]{0,2,1:T(8,128)(2,1)}, u32[]{:S(2)}) copy-start(bf16[256,2,96]{0,2,1:T(8,128)(2,1)} %param.43) | copy-start | bytes 294916
  3.7 3.3 %copy-start.7 = (bf16[256,2,96]{0,2,1:T(8,128)(2,1)S(1)}, bf16[256,2,96]{0,2,1:T(8,128)(2,1)}, u32[]{:S(2)}) copy-start(bf16[256,2,96]{0,2,1:T(8,128)(2,1)} %param.23) | copy-start | bytes 294916
  3.8 14.1 %copy-start.8 = (bf16[384,96]{0,1:T(8,128)(2,1)S(1)}, bf16[384,96]{0,1:T(8,128)(2,1)}, u32[]{:S(2)}) copy-start(bf16[384,96]{0,1:T(8,128)(2,1)} %param.42) | copy-start | bytes 221188
  3.8 14.8 %copy-start.4 = (bf16[768,96]{0,1:T(8,128)(2,1)S(1)}, bf16[768,96]{0,1:T(8,128)(2,1)}, u32[]{:S(2)}) copy-start(bf16[768,96]{0,1:T(8,128)(2,1)} %param.33) | copy-start | bytes 442372
  3.8 12.1 %collective-permute-start = (bf16[256,768]{1,0:T(8,128)(2,1)S(1)}, bf16[256,768]{1,0:T(8,128)(2,1)S(1)}, u32[]{:S(2)}, u32[]{:S(2)}) collective-permute-start(bf16[256,768]{1,0:T(8,128)(2,1)S(1)} %bitcast.31), channel_id=1, source_target_pairs={{0,2},{1,3},{2,0},{3,1},{4,6},{5,7},{6,4},{7,5},{8,10},{9,11},{10,... | collective-permute-start | bytes 1179656 | tf_op jit(solution)/shard_map/ppermute | solution.py:593
  6.8 12.6 %copy-start.10 = (bf16[768]{0:T(1024)(128)(2,1)S(1)}, bf16[768]{0:T(1024)(128)(2,1)}, u32[]{:S(2)}) copy-start(bf16[768]{0:T(1024)(128)(2,1)} %param.25) | copy-start | bytes 4612
  6.8 13.9 %copy-start.12 = (f32[96]{0:T(128)S(1)}, f32[96]{0:T(128)}, u32[]{:S(2)}) copy-start(f32[96]{0:T(128)} %param.40) | copy-start | bytes 1156
  6.8 13.9 %copy-start.13 = (f32[96]{0:T(128)S(1)}, f32[96]{0:T(128)}, u32[]{:S(2)}) copy-start(f32[96]{0:T(128)} %param.35) | copy-start | bytes 1156
  6.8 13.9 %copy-start.14 = (f32[96]{0:T(128)S(1)}, f32[96]{0:T(128)}, u32[]{:S(2)}) copy-start(f32[96]{0:T(128)} %param.34) | copy-start | bytes 1156
  6.8 14.7 %copy-start.11 = (bf16[768]{0:T(1024)(128)(2,1)S(1)}, bf16[768]{0:T(1024)(128)(2,1)}, u32[]{:S(2)}) copy-start(bf16[768]{0:T(1024)(128)(2,1)} %param.30) | copy-start | bytes 4612
  6.9 19.1 %copy-start.2 = (bf16[256,1,768]{2,0,1:T(8,128)(2,1)}, bf16[256,1,768]{2,0,1:T(8,128)(2,1)S(1)}, u32[]{:S(2)}) copy-start(bf16[256,1,768]{2,0,1:T(8,128)(2,1)S(1)} %copy.89) | copy-start | bytes 1179652
  6.9 19.1 %collective-permute-start.2 = (bf16[256,768]{1,0:T(8,128)(2,1)S(1)}, bf16[256,768]{1,0:T(8,128)(2,1)S(1)}, u32[]{:S(2)}, u32[]{:S(2)}) collective-permute-start(bf16[256,768]{1,0:T(8,128)(2,1)S(1)} %bitcast.28), channel_id=1, source_target_pairs={{0,1},{1,0},{2,3},{3,2},{4,5},{5,4},{6,7},{7,6},{8,9},{9,8},{10,11... | collective-permute-start | bytes 1179656 | tf_op jit(solution)/shard_map/ppermute | solution.py:593
  15.9 10.0 %copy-start.16 = (bf16[256,768]{1,0:T(8,128)(2,1)}, bf16[256,768]{1,0:T(8,128)(2,1)S(1)}, u32[]{:S(2)}) copy-start(bf16[256,768]{1,0:T(8,128)(2,1)S(1)} %collective-permute-done.far) | copy-start | bytes 1179652
  16.0 15.8 %collective-permute-start.1 = (bf16[256,768]{1,0:T(8,128)(2,1)S(1)}, bf16[256,768]{1,0:T(8,128)(2,1)S(1)}, u32[]{:S(2)}, u32[]{:S(2)}) collective-permute-start(bf16[256,768]{1,0:T(8,128)(2,1)S(1)} %collective-permute-done.far), channel_id=1, source_target_pairs={{0,1},{1,0},{2,3},{3,2},{4,5},{5,4},{6,7},{7,6},{8,9},{9,8},{10,11... | collective-permute-start | bytes 1179656 | tf_op jit(solution)/shard_map/ppermute | solution.py:593
  16.1 15.6 %collective-permute-start.3 = (bf16[256,192]{1,0:T(8,128)(2,1)S(1)}, bf16[256,192]{1,0:T(8,128)(2,1)S(1)}, u32[]{:S(2)}, u32[]{:S(2)}) collective-permute-start(bf16[256,192]{1,0:T(8,128)(2,1)S(1)} %pad_maximum_fusion.2), channel_id=1, source_target_pairs={{0,2},{1,3},{2,0},{3,1},{4,6},{5,7},{6,4},{7,5},{8,10},{9,11},{10,... | collective-permute-start | bytes 294920 | tf_op jit(solution)/shard_map/ppermute | solution.py:593
  26.0 0.8 copy-start.17
  31.7 0.7 copy-start.21
  31.7 0.8 copy-start.18
  52.8 1.6 %collective-permute-start.5 = (bf16[512,96]{1,0:T(8,128)(2,1)}, bf16[512,96]{1,0:T(8,128)(2,1)S(1)}, u32[]{:S(2)}, u32[]{:S(2)}) collective-permute-start(bf16[512,96]{1,0:T(8,128)(2,1)} %get-tuple-element.55.sn_own), channel_id=1, source_target_pairs={{0,1},{1,0},{2,3},{3,2},{4,5},{5,4},{6,7},{7,6},{8,9},{9,8},{10,11... | collective-permute-start | bytes 294920 | tf_op jit(solution)/shard_map/ppermute | solution.py:593
  54.4 0.7 copy-start.22
  78.6 1.7 %collective-permute-start.7 = (bf16[192,512]{1,0:T(8,128)(2,1)}, bf16[192,512]{1,0:T(8,128)(2,1)S(1)}, u32[]{:S(2)}, u32[]{:S(2)}) collective-permute-start(bf16[192,512]{1,0:T(8,128)(2,1)} %get-tuple-element.64), channel_id=1, source_target_pairs={{0,1},{1,0},{2,3},{3,2},{4,5},{5,4},{6,7},{7,6},{8,9},{9,8},{10,11... | collective-permute-start | bytes 589832 | tf_op jit(solution)/shard_map/ppermute | solution.py:593
  80.3 0.7 copy-start.19
  81.0 6.3 %copy-start.15 = (bf16[256,768]{1,0:T(8,128)(2,1)S(1)}, bf16[256,768]{1,0:T(8,128)(2,1)}, u32[]{:S(2)}) copy-start(bf16[256,768]{1,0:T(8,128)(2,1)} %get-tuple-element.54.out_far) | copy-start | bytes 1179652
  81.0 8.1 %copy-start.23 = (bf16[256,96]{1,0:T(8,128)(2,1)S(1)}, bf16[256,96]{1,0:T(8,128)(2,1)}, u32[]{:S(2)}) copy-start(bf16[256,96]{1,0:T(8,128)(2,1)} %get-tuple-element.61) | copy-start | bytes 147460
  84.2 19.7 %copy-start.9 = (bf16[256,96]{1,0:T(8,128)(2,1)S(1)}, bf16[256,96]{1,0:T(8,128)(2,1)}, u32[]{:S(2)}) copy-start(bf16[256,96]{1,0:T(8,128)(2,1)} %get-tuple-element.60) | copy-start | bytes 147460
  84.2 20.5 %copy-start.20 = (f32[256,96]{1,0:T(8,128)S(1)}, f32[256,96]{1,0:T(8,128)}, u32[]{:S(2)}) copy-start(f32[256,96]{1,0:T(8,128)} %get-tuple-element.70) | copy-start | bytes 294916
  84.2 1.7 %collective-permute-start.9 = (bf16[96,1024]{1,0:T(8,128)(2,1)}, bf16[96,1024]{1,0:T(8,128)(2,1)S(1)}, u32[]{:S(2)}, u32[]{:S(2)}) collective-permute-start(bf16[96,1024]{1,0:T(8,128)(2,1)} %get-tuple-element.72), channel_id=1, source_target_pairs={{0,1},{1,0},{2,3},{3,2},{4,5},{5,4},{6,7},{7,6},{8,9},{9,8},{10,11... | collective-permute-start | bytes 589832 | tf_op jit(solution)/shard_map/ppermute | solution.py:593
  85.9 21.0 %copy-start.1 = (bf16[256,768]{1,0:T(8,128)(2,1)S(1)}, bf16[256,768]{1,0:T(8,128)(2,1)}, u32[]{:S(2)}) copy-start(bf16[256,768]{1,0:T(8,128)(2,1)} %get-tuple-element.53.out_own) | copy-start | bytes 1179652
  86.9 7.8 %collective-permute-start.10 = (bf16[96,1024]{1,0:T(8,128)(2,1)S(1)}, bf16[96,1024]{1,0:T(8,128)(2,1)S(1)}, u32[]{:S(2)}, u32[]{:S(2)}) collective-permute-start(bf16[96,1024]{1,0:T(8,128)(2,1)S(1)} %add_convert_fusion.4), channel_id=1, source_target_pairs={{0,2},{1,3},{2,0},{3,1},{4,6},{5,7},{6,4},{7,5},{8,10},{9,11},{10,... | collective-permute-start | bytes 589832 | tf_op jit(solution)/shard_map/ppermute | solution.py:593
  87.3 19.7 %collective-permute-start.4 = (bf16[256,768]{1,0:T(8,128)(2,1)S(1)}, bf16[256,768]{1,0:T(8,128)(2,1)S(1)}, u32[]{:S(2)}, u32[]{:S(2)}) collective-permute-start(bf16[256,768]{1,0:T(8,128)(2,1)S(1)} %copy-done.15), channel_id=1, source_target_pairs={{0,2},{1,3},{2,0},{3,1},{4,6},{5,7},{6,4},{7,5},{8,10},{9,11},{10,... | collective-permute-start | bytes 1179656 | tf_op jit(solution)/shard_map/ppermute | solution.py:593
  89.0 14.8 %collective-permute-start.6 = (bf16[256,96]{1,0:T(8,128)(2,1)S(1)}, bf16[256,96]{1,0:T(8,128)(2,1)S(1)}, u32[]{:S(2)}, u32[]{:S(2)}) collective-permute-start(bf16[256,96]{1,0:T(8,128)(2,1)S(1)} %copy-done.23), channel_id=1, source_target_pairs={{0,2},{1,3},{2,0},{3,1},{4,6},{5,7},{6,4},{7,5},{8,10},{9,11},{10,... | collective-permute-start | bytes 147464 | tf_op jit(solution)/shard_map/ppermute | solution.py:593
  94.8 10.2 %collective-permute-start.11 = (bf16[96,1024]{1,0:T(8,128)(2,1)S(1)}, bf16[96,1024]{1,0:T(8,128)(2,1)S(1)}, u32[]{:S(2)}, u32[]{:S(2)}) collective-permute-start(bf16[96,1024]{1,0:T(8,128)(2,1)S(1)} %add_convert_fusion.3), channel_id=1, source_target_pairs={{0,4},{4,0},{8,12},{12,8},{16,20},{20,16},{24,28},{28,24},{1,5},{5... | collective-permute-start | bytes 589832 | tf_op jit(solution)/shard_map/ppermute | solution.py:593
  104.7 9.3 %collective-permute-start.8 = (f32[256,96]{1,0:T(8,128)S(1)}, f32[256,96]{1,0:T(8,128)S(1)}, u32[]{:S(2)}, u32[]{:S(2)}) collective-permute-start(f32[256,96]{1,0:T(8,128)S(1)} %copy-done.20), channel_id=1, source_target_pairs={{0,2},{1,3},{2,0},{3,1},{4,6},{5,7},{6,4},{7,5},{8,10},{9,11},{10,... | collective-permute-start | bytes 294920 | tf_op jit(solution)/shard_map/ppermute | solution.py:593
  105.0 9.0 %copy-start.5 = (f32[256,96]{1,0:T(8,128)S(1)}, f32[256,96]{1,0:T(8,128)}, u32[]{:S(2)}) copy-start(f32[256,96]{1,0:T(8,128)} %get-tuple-element.69) | copy-start | bytes 294916
  105.0 6.1 %collective-permute-start.12 = (bf16[96,1024]{1,0:T(8,128)(2,1)S(1)}, bf16[96,1024]{1,0:T(8,128)(2,1)S(1)}, u32[]{:S(2)}, u32[]{:S(2)}) collective-permute-start(bf16[96,1024]{1,0:T(8,128)(2,1)S(1)} %add_convert_fusion.2), channel_id=1, source_target_pairs={{0,8},{4,12},{8,0},{12,4},{16,24},{20,28},{24,16},{28,20},{1,9},{5... | collective-permute-start | bytes 589832 | tf_op jit(solution)/shard_map/ppermute | solution.py:593
  111.2 10.3 %collective-permute-start.13 = (bf16[96,1024]{1,0:T(8,128)(2,1)S(1)}, bf16[96,1024]{1,0:T(8,128)(2,1)S(1)}, u32[]{:S(2)}, u32[]{:S(2)}) collective-permute-start(bf16[96,1024]{1,0:T(8,128)(2,1)S(1)} %add_convert_fusion.1), channel_id=1, source_target_pairs={{0,16},{4,20},{8,24},{12,28},{16,0},{20,4},{24,8},{28,12},{1,17},{... | collective-permute-start | bytes 589832 | tf_op jit(solution)/shard_map/ppermute | solution.py:593
  121.5 1.0 copy-start
  121.6 2.7 %collective-permute-start.14 = (bf16[96,1024]{1,0:T(8,128)(2,1)S(1)}, bf16[96,1024]{1,0:T(8,128)(2,1)S(1)}, u32[]{:S(2)}, u32[]{:S(2)}) collective-permute-start(bf16[96,1024]{1,0:T(8,128)(2,1)S(1)} %add_convert_fusion.half), channel_id=1, source_target_pairs={{0,1},{1,0},{2,3},{3,2},{4,5},{5,4},{6,7},{7,6},{8,9},{9,8},{10,11... | collective-permute-start | bytes 589832 | tf_op jit(solution)/shard_map/ppermute | solution.py:593
  124.2 0.7 copy-start.3

commit v3 on v2

--- a/solution.py
+++ b/solution.py
@@ -13,7 +13,6 @@
 LOG2E = math.log2(math.e)
 FAR = 2.0**100
 LOW_TOTAL, HIGH_TOTAL = 2.0**-80, 2.0**100
-VMEM_BYTES = 60 * 2**20
 
 f32, bf16, i32 = jnp.float32, jnp.bfloat16, jnp.int32
 
@@ -24,6 +23,10 @@
 
 def nt(left, right):
     return lax.dot_general(left, right, (((1,), (1,)), ((), ())), preferred_element_type=f32)
+
+
+def tn(left, right):
+    return lax.dot_general(left, right, (((0,), (0,)), ((), ())), preferred_element_type=f32)
 
 
 def ones_where(condition):
@@ -51,7 +54,7 @@
     return 0.5 * (1.0 + lax.erf(value * math.sqrt(0.5))) + value * bell
 
 
-def kernel_call(body, outs, ins, *, scratch=(), whole=(), scalars=(), cost=(0, 0, 0)):
+def kernel_call(body, outs, ins, *, vmem, scratch=(), whole=(), scalars=(), cost=(0, 0, 0)):
     specs = [
         pl.BlockSpec(
             memory_space=pl.ANY if i in whole else pltpu.SMEM if i in scalars else pltpu.VMEM
@@ -64,7 +67,7 @@
         in_specs=specs,
         out_specs=[pl.BlockSpec(memory_space=pltpu.VMEM)] * len(outs),
         scratch_shapes=list(scratch),
-        compiler_params=pltpu.CompilerParams(vmem_limit_bytes=VMEM_BYTES),
+        compiler_params=pltpu.CompilerParams(vmem_limit_bytes=vmem * 2**20),
         cost_estimate=pl.CostEstimate(flops=cost[0], bytes_accessed=cost[1], transcendentals=cost[2]),
     )(*ins)
 
@@ -78,37 +81,38 @@
 
 
 def prepare_body(
-    w_value, w_down, s_query, s_key, s_value, s_out, s_inner, s_outer, value_t, dup, dup_t, tall_t, wide_t
+    w_value, s_query, s_key, s_value, s_out, s_inner, gate, gain_in, gain_mid, value_t, dup, dup_t, tall_t, columns, lines
 ):
-    width, side = w_down.shape
+    side = s_out.shape[0]
     feature = side // SHEADS
     hidden = s_inner.shape[1]
-    value_t[...] = nt(eye(width), w_value[...]).astype(bf16)
+    value_t[...] = nt(eye(w_value.shape[0]), w_value[...]).astype(bf16)
     spread = doubled(side, dup.shape[1], feature, False)
     dup[0:side] = nn(s_key[...], spread).astype(bf16)
     dup[side : 2 * side] = nn(s_value[...], spread).astype(bf16)
     spread_t = doubled(2 * side, side, feature, True)
     for i, weight in enumerate((s_query, s_key, s_value)):
         dup_t[2 * side * i : 2 * side * (i + 1)] = nt(spread_t, weight[...]).astype(bf16)
-    one = eye(side)
-    tall_t[0:side] = nt(one, s_out[...]).astype(bf16)
+    tall_t[0:side] = nt(eye(side), s_out[...]).astype(bf16)
     tall_t[side : side + hidden] = nt(eye(hidden), s_inner[...]).astype(bf16)
-    wide_t[:, 0:hidden] = nt(one, s_outer[...]).astype(bf16)
-    wide_t[:, hidden : hidden + width] = nt(one, w_down[...]).astype(bf16)
+    lines[...] = jnp.zeros(lines.shape, f32)
+    for i, line in enumerate((gate, gain_in, gain_mid)):
+        lines[i : i + 1, 0:side] = line[...]
+    columns[...] = lines[...].T[0:side]
 
 
 def project(tokens, gain, w_query, w_key, value_t, scale, queries):
-    normed = norm_lanes(tokens.astype(f32), gain.astype(f32)).astype(bf16)
+    normed = norm_lanes(tokens.astype(f32), gain).astype(bf16)
     query = (nn(normed[0:queries], w_query[...]) * scale).astype(bf16)
     return query, nn(normed, w_key[...]).astype(bf16), nt(value_t[...], normed).astype(bf16)
 
 
-def first_body(own, mate, norm_in, w_query, w_key, value_t, query, key, value):
+def first_body(own, mate, gains, w_query, w_key, value_t, query, key, value):
     span, width = own.shape
     scale = LOG2E * (width // HEADS) ** -0.5
     tokens = jnp.concatenate([own[...], mate[...]], axis=0)
     query[...], key[...], value[...] = project(
-        tokens, norm_in[...], w_query, w_key, value_t, scale, span
+        tokens, gains[0:1], w_query, w_key, value_t, scale, span
     )
 
 
@@ -151,14 +155,13 @@
     query_own,
     key_near,
     value_near,
-    norm_in,
+    gains,
     w_query,
     w_key,
     value_t,
-    norm_mid,
-    wide_t,
+    down_w,
     columns,
-    state_own,
+    state,
     side_far,
     w_out_hbm,
     w_inner_hbm,
@@ -201,7 +204,7 @@
 
     tokens = jnp.concatenate([far[...], far_mate[...]], axis=0)
     query_far, key_far, value_far = project(
-        tokens, norm_in[...], w_query, w_key, value_t, LOG2E * head**-0.5, span
+        tokens, gains[0:1], w_query, w_key, value_t, LOG2E * head**-0.5, span
     )
     query[0:span] = query_own[...]
     query[span : 2 * span] = query_far
@@ -251,7 +254,7 @@
     copies[0].wait()
     after[0:span] = own[...].astype(f32) + nn(attended[0:span], w_out[...])
     after[span : 2 * span] = far[...].astype(f32) + nn(attended[span : 2 * span], w_out[...])
-    middle = norm_lanes(after[...], norm_mid[...].astype(f32)).astype(bf16)
+    middle = norm_lanes(after[...], gains[1:2]).astype(bf16)
     copies[1].wait()
     copies[2].wait()
     hidden = w_inner.shape[1]
@@ -264,16 +267,9 @@
     out_own[...] = out[0:span]
     out_far[...] = out[span : 2 * span]
 
-    side = state_own.shape[1]
-    skip = wide_t.shape[1] - width
-    down_t = nt(wide_t[:, skip : skip + width], out)
-    state_t = jnp.concatenate(
-        [
-            nt(eye(side), state_own[...]),
-            nt(ones_where(iota((side, 2 * side), 0) == iota((side, 2 * side), 1)), side_far[...]),
-        ],
-        axis=1,
-    )
+    side = state.shape[1]
+    down_t = nt(down_w[...], out)
+    state_t = jnp.concatenate([state[row], side_far[0:side]], axis=1).astype(f32)
     gate_open = jax.nn.sigmoid(columns[:, 0:1])
     mixed = gate_open * down_t + (1.0 - gate_open) * state_t
     normed = (
@@ -290,15 +286,14 @@
     sn_own,
     sn_mate,
     mixed_t,
-    cot_own,
+    cot,
     side_far,
     dup,
     dup_t,
     tall_t,
-    wide_t,
+    s_outer_t,
     s_out,
     s_inner,
-    s_outer,
     columns,
     out_own,
     out_far,
@@ -401,15 +396,14 @@
     normed = (unit * gain).astype(bf16)
     inner = nn(tall_t[side : side + hidden], normed)
     act = gelu(inner).astype(bf16)
-    out = (mid + nn(wide_t[:, 0:hidden], act)).T.astype(bf16)
-    out_own[...] = out[0:span]
-    out_far[...] = out[span : 2 * span]
-
-    pick = ones_where(iota((side, 2 * side), 0) + side == iota((side, 2 * side), 1))
-    dy = jnp.concatenate([nt(eye(side), cot_own[...]), nt(pick, side_far[...])], axis=1)
-    dy_low = dy.astype(bf16)
+    out = (mid + nn(s_outer_t[...], act)).astype(bf16)
+    out_own[...] = out[:, 0:span]
+    out_far[...] = out[:, span : 2 * span]
+
+    dy_low = jnp.concatenate([cot[row], side_far[side : 2 * side]], axis=1)
+    dy = dy_low.astype(f32)
     early[:, hidden : 2 * hidden] = nt(dy_low, act)
-    dinner = (gelu_slope(inner) * nn(s_outer[...], dy_low)).astype(bf16)
+    dinner = (gelu_slope(inner) * tn(s_outer_t[...], dy_low)).astype(bf16)
     early[:, 0:hidden] = nt(normed, dinner)
     dnormed = nn(s_inner[...], dinner)
     grad_gain = jnp.sum(dnormed * unit, axis=1, keepdims=True)
@@ -483,8 +477,9 @@
     s_value,
     columns,
     early,
+    side_out_far,
     state_own,
-    state_far,
+    far,
     keep,
     send,
     pack,
@@ -507,9 +502,10 @@
     gate_open = jax.nn.sigmoid(columns[:, 0:1])
     grad_gain = jnp.sum(dnormed * unit, axis=1, keepdims=True)
     grad_gate = jnp.sum(dmixed * lead_t[...], axis=1, keepdims=True) * gate_open * (1.0 - gate_open)
-    state = ((1.0 - gate_open) * dmixed).T
-    state_own[...] = state[0:span]
-    state_far[...] = state[span : 2 * span]
+    state = (1.0 - gate_open) * dmixed
+    state_own[...] = state[:, 0:span]
+    far[0:side] = side_out_far[...]
+    far[side : 2 * side] = state[:, span:tokens].astype(bf16)
     ddown = (gate_open * dmixed).astype(bf16)
     pack[:, 0:width] = nn(ddown[:, 0:span], out_own[...]) + nn(ddown[:, span:tokens], out_far[...])
     at = width
@@ -530,16 +526,31 @@
 
 
 def spread_body(
-    half, other, grad_down, grad_gate, gain_in, grad_query, grad_key, grad_value, grad_out, gain_mid, grad_inner, grad_outer
+    part,
+    part_x,
+    part_core,
+    part_both,
+    grad_down,
+    grad_gate,
+    gain_in,
+    grad_query,
+    grad_key,
+    grad_value,
+    grad_out,
+    gain_mid,
+    grad_inner,
+    grad_outer,
 ):
-    side = grad_query.shape[0]
-    width = grad_down.shape[0]
+    side, width = grad_down.shape
     hidden = grad_inner.shape[1]
-    even = lax.axis_index("blk") % 2 == 0
-    first = jnp.where(even, half[...].astype(f32), other[...].astype(f32))
-    second = jnp.where(even, other[...].astype(f32), half[...].astype(f32))
-    whole = jnp.concatenate([first, second], axis=1)
-    grad_down[...] = whole[:, 0:width].T
+    place = lax.axis_index("blk")
+    core, chip = place % 2, place // 2
+    mine, cross, beside, both = (ref[...].astype(f32) for ref in (part, part_x, part_core, part_both))
+    near = [jnp.where(chip == 0, mine, cross), jnp.where(chip == 0, cross, mine)]
+    far = [jnp.where(chip == 0, beside, both), jnp.where(chip == 0, both, beside)]
+    pieces = [jnp.where(core == 0, a, b) for a, b in zip(near + far, far + near)]
+    whole = jnp.concatenate(pieces, axis=1)
+    grad_down[...] = whole[:, 0:width]
     at = width
     for target in (grad_query, grad_key, grad_value):
         target[...] = whole[:, at : at + side]
@@ -552,7 +563,7 @@
     grad_gate[...] = rows[side + 2 : side + 3]
     at += 128
     grad_inner[...] = whole[:, at : at + hidden]
-    grad_outer[...] = whole[:, at + hidden : at + 2 * hidden].T
+    grad_outer[...] = whole[:, at + hidden : at + 2 * hidden]
 
 
 def per_device(
@@ -601,33 +612,41 @@
     def of_row(array, which):
         return lax.dynamic_index_in_dim(array, which, 1, keepdims=False)
 
-    hidden_far = across(of_row(hidden, 1 - row))
+    leaving = of_row(hidden, 1 - row)
+    hidden_far = across(leaving)
+    hidden_own = of_row(lax.optimization_barrier((hidden, leaving))[0], row)
+    hidden_mate = beside(hidden_own)
+    state, cot = (jnp.transpose(array, (1, 2, 0)) for array in (side_state, cotangent))
     side_far = across(
-        jnp.concatenate([of_row(side_state, 1 - row), of_row(cotangent, 1 - row)], axis=1)
-    )
-    hidden_own = of_row(hidden, row)
-    hidden_mate = beside(hidden_own)
-    state_own, cot_own = of_row(side_state, row), of_row(cotangent, row)
-    columns = jnp.stack([gate, side_norm_in, side_norm_mid], axis=1)
-    gain_in, gain_mid = norm_in.reshape(1, width), norm_mid.reshape(1, width)
-
-    value_t, dup, dup_t, tall_t, wide_t = kernel_call(
+        lax.dynamic_index_in_dim(jnp.concatenate([state, cot], axis=1), 1 - row, 0, keepdims=False)
+    )
+    gains = jnp.stack([norm_in, norm_mid]).astype(f32)
+    lines = [line.reshape(1, side) for line in (gate, side_norm_in, side_norm_mid)]
+    down_w, s_outer_t = w_down.T, s_outer.T
+
+    value_t, dup, dup_t, tall_t, columns = kernel_call(
         prepare_body,
         [
             ((width, width), bf16),
             ((2 * side, 256), bf16),
             ((6 * side, side), bf16),
             ((side + sff, side), bf16),
-            ((side, sff + width), bf16),
-        ],
-        [w_value, w_down, s_query, s_key, s_value, s_out, s_inner, s_outer],
+            ((side, 128), f32),
+        ],
+        [w_value, s_query, s_key, s_value, s_out, s_inner, *lines],
+        vmem=12,
+        scratch=[pltpu.VMEM((128, 128), f32)],
         cost=(2 * width**3, 4 * width * width, 0),
     )
     query_own, key_near, value_near = kernel_call(
         first_body,
         [((span, width), bf16), ((tokens, width), bf16), ((width, tokens), bf16)],
-        [hidden_own, hidden_mate, gain_in, w_query, w_key, value_t],
+        [hidden_own, hidden_mate, gains, w_query, w_key, value_t],
+        vmem=20,
         cost=(5 * tokens * width * width, 8 * width * width, 0),
+    )
+    hidden_far, side_far, query_own, key_near, value_near = lax.optimization_barrier(
+        (hidden_far, side_far, query_own, key_near, value_near)
     )
     far_mate = beside(hidden_far)
     stride = width // HEADS + 16
@@ -649,21 +668,21 @@
             query_own,
             key_near,
             value_near,
-            gain_in,
+            gains,
             w_query,
             w_key,
             value_t,
-            gain_mid,
-            wide_t,
+            down_w,
             columns,
-            state_own,
+            state,
             side_far,
             w_out,
             w_inner,
             w_outer,
         ],
+        vmem=44,
         scalars=(0,),
-        whole=(16, 17, 18),
+        whole=(15, 16, 17),
         scratch=[
             pltpu.VMEM((tokens, width), bf16),
             pltpu.VMEM((2 * tokens, width), bf16),
@@ -681,11 +700,12 @@
         cost=(20 * 10**9, 16 * 10**6, 0),
     )
     sn_mate = beside(sn_rows)
+    out_back = across(out_far)
     side_own, side_back, dquery, dkv_own, dkv_mate, dmid_t, early = kernel_call(
         side_body,
         [
-            ((span, side), bf16),
-            ((span, side), bf16),
+            ((side, span), bf16),
+            ((side, span), bf16),
             ((side, tokens), f32),
             ((2 * side, tokens), f32),
             ((2 * side, tokens), bf16),
@@ -697,17 +717,17 @@
             sn_rows,
             sn_mate,
             mixed_t,
-            cot_own,
+            cot,
             side_far,
             dup,
             dup_t,
             tall_t,
-            wide_t,
+            s_outer_t,
             s_out,
             s_inner,
-            s_outer,
             columns,
         ],
+        vmem=36,
         scalars=(0,),
         scratch=[
             pltpu.VMEM((SHEADS, 2 * tokens, tokens), bf16),
@@ -729,12 +749,13 @@
         cost=(30 * 10**9, 3 * 10**6, 0),
     )
     dkv_back = beside(dkv_mate)
+    dkv_back, out_back = lax.optimization_barrier((dkv_back, out_back))
     packed = width + 4 * 128 + 2 * sff
-    grad_own, grad_far, keep, send = kernel_call(
+    grad_own, far, keep, send = kernel_call(
         last_body,
         [
-            ((span, side), f32),
-            ((span, side), f32),
+            ((side, span), f32),
+            ((2 * side, span), bf16),
             ((side, packed // 2), bf16),
             ((side, packed // 2), bf16),
         ],
@@ -753,7 +774,9 @@
             s_value,
             columns,
             early,
-        ],
+            side_back,
+        ],
+        vmem=16,
         scratch=[pltpu.VMEM((side, packed), f32)],
         cost=(10**9, 3 * 10**6, 0),
     )
@@ -761,18 +784,25 @@
     def add(left, right):
         return (left.astype(f32) + right.astype(f32)).astype(bf16)
 
+    quarter = packed // 4
+    chip = (place // 2) % 2
     total = add(keep, beside(send))
-    for axis, size, hop in (("blk", blk_size, 2), ("dp", dp_size, 1)):
-        while hop < size:
-            total = add(total, swap(total, axis, size, hop))
-            hop *= 2
-    other = beside(total)
+    leaving = lax.dynamic_slice_in_dim(total, (1 - chip) * quarter, quarter, 1)
+    total = lax.dynamic_slice_in_dim(total, chip * quarter, quarter, 1)
+    total = add(total, swap(leaving, "blk", blk_size, 2))
+    hop = 1
+    while hop < dp_size:
+        total = add(total, swap(total, "dp", dp_size, hop))
+        hop *= 2
+    total_x = swap(total, "blk", blk_size, 2)
+    total_core = beside(total)
+    total_both = beside(total_x)
     vector = ((1, side), f32)
     square = ((side, side), f32)
     grads = kernel_call(
         spread_body,
         [
-            ((width, side), f32),
+            ((side, width), f32),
             vector,
             vector,
             square,
@@ -781,22 +811,25 @@
             square,
             vector,
             ((side, sff), f32),
-            ((sff, side), f32),
-        ],
-        [total, other],
+            ((side, sff), f32),
+        ],
+        [total, total_x, total_core, total_both],
+        vmem=16,
         cost=(0, 2 * 10**6, 0),
     )
     grads = [grad.reshape(side) if grad.shape[0] == 1 else grad for grad in grads]
-
-    def both_rows(own, far):
-        first = jnp.where(row == 0, own, far)
-        second = jnp.where(row == 0, far, own)
-        return jnp.stack([first, second], axis=1)
-
+    grads[0], grads[-1] = grads[0].T, grads[-1].T
+
+    def both_rows(own, back, axis):
+        first = jnp.where(row == 0, own, back)
+        second = jnp.where(row == 0, back, own)
+        return jnp.stack([first, second], axis=axis)
+
+    far = across(far)
     return (
-        both_rows(out_own, across(out_far)),
-        both_rows(side_own, across(side_back)),
-        both_rows(grad_own, across(grad_far)),
+        both_rows(out_own, out_back, 1),
+        jnp.transpose(both_rows(side_own, far[0:side], 0), (2, 0, 1)),
+        jnp.transpose(both_rows(grad_own, far[side : 2 * side].astype(f32), 0), (2, 0, 1)),
         *grads,
     )
 

time: 131 us -> 92.6 us (0.71)
  local copies, waits for them, and re-layouts: 18.7 us -> 4.29 us
  Pallas kernels: 57.9 us -> 43.8 us
  waiting for transfers between devices: 36.7 us -> 25.8 us
    pallas_call x6, Pallas kernels: 57.9 us -> 43.8 us  [kernel_call(): pl.pallas_call(body, out_shape=[jax.ShapeDtypeStruct(shape, kind) for sha...]
    ppermute x15 -> x16, waiting for transfers between devices: 36.7 us -> 25.8 us  [swap(): return lax.ppermute(value, axis, [(i, i ^ hop) for i in range(size)])]
    unnamed x57 -> x42, local copies, waits for them, and re-layouts: 12.1 us -> 2.13 us
    dynamic_slice x6 -> x1, local copies, waits for them, and re-layouts: 4.75 us -> 2.02 us  [of_row(): return lax.dynamic_index_in_dim(array, which, 1, keepdims=False)]
    transpose x0 -> x2, other arithmetic: none -> 1.34 us  [the longest x1 0.69 us: per_device(): jnp.transpose(both_rows(grad_own, far[side:2 * side].astype(f32), 0), (2,...]
    ppermute x15 -> x16, starting transfers between devices: 14.7 us -> 15.7 us  [swap(): return lax.ppermute(value, axis, [(i, i ^ hop) for i in range(size)])]
  transfers between devices with their start and end apart: 15 -> 16, of which waited for: 8 -> 10; matrix products, arithmetic and copies ran while one was open for 7% -> 4% of each run, Pallas kernels for 7% -> 27%
where the time goes in v3:
time: 92.6 us; the launch traced here: 92.4 us
  Pallas kernels  43.8 us (47%)
  waiting for transfers between devices  25.8 us (28%)
  starting transfers between devices  15.7 us (17%)
  local copies, waits for them, and re-layouts  4.29 us (5%)
  other arithmetic  1.67 us (2%)
  between operations  1.06 us (1%)
    pallas_call x6, Pallas kernels, kernel_call(): pl.pallas_call(body, out_shape=[jax.ShapeDtypeStruct(shape, kind) for sha...  43.8 us
    ppermute x16, waiting for transfers between devices, swap(): return lax.ppermute(value, axis, [(i, i ^ hop) for i in range(size)])  25.8 us
    ppermute x16, starting transfers between devices, swap(): return lax.ppermute(value, axis, [(i, i ^ hop) for i in range(size)])  15.7 us
    unnamed x42, local copies, waits for them, and re-layouts  2.13 us
    dynamic_slice x1, local copies, waits for them, and re-layouts, of_row(): return lax.dynamic_index_in_dim(array, which, 1, keepdims=False)  2.02 us
  transfers between devices with their start and end apart: 16, of which 10 were waited for; matrix products, arithmetic and copies ran while one was open for 4% of the time, Pallas kernels for 27%

profile of v3, /device:TPU:0, one launch (start us, length us, event | category | flops | bytes accessed | tf_op | source)
XLA Modules:
  0.0 92.4 jit_solution(14977528443636305058)
XLA Ops:
  0.7 2.0 %constant_dynamic-slice_fusion.1 = bf16[256,1,768]{2,1,0:T(2,128)(2,1)S(1)} fusion(bf16[256,2,768]{2,1,0:T(2,128)(2,1)} %param.22, s32[]{:T(128)S(6)} %select_n.63), kind=kLoop, calls=%fused_computation.24 | loop fusion | bytes 786436 | tf_op jit(solution)/shard_map/jit(dynamic_index_in_dim)/dynamic_slice | solution.py:613
  2.8 0.0 copy-start
  2.8 0.0 copy-start.1
  2.8 0.0 copy-start.18
  2.8 0.0 copy-start.19
  2.8 0.0 copy-start.2
  2.8 0.0 copy-start.7
  2.8 0.0 copy-start.9
  2.9 0.0 copy-start.11
  2.9 0.0 copy-start.12
  2.9 0.0 copy-start.16
  2.9 0.1 copy.37
  3.1 0.5 collective-permute-start.2
  3.6 2.6 %collective-permute-start = (bf16[256,768]{1,0:T(8,128)(2,1)S(1)}, bf16[256,768]{1,0:T(8,128)(2,1)S(1)}, u32[]{:S(2)}, u32[]{:S(2)}) collective-permute-start(bf16[256,768]{1,0:T(8,128)(2,1)S(1)} %bitcast.44), channel_id=1, source_target_pairs={{0,2},{1,3},{2,0},{3,1},{4,6},{5,7},{6,4},{7,5},{8,10},{9,11},{10,... | collective-permute-start | bytes 1179656 | tf_op jit(solution)/shard_map/ppermute | solution.py:604
  6.2 0.6 collective-permute-start.1
  6.9 1.3 %shard_map.309 = (bf16[768,768]{1,0:T(8,128)(2,1)S(1)}, bf16[192,256]{1,0:T(8,128)(2,1)S(1)}, bf16[576,96]{1,0:T(8,128)(2,1)S(1)}, bf16[480,96]{1,0:T(8,128)(2,1)S(1)}, f32[96,128]{1,0:T(8,128)S(1)}) custom-call(bf16[768,768]{1,0:T(8,128)(2,1)S(1)} %copy-done.2, bf16[96,96]{1,0:T(8,128)(2,1)S(1)} %copy-done.10, bf16[96,96]{1,0:T(8,128)(2,1)S(1)} %copy-done.11, ...), custom_call_target="tpu_custom_call" | custom-call | flops 905969664 | bytes 2359296 | tf_op jit(solution)/shard_map/pallas_call | solution.py:64
  8.2 0.3 copy-done.4
  8.5 1.8 %shard_map.310 = (bf16[256,768]{1,0:T(8,128)(2,1)S(1)}, bf16[512,768]{1,0:T(8,128)(2,1)S(1)}, bf16[768,512]{1,0:T(8,128)(2,1)S(1)}) custom-call(bf16[256,768]{1,0:T(8,128)(2,1)S(1)} %dynamic-slice_bitcast_fusion.own, bf16[256,768]{1,0:T(8,128)(2,1)S(1)} %collective-permute-done.2.mate, f32[2,768]{1,0:T(2,128)S(1)} %maximum_convert_fusion.gains, ...), custom_call_target="tpu_custom_call" | custom-call | flops 1509949440 | bytes 4718592 | tf_op jit(solution)/shard_map/pallas_call | solution.py:64
  10.3 7.6 %collective-permute-done.1.side_far = bf16[192,256]{1,0:T(8,128)(2,1)S(1)} collective-permute-done((bf16[192,256]{1,0:T(8,128)(2,1)S(1)}, bf16[192,256]{1,0:T(8,128)(2,1)S(1)}, u32[]{:S(2)}, u32[]{:S(2)}) %collective-permute-start.1) | collective-permute-done | bytes 98336 | tf_op jit(solution)/shard_map/ppermute | solution.py:604
  18.0 1.7 %collective-permute-done.3.far_mate = bf16[256,768]{1,0:T(8,128)(2,1)S(1)} collective-permute-done((bf16[256,768]{1,0:T(8,128)(2,1)S(1)}, bf16[256,768]{1,0:T(8,128)(2,1)S(1)}, u32[]{:S(2)}, u32[]{:S(2)}) %collective-permute-start.3) | collective-permute-done | bytes 393248 | tf_op jit(solution)/shard_map/ppermute | solution.py:604
  19.7 0.0 copy-start.8
  19.7 17.3 %shard_map.311 = (bf16[256,768]{1,0:T(8,128)(2,1)S(1)}, bf16[256,768]{1,0:T(8,128)(2,1)S(1)}, bf16[512,96]{1,0:T(8,128)(2,1)S(1)}, bf16[96,512]{1,0:T(8,128)(2,1...) custom-call(s32[2,8]{1,0:T(2,128)S(1)} %copy-done.13, bf16[256,768]{1,0:T(8,128)(2,1)S(1)} %dynamic-slice_bitcast_fusion.own, ...), custom_call_target="tpu_custom_call" | custom-call | flops 20000000000 | bytes 16000000 | tf_op jit(solution)/shard_map/pallas_call | solution.py:64
  37.0 0.2 collective-permute-start.4
  37.2 1.8 %collective-permute-start.6 = (bf16[256,768]{1,0:T(8,128)(2,1)S(1)}, bf16[256,768]{1,0:T(8,128)(2,1)S(1)}, u32[]{:S(2)}, u32[]{:S(2)}) collective-permute-start(bf16[256,768]{1,0:T(8,128)(2,1)S(1)} %get-tuple-element.74.out_far), channel_id=1, source_target_pairs={{0,2},{1,3},{2,0},{3,1},{4,6},{5,7},{6,4},{7,5},{8,10},{9,11},{10,... | collective-permute-start | bytes 1179656 | tf_op jit(solution)/shard_map/ppermute | solution.py:604
  39.0 21.8 %shard_map.312 = (bf16[96,256]{1,0:T(8,128)(2,1)S(1)}, bf16[96,256]{1,0:T(8,128)(2,1)S(1)}, f32[96,512]{1,0:T(8,128)S(1)}, f32[192,512]{1,0:T(8,128)S(1)}, bf16[...) custom-call(s32[2,8]{1,0:T(2,128)S(1)} %copy-done.13, ...), custom_call_target="tpu_custom_call" | custom-call | flops 30000001024 | bytes 3000000 | tf_op jit(solution)/shard_map/pallas_call | solution.py:64
  60.8 0.1 collective-permute-start.5
  60.9 1.4 %collective-permute-done.5.dkv_back = bf16[192,512]{1,0:T(8,128)(2,1)S(1)} collective-permute-done((bf16[192,512]{1,0:T(8,128)(2,1)S(1)}, bf16[192,512]{1,0:T(8,128)(2,1)S(1)}, u32[]{:S(2)}, u32[]{:S(2)}) %collective-permute-start.5) | collective-permute-done | bytes 196640 | tf_op jit(solution)/shard_map/ppermute | solution.py:604
  62.3 0.7 shard_map.313
  63.0 0.2 collective-permute-start.8
  63.2 1.2 %collective-permute-start.7 = (bf16[192,256]{1,0:T(8,128)(2,1)S(1)}, bf16[192,256]{1,0:T(8,128)(2,1)S(1)}, u32[]{:S(2)}, u32[]{:S(2)}) collective-permute-start(bf16[192,256]{1,0:T(8,128)(2,1)S(1)} %get-tuple-element.85), channel_id=1, source_target_pairs={{0,2},{1,3},{2,0},{3,1},{4,6},{5,7},{6,4},{7,5},{8,10},{9,11},{10,... | collective-permute-start | bytes 294920 | tf_op jit(solution)/shard_map/ppermute | solution.py:604
  64.4 0.1 collective-permute-done.8
  64.6 1.3 %collective-permute-start.9 = (bf16[96,512]{1,0:T(8,128)(2,1)S(1)}, bf16[96,512]{1,0:T(8,128)(2,1)S(1)}, u32[]{:S(2)}, u32[]{:S(2)}) collective-permute-start(bf16[96,512]{1,0:T(8,128)(2,1)S(1)} %constant_dynamic-slice_fusion), channel_id=1, source_target_pairs={{0,2},{1,3},{2,0},{3,1},{4,6},{5,7},{6,4},{7,5},{8,10},{9,11},{10,... | collective-permute-start | bytes 294920 | tf_op jit(solution)/shard_map/ppermute | solution.py:604
  65.8 0.1 select_bitcast_fusion.1
  65.9 4.5 %collective-permute-done.9 = bf16[96,512]{1,0:T(8,128)(2,1)S(1)} collective-permute-done((bf16[96,512]{1,0:T(8,128)(2,1)S(1)}, bf16[96,512]{1,0:T(8,128)(2,1)S(1)}, u32[]{:S(2)}, u32[]{:S(2)}) %collective-permute-start.9) | collective-permute-done | bytes 98336 | tf_op jit(solution)/shard_map/ppermute | solution.py:604
  70.4 1.6 %collective-permute-start.10 = (bf16[96,512]{1,0:T(8,128)(2,1)S(1)}, bf16[96,512]{1,0:T(8,128)(2,1)S(1)}, u32[]{:S(2)}, u32[]{:S(2)}) collective-permute-start(bf16[96,512]{1,0:T(8,128)(2,1)S(1)} %add_convert_fusion.4), channel_id=1, source_target_pairs={{0,4},{4,0},{8,12},{12,8},{16,20},{20,16},{24,28},{28,24},{1,5},{5... | collective-permute-start | bytes 294920 | tf_op jit(solution)/shard_map/ppermute | solution.py:604
  72.0 0.1 pad_maximum_fusion
  72.1 1.7 %copy.38 = bf16[256,2,768]{2,1,0:T(2,128)(2,1)} copy(bf16[256,2,768]{2,0,1:T(8,128)(2,1)S(1)} %pad_maximum_fusion) | data formatting | bytes 1572864
  73.7 1.3 %collective-permute-done.10 = bf16[96,512]{1,0:T(8,128)(2,1)S(1)} collective-permute-done((bf16[96,512]{1,0:T(8,128)(2,1)S(1)}, bf16[96,512]{1,0:T(8,128)(2,1)S(1)}, u32[]{:S(2)}, u32[]{:S(2)}) %collective-permute-start.10) | collective-permute-done | bytes 98336 | tf_op jit(solution)/shard_map/ppermute | solution.py:604
  75.1 1.7 %collective-permute-start.11 = (bf16[96,512]{1,0:T(8,128)(2,1)S(1)}, bf16[96,512]{1,0:T(8,128)(2,1)S(1)}, u32[]{:S(2)}, u32[]{:S(2)}) collective-permute-start(bf16[96,512]{1,0:T(8,128)(2,1)S(1)} %add_convert_fusion.3), channel_id=1, source_target_pairs={{0,8},{4,12},{8,0},{12,4},{16,24},{20,28},{24,16},{28,20},{1,9},{5... | collective-permute-start | bytes 294920 | tf_op jit(solution)/shard_map/ppermute | solution.py:604
  76.8 3.0 %collective-permute-done.11 = bf16[96,512]{1,0:T(8,128)(2,1)S(1)} collective-permute-done((bf16[96,512]{1,0:T(8,128)(2,1)S(1)}, bf16[96,512]{1,0:T(8,128)(2,1)S(1)}, u32[]{:S(2)}, u32[]{:S(2)}) %collective-permute-start.11) | collective-permute-done | bytes 98336 | tf_op jit(solution)/shard_map/ppermute | solution.py:604
  79.8 2.8 %collective-permute-start.12 = (bf16[96,512]{1,0:T(8,128)(2,1)S(1)}, bf16[96,512]{1,0:T(8,128)(2,1)S(1)}, u32[]{:S(2)}, u32[]{:S(2)}) collective-permute-start(bf16[96,512]{1,0:T(8,128)(2,1)S(1)} %add_convert_fusion.2), channel_id=1, source_target_pairs={{0,16},{4,20},{8,24},{12,28},{16,0},{20,4},{24,8},{28,12},{1,17},{... | collective-permute-start | bytes 294920 | tf_op jit(solution)/shard_map/ppermute | solution.py:604
  82.6 2.8 %collective-permute-done.12 = bf16[96,512]{1,0:T(8,128)(2,1)S(1)} collective-permute-done((bf16[96,512]{1,0:T(8,128)(2,1)S(1)}, bf16[96,512]{1,0:T(8,128)(2,1)S(1)}, u32[]{:S(2)}, u32[]{:S(2)}) %collective-permute-start.12) | collective-permute-done | bytes 98336 | tf_op jit(solution)/shard_map/ppermute | solution.py:604
  85.4 1.3 %collective-permute-start.13 = (bf16[96,512]{1,0:T(8,128)(2,1)S(1)}, bf16[96,512]{1,0:T(8,128)(2,1)S(1)}, u32[]{:S(2)}, u32[]{:S(2)}) collective-permute-start(bf16[96,512]{1,0:T(8,128)(2,1)S(1)} %add_convert_fusion.1.part), channel_id=1, source_target_pairs={{0,2},{1,3},{2,0},{3,1},{4,6},{5,7},{6,4},{7,5},{8,10},{9,11},{10,... | collective-permute-start | bytes 294920 | tf_op jit(solution)/shard_map/ppermute | solution.py:604
  86.7 0.7 maximum_bitcast_fusion
  87.4 2.7 %collective-permute-done.13.part_x = bf16[96,512]{1,0:T(8,128)(2,1)S(1)} collective-permute-done((bf16[96,512]{1,0:T(8,128)(2,1)S(1)}, bf16[96,512]{1,0:T(8,128)(2,1)S(1)}, u32[]{:S(2)}, u32[]{:S(2)}) %collective-permute-start.13) | collective-permute-done | bytes 98336 | tf_op jit(solution)/shard_map/ppermute | solution.py:604
  90.1 0.7 maximum_bitcast_fusion.1
  90.8 0.6 collective-permute-done.15.part_both
  91.4 1.0 %shard_map.314 = (f32[96,768]{1,0:T(8,128)}, f32[1,96]{1,0:T(1,128)}, f32[1,96]{1,0:T(1,128)}, f32[96,96]{1,0:T(8,128)}, f32[96,96]{1,0:T(8,128)}, /*index=5*/f3...) custom-call(bf16[96,512]{1,0:T(8,128)(2,1)S(1)} %add_convert_fusion.1.part, ...), custom_call_target="tpu_custom_call" | custom-call | bytes 2000000 | tf_op jit(solution)/shard_map/pallas_call | solution.py:64
  (51 shorter events, 0.4 us)
Async XLA Ops:
  0.7 2.1 %copy-start.17 = (bf16[256,2,768]{2,1,0:T(2,128)(2,1)S(1)}, bf16[256,2,768]{2,1,0:T(2,128)(2,1)}, u32[]{:S(2)}) copy-start(bf16[256,2,768]{2,1,0:T(2,128)(2,1)} %param.22) | copy-start | bytes 2359300
  2.8 3.4 %copy-start = (bf16[256,2,96]{0,2,1:T(8,128)(2,1)S(1)}, bf16[256,2,96]{0,2,1:T(8,128)(2,1)}, u32[]{:S(2)}) copy-start(bf16[256,2,96]{0,2,1:T(8,128)(2,1)} %param.23) | copy-start | bytes 294916
  2.8 3.4 %copy-start.1 = (bf16[256,2,96]{0,2,1:T(8,128)(2,1)S(1)}, bf16[256,2,96]{0,2,1:T(8,128)(2,1)}, u32[]{:S(2)}) copy-start(bf16[256,2,96]{0,2,1:T(8,128)(2,1)} %param.43) | copy-start | bytes 294916
  2.8 3.9 %copy-start.18 = (bf16[768]{0:T(1024)(128)(2,1)S(1)}, bf16[768]{0:T(1024)(128)(2,1)}, u32[]{:S(2)}) copy-start(bf16[768]{0:T(1024)(128)(2,1)} %param.25) | copy-start | bytes 4612
  2.8 3.9 %copy-start.19 = (bf16[768]{0:T(1024)(128)(2,1)S(1)}, bf16[768]{0:T(1024)(128)(2,1)}, u32[]{:S(2)}) copy-start(bf16[768]{0:T(1024)(128)(2,1)} %param.30) | copy-start | bytes 4612
  2.8 3.9 %copy-start.2 = (bf16[768,768]{1,0:T(8,128)(2,1)S(1)}, bf16[768,768]{1,0:T(8,128)(2,1)}, u32[]{:S(2)}) copy-start(bf16[768,768]{1,0:T(8,128)(2,1)} %w_value.1) | copy-start | bytes 3538948
  2.8 3.9 %copy-start.7 = (bf16[96,384]{1,0:T(8,128)(2,1)S(1)}, bf16[96,384]{1,0:T(8,128)(2,1)}, u32[]{:S(2)}) copy-start(bf16[96,384]{1,0:T(8,128)(2,1)} %s_inner.3) | copy-start | bytes 221188
  2.8 3.9 %copy-start.9 = (bf16[96,96]{1,0:T(8,128)(2,1)S(1)}, bf16[96,96]{1,0:T(8,128)(2,1)}, u32[]{:S(2)}) copy-start(bf16[96,96]{1,0:T(8,128)(2,1)} %s_out.3) | copy-start | bytes 55300
  2.8 3.9 %copy-start.10 = (bf16[96,96]{1,0:T(8,128)(2,1)S(1)}, bf16[96,96]{1,0:T(8,128)(2,1)}, u32[]{:S(2)}) copy-start(bf16[96,96]{1,0:T(8,128)(2,1)} %s_query.3) | copy-start | bytes 55300
  2.9 3.9 %copy-start.11 = (bf16[96,96]{1,0:T(8,128)(2,1)S(1)}, bf16[96,96]{1,0:T(8,128)(2,1)}, u32[]{:S(2)}) copy-start(bf16[96,96]{1,0:T(8,128)(2,1)} %s_key.3) | copy-start | bytes 55300
  2.9 3.9 %copy-start.12 = (bf16[96,96]{1,0:T(8,128)(2,1)S(1)}, bf16[96,96]{1,0:T(8,128)(2,1)}, u32[]{:S(2)}) copy-start(bf16[96,96]{1,0:T(8,128)(2,1)} %s_value.3) | copy-start | bytes 55300
  2.9 3.9 %copy-start.14 = (f32[96]{0:T(128)S(1)}, f32[96]{0:T(128)}, u32[]{:S(2)}) copy-start(f32[96]{0:T(128)} %param.34) | copy-start | bytes 1156
  2.9 3.9 %copy-start.15 = (f32[96]{0:T(128)S(1)}, f32[96]{0:T(128)}, u32[]{:S(2)}) copy-start(f32[96]{0:T(128)} %param.35) | copy-start | bytes 1156
  2.9 3.9 %copy-start.16 = (f32[96]{0:T(128)S(1)}, f32[96]{0:T(128)}, u32[]{:S(2)}) copy-start(f32[96]{0:T(128)} %param.40) | copy-start | bytes 1156
  3.1 5.1 %collective-permute-start.2 = (bf16[256,768]{1,0:T(8,128)(2,1)S(1)}, bf16[256,768]{1,0:T(8,128)(2,1)S(1)}, u32[]{:S(2)}, u32[]{:S(2)}) collective-permute-start(bf16[256,768]{1,0:T(8,128)(2,1)S(1)} %dynamic-slice_bitcast_fusion.own), channel_id=1, source_target_pairs={{0,1},{1,0},{2,3},{3,2},{4,5},{5,4},{6,7},{7,6},{8,9},{9,8},{10,11... | collective-permute-start | bytes 1179656 | tf_op jit(solution)/shard_map/ppermute | solution.py:604
  3.6 14.4 %collective-permute-start = (bf16[256,768]{1,0:T(8,128)(2,1)S(1)}, bf16[256,768]{1,0:T(8,128)(2,1)S(1)}, u32[]{:S(2)}, u32[]{:S(2)}) collective-permute-start(bf16[256,768]{1,0:T(8,128)(2,1)S(1)} %bitcast.44), channel_id=1, source_target_pairs={{0,2},{1,3},{2,0},{3,1},{4,6},{5,7},{6,4},{7,5},{8,10},{9,11},{10,... | collective-permute-start | bytes 1179656 | tf_op jit(solution)/shard_map/ppermute | solution.py:604
  6.2 11.8 %collective-permute-start.1 = (bf16[192,256]{1,0:T(8,128)(2,1)S(1)}, bf16[192,256]{1,0:T(8,128)(2,1)S(1)}, u32[]{:S(2)}, u32[]{:S(2)}) collective-permute-start(bf16[192,256]{1,0:T(8,128)(2,1)S(1)} %fusion.3), channel_id=1, source_target_pairs={{0,2},{1,3},{2,0},{3,1},{4,6},{5,7},{6,4},{7,5},{8,10},{9,11},{10,... | collective-permute-start | bytes 294920 | tf_op jit(solution)/shard_map/ppermute | solution.py:604
  6.8 1.3 %copy-start.3 = (bf16[768,768]{1,0:T(8,128)(2,1)S(1)}, bf16[768,768]{1,0:T(8,128)(2,1)}, u32[]{:S(2)}) copy-start(bf16[768,768]{1,0:T(8,128)(2,1)} %w_query.3) | copy-start | bytes 3538948
  6.8 1.6 %copy-start.4 = (bf16[768,768]{1,0:T(8,128)(2,1)S(1)}, bf16[768,768]{1,0:T(8,128)(2,1)}, u32[]{:S(2)}) copy-start(bf16[768,768]{1,0:T(8,128)(2,1)} %w_key.3) | copy-start | bytes 3538948
  8.5 11.2 %copy-start.5 = (bf16[768,768]{1,0:T(8,128)(2,1)S(1)}, bf16[768,768]{1,0:T(8,128)(2,1)}, u32[]{:S(2)}) copy-start(bf16[768,768]{1,0:T(8,128)(2,1)} %w_out_hbm.1) | copy-start | bytes 3538948
  8.5 11.2 %copy-start.6 = (bf16[768,96]{0,1:T(8,128)(2,1)S(1)}, bf16[768,96]{0,1:T(8,128)(2,1)}, u32[]{:S(2)}) copy-start(bf16[768,96]{0,1:T(8,128)(2,1)} %param.33) | copy-start | bytes 442372
  8.5 11.2 %copy-start.13 = (s32[2,8]{1,0:T(2,128)S(1)}, s32[2,8]{1,0:T(2,128)}, u32[]{:S(2)}) copy-start(s32[2,8]{1,0:T(2,128)} %doc_lengths.3) | copy-start | bytes 196
  18.0 1.7 %collective-permute-start.3 = (bf16[256,768]{1,0:T(8,128)(2,1)S(1)}, bf16[256,768]{1,0:T(8,128)(2,1)S(1)}, u32[]{:S(2)}, u32[]{:S(2)}) collective-permute-start(bf16[256,768]{1,0:T(8,128)(2,1)S(1)} %collective-permute-done.far), channel_id=1, source_target_pairs={{0,1},{1,0},{2,3},{3,2},{4,5},{5,4},{6,7},{7,6},{8,9},{9,8},{10,11... | collective-permute-start | bytes 1179656 | tf_op jit(solution)/shard_map/ppermute | solution.py:604
  19.7 19.3 %copy-start.8 = (bf16[384,96]{0,1:T(8,128)(2,1)S(1)}, bf16[384,96]{0,1:T(8,128)(2,1)}, u32[]{:S(2)}) copy-start(bf16[384,96]{0,1:T(8,128)(2,1)} %param.42) | copy-start | bytes 221188
  37.0 2.0 %collective-permute-start.4 = (bf16[512,96]{1,0:T(8,128)(2,1)S(1)}, bf16[512,96]{1,0:T(8,128)(2,1)S(1)}, u32[]{:S(2)}, u32[]{:S(2)}) collective-permute-start(bf16[512,96]{1,0:T(8,128)(2,1)S(1)} %get-tuple-element.68.sn_own), channel_id=1, source_target_pairs={{0,1},{1,0},{2,3},{3,2},{4,5},{5,4},{6,7},{7,6},{8,9},{9,8},{10,11... | collective-permute-start | bytes 294920 | tf_op jit(solution)/shard_map/ppermute | solution.py:604
  37.2 25.1 %collective-permute-start.6 = (bf16[256,768]{1,0:T(8,128)(2,1)S(1)}, bf16[256,768]{1,0:T(8,128)(2,1)S(1)}, u32[]{:S(2)}, u32[]{:S(2)}) collective-permute-start(bf16[256,768]{1,0:T(8,128)(2,1)S(1)} %get-tuple-element.74.out_far), channel_id=1, source_target_pairs={{0,2},{1,3},{2,0},{3,1},{4,6},{5,7},{6,4},{7,5},{8,10},{9,11},{10,... | collective-permute-start | bytes 1179656 | tf_op jit(solution)/shard_map/ppermute | solution.py:604
  60.8 1.5 %collective-permute-start.5 = (bf16[192,512]{1,0:T(8,128)(2,1)S(1)}, bf16[192,512]{1,0:T(8,128)(2,1)S(1)}, u32[]{:S(2)}, u32[]{:S(2)}) collective-permute-start(bf16[192,512]{1,0:T(8,128)(2,1)S(1)} %get-tuple-element.73), channel_id=1, source_target_pairs={{0,1},{1,0},{2,3},{3,2},{4,5},{5,4},{6,7},{7,6},{8,9},{9,8},{10,11... | collective-permute-start | bytes 589832 | tf_op jit(solution)/shard_map/ppermute | solution.py:604
  63.0 1.5 %collective-permute-start.8 = (bf16[96,1024]{1,0:T(8,128)(2,1)S(1)}, bf16[96,1024]{1,0:T(8,128)(2,1)S(1)}, u32[]{:S(2)}, u32[]{:S(2)}) collective-permute-start(bf16[96,1024]{1,0:T(8,128)(2,1)S(1)} %get-tuple-element.88), channel_id=1, source_target_pairs={{0,1},{1,0},{2,3},{3,2},{4,5},{5,4},{6,7},{7,6},{8,9},{9,8},{10,11... | collective-permute-start | bytes 589832 | tf_op jit(solution)/shard_map/ppermute | solution.py:604
  63.2 13.6 %collective-permute-start.7 = (bf16[192,256]{1,0:T(8,128)(2,1)S(1)}, bf16[192,256]{1,0:T(8,128)(2,1)S(1)}, u32[]{:S(2)}, u32[]{:S(2)}) collective-permute-start(bf16[192,256]{1,0:T(8,128)(2,1)S(1)} %get-tuple-element.85), channel_id=1, source_target_pairs={{0,2},{1,3},{2,0},{3,1},{4,6},{5,7},{6,4},{7,5},{8,10},{9,11},{10,... | collective-permute-start | bytes 294920 | tf_op jit(solution)/shard_map/ppermute | solution.py:604
  64.6 5.8 %collective-permute-start.9 = (bf16[96,512]{1,0:T(8,128)(2,1)S(1)}, bf16[96,512]{1,0:T(8,128)(2,1)S(1)}, u32[]{:S(2)}, u32[]{:S(2)}) collective-permute-start(bf16[96,512]{1,0:T(8,128)(2,1)S(1)} %constant_dynamic-slice_fusion), channel_id=1, source_target_pairs={{0,2},{1,3},{2,0},{3,1},{4,6},{5,7},{6,4},{7,5},{8,10},{9,11},{10,... | collective-permute-start | bytes 294920 | tf_op jit(solution)/shard_map/ppermute | solution.py:604
  70.4 4.7 %collective-permute-start.10 = (bf16[96,512]{1,0:T(8,128)(2,1)S(1)}, bf16[96,512]{1,0:T(8,128)(2,1)S(1)}, u32[]{:S(2)}, u32[]{:S(2)}) collective-permute-start(bf16[96,512]{1,0:T(8,128)(2,1)S(1)} %add_convert_fusion.4), channel_id=1, source_target_pairs={{0,4},{4,0},{8,12},{12,8},{16,20},{20,16},{24,28},{28,24},{1,5},{5... | collective-permute-start | bytes 294920 | tf_op jit(solution)/shard_map/ppermute | solution.py:604
  75.1 4.7 %collective-permute-start.11 = (bf16[96,512]{1,0:T(8,128)(2,1)S(1)}, bf16[96,512]{1,0:T(8,128)(2,1)S(1)}, u32[]{:S(2)}, u32[]{:S(2)}) collective-permute-start(bf16[96,512]{1,0:T(8,128)(2,1)S(1)} %add_convert_fusion.3), channel_id=1, source_target_pairs={{0,8},{4,12},{8,0},{12,4},{16,24},{20,28},{24,16},{28,20},{1,9},{5... | collective-permute-start | bytes 294920 | tf_op jit(solution)/shard_map/ppermute | solution.py:604
  79.8 5.6 %collective-permute-start.12 = (bf16[96,512]{1,0:T(8,128)(2,1)S(1)}, bf16[96,512]{1,0:T(8,128)(2,1)S(1)}, u32[]{:S(2)}, u32[]{:S(2)}) collective-permute-start(bf16[96,512]{1,0:T(8,128)(2,1)S(1)} %add_convert_fusion.2), channel_id=1, source_target_pairs={{0,16},{4,20},{8,24},{12,28},{16,0},{20,4},{24,8},{28,12},{1,17},{... | collective-permute-start | bytes 294920 | tf_op jit(solution)/shard_map/ppermute | solution.py:604
  85.4 4.7 %collective-permute-start.13 = (bf16[96,512]{1,0:T(8,128)(2,1)S(1)}, bf16[96,512]{1,0:T(8,128)(2,1)S(1)}, u32[]{:S(2)}, u32[]{:S(2)}) collective-permute-start(bf16[96,512]{1,0:T(8,128)(2,1)S(1)} %add_convert_fusion.1.part), channel_id=1, source_target_pairs={{0,2},{1,3},{2,0},{3,1},{4,6},{5,7},{6,4},{7,5},{8,10},{9,11},{10,... | collective-permute-start | bytes 294920 | tf_op jit(solution)/shard_map/ppermute | solution.py:604
  87.4 3.4 %collective-permute-start.14 = (bf16[96,512]{1,0:T(8,128)(2,1)S(1)}, bf16[96,512]{1,0:T(8,128)(2,1)S(1)}, u32[]{:S(2)}, u32[]{:S(2)}) collective-permute-start(bf16[96,512]{1,0:T(8,128)(2,1)S(1)} %add_convert_fusion.1.part), channel_id=1, source_target_pairs={{0,1},{1,0},{2,3},{3,2},{4,5},{5,4},{6,7},{7,6},{8,9},{9,8},{10,11... | collective-permute-start | bytes 294920 | tf_op jit(solution)/shard_map/ppermute | solution.py:604
  90.1 1.3 %collective-permute-start.15 = (bf16[96,512]{1,0:T(8,128)(2,1)S(1)}, bf16[96,512]{1,0:T(8,128)(2,1)S(1)}, u32[]{:S(2)}, u32[]{:S(2)}) collective-permute-start(bf16[96,512]{1,0:T(8,128)(2,1)S(1)} %collective-permute-done.13.part_x), channel_id=1, source_target_pairs={{0,1},{1,0},{2,3},{3,2},{4,5},{5,4},{6,7},{7,6},{8,9},{9,8},{10,11... | collective-permute-start | bytes 294920 | tf_op jit(solution)/shard_map/ppermute | solution.py:604

commit v4 on v3

--- a/solution.py
+++ b/solution.py
@@ -9,6 +9,8 @@
 
 HEADS = 12
 SHEADS = 12
+GROUP = 4
+SPARE = 64
 EPS = 1e-06
 LOG2E = math.log2(math.e)
 FAR = 2.0**100
@@ -80,13 +82,37 @@
     return ones_where(source == thin)
 
 
-def prepare_body(
-    w_value, s_query, s_key, s_value, s_out, s_inner, gate, gain_in, gain_mid, value_t, dup, dup_t, tall_t, columns, lines
+def bounds(doc_lengths, row):
+    starts, ends, at = [], [], jnp.int32(0)
+    for d in range(doc_lengths.shape[1]):
+        starts.append(at)
+        at = at + doc_lengths[row, d]
+        ends.append(at)
+    return starts, ends
+
+
+def in_doc(doc_lengths, row, runs, length, shape, token_dim):
+    starts, ends = bounds(doc_lengths, row)
+    parts = []
+    part_shape = list(shape)
+    part_shape[token_dim] = length
+    number = iota(tuple(part_shape), 1 - token_dim)
+    first = jnp.zeros(tuple(part_shape), i32)
+    last = first
+    for d, (start, end) in enumerate(zip(starts, ends)):
+        first = jnp.where(number == d, start, first)
+        last = jnp.where(number == d, end, last)
+    for run in runs:
+        position = iota(tuple(part_shape), token_dim) + run
+        parts.append(jnp.where((position >= first) & (position < last), 1.0, 0.0))
+    return jnp.concatenate(parts, axis=token_dim)
+
+
+def side_weights_body(
+    s_query, s_key, s_value, s_out, s_inner, gate, gain_in, gain_mid, dup, dup_t, tall_t, columns, lines
 ):
-    side = s_out.shape[0]
+    side, hidden = s_inner.shape
     feature = side // SHEADS
-    hidden = s_inner.shape[1]
-    value_t[...] = nt(eye(w_value.shape[0]), w_value[...]).astype(bf16)
     spread = doubled(side, dup.shape[1], feature, False)
     dup[0:side] = nn(s_key[...], spread).astype(bf16)
     dup[side : 2 * side] = nn(s_value[...], spread).astype(bf16)
@@ -97,8 +123,32 @@
     tall_t[side : side + hidden] = nt(eye(hidden), s_inner[...]).astype(bf16)
     lines[...] = jnp.zeros(lines.shape, f32)
     for i, line in enumerate((gate, gain_in, gain_mid)):
-        lines[i : i + 1, 0:side] = line[...]
+        lines[i : i + 1, 0:side] = line[...].reshape(1, side)
     columns[...] = lines[...].T[0:side]
+
+
+def prepare_body(
+    doc_lengths, w_value, norm_in, norm_mid, value_t, gains, key_doc, query_doc, side_key_doc, side_query_doc
+):
+    value_t[...] = nt(eye(w_value.shape[0]), w_value[...]).astype(bf16)
+    for i, line in enumerate((norm_in, norm_mid)):
+        gains[i : i + 1] = line[...].astype(f32).reshape(1, line.shape[0])
+    keys, tokens = key_doc.shape[0], query_doc.shape[0]
+    span = tokens // 2
+    place, half = lax.axis_index("blk"), lax.axis_size("blk") // 2
+    row = place // half
+    own, mate = place * span, (place ^ 1) * span
+    far, far_mate = (place ^ half) * span, (place ^ half ^ 1) * span
+    found = in_doc(doc_lengths, row, (own, mate, far, far_mate), span, (keys, 128), 0)
+    key_doc[...] = (found - 1.0).astype(bf16)
+    mine = jnp.concatenate([found[0:span], found[tokens : tokens + span]], axis=0)
+    query_doc[...] = (mine * FAR).astype(bf16)
+    mates = jnp.concatenate([found[span:tokens], found[tokens + span : keys]], axis=0)
+    spare = SPARE
+    low = iota((keys, 128), 1) < spare
+    ordered = pltpu.roll(jnp.concatenate([mine, mates], axis=0), spare, 1)
+    side_key_doc[...] = jnp.where(low, 0.0, ordered - 1.0).astype(bf16)
+    side_query_doc[...] = (in_doc(doc_lengths, row, (own, far), span, (16, tokens), 1) * FAR).astype(bf16)
 
 
 def project(tokens, gain, w_query, w_key, value_t, scale, queries):
@@ -107,39 +157,55 @@
     return query, nn(normed, w_key[...]).astype(bf16), nt(value_t[...], normed).astype(bf16)
 
 
-def first_body(own, mate, gains, w_query, w_key, value_t, query, key, value):
-    span, width = own.shape
-    scale = LOG2E * (width // HEADS) ** -0.5
-    tokens = jnp.concatenate([own[...], mate[...]], axis=0)
-    query[...], key[...], value[...] = project(
-        tokens, gains[0:1], w_query, w_key, value_t, scale, span
-    )
-
-
-def bounds(doc_lengths, row):
-    starts, ends, at = [], [], jnp.int32(0)
-    for d in range(doc_lengths.shape[1]):
-        starts.append(at)
-        at = at + doc_lengths[row, d]
-        ends.append(at)
-    return starts, ends
-
-
-def in_doc(doc_lengths, row, blocks, span, shape, token_dim):
-    starts, ends = bounds(doc_lengths, row)
-    parts = []
-    part_shape = list(shape)
-    part_shape[token_dim] = span
-    number = iota(tuple(part_shape), 1 - token_dim)
-    first = jnp.zeros(tuple(part_shape), i32)
-    last = first
-    for d, (start, end) in enumerate(zip(starts, ends)):
-        first = jnp.where(number == d, start, first)
-        last = jnp.where(number == d, end, last)
-    for block in blocks:
-        position = iota(tuple(part_shape), token_dim) + block * span
-        parts.append(jnp.where((position >= first) & (position < last), 1.0, 0.0))
-    return jnp.concatenate(parts, axis=token_dim)
+def padded(value_t, head):
+    ones = jnp.ones((16, value_t.shape[1]), bf16)
+    pieces = []
+    for at in range(0, value_t.shape[0], head):
+        pieces += [value_t[at : at + head], ones]
+    return jnp.concatenate(pieces, axis=0)
+
+
+def pair_lanes(j):
+    return pl.ds(pl.multiple_of(j * 128, 128), 128)
+
+
+def pair_sums(j, queries, query_doc, keys, key_doc, values, shifted=False):
+    width = queries[0].shape[1]
+    head = width // HEADS
+    stride = values[0].shape[0] // HEADS
+    lanes = pair_lanes(j)
+    key = jnp.concatenate([ref[:, lanes] for ref in keys], axis=0)
+    key = jnp.concatenate([key, key_doc], axis=1)
+    query = jnp.concatenate([ref[:, lanes] for ref in queries], axis=0)
+    rows = pl.ds(pl.multiple_of(j * 2 * stride, 16), 2 * stride)
+    value = jnp.concatenate([ref[rows, :] for ref in values], axis=1)
+    lane = iota((1, 128), 1) // head
+    masked = [jnp.concatenate([query * ones_where(lane == i), query_doc], axis=1) for i in range(2)]
+    count = query.shape[0]
+
+    scores = nt(key, jnp.concatenate(masked, axis=0))
+    if shifted:
+        scores = scores - jnp.max(scores, axis=0, keepdims=True)
+    both = nn(value, jnp.exp2(scores).astype(bf16))
+    return [both[i * stride : i * stride + head + 8, i * count : (i + 1) * count] for i in range(2)]
+
+
+def first_body(own, mate, gains, w_query, w_key, value_t, key_doc, query_doc, query, key, value, part):
+    _, span, width = own.shape
+    head = width // HEADS
+    row = lax.axis_index("blk") // (lax.axis_size("blk") // 2)
+    tokens = jnp.concatenate([own[row], mate[row]], axis=0)
+    query[...], key[...], value_new = project(
+        tokens, gains[0:1], w_query, w_key, value_t, LOG2E * head**-0.5, span
+    )
+    value[...] = padded(value_new, head)
+
+    def pair(j, carry):
+        sums = pair_sums(j, [query], query_doc[0:span], [key], key_doc[0 : 2 * span], [value])
+        part[j] = jnp.concatenate(sums, axis=0)
+        return carry
+
+    lax.fori_loop(0, HEADS // 2, pair, 0, unroll=3)
 
 
 def out_of_range(totals):
@@ -147,122 +213,74 @@
     return jnp.logical_not((lowest > LOW_TOTAL) & (highest < HIGH_TOTAL))
 
 
-def backbone_body(
-    doc_lengths,
-    own,
+def second_body(
     far,
     far_mate,
-    query_own,
-    key_near,
-    value_near,
     gains,
     w_query,
     w_key,
     value_t,
-    down_w,
-    columns,
-    state,
-    side_far,
-    w_out_hbm,
-    w_inner_hbm,
-    w_outer_hbm,
-    out_own,
-    out_far,
-    sn_rows,
-    sn_t,
-    mixed_t,
-    lead_t,
+    key_doc,
+    query_doc,
+    query_a,
+    key_a,
+    value_a,
+    part_a,
+    attended,
     query,
     key,
     value,
-    key_doc,
-    query_doc,
     totals,
-    attended,
-    after,
-    w_out,
-    w_inner,
-    w_outer,
-    sems,
 ):
-    copies = [
-        pltpu.make_async_copy(source, target, sems.at[i])
-        for i, (source, target) in enumerate(
-            ((w_out_hbm, w_out), (w_inner_hbm, w_inner), (w_outer_hbm, w_outer))
-        )
-    ]
-    for copy in copies:
-        copy.start()
-    span, width = own.shape
+    span, width = far.shape
     head = width // HEADS
-    stride = value.shape[0] // HEADS
-    place = lax.axis_index("blk")
-    half = lax.axis_size("blk") // 2
-    row = place // half
-    near, opposite = place ^ 1, place ^ half
-    opposite_near = opposite ^ 1
-
     tokens = jnp.concatenate([far[...], far_mate[...]], axis=0)
-    query_far, key_far, value_far = project(
+    query[...], key[...], value_new = project(
         tokens, gains[0:1], w_query, w_key, value_t, LOG2E * head**-0.5, span
     )
-    query[0:span] = query_own[...]
-    query[span : 2 * span] = query_far
-    key[0 : 2 * span] = key_near[...]
-    key[2 * span : 4 * span] = key_far
-    for h in range(HEADS):
-        base = h * stride
-        value[base : base + head, 0 : 2 * span] = value_near[h * head : (h + 1) * head]
-        value[base : base + head, 2 * span : 4 * span] = value_far[h * head : (h + 1) * head]
-        value[base + head : base + stride] = jnp.ones((stride - head, 4 * span), bf16)
-    keys_in = in_doc(doc_lengths, row, (place, near, opposite, opposite_near), span, (4 * span, 128), 0)
-    key_doc[...] = (keys_in - 1.0).astype(bf16)
-    query_doc[...] = (
-        in_doc(doc_lengths, row, (place, opposite), span, (2 * span, 128), 0) * FAR
-    ).astype(bf16)
-
-    def attend(shifted):
-        def pair(j, carry):
-            lanes = pl.ds(pl.multiple_of(j * 128, 128), 128)
-            keys = jnp.concatenate([key[:, lanes], key_doc[...]], axis=1)
-            results = []
-            for side in range(128 // head):
-                mine = ones_where(iota((1, 128), 1) // head == side)
-                queries = jnp.concatenate([query[:, lanes] * mine, query_doc[...]], axis=1)
-                scores = nt(keys, queries)
-                if shifted:
-                    scores = scores - jnp.max(scores, axis=0, keepdims=True)
-                weights = jnp.exp2(scores).astype(bf16)
-                at = (j * (128 // head) + side) * stride
-                summed = nn(value[pl.ds(pl.multiple_of(at, 16), stride), :], weights)
-                total = summed[head : head + 1]
-                slot = pl.multiple_of((j * (128 // head) + side) * 8, 8)
-                totals[pl.ds(slot, 8), :] = summed[head : head + 8]
-                results.append(summed[0:head] * (1.0 / total))
-            joined = jnp.concatenate(results, axis=0)
-            attended[:, lanes] = joined.T.astype(bf16)
-            return carry
-
-        lax.fori_loop(0, width // 128, pair, 0)
-
-    attend(False)
+    value[...] = padded(value_new, head)
+    keys, values, queries = [key_a, key], [value_a, value], [query_a, query]
+
+    def finish(j, sums):
+        results = []
+        for i, summed in enumerate(sums):
+            totals[pl.ds(pl.multiple_of((2 * j + i) * 8, 8), 8), :] = summed[head : head + 8]
+            results.append(summed[0:head] * (1.0 / summed[head : head + 1]))
+        attended[:, pair_lanes(j)] = jnp.concatenate(results, axis=0).T.astype(bf16)
+
+    def pair(j, carry):
+        old = pair_sums(j, [query_a], query_doc[0:span], [key], key_doc[2 * span : 4 * span], [value])
+        new = pair_sums(j, [query], query_doc[span : 2 * span], keys, key_doc[...], values)
+        sums = []
+        for i in range(2):
+            rows = slice(i * (head + 8), (i + 1) * (head + 8))
+            sums.append(jnp.concatenate([old[i] + part_a[j, rows], new[i]], axis=1))
+        finish(j, sums)
+        return carry
+
+    lax.fori_loop(0, HEADS // 2, pair, 0, unroll=3)
 
     @pl.when(out_of_range(totals[...]))
     def _():
-        attend(True)
-
-    copies[0].wait()
-    after[0:span] = own[...].astype(f32) + nn(attended[0:span], w_out[...])
-    after[span : 2 * span] = far[...].astype(f32) + nn(attended[span : 2 * span], w_out[...])
-    middle = norm_lanes(after[...], gains[1:2]).astype(bf16)
-    copies[1].wait()
-    copies[2].wait()
-    hidden = w_inner.shape[1]
-    step = width
-    result = after[...]
-    for at in range(0, hidden, step):
-        act = gelu(nn(middle, w_inner[:, at : at + step])).astype(bf16)
-        result = result + nn(act, w_outer[at : at + step, :])
+        def again(j, carry):
+            finish(j, pair_sums(j, queries, query_doc[...], keys, key_doc[...], values, shifted=True))
+            return carry
+
+        lax.fori_loop(0, HEADS // 2, again, 0)
+
+
+def dense_body(
+    own, far, attended, gains, w_out, w_inner, w_outer, down_w, columns, state, side_far, out_own, out_far, sn_rows, sn_t, mixed_t, lead_t
+):
+    _, span, width = own.shape
+    row = lax.axis_index("blk") // (lax.axis_size("blk") // 2)
+    tokens = jnp.concatenate([own[row], far[...]], axis=0)
+    after = tokens.astype(f32) + nn(attended[...], w_out[...])
+    middle = norm_lanes(after, gains[1:2]).astype(bf16)
+    result = after
+    for at in range(0, w_inner.shape[1], width):
+        act = gelu(nn(middle, w_inner[:, at : at + width])).astype(bf16)
+        result = result + nn(act, w_outer[at : at + width, :])
     out = result.astype(bf16)
     out_own[...] = out[0:span]
     out_far[...] = out[span : 2 * span]
@@ -282,7 +300,6 @@
 
 
 def side_body(
-    doc_lengths,
     sn_own,
     sn_mate,
     mixed_t,
@@ -295,6 +312,8 @@
     s_out,
     s_inner,
     columns,
+    key_doc,
+    query_doc,
     out_own,
     out_far,
     dquery,
@@ -326,21 +345,13 @@
     place = lax.axis_index("blk")
     half = lax.axis_size("blk") // 2
     row = place // half
-    near, opposite = place ^ 1, place ^ half
-    opposite_near = opposite ^ 1
     scale = feature**-0.5
 
     sn = jnp.concatenate([sn_own[...], sn_mate[...]], axis=0)
-    lane = iota((2 * tokens, keys.shape[1]), 1)
-    docs = in_doc(
-        doc_lengths, row, (place, opposite, near, opposite_near), span, (2 * tokens, 128), 0
-    )
-    shift = wide % 128
-    docs = pltpu.roll(docs, shift, 1)
     projected = nn(sn, dup[0:side]).astype(bf16)
-    low_lane = iota((2 * tokens, 128), 1) < shift
     keys[:, 0:128] = projected[:, 0:128]
-    keys[:, 128:256] = jnp.where(low_lane, projected[:, 128:256].astype(f32), docs - 1.0).astype(bf16)
+    keys[:, 128:256] = projected[:, 128:256] + key_doc[...]
+    low_lane = iota((2 * tokens, 128), 1) < SPARE
     projected = nn(sn, dup[side : 2 * side]).astype(bf16)
     values[:, 0:128] = projected[:, 0:128]
     values[:, 128:256] = jnp.where(low_lane, projected[:, 128:256].astype(f32), 1.0).astype(bf16)
@@ -353,15 +364,14 @@
     high = scaled.astype(bf16).astype(f32)
     second = iota((wide, tokens), 0) % (2 * feature) >= feature
     query_s[...] = jnp.where(second, scaled - high, high).astype(bf16)
-    query_docs = in_doc(doc_lengths, row, (place, opposite), span, (16, tokens), 1) * FAR
-    for i in range(2):
+    for i in range(GROUP):
         query_h[i] = jnp.zeros(query_h.shape[1:], bf16)
-        query_h[i, wide : wide + 16] = query_docs.astype(bf16)
+        query_h[i, wide : wide + 16] = query_doc[...]
 
     def attend(shifted):
         def pair(j, carry):
-            for i in range(2):
-                h = 2 * j + i
+            for i in range(GROUP):
+                h = GROUP * j + i
                 rows = pl.ds(pl.multiple_of(h * 16, 16), 16)
                 eight = pl.ds(pl.multiple_of(h * 8, 8), 8)
                 query_h[i, rows, :] = query_s[rows, :]
@@ -379,7 +389,7 @@
                 attn_t[eight, :] = summed[0:feature] * invert
             return carry
 
-        lax.fori_loop(0, SHEADS // 2, pair, 0)
+        lax.fori_loop(0, SHEADS // GROUP, pair, 0)
 
     attend(False)
 
@@ -436,12 +446,12 @@
         dterm_s[h * 16 : (h + 1) * 16] = jnp.concatenate(
             [piece, jnp.zeros_like(piece)], axis=0
         ).astype(bf16)
-    for i in range(2):
+    for i in range(GROUP):
         dattn_h[i] = jnp.zeros(dattn_h.shape[1:], bf16)
 
     def back(j, carry):
-        for i in range(2):
-            h = 2 * j + i
+        for i in range(GROUP):
+            h = GROUP * j + i
             rows = pl.ds(pl.multiple_of(h * 16, 16), 16)
             eight = pl.ds(pl.multiple_of(h * 8, 8), 8)
             eight_v = pl.ds(pl.multiple_of(side + h * 8, 8), 8)
@@ -457,7 +467,7 @@
             dkv_t[eight_v, :] = both[0:feature] + both[feature : 2 * feature]
         return carry
 
-    lax.fori_loop(0, SHEADS // 2, back, 0)
+    lax.fori_loop(0, SHEADS // GROUP, back, 0)
     dkv_own[...] = dkv_t[:, 0:tokens]
     dkv_mate[...] = dkv_t[:, tokens : 2 * tokens].astype(bf16)
 
@@ -609,49 +619,80 @@
     def beside(value):
         return swap(value, "blk", blk_size, 1)
 
-    def of_row(array, which):
-        return lax.dynamic_index_in_dim(array, which, 1, keepdims=False)
-
-    leaving = of_row(hidden, 1 - row)
-    hidden_far = across(leaving)
-    hidden_own = of_row(lax.optimization_barrier((hidden, leaving))[0], row)
-    hidden_mate = beside(hidden_own)
+    hidden = jnp.transpose(hidden, (1, 0, 2))
+    hidden_far = across(lax.dynamic_index_in_dim(hidden, 1 - row, 0, keepdims=False))
+    hidden_mate = beside(hidden)
     state, cot = (jnp.transpose(array, (1, 2, 0)) for array in (side_state, cotangent))
     side_far = across(
         lax.dynamic_index_in_dim(jnp.concatenate([state, cot], axis=1), 1 - row, 0, keepdims=False)
     )
-    gains = jnp.stack([norm_in, norm_mid]).astype(f32)
-    lines = [line.reshape(1, side) for line in (gate, side_norm_in, side_norm_mid)]
     down_w, s_outer_t = w_down.T, s_outer.T
 
-    value_t, dup, dup_t, tall_t, columns = kernel_call(
+    value_t, gains, key_doc, query_doc, side_key_doc, side_query_doc = kernel_call(
         prepare_body,
         [
             ((width, width), bf16),
+            ((2, width), f32),
+            ((2 * tokens, 128), bf16),
+            ((tokens, 128), bf16),
+            ((2 * tokens, 128), bf16),
+            ((16, tokens), bf16),
+        ],
+        [doc_lengths, w_value, norm_in, norm_mid],
+        vmem=16,
+        scalars=(0,),
+        cost=(1000, 1000, 0),
+    )
+    head = width // HEADS
+    stride = head + 16
+    projections = (gains, w_query, w_key, value_t, key_doc, query_doc)
+
+    def state_of(queries, keys, columns):
+        return [
+            ((queries, width), bf16),
+            ((keys, width), bf16),
+            ((HEADS * stride, keys), bf16),
+            ((HEADS // 2, 2 * (head + 8), columns), f32),
+        ]
+
+    state_a = kernel_call(
+        first_body,
+        state_of(span, tokens, span),
+        [hidden, hidden_mate, *projections],
+        vmem=24,
+        cost=(1000, 1000, 0),
+    )
+    small = (s_query, s_key, s_value, s_out, s_inner, gate, side_norm_in, side_norm_mid)
+    hidden_far, small, *state_a = lax.optimization_barrier((hidden_far, small, *state_a))
+    dup, dup_t, tall_t, columns = kernel_call(
+        side_weights_body,
+        [
             ((2 * side, 256), bf16),
             ((6 * side, side), bf16),
             ((side + sff, side), bf16),
             ((side, 128), f32),
         ],
-        [w_value, s_query, s_key, s_value, s_out, s_inner, *lines],
-        vmem=12,
+        small,
+        vmem=8,
         scratch=[pltpu.VMEM((128, 128), f32)],
-        cost=(2 * width**3, 4 * width * width, 0),
-    )
-    query_own, key_near, value_near = kernel_call(
-        first_body,
-        [((span, width), bf16), ((tokens, width), bf16), ((width, tokens), bf16)],
-        [hidden_own, hidden_mate, gains, w_query, w_key, value_t],
-        vmem=20,
-        cost=(5 * tokens * width * width, 8 * width * width, 0),
-    )
-    hidden_far, side_far, query_own, key_near, value_near = lax.optimization_barrier(
-        (hidden_far, side_far, query_own, key_near, value_near)
-    )
-    far_mate = beside(hidden_far)
-    stride = width // HEADS + 16
+        cost=(1000, 1000, 0),
+    )
+    (attended,) = kernel_call(
+        second_body,
+        [((tokens, width), bf16)],
+        [hidden_far, beside(hidden_far), *projections, *state_a],
+        vmem=30,
+        scratch=[
+            pltpu.VMEM((span, width), bf16),
+            pltpu.VMEM((tokens, width), bf16),
+            pltpu.VMEM((HEADS * stride, tokens), bf16),
+            pltpu.VMEM((HEADS * 8, tokens), f32),
+        ],
+        cost=(8 * 10**9, 8 * 10**6, 0),
+    )
+    side_far, attended = lax.optimization_barrier((side_far, attended))
     out_own, out_far, sn_rows, sn_t, mixed_t, lead_t = kernel_call(
-        backbone_body,
+        dense_body,
         [
             ((span, width), bf16),
             ((span, width), bf16),
@@ -661,43 +702,20 @@
             ((side, tokens), f32),
         ],
         [
-            doc_lengths,
-            hidden_own,
+            hidden,
             hidden_far,
-            far_mate,
-            query_own,
-            key_near,
-            value_near,
+            attended,
             gains,
-            w_query,
-            w_key,
-            value_t,
+            w_out,
+            w_inner,
+            w_outer,
             down_w,
             columns,
             state,
             side_far,
-            w_out,
-            w_inner,
-            w_outer,
-        ],
-        vmem=44,
-        scalars=(0,),
-        whole=(15, 16, 17),
-        scratch=[
-            pltpu.VMEM((tokens, width), bf16),
-            pltpu.VMEM((2 * tokens, width), bf16),
-            pltpu.VMEM((HEADS * stride, 2 * tokens), bf16),
-            pltpu.VMEM((2 * tokens, 128), bf16),
-            pltpu.VMEM((tokens, 128), bf16),
-            pltpu.VMEM((HEADS * 8, tokens), f32),
-            pltpu.VMEM((tokens, width), bf16),
-            pltpu.VMEM((tokens, width), f32),
-            pltpu.VMEM((width, width), bf16),
-            pltpu.VMEM((width, ff), bf16),
-            pltpu.VMEM((ff, width), bf16),
-            pltpu.SemaphoreType.DMA((3,)),
-        ],
-        cost=(20 * 10**9, 16 * 10**6, 0),
+        ],
+        vmem=28,
+        cost=(10 * 10**9, 14 * 10**6, 0),
     )
     sn_mate = beside(sn_rows)
     out_back = across(out_far)
@@ -713,7 +731,6 @@
             ((side, 2 * sff + 128), f32),
         ],
         [
-            doc_lengths,
             sn_rows,
             sn_mate,
             mixed_t,
@@ -726,9 +743,10 @@
             s_out,
             s_inner,
             columns,
+            side_key_doc,
+            side_query_doc,
         ],
         vmem=36,
-        scalars=(0,),
         scratch=[
             pltpu.VMEM((SHEADS, 2 * tokens, tokens), bf16),
             pltpu.VMEM((2 * tokens, 256), bf16),
@@ -737,13 +755,13 @@
             pltpu.VMEM((2 * side, 2 * tokens), bf16),
             pltpu.VMEM((2 * side, tokens), bf16),
             pltpu.VMEM((2 * side, tokens), bf16),
-            pltpu.VMEM((2, 256, tokens), bf16),
+            pltpu.VMEM((GROUP, 256, tokens), bf16),
             pltpu.VMEM((side, tokens), f32),
             pltpu.VMEM((side, tokens), f32),
             pltpu.VMEM((side, tokens), f32),
             pltpu.VMEM((2 * side, tokens), bf16),
             pltpu.VMEM((2 * side, tokens), bf16),
-            pltpu.VMEM((2, 256, tokens), bf16),
+            pltpu.VMEM((GROUP, 256, tokens), bf16),
             pltpu.VMEM((2 * side, 2 * tokens), f32),
         ],
         cost=(30 * 10**9, 3 * 10**6, 0),
@@ -790,6 +808,7 @@
     leaving = lax.dynamic_slice_in_dim(total, (1 - chip) * quarter, quarter, 1)
     total = lax.dynamic_slice_in_dim(total, chip * quarter, quarter, 1)
     total = add(total, swap(leaving, "blk", blk_size, 2))
+    total, far = lax.optimization_barrier((total, far))
     hop = 1
     while hop < dp_size:
         total = add(total, swap(total, "dp", dp_size, hop))
@@ -820,16 +839,16 @@
     grads = [grad.reshape(side) if grad.shape[0] == 1 else grad for grad in grads]
     grads[0], grads[-1] = grads[0].T, grads[-1].T
 
-    def both_rows(own, back, axis):
+    def both_rows(own, back):
         first = jnp.where(row == 0, own, back)
         second = jnp.where(row == 0, back, own)
-        return jnp.stack([first, second], axis=axis)
+        return jnp.stack([first, second])
 
     far = across(far)
     return (
-        both_rows(out_own, out_back, 1),
-        jnp.transpose(both_rows(side_own, far[0:side], 0), (2, 0, 1)),
-        jnp.transpose(both_rows(grad_own, far[side : 2 * side].astype(f32), 0), (2, 0, 1)),
+        jnp.transpose(both_rows(out_own, out_back), (1, 0, 2)),
+        jnp.transpose(both_rows(side_own, far[0:side]), (2, 0, 1)),
+        jnp.transpose(both_rows(grad_own, far[side : 2 * side].astype(f32)), (2, 0, 1)),
         *grads,
     )
 

time: 92.6 us -> 84.9 us (0.917)
  waiting for transfers between devices: 25.8 us -> 16.8 us
    ppermute x16, waiting for transfers between devices: 25.8 us -> 16.8 us  [swap(): return lax.ppermute(value, axis, [(i, i ^ hop) for i in range(size)])]
    unnamed x42 -> x48, local copies, waits for them, and re-layouts: 2.13 us -> 4.38 us
    dynamic_slice x1 -> x0, local copies, waits for them, and re-layouts: 2.02 us -> none  [of_row(): return lax.dynamic_index_in_dim(array, which, 1, keepdims=False)]
    pallas_call x6 -> x8, Pallas kernels: 43.8 us -> 44.5 us  [kernel_call(): pl.pallas_call(body, out_shape=[jax.ShapeDtypeStruct(shape, kind) for sha...]
  transfers between devices with their start and end apart: 16 -> 16, of which waited for: 10 -> 10; matrix products, arithmetic and copies ran while one was open for 4% -> 4% of each run, Pallas kernels for 27% -> 43%
where the time goes in v4:
time: 84.9 us; the launch traced here: 84.7 us
  Pallas kernels  44.5 us (52%)
  waiting for transfers between devices  16.8 us (20%)
  starting transfers between devices  16.2 us (19%)
  local copies, waits for them, and re-layouts  4.43 us (5%)
  other arithmetic  1.67 us (2%)
  between operations  1.06 us (1%)
    pallas_call x8, Pallas kernels, kernel_call(): pl.pallas_call(body, out_shape=[jax.ShapeDtypeStruct(shape, kind) for sha...  44.5 us
    ppermute x16, waiting for transfers between devices, swap(): return lax.ppermute(value, axis, [(i, i ^ hop) for i in range(size)])  16.8 us
    ppermute x16, starting transfers between devices, swap(): return lax.ppermute(value, axis, [(i, i ^ hop) for i in range(size)])  16.2 us
    unnamed x48, local copies, waits for them, and re-layouts  4.38 us
  transfers between devices with their start and end apart: 16, of which 10 were waited for; matrix products, arithmetic and copies ran while one was open for 4% of the time, Pallas kernels for 43%

profile of v4, /device:TPU:0, one launch (start us, length us, event | category | flops | bytes accessed | tf_op | source)
XLA Modules:
  0.0 84.7 jit_solution(8251466689572382686)
XLA Ops:
  0.7 1.3 %copy.42 = bf16[256,2,768]{2,0,1:T(8,128)(2,1)S(1)} copy(bf16[256,2,768]{2,1,0:T(2,128)(2,1)} %param.22) | data formatting | bytes 1572864 | tf_op args[0]
  2.0 0.0 copy-start.1
  2.0 0.5 collective-permute-start.1
  2.6 2.6 %collective-permute-start = (bf16[256,768]{1,0:T(8,128)(2,1)S(1)}, bf16[256,768]{1,0:T(8,128)(2,1)S(1)}, u32[]{:S(2)}, u32[]{:S(2)}) collective-permute-start(bf16[256,768]{1,0:T(8,128)(2,1)S(1)} %dynamic-slice_bitcast_fusion), channel_id=1, source_target_pairs={{0,2},{1,3},{2,0},{3,1},{4,6},{5,7},{6,4},{7,5},{8,10},{9,11},{10,... | collective-permute-start | bytes 1179656 | tf_op jit(solution)/shard_map/ppermute | solution.py:614
  5.2 1.7 %shard_map.309 = (bf16[768,768]{1,0:T(8,128)(2,1)S(1)}, f32[2,768]{1,0:T(2,128)S(1)}, bf16[1024,128]{1,0:T(8,128)(2,1)S(1)}, bf16[512,128]{1,0:T(8,128)(2,1)S(1)...) custom-call(s32[2,8]{1,0:T(2,128)S(1)} %copy-done.12, bf16[768,768]{1,0:T(8,128)(2,1)S(1)} %copy-done, ...), custom_call_target="tpu_custom_call" | custom-call | flops 1000 | bytes 1000 | tf_op jit(solution)/shard_map/pallas_call | solution.py:66
  6.9 1.3 %copy-done.2 = bf16[768,768]{1,0:T(8,128)(2,1)S(1)} copy-done((bf16[768,768]{1,0:T(8,128)(2,1)S(1)}, bf16[768,768]{1,0:T(8,128)(2,1)}, u32[]{:S(2)}) %copy-start.2) | copy-done | bytes 1179672
  8.2 0.0 copy-start.7
  8.2 0.0 copy-start.8
  8.2 0.0 copy-start.14
  8.2 0.0 copy-start.15
  8.2 5.7 %shard_map.310 = (bf16[256,768]{1,0:T(8,128)(2,1)S(1)}, bf16[512,768]{1,0:T(8,128)(2,1)S(1)}, bf16[960,512]{1,0:T(8,128)(2,1)S(1)}, f32[6,144,256]{2,1,0:T(8,128)S(1)}) custom-call(bf16[2,256,768]{2,1,0:T(8,128)(2,1)S(1)} %bitcast.34, bf16[2,256,768]{2,1,0:T(8,128)(2,1)} %collective-permute-done.1.mate, f32[2,768]{1,0:T(2,128)S(1)} %get-tuple-element.73.gains, ...), custom_call_target="tpu_custom_call" | custom-call | flops 1000 | bytes 1000 | tf_op jit(solution)/shard_map/pallas_call | solution.py:66
  13.9 1.0 %collective-permute-done.far = bf16[256,768]{1,0:T(8,128)(2,1)S(1)} collective-permute-done((bf16[256,768]{1,0:T(8,128)(2,1)S(1)}, bf16[256,768]{1,0:T(8,128)(2,1)S(1)}, u32[]{:S(2)}, u32[]{:S(2)}) %collective-permute-start) | collective-permute-done | bytes 393248 | tf_op jit(solution)/shard_map/ppermute | solution.py:614
  14.9 1.8 %collective-permute-start.2 = (bf16[192,256]{1,0:T(8,128)(2,1)S(1)}, bf16[192,256]{1,0:T(8,128)(2,1)S(1)}, u32[]{:S(2)}, u32[]{:S(2)}) collective-permute-start(bf16[192,256]{1,0:T(8,128)(2,1)S(1)} %fusion.3), channel_id=1, source_target_pairs={{0,2},{1,3},{2,0},{3,1},{4,6},{5,7},{6,4},{7,5},{8,10},{9,11},{10,... | collective-permute-start | bytes 294920 | tf_op jit(solution)/shard_map/ppermute | solution.py:614
  16.8 0.0 slice-start
  16.8 0.0 slice-start.2
  16.8 0.3 shard_map.312
  17.1 0.0 slice-start.1
  17.1 0.0 slice-start.3
  17.2 8.0 %shard_map.311.attended = bf16[512,768]{1,0:T(8,128)(2,1)S(1)} custom-call(bf16[256,768]{1,0:T(8,128)(2,1)S(1)} %collective-permute-done.far, bf16[256,768]{1,0:T(8,128)(2,1)S(1)} %collective-permute-done.3.far_mate, f32[2,768]{1,0:T(2,128)S(1)} %get-tuple-element.73.gains, bf16[768,768]{1,0:T(8,128)(2,1)S(1)} %copy-done.1, bf16[768,768]{1,0:T(8,128)(2,1)S(1)} %copy-done.2, ...), custom_call_target="tpu_custom_call" | custom-call | flops 8000000000 | bytes 8000000 | tf_op jit(solution)/shard_map/pallas_call | solution.py:66
  25.3 6.7 %shard_map.313 = (bf16[256,768]{1,0:T(8,128)(2,1)S(1)}, bf16[256,768]{1,0:T(8,128)(2,1)S(1)}, bf16[512,96]{1,0:T(8,128)(2,1)S(1)}, bf16[96,512]{1,0:T(8,128)(2,1...) custom-call(bf16[2,256,768]{2,1,0:T(8,128)(2,1)S(1)} %bitcast.35, bf16[256,768]{1,0:T(8,128)(2,1)S(1)} %collective-permute-done.far, ...), custom_call_target="tpu_custom_call" | custom-call | flops 10000000000 | bytes 14000000 | tf_op jit(solution)/shard_map/pallas_call | solution.py:66
  32.0 0.3 collective-permute-start.4
  32.2 1.1 %collective-permute-start.6 = (bf16[256,768]{1,0:T(8,128)(2,1)S(1)}, bf16[256,768]{1,0:T(8,128)(2,1)S(1)}, u32[]{:S(2)}, u32[]{:S(2)}) collective-permute-start(bf16[256,768]{1,0:T(8,128)(2,1)S(1)} %get-tuple-element.106.out_far), channel_id=1, source_target_pairs={{0,2},{1,3},{2,0},{3,1},{4,6},{5,7},{6,4},{7,5},{8,10},{9,11},{10,... | collective-permute-start | bytes 1179656 | tf_op jit(solution)/shard_map/ppermute | solution.py:614
  33.3 0.0 collective-permute-done.4.sn_mate
  33.4 20.5 %shard_map.314 = (bf16[96,256]{1,0:T(8,128)(2,1)S(1)}, bf16[96,256]{1,0:T(8,128)(2,1)S(1)}, f32[96,512]{1,0:T(8,128)S(1)}, f32[192,512]{1,0:T(8,128)S(1)}, bf16[...) custom-call(bf16[512,96]{1,0:T(8,128)(2,1)S(1)} %get-tuple-element.98.sn_own, ...), custom_call_target="tpu_custom_call" | custom-call | flops 30000001024 | bytes 3000000 | tf_op jit(solution)/shard_map/pallas_call | solution.py:66
  53.9 0.3 collective-permute-start.5
  54.2 1.2 %collective-permute-done.5.dkv_back = bf16[192,512]{1,0:T(8,128)(2,1)S(1)} collective-permute-done((bf16[192,512]{1,0:T(8,128)(2,1)S(1)}, bf16[192,512]{1,0:T(8,128)(2,1)S(1)}, u32[]{:S(2)}, u32[]{:S(2)}) %collective-permute-start.5) | collective-permute-done | bytes 196640 | tf_op jit(solution)/shard_map/ppermute | solution.py:614
  55.4 0.7 shard_map.315
  56.1 0.3 collective-permute-start.7
  56.4 1.2 %collective-permute-done.7 = bf16[96,1024]{1,0:T(8,128)(2,1)S(1)} collective-permute-done((bf16[96,1024]{1,0:T(8,128)(2,1)S(1)}, bf16[96,1024]{1,0:T(8,128)(2,1)S(1)}, u32[]{:S(2)}, u32[]{:S(2)}) %collective-permute-start.7) | collective-permute-done | bytes 196640 | tf_op jit(solution)/shard_map/ppermute | solution.py:614
  57.7 1.2 %collective-permute-start.8 = (bf16[96,512]{1,0:T(8,128)(2,1)S(1)}, bf16[96,512]{1,0:T(8,128)(2,1)S(1)}, u32[]{:S(2)}, u32[]{:S(2)}) collective-permute-start(bf16[96,512]{1,0:T(8,128)(2,1)S(1)} %constant_dynamic-slice_fusion), channel_id=1, source_target_pairs={{0,2},{1,3},{2,0},{3,1},{4,6},{5,7},{6,4},{7,5},{8,10},{9,11},{10,... | collective-permute-start | bytes 294920 | tf_op jit(solution)/shard_map/ppermute | solution.py:614
  58.9 0.1 select_bitcast_fusion.1
  59.0 3.7 %collective-permute-done.8 = bf16[96,512]{1,0:T(8,128)(2,1)S(1)} collective-permute-done((bf16[96,512]{1,0:T(8,128)(2,1)S(1)}, bf16[96,512]{1,0:T(8,128)(2,1)S(1)}, u32[]{:S(2)}, u32[]{:S(2)}) %collective-permute-start.8) | collective-permute-done | bytes 98336 | tf_op jit(solution)/shard_map/ppermute | solution.py:614
  62.7 1.6 %collective-permute-start.10 = (bf16[96,512]{1,0:T(8,128)(2,1)S(1)}, bf16[96,512]{1,0:T(8,128)(2,1)S(1)}, u32[]{:S(2)}, u32[]{:S(2)}) collective-permute-start(bf16[96,512]{1,0:T(8,128)(2,1)S(1)} %add_convert_fusion.4), channel_id=1, source_target_pairs={{0,4},{4,0},{8,12},{12,8},{16,20},{20,16},{24,28},{28,24},{1,5},{5... | collective-permute-start | bytes 294920 | tf_op jit(solution)/shard_map/ppermute | solution.py:614
  64.3 0.1 maximum_bitcast_fusion
  64.4 1.7 %copy.39 = bf16[256,2,768]{2,1,0:T(2,128)(2,1)} copy(bf16[256,2,768]{2,0,1:T(8,128)(2,1)S(1)} %maximum_bitcast_fusion) | data formatting | bytes 1572864
  66.0 1.1 %collective-permute-start.9 = (bf16[192,256]{1,0:T(8,128)(2,1)S(1)}, bf16[192,256]{1,0:T(8,128)(2,1)S(1)}, u32[]{:S(2)}, u32[]{:S(2)}) collective-permute-start(bf16[192,256]{1,0:T(8,128)(2,1)S(1)} %get-tuple-element.120), channel_id=1, source_target_pairs={{0,2},{1,3},{2,0},{3,1},{4,6},{5,7},{6,4},{7,5},{8,10},{9,11},{10,... | collective-permute-start | bytes 294920 | tf_op jit(solution)/shard_map/ppermute | solution.py:614
  67.2 0.2 collective-permute-done.10
  67.4 1.6 %collective-permute-start.11 = (bf16[96,512]{1,0:T(8,128)(2,1)S(1)}, bf16[96,512]{1,0:T(8,128)(2,1)S(1)}, u32[]{:S(2)}, u32[]{:S(2)}) collective-permute-start(bf16[96,512]{1,0:T(8,128)(2,1)S(1)} %add_convert_fusion.3), channel_id=1, source_target_pairs={{0,8},{4,12},{8,0},{12,4},{16,24},{20,28},{24,16},{28,20},{1,9},{5... | collective-permute-start | bytes 294920 | tf_op jit(solution)/shard_map/ppermute | solution.py:614
  69.1 1.6 %collective-permute-done.9 = bf16[192,256]{1,0:T(8,128)(2,1)S(1)} collective-permute-done((bf16[192,256]{1,0:T(8,128)(2,1)S(1)}, bf16[192,256]{1,0:T(8,128)(2,1)S(1)}, u32[]{:S(2)}, u32[]{:S(2)}) %collective-permute-start.9) | collective-permute-done | bytes 98336 | tf_op jit(solution)/shard_map/ppermute | solution.py:614
  70.7 1.4 %collective-permute-done.11 = bf16[96,512]{1,0:T(8,128)(2,1)S(1)} collective-permute-done((bf16[96,512]{1,0:T(8,128)(2,1)S(1)}, bf16[96,512]{1,0:T(8,128)(2,1)S(1)}, u32[]{:S(2)}, u32[]{:S(2)}) %collective-permute-start.11) | collective-permute-done | bytes 98336 | tf_op jit(solution)/shard_map/ppermute | solution.py:614
  72.1 2.7 %collective-permute-start.12 = (bf16[96,512]{1,0:T(8,128)(2,1)S(1)}, bf16[96,512]{1,0:T(8,128)(2,1)S(1)}, u32[]{:S(2)}, u32[]{:S(2)}) collective-permute-start(bf16[96,512]{1,0:T(8,128)(2,1)S(1)} %add_convert_fusion.2), channel_id=1, source_target_pairs={{0,16},{4,20},{8,24},{12,28},{16,0},{20,4},{24,8},{28,12},{1,17},{... | collective-permute-start | bytes 294920 | tf_op jit(solution)/shard_map/ppermute | solution.py:614
  74.8 2.9 %collective-permute-done.12 = bf16[96,512]{1,0:T(8,128)(2,1)S(1)} collective-permute-done((bf16[96,512]{1,0:T(8,128)(2,1)S(1)}, bf16[96,512]{1,0:T(8,128)(2,1)S(1)}, u32[]{:S(2)}, u32[]{:S(2)}) %collective-permute-start.12) | collective-permute-done | bytes 98336 | tf_op jit(solution)/shard_map/ppermute | solution.py:614
  77.7 1.2 %collective-permute-start.13 = (bf16[96,512]{1,0:T(8,128)(2,1)S(1)}, bf16[96,512]{1,0:T(8,128)(2,1)S(1)}, u32[]{:S(2)}, u32[]{:S(2)}) collective-permute-start(bf16[96,512]{1,0:T(8,128)(2,1)S(1)} %add_convert_fusion.1.part), channel_id=1, source_target_pairs={{0,2},{1,3},{2,0},{3,1},{4,6},{5,7},{6,4},{7,5},{8,10},{9,11},{10,... | collective-permute-start | bytes 294920 | tf_op jit(solution)/shard_map/ppermute | solution.py:614
  78.9 0.7 maximum_bitcast_fusion.1
  79.6 2.8 %collective-permute-done.13.part_x = bf16[96,512]{1,0:T(8,128)(2,1)S(1)} collective-permute-done((bf16[96,512]{1,0:T(8,128)(2,1)S(1)}, bf16[96,512]{1,0:T(8,128)(2,1)S(1)}, u32[]{:S(2)}, u32[]{:S(2)}) %collective-permute-start.13) | collective-permute-done | bytes 98336 | tf_op jit(solution)/shard_map/ppermute | solution.py:614
  82.4 0.7 maximum_bitcast_fusion.2
  83.1 0.6 collective-permute-done.15.part_both
  83.7 1.0 %shard_map.316 = (f32[96,768]{1,0:T(8,128)}, f32[1,96]{1,0:T(1,128)}, f32[1,96]{1,0:T(1,128)}, f32[96,96]{1,0:T(8,128)}, f32[96,96]{1,0:T(8,128)}, /*index=5*/f3...) custom-call(bf16[96,512]{1,0:T(8,128)(2,1)S(1)} %add_convert_fusion.1.part, ...), custom_call_target="tpu_custom_call" | custom-call | bytes 2000000 | tf_op jit(solution)/shard_map/pallas_call | solution.py:66
  (56 shorter events, 0.3 us)
Async XLA Ops:
  0.6 4.5 %copy-start.12 = (s32[2,8]{1,0:T(2,128)S(1)}, s32[2,8]{1,0:T(2,128)}, u32[]{:S(2)}) copy-start(s32[2,8]{1,0:T(2,128)} %doc_lengths.1) | copy-start | bytes 196
  0.7 4.5 %copy-start = (bf16[768,768]{1,0:T(8,128)(2,1)S(1)}, bf16[768,768]{1,0:T(8,128)(2,1)}, u32[]{:S(2)}) copy-start(bf16[768,768]{1,0:T(8,128)(2,1)} %w_value.1) | copy-start | bytes 3538948
  0.7 4.5 %copy-start.10 = (bf16[768]{0:T(1024)(128)(2,1)S(1)}, bf16[768]{0:T(1024)(128)(2,1)}, u32[]{:S(2)}) copy-start(bf16[768]{0:T(1024)(128)(2,1)} %norm_in.1) | copy-start | bytes 4612
  0.7 4.5 %copy-start.11 = (bf16[768]{0:T(1024)(128)(2,1)S(1)}, bf16[768]{0:T(1024)(128)(2,1)}, u32[]{:S(2)}) copy-start(bf16[768]{0:T(1024)(128)(2,1)} %norm_mid.1) | copy-start | bytes 4612
  2.0 4.9 %copy-start.1 = (bf16[768,768]{1,0:T(8,128)(2,1)S(1)}, bf16[768,768]{1,0:T(8,128)(2,1)}, u32[]{:S(2)}) copy-start(bf16[768,768]{1,0:T(8,128)(2,1)} %w_query.3) | copy-start | bytes 3538948
  2.0 4.9 %collective-permute-start.1 = (bf16[2,256,768]{2,1,0:T(8,128)(2,1)S(1)}, bf16[2,256,768]{2,1,0:T(8,128)(2,1)}, u32[]{:S(2)}, u32[]{:S(2)}) collective-permute-start(bf16[2,256,768]{2,1,0:T(8,128)(2,1)S(1)} %bitcast.33), channel_id=1, source_target_pairs={{0,1},{1,0},{2,3},{3,2},{4,5},{5,4},{6,7},{7,6},{8,9},{9,8},{10,11... | collective-permute-start | bytes 2359304 | tf_op jit(solution)/shard_map/ppermute | solution.py:614
  2.6 12.3 %collective-permute-start = (bf16[256,768]{1,0:T(8,128)(2,1)S(1)}, bf16[256,768]{1,0:T(8,128)(2,1)S(1)}, u32[]{:S(2)}, u32[]{:S(2)}) collective-permute-start(bf16[256,768]{1,0:T(8,128)(2,1)S(1)} %dynamic-slice_bitcast_fusion), channel_id=1, source_target_pairs={{0,2},{1,3},{2,0},{3,1},{4,6},{5,7},{6,4},{7,5},{8,10},{9,11},{10,... | collective-permute-start | bytes 1179656 | tf_op jit(solution)/shard_map/ppermute | solution.py:614
  6.9 1.3 %copy-start.2 = (bf16[768,768]{1,0:T(8,128)(2,1)S(1)}, bf16[768,768]{1,0:T(8,128)(2,1)}, u32[]{:S(2)}) copy-start(bf16[768,768]{1,0:T(8,128)(2,1)} %w_key.3) | copy-start | bytes 3538948
  8.2 6.7 %copy-start.3 = (bf16[256,2,96]{0,2,1:T(8,128)(2,1)S(1)}, bf16[256,2,96]{0,2,1:T(8,128)(2,1)}, u32[]{:S(2)}) copy-start(bf16[256,2,96]{0,2,1:T(8,128)(2,1)} %param.23) | copy-start | bytes 294916
  8.2 6.7 %copy-start.4 = (bf16[256,2,96]{0,2,1:T(8,128)(2,1)S(1)}, bf16[256,2,96]{0,2,1:T(8,128)(2,1)}, u32[]{:S(2)}) copy-start(bf16[256,2,96]{0,2,1:T(8,128)(2,1)} %param.43) | copy-start | bytes 294916
  8.2 8.6 %copy-start.5 = (bf16[96,384]{1,0:T(8,128)(2,1)S(1)}, bf16[96,384]{1,0:T(8,128)(2,1)}, u32[]{:S(2)}) copy-start(bf16[96,384]{1,0:T(8,128)(2,1)} %s_inner.2) | copy-start | bytes 221188
  8.2 8.6 %copy-start.6 = (bf16[96,96]{1,0:T(8,128)(2,1)S(1)}, bf16[96,96]{1,0:T(8,128)(2,1)}, u32[]{:S(2)}) copy-start(bf16[96,96]{1,0:T(8,128)(2,1)} %s_out.2) | copy-start | bytes 55300
  8.2 8.6 %copy-start.7 = (bf16[96,96]{1,0:T(8,128)(2,1)S(1)}, bf16[96,96]{1,0:T(8,128)(2,1)}, u32[]{:S(2)}) copy-start(bf16[96,96]{1,0:T(8,128)(2,1)} %s_query.2) | copy-start | bytes 55300
  8.2 8.6 %copy-start.8 = (bf16[96,96]{1,0:T(8,128)(2,1)S(1)}, bf16[96,96]{1,0:T(8,128)(2,1)}, u32[]{:S(2)}) copy-start(bf16[96,96]{1,0:T(8,128)(2,1)} %s_key.2) | copy-start | bytes 55300
  8.2 8.6 %copy-start.9 = (bf16[96,96]{1,0:T(8,128)(2,1)S(1)}, bf16[96,96]{1,0:T(8,128)(2,1)}, u32[]{:S(2)}) copy-start(bf16[96,96]{1,0:T(8,128)(2,1)} %s_value.2) | copy-start | bytes 55300
  8.2 8.6 %copy-start.13 = (f32[96]{0:T(128)S(1)}, f32[96]{0:T(128)}, u32[]{:S(2)}) copy-start(f32[96]{0:T(128)} %gate) | copy-start | bytes 1156
  8.2 8.6 %copy-start.14 = (f32[96]{0:T(128)S(1)}, f32[96]{0:T(128)}, u32[]{:S(2)}) copy-start(f32[96]{0:T(128)} %gain_in) | copy-start | bytes 1156
  8.2 8.5 %copy-start.15 = (f32[96]{0:T(128)S(1)}, f32[96]{0:T(128)}, u32[]{:S(2)}) copy-start(f32[96]{0:T(128)} %gain_mid) | copy-start | bytes 1156
  14.9 2.3 %collective-permute-start.3 = (bf16[256,768]{1,0:T(8,128)(2,1)S(1)}, bf16[256,768]{1,0:T(8,128)(2,1)S(1)}, u32[]{:S(2)}, u32[]{:S(2)}) collective-permute-start(bf16[256,768]{1,0:T(8,128)(2,1)S(1)} %collective-permute-done.far), channel_id=1, source_target_pairs={{0,1},{1,0},{2,3},{3,2},{4,5},{5,4},{6,7},{7,6},{8,9},{9,8},{10,11... | collective-permute-start | bytes 1179656 | tf_op jit(solution)/shard_map/ppermute | solution.py:614
  14.9 10.2 %collective-permute-start.2 = (bf16[192,256]{1,0:T(8,128)(2,1)S(1)}, bf16[192,256]{1,0:T(8,128)(2,1)S(1)}, u32[]{:S(2)}, u32[]{:S(2)}) collective-permute-start(bf16[192,256]{1,0:T(8,128)(2,1)S(1)} %fusion.3), channel_id=1, source_target_pairs={{0,2},{1,3},{2,0},{3,1},{4,6},{5,7},{6,4},{7,5},{8,10},{9,11},{10,... | collective-permute-start | bytes 294920 | tf_op jit(solution)/shard_map/ppermute | solution.py:614
  16.8 8.4 %slice-start = ((s8[4718592]{0:T(1024)(128)(4,1)}), s8[4194304]{0:T(1024)(128)(4,1)S(1)}, s32[]{:S(2)}) async-start(s8[4718592]{0:T(1024)(128)(4,1)} %bitcast.40), calls=%async_computation | async-start | bytes 8388608
  16.8 8.4 %slice-start.2 = ((s8[4718592]{0:T(1024)(128)(4,1)}), s8[4194304]{0:T(1024)(128)(4,1)S(1)}, s32[]{:S(2)}) async-start(s8[4718592]{0:T(1024)(128)(4,1)} %bitcast.42), calls=%async_computation.2 | async-start | bytes 8388608
  17.1 8.1 %slice-start.1 = ((s8[4718592]{0:T(1024)(128)(4,1)}), s8[524288]{0:T(1024)(128)(4,1)S(1)}, s32[]{:S(2)}) async-start(s8[4718592]{0:T(1024)(128)(4,1)} %bitcast.40), calls=%async_computation.1 | async-start | bytes 1048576
  17.1 8.1 %slice-start.3 = ((s8[4718592]{0:T(1024)(128)(4,1)}), s8[524288]{0:T(1024)(128)(4,1)S(1)}, s32[]{:S(2)}) async-start(s8[4718592]{0:T(1024)(128)(4,1)} %bitcast.42), calls=%async_computation.3 | async-start | bytes 1048576
  17.2 8.1 %copy-start.16 = (bf16[768,768]{1,0:T(8,128)(2,1)S(1)}, bf16[768,768]{1,0:T(8,128)(2,1)}, u32[]{:S(2)}) copy-start(bf16[768,768]{1,0:T(8,128)(2,1)} %w_out.1) | copy-start | bytes 3538948
  17.2 8.1 %copy-start.17 = (bf16[768,96]{0,1:T(8,128)(2,1)S(1)}, bf16[768,96]{0,1:T(8,128)(2,1)}, u32[]{:S(2)}) copy-start(bf16[768,96]{0,1:T(8,128)(2,1)} %param.33) | copy-start | bytes 442372
  25.3 8.1 %copy-start.18 = (bf16[384,96]{0,1:T(8,128)(2,1)S(1)}, bf16[384,96]{0,1:T(8,128)(2,1)}, u32[]{:S(2)}) copy-start(bf16[384,96]{0,1:T(8,128)(2,1)} %param.42) | copy-start | bytes 221188
  32.0 1.4 %collective-permute-start.4 = (bf16[512,96]{1,0:T(8,128)(2,1)S(1)}, bf16[512,96]{1,0:T(8,128)(2,1)S(1)}, u32[]{:S(2)}, u32[]{:S(2)}) collective-permute-start(bf16[512,96]{1,0:T(8,128)(2,1)S(1)} %get-tuple-element.98.sn_own), channel_id=1, source_target_pairs={{0,1},{1,0},{2,3},{3,2},{4,5},{5,4},{6,7},{7,6},{8,9},{9,8},{10,11... | collective-permute-start | bytes 294920 | tf_op jit(solution)/shard_map/ppermute | solution.py:614
  32.2 23.2 %collective-permute-start.6 = (bf16[256,768]{1,0:T(8,128)(2,1)S(1)}, bf16[256,768]{1,0:T(8,128)(2,1)S(1)}, u32[]{:S(2)}, u32[]{:S(2)}) collective-permute-start(bf16[256,768]{1,0:T(8,128)(2,1)S(1)} %get-tuple-element.106.out_far), channel_id=1, source_target_pairs={{0,2},{1,3},{2,0},{3,1},{4,6},{5,7},{6,4},{7,5},{8,10},{9,11},{10,... | collective-permute-start | bytes 1179656 | tf_op jit(solution)/shard_map/ppermute | solution.py:614
  53.9 1.5 %collective-permute-start.5 = (bf16[192,512]{1,0:T(8,128)(2,1)S(1)}, bf16[192,512]{1,0:T(8,128)(2,1)S(1)}, u32[]{:S(2)}, u32[]{:S(2)}) collective-permute-start(bf16[192,512]{1,0:T(8,128)(2,1)S(1)} %get-tuple-element.105), channel_id=1, source_target_pairs={{0,1},{1,0},{2,3},{3,2},{4,5},{5,4},{6,7},{7,6},{8,9},{9,8},{10,11... | collective-permute-start | bytes 589832 | tf_op jit(solution)/shard_map/ppermute | solution.py:614
  56.1 1.5 %collective-permute-start.7 = (bf16[96,1024]{1,0:T(8,128)(2,1)S(1)}, bf16[96,1024]{1,0:T(8,128)(2,1)S(1)}, u32[]{:S(2)}, u32[]{:S(2)}) collective-permute-start(bf16[96,1024]{1,0:T(8,128)(2,1)S(1)} %get-tuple-element.118), channel_id=1, source_target_pairs={{0,1},{1,0},{2,3},{3,2},{4,5},{5,4},{6,7},{7,6},{8,9},{9,8},{10,11... | collective-permute-start | bytes 589832 | tf_op jit(solution)/shard_map/ppermute | solution.py:614
  57.7 5.0 %collective-permute-start.8 = (bf16[96,512]{1,0:T(8,128)(2,1)S(1)}, bf16[96,512]{1,0:T(8,128)(2,1)S(1)}, u32[]{:S(2)}, u32[]{:S(2)}) collective-permute-start(bf16[96,512]{1,0:T(8,128)(2,1)S(1)} %constant_dynamic-slice_fusion), channel_id=1, source_target_pairs={{0,2},{1,3},{2,0},{3,1},{4,6},{5,7},{6,4},{7,5},{8,10},{9,11},{10,... | collective-permute-start | bytes 294920 | tf_op jit(solution)/shard_map/ppermute | solution.py:614
  62.7 4.7 %collective-permute-start.10 = (bf16[96,512]{1,0:T(8,128)(2,1)S(1)}, bf16[96,512]{1,0:T(8,128)(2,1)S(1)}, u32[]{:S(2)}, u32[]{:S(2)}) collective-permute-start(bf16[96,512]{1,0:T(8,128)(2,1)S(1)} %add_convert_fusion.4), channel_id=1, source_target_pairs={{0,4},{4,0},{8,12},{12,8},{16,20},{20,16},{24,28},{28,24},{1,5},{5... | collective-permute-start | bytes 294920 | tf_op jit(solution)/shard_map/ppermute | solution.py:614
  66.0 4.6 %collective-permute-start.9 = (bf16[192,256]{1,0:T(8,128)(2,1)S(1)}, bf16[192,256]{1,0:T(8,128)(2,1)S(1)}, u32[]{:S(2)}, u32[]{:S(2)}) collective-permute-start(bf16[192,256]{1,0:T(8,128)(2,1)S(1)} %get-tuple-element.120), channel_id=1, source_target_pairs={{0,2},{1,3},{2,0},{3,1},{4,6},{5,7},{6,4},{7,5},{8,10},{9,11},{10,... | collective-permute-start | bytes 294920 | tf_op jit(solution)/shard_map/ppermute | solution.py:614
  67.4 4.7 %collective-permute-start.11 = (bf16[96,512]{1,0:T(8,128)(2,1)S(1)}, bf16[96,512]{1,0:T(8,128)(2,1)S(1)}, u32[]{:S(2)}, u32[]{:S(2)}) collective-permute-start(bf16[96,512]{1,0:T(8,128)(2,1)S(1)} %add_convert_fusion.3), channel_id=1, source_target_pairs={{0,8},{4,12},{8,0},{12,4},{16,24},{20,28},{24,16},{28,20},{1,9},{5... | collective-permute-start | bytes 294920 | tf_op jit(solution)/shard_map/ppermute | solution.py:614
  72.1 5.6 %collective-permute-start.12 = (bf16[96,512]{1,0:T(8,128)(2,1)S(1)}, bf16[96,512]{1,0:T(8,128)(2,1)S(1)}, u32[]{:S(2)}, u32[]{:S(2)}) collective-permute-start(bf16[96,512]{1,0:T(8,128)(2,1)S(1)} %add_convert_fusion.2), channel_id=1, source_target_pairs={{0,16},{4,20},{8,24},{12,28},{16,0},{20,4},{24,8},{28,12},{1,17},{... | collective-permute-start | bytes 294920 | tf_op jit(solution)/shard_map/ppermute | solution.py:614
  77.7 4.7 %collective-permute-start.13 = (bf16[96,512]{1,0:T(8,128)(2,1)S(1)}, bf16[96,512]{1,0:T(8,128)(2,1)S(1)}, u32[]{:S(2)}, u32[]{:S(2)}) collective-permute-start(bf16[96,512]{1,0:T(8,128)(2,1)S(1)} %add_convert_fusion.1.part), channel_id=1, source_target_pairs={{0,2},{1,3},{2,0},{3,1},{4,6},{5,7},{6,4},{7,5},{8,10},{9,11},{10,... | collective-permute-start | bytes 294920 | tf_op jit(solution)/shard_map/ppermute | solution.py:614
  79.6 3.5 %collective-permute-start.14 = (bf16[96,512]{1,0:T(8,128)(2,1)S(1)}, bf16[96,512]{1,0:T(8,128)(2,1)S(1)}, u32[]{:S(2)}, u32[]{:S(2)}) collective-permute-start(bf16[96,512]{1,0:T(8,128)(2,1)S(1)} %add_convert_fusion.1.part), channel_id=1, source_target_pairs={{0,1},{1,0},{2,3},{3,2},{4,5},{5,4},{6,7},{7,6},{8,9},{9,8},{10,11... | collective-permute-start | bytes 294920 | tf_op jit(solution)/shard_map/ppermute | solution.py:614
  82.4 1.3 %collective-permute-start.15 = (bf16[96,512]{1,0:T(8,128)(2,1)S(1)}, bf16[96,512]{1,0:T(8,128)(2,1)S(1)}, u32[]{:S(2)}, u32[]{:S(2)}) collective-permute-start(bf16[96,512]{1,0:T(8,128)(2,1)S(1)} %collective-permute-done.13.part_x), channel_id=1, source_target_pairs={{0,1},{1,0},{2,3},{3,2},{4,5},{5,4},{6,7},{7,6},{8,9},{9,8},{10,11... | collective-permute-start | bytes 294920 | tf_op jit(solution)/shard_map/ppermute | solution.py:614

commit v5 on v4

--- a/solution.py
+++ b/solution.py
@@ -9,7 +9,7 @@
 
 HEADS = 12
 SHEADS = 12
-GROUP = 4
+GROUP = 6
 SPARE = 64
 EPS = 1e-06
 LOG2E = math.log2(math.e)
@@ -114,8 +114,7 @@
     side, hidden = s_inner.shape
     feature = side // SHEADS
     spread = doubled(side, dup.shape[1], feature, False)
-    dup[0:side] = nn(s_key[...], spread).astype(bf16)
-    dup[side : 2 * side] = nn(s_value[...], spread).astype(bf16)
+    dup[...] = nn(s_key[...], spread).astype(bf16)
     spread_t = doubled(2 * side, side, feature, True)
     for i, weight in enumerate((s_query, s_key, s_value)):
         dup_t[2 * side * i : 2 * side * (i + 1)] = nt(spread_t, weight[...]).astype(bf16)
@@ -205,7 +204,7 @@
         part[j] = jnp.concatenate(sums, axis=0)
         return carry
 
-    lax.fori_loop(0, HEADS // 2, pair, 0, unroll=3)
+    lax.fori_loop(0, HEADS // 2, pair, 0, unroll=6)
 
 
 def out_of_range(totals):
@@ -258,7 +257,7 @@
         finish(j, sums)
         return carry
 
-    lax.fori_loop(0, HEADS // 2, pair, 0, unroll=3)
+    lax.fori_loop(0, HEADS // 2, pair, 0, unroll=6)
 
     @pl.when(out_of_range(totals[...]))
     def _():
@@ -297,6 +296,23 @@
     lead_t[...] = down_t - state_t
     sn_t[...] = normed.astype(bf16)
     sn_rows[...] = normed.T.astype(bf16)
+
+
+def outer_rows(left, right):
+    return jnp.concatenate([left[f : f + 1] * right for f in range(left.shape[0])], axis=0)
+
+
+def inner_rows(left, products):
+    count = left.shape[0]
+    total = left[0:1] * products[0:count]
+    for f in range(1, count):
+        total = total + left[f : f + 1] * products[f * count : (f + 1) * count]
+    return total
+
+
+def two_parts(value):
+    high = value.astype(bf16).astype(f32)
+    return [high, value - high]
 
 
 def side_body(
@@ -323,7 +339,6 @@
     early,
     weights,
     keys,
-    values,
     key_t,
     value_t,
     query_t,
@@ -332,9 +347,8 @@
     attn_t,
     inverse,
     totals,
-    dattn_s,
-    dterm_s,
-    dattn_h,
+    moments,
+    back_rows,
     dkv_t,
 ):
     tokens, side = sn_own.shape
@@ -342,19 +356,13 @@
     feature = side // SHEADS
     hidden = s_inner.shape[1]
     wide = 2 * side
-    place = lax.axis_index("blk")
-    half = lax.axis_size("blk") // 2
-    row = place // half
+    row = lax.axis_index("blk") // (lax.axis_size("blk") // 2)
     scale = feature**-0.5
 
     sn = jnp.concatenate([sn_own[...], sn_mate[...]], axis=0)
-    projected = nn(sn, dup[0:side]).astype(bf16)
+    projected = nn(sn, dup[...]).astype(bf16)
     keys[:, 0:128] = projected[:, 0:128]
     keys[:, 128:256] = projected[:, 128:256] + key_doc[...]
-    low_lane = iota((2 * tokens, 128), 1) < SPARE
-    projected = nn(sn, dup[side : 2 * side]).astype(bf16)
-    values[:, 0:128] = projected[:, 0:128]
-    values[:, 128:256] = jnp.where(low_lane, projected[:, 128:256].astype(f32), 1.0).astype(bf16)
     key_t[...] = nt(dup_t[wide : 2 * wide], sn).astype(bf16)
     second = iota((wide, 2 * tokens), 0) % (2 * feature) >= feature
     value_t[...] = jnp.where(second, 1.0, nt(dup_t[2 * wide : 3 * wide], sn)).astype(bf16)
@@ -368,12 +376,14 @@
         query_h[i] = jnp.zeros(query_h.shape[1:], bf16)
         query_h[i, wide : wide + 16] = query_doc[...]
 
+    def head_rows(h, count):
+        return pl.ds(pl.multiple_of(h * count, count), count)
+
     def attend(shifted):
-        def pair(j, carry):
+        def group(j, carry):
             for i in range(GROUP):
                 h = GROUP * j + i
-                rows = pl.ds(pl.multiple_of(h * 16, 16), 16)
-                eight = pl.ds(pl.multiple_of(h * 8, 8), 8)
+                rows, eight = head_rows(h, 16), head_rows(h, 8)
                 query_h[i, rows, :] = query_s[rows, :]
                 scores = nn(keys[...], query_h[i])
                 query_h[i, rows, :] = jnp.zeros((16, tokens), bf16)
@@ -381,15 +391,22 @@
                     scores = scores - jnp.max(scores, axis=0, keepdims=True)
                 weight = jnp.exp2(scores).astype(bf16)
                 weights[h] = weight
-                summed = nn(value_t[rows, :], weight)
+                value, key = value_t[rows, :], key_t[rows, :]
+                products = outer_rows(value[0:feature].astype(f32), key[0:feature].astype(f32))
+                products = jnp.concatenate(two_parts(products), axis=0).astype(bf16)
+                summed = nn(jnp.concatenate([value, key, products], axis=0), weight)
                 total = summed[feature : 2 * feature]
                 totals[eight, :] = total
                 invert = 1.0 / total
                 inverse[eight, :] = invert
                 attn_t[eight, :] = summed[0:feature] * invert
+                at = 4 * feature + feature * feature
+                moments[h] = jnp.concatenate(
+                    [summed[2 * feature : 4 * feature], summed[4 * feature : at] + summed[at:]], axis=0
+                )
             return carry
 
-        lax.fori_loop(0, SHEADS // GROUP, pair, 0)
+        lax.fori_loop(0, SHEADS // GROUP, group, 0)
 
     attend(False)
 
@@ -421,50 +438,37 @@
     dmid = dy + mid_scale * (scaled - unit * jnp.mean(scaled * unit, axis=0, keepdims=True))
     dmid_t[...] = dmid
     dmid_low = dmid.astype(bf16)
-    last = jnp.concatenate(
-        [nt(attn_low, dmid_low), jnp.zeros((side, 128 - side), f32)], axis=1
-    )
+    last = jnp.concatenate([nt(attn_low, dmid_low), jnp.zeros((side, 128 - side), f32)], axis=1)
     early[:, 2 * hidden : 2 * hidden + 128] = jnp.where(
         iota((side, 128), 1) == side, grad_gain, last
     )
     dattn = nn(s_out[...], dmid_low).astype(bf16).astype(f32)
 
-    number = iota((feature, tokens), 0)
     for h in range(SHEADS):
         eight = slice(h * feature, (h + 1) * feature)
         invert = inverse[eight, :]
-        part = dattn[eight] * invert
-        high = part.astype(bf16).astype(f32)
-        dattn_s[h * 16 : (h + 1) * 16] = jnp.concatenate([high, part - high], axis=0).astype(bf16)
-        term = -jnp.sum(dattn[eight] * attn[eight], axis=0, keepdims=True) * invert
-        first = term.astype(bf16).astype(f32)
-        rest = term - first
-        middle = rest.astype(bf16).astype(f32)
-        piece = jnp.where(
-            number == 0, first, jnp.where(number == 1, middle, jnp.where(number == 2, rest - middle, 0.0))
-        )
-        dterm_s[h * 16 : (h + 1) * 16] = jnp.concatenate(
-            [piece, jnp.zeros_like(piece)], axis=0
+        term = jnp.sum(dattn[eight] * attn[eight], axis=0, keepdims=True)
+        moment = moments[h]
+        raw = inner_rows(dattn[eight], moment[2 * feature :]) - term * moment[0:feature]
+        dquery[eight, :] = raw * invert * scale
+        query = query_t[2 * h * feature : (2 * h + 1) * feature].astype(f32)
+        share = dattn[eight] * invert
+        back_rows[h] = jnp.concatenate(
+            two_parts(share) + two_parts(term * invert * query) + two_parts(outer_rows(share, query)), axis=0
         ).astype(bf16)
-    for i in range(GROUP):
-        dattn_h[i] = jnp.zeros(dattn_h.shape[1:], bf16)
 
     def back(j, carry):
         for i in range(GROUP):
             h = GROUP * j + i
-            rows = pl.ds(pl.multiple_of(h * 16, 16), 16)
-            eight = pl.ds(pl.multiple_of(h * 8, 8), 8)
-            eight_v = pl.ds(pl.multiple_of(side + h * 8, 8), 8)
-            dattn_h[i, rows, :] = dattn_s[rows, :]
-            dattn_h[i, wide : wide + 16] = dterm_s[rows, :]
-            slope = nn(values[...], dattn_h[i])
-            dattn_h[i, rows, :] = jnp.zeros((16, tokens), bf16)
-            weight = weights[h]
-            dscores = (weight.astype(f32) * slope).astype(bf16)
-            dquery[eight, :] = nn(key_t[rows, :], dscores)[0:feature] * scale
-            dkv_t[eight, :] = nt(query_t[rows, :], dscores)[0:feature] * scale
-            both = nt(dattn_s[rows, :], weight)
-            dkv_t[eight_v, :] = both[0:feature] + both[feature : 2 * feature]
+            summed = nt(back_rows[h], weights[h])
+            dkv_t[pl.ds(pl.multiple_of(side + h * feature, feature), feature), :] = (
+                summed[0:feature] + summed[feature : 2 * feature]
+            )
+            value = value_t[head_rows(h, 16), :][0:feature].astype(f32)
+            at = 4 * feature + feature * feature
+            raw = inner_rows(value, summed[4 * feature : at] + summed[at:])
+            raw = raw - (summed[2 * feature : 3 * feature] + summed[3 * feature : 4 * feature])
+            dkv_t[head_rows(h, feature), :] = raw * scale
         return carry
 
     lax.fori_loop(0, SHEADS // GROUP, back, 0)
@@ -605,6 +609,7 @@
     ff = w_inner.shape[1]
     sff = s_inner.shape[1]
     tokens = 2 * span
+    feature = side // SHEADS
     blk_size, dp_size = lax.axis_size("blk"), lax.axis_size("dp")
     half = blk_size // 2
     place = lax.axis_index("blk")
@@ -667,7 +672,7 @@
     dup, dup_t, tall_t, columns = kernel_call(
         side_weights_body,
         [
-            ((2 * side, 256), bf16),
+            ((side, 256), bf16),
             ((6 * side, side), bf16),
             ((side + sff, side), bf16),
             ((side, 128), f32),
@@ -750,7 +755,6 @@
         scratch=[
             pltpu.VMEM((SHEADS, 2 * tokens, tokens), bf16),
             pltpu.VMEM((2 * tokens, 256), bf16),
-            pltpu.VMEM((2 * tokens, 256), bf16),
             pltpu.VMEM((2 * side, 2 * tokens), bf16),
             pltpu.VMEM((2 * side, 2 * tokens), bf16),
             pltpu.VMEM((2 * side, tokens), bf16),
@@ -759,9 +763,8 @@
             pltpu.VMEM((side, tokens), f32),
             pltpu.VMEM((side, tokens), f32),
             pltpu.VMEM((side, tokens), f32),
-            pltpu.VMEM((2 * side, tokens), bf16),
-            pltpu.VMEM((2 * side, tokens), bf16),
-            pltpu.VMEM((GROUP, 256, tokens), bf16),
+            pltpu.VMEM((SHEADS, feature * (feature + 2), tokens), f32),
+            pltpu.VMEM((SHEADS, feature * (2 * feature + 4), tokens), bf16),
             pltpu.VMEM((2 * side, 2 * tokens), f32),
         ],
         cost=(30 * 10**9, 3 * 10**6, 0),

time: 84.9 us -> 77 us (0.907)
  Pallas kernels: 44.5 us -> 36.3 us
    pallas_call x8, Pallas kernels: 44.5 us -> 36.3 us  [kernel_call(): pl.pallas_call(body, out_shape=[jax.ShapeDtypeStruct(shape, kind) for sha...]
  transfers between devices with their start and end apart: 16 -> 16, of which waited for: 10 -> 10; matrix products, arithmetic and copies ran while one was open for 4% -> 4% of each run, Pallas kernels for 43% -> 36%
where the time goes in v5:
time: 77 us; the launch traced here: 76.8 us
  Pallas kernels  36.3 us (47%)
  waiting for transfers between devices  17.2 us (22%)
  starting transfers between devices  16.2 us (21%)
  local copies, waits for them, and re-layouts  4.43 us (6%)
  other arithmetic  1.67 us (2%)
  between operations  1.06 us (1%)
    pallas_call x8, Pallas kernels, kernel_call(): pl.pallas_call(body, out_shape=[jax.ShapeDtypeStruct(shape, kind) for sha...  36.3 us
    ppermute x16, waiting for transfers between devices, swap(): return lax.ppermute(value, axis, [(i, i ^ hop) for i in range(size)])  17.2 us
    ppermute x16, starting transfers between devices, swap(): return lax.ppermute(value, axis, [(i, i ^ hop) for i in range(size)])  16.2 us
    unnamed x48, local copies, waits for them, and re-layouts  4.38 us
  transfers between devices with their start and end apart: 16, of which 10 were waited for; matrix products, arithmetic and copies ran while one was open for 4% of the time, Pallas kernels for 36%

profile of v5, /device:TPU:0, one launch (start us, length us, event | category | flops | bytes accessed | tf_op | source)
XLA Modules:
  0.0 76.8 jit_solution(32523498520739303)
XLA Ops:
  0.7 1.3 %copy.42 = bf16[256,2,768]{2,0,1:T(8,128)(2,1)S(1)} copy(bf16[256,2,768]{2,1,0:T(2,128)(2,1)} %param.22) | data formatting | bytes 1572864 | tf_op args[0]
  2.0 0.0 copy-start.1
  2.0 0.5 collective-permute-start.1
  2.6 2.6 %collective-permute-start = (bf16[256,768]{1,0:T(8,128)(2,1)S(1)}, bf16[256,768]{1,0:T(8,128)(2,1)S(1)}, u32[]{:S(2)}, u32[]{:S(2)}) collective-permute-start(bf16[256,768]{1,0:T(8,128)(2,1)S(1)} %dynamic-slice_bitcast_fusion), channel_id=1, source_target_pairs={{0,2},{1,3},{2,0},{3,1},{4,6},{5,7},{6,4},{7,5},{8,10},{9,11},{10,... | collective-permute-start | bytes 1179656 | tf_op jit(solution)/shard_map/ppermute | solution.py:619
  5.2 1.7 %shard_map.309 = (bf16[768,768]{1,0:T(8,128)(2,1)S(1)}, f32[2,768]{1,0:T(2,128)S(1)}, bf16[1024,128]{1,0:T(8,128)(2,1)S(1)}, bf16[512,128]{1,0:T(8,128)(2,1)S(1)...) custom-call(s32[2,8]{1,0:T(2,128)S(1)} %copy-done.12, bf16[768,768]{1,0:T(8,128)(2,1)S(1)} %copy-done, ...), custom_call_target="tpu_custom_call" | custom-call | flops 1000 | bytes 1000 | tf_op jit(solution)/shard_map/pallas_call | solution.py:66
  6.9 1.3 %copy-done.2 = bf16[768,768]{1,0:T(8,128)(2,1)S(1)} copy-done((bf16[768,768]{1,0:T(8,128)(2,1)S(1)}, bf16[768,768]{1,0:T(8,128)(2,1)}, u32[]{:S(2)}) %copy-start.2) | copy-done | bytes 1179672
  8.2 0.0 copy-start.7
  8.2 0.0 copy-start.8
  8.2 0.0 copy-start.14
  8.2 0.0 copy-start.15
  8.2 5.3 %shard_map.310 = (bf16[256,768]{1,0:T(8,128)(2,1)S(1)}, bf16[512,768]{1,0:T(8,128)(2,1)S(1)}, bf16[960,512]{1,0:T(8,128)(2,1)S(1)}, f32[6,144,256]{2,1,0:T(8,128)S(1)}) custom-call(bf16[2,256,768]{2,1,0:T(8,128)(2,1)S(1)} %bitcast.34, bf16[2,256,768]{2,1,0:T(8,128)(2,1)} %collective-permute-done.1.mate, f32[2,768]{1,0:T(2,128)S(1)} %get-tuple-element.73.gains, ...), custom_call_target="tpu_custom_call" | custom-call | flops 1000 | bytes 1000 | tf_op jit(solution)/shard_map/pallas_call | solution.py:66
  13.5 1.4 %collective-permute-done.far = bf16[256,768]{1,0:T(8,128)(2,1)S(1)} collective-permute-done((bf16[256,768]{1,0:T(8,128)(2,1)S(1)}, bf16[256,768]{1,0:T(8,128)(2,1)S(1)}, u32[]{:S(2)}, u32[]{:S(2)}) %collective-permute-start) | collective-permute-done | bytes 393248 | tf_op jit(solution)/shard_map/ppermute | solution.py:619
  14.9 1.8 %collective-permute-start.2 = (bf16[192,256]{1,0:T(8,128)(2,1)S(1)}, bf16[192,256]{1,0:T(8,128)(2,1)S(1)}, u32[]{:S(2)}, u32[]{:S(2)}) collective-permute-start(bf16[192,256]{1,0:T(8,128)(2,1)S(1)} %fusion.3), channel_id=1, source_target_pairs={{0,2},{1,3},{2,0},{3,1},{4,6},{5,7},{6,4},{7,5},{8,10},{9,11},{10,... | collective-permute-start | bytes 294920 | tf_op jit(solution)/shard_map/ppermute | solution.py:619
  16.8 0.0 slice-start
  16.8 0.0 slice-start.2
  16.8 0.3 shard_map.312
  17.1 0.0 slice-start.1
  17.1 0.0 slice-start.3
  17.2 7.3 %shard_map.311.attended = bf16[512,768]{1,0:T(8,128)(2,1)S(1)} custom-call(bf16[256,768]{1,0:T(8,128)(2,1)S(1)} %collective-permute-done.far, bf16[256,768]{1,0:T(8,128)(2,1)S(1)} %collective-permute-done.3.far_mate, f32[2,768]{1,0:T(2,128)S(1)} %get-tuple-element.73.gains, bf16[768,768]{1,0:T(8,128)(2,1)S(1)} %copy-done.1, bf16[768,768]{1,0:T(8,128)(2,1)S(1)} %copy-done.2, ...), custom_call_target="tpu_custom_call" | custom-call | flops 8000000000 | bytes 8000000 | tf_op jit(solution)/shard_map/pallas_call | solution.py:66
  24.6 6.7 %shard_map.313 = (bf16[256,768]{1,0:T(8,128)(2,1)S(1)}, bf16[256,768]{1,0:T(8,128)(2,1)S(1)}, bf16[512,96]{1,0:T(8,128)(2,1)S(1)}, bf16[96,512]{1,0:T(8,128)(2,1...) custom-call(bf16[2,256,768]{2,1,0:T(8,128)(2,1)S(1)} %bitcast.35, bf16[256,768]{1,0:T(8,128)(2,1)S(1)} %collective-permute-done.far, ...), custom_call_target="tpu_custom_call" | custom-call | flops 10000000000 | bytes 14000000 | tf_op jit(solution)/shard_map/pallas_call | solution.py:66
  31.3 0.3 collective-permute-start.4
  31.5 1.1 %collective-permute-start.6 = (bf16[256,768]{1,0:T(8,128)(2,1)S(1)}, bf16[256,768]{1,0:T(8,128)(2,1)S(1)}, u32[]{:S(2)}, u32[]{:S(2)}) collective-permute-start(bf16[256,768]{1,0:T(8,128)(2,1)S(1)} %get-tuple-element.106.out_far), channel_id=1, source_target_pairs={{0,2},{1,3},{2,0},{3,1},{4,6},{5,7},{6,4},{7,5},{8,10},{9,11},{10,... | collective-permute-start | bytes 1179656 | tf_op jit(solution)/shard_map/ppermute | solution.py:619
  32.6 0.1 collective-permute-done.4.sn_mate
  32.7 13.3 %shard_map.314 = (bf16[96,256]{1,0:T(8,128)(2,1)S(1)}, bf16[96,256]{1,0:T(8,128)(2,1)S(1)}, f32[96,512]{1,0:T(8,128)S(1)}, f32[192,512]{1,0:T(8,128)S(1)}, bf16[...) custom-call(bf16[512,96]{1,0:T(8,128)(2,1)S(1)} %get-tuple-element.98.sn_own, ...), custom_call_target="tpu_custom_call" | custom-call | flops 30000001024 | bytes 3000000 | tf_op jit(solution)/shard_map/pallas_call | solution.py:66
  46.0 0.3 collective-permute-start.5
  46.3 1.2 %collective-permute-done.5.dkv_back = bf16[192,512]{1,0:T(8,128)(2,1)S(1)} collective-permute-done((bf16[192,512]{1,0:T(8,128)(2,1)S(1)}, bf16[192,512]{1,0:T(8,128)(2,1)S(1)}, u32[]{:S(2)}, u32[]{:S(2)}) %collective-permute-start.5) | collective-permute-done | bytes 196640 | tf_op jit(solution)/shard_map/ppermute | solution.py:619
  47.5 0.7 shard_map.315
  48.2 0.3 collective-permute-start.7
  48.5 1.2 %collective-permute-done.7 = bf16[96,1024]{1,0:T(8,128)(2,1)S(1)} collective-permute-done((bf16[96,1024]{1,0:T(8,128)(2,1)S(1)}, bf16[96,1024]{1,0:T(8,128)(2,1)S(1)}, u32[]{:S(2)}, u32[]{:S(2)}) %collective-permute-start.7) | collective-permute-done | bytes 196640 | tf_op jit(solution)/shard_map/ppermute | solution.py:619
  49.8 1.2 %collective-permute-start.8 = (bf16[96,512]{1,0:T(8,128)(2,1)S(1)}, bf16[96,512]{1,0:T(8,128)(2,1)S(1)}, u32[]{:S(2)}, u32[]{:S(2)}) collective-permute-start(bf16[96,512]{1,0:T(8,128)(2,1)S(1)} %constant_dynamic-slice_fusion), channel_id=1, source_target_pairs={{0,2},{1,3},{2,0},{3,1},{4,6},{5,7},{6,4},{7,5},{8,10},{9,11},{10,... | collective-permute-start | bytes 294920 | tf_op jit(solution)/shard_map/ppermute | solution.py:619
  51.0 0.1 select_bitcast_fusion.1
  51.1 3.7 %collective-permute-done.8 = bf16[96,512]{1,0:T(8,128)(2,1)S(1)} collective-permute-done((bf16[96,512]{1,0:T(8,128)(2,1)S(1)}, bf16[96,512]{1,0:T(8,128)(2,1)S(1)}, u32[]{:S(2)}, u32[]{:S(2)}) %collective-permute-start.8) | collective-permute-done | bytes 98336 | tf_op jit(solution)/shard_map/ppermute | solution.py:619
  54.8 1.6 %collective-permute-start.10 = (bf16[96,512]{1,0:T(8,128)(2,1)S(1)}, bf16[96,512]{1,0:T(8,128)(2,1)S(1)}, u32[]{:S(2)}, u32[]{:S(2)}) collective-permute-start(bf16[96,512]{1,0:T(8,128)(2,1)S(1)} %add_convert_fusion.4), channel_id=1, source_target_pairs={{0,4},{4,0},{8,12},{12,8},{16,20},{20,16},{24,28},{28,24},{1,5},{5... | collective-permute-start | bytes 294920 | tf_op jit(solution)/shard_map/ppermute | solution.py:619
  56.4 0.1 maximum_bitcast_fusion
  56.5 1.7 %copy.39 = bf16[256,2,768]{2,1,0:T(2,128)(2,1)} copy(bf16[256,2,768]{2,0,1:T(8,128)(2,1)S(1)} %maximum_bitcast_fusion) | data formatting | bytes 1572864
  58.2 1.1 %collective-permute-start.9 = (bf16[192,256]{1,0:T(8,128)(2,1)S(1)}, bf16[192,256]{1,0:T(8,128)(2,1)S(1)}, u32[]{:S(2)}, u32[]{:S(2)}) collective-permute-start(bf16[192,256]{1,0:T(8,128)(2,1)S(1)} %get-tuple-element.120), channel_id=1, source_target_pairs={{0,2},{1,3},{2,0},{3,1},{4,6},{5,7},{6,4},{7,5},{8,10},{9,11},{10,... | collective-permute-start | bytes 294920 | tf_op jit(solution)/shard_map/ppermute | solution.py:619
  59.3 0.2 collective-permute-done.10
  59.5 1.6 %collective-permute-start.11 = (bf16[96,512]{1,0:T(8,128)(2,1)S(1)}, bf16[96,512]{1,0:T(8,128)(2,1)S(1)}, u32[]{:S(2)}, u32[]{:S(2)}) collective-permute-start(bf16[96,512]{1,0:T(8,128)(2,1)S(1)} %add_convert_fusion.3), channel_id=1, source_target_pairs={{0,8},{4,12},{8,0},{12,4},{16,24},{20,28},{24,16},{28,20},{1,9},{5... | collective-permute-start | bytes 294920 | tf_op jit(solution)/shard_map/ppermute | solution.py:619
  61.2 1.6 %collective-permute-done.9 = bf16[192,256]{1,0:T(8,128)(2,1)S(1)} collective-permute-done((bf16[192,256]{1,0:T(8,128)(2,1)S(1)}, bf16[192,256]{1,0:T(8,128)(2,1)S(1)}, u32[]{:S(2)}, u32[]{:S(2)}) %collective-permute-start.9) | collective-permute-done | bytes 98336 | tf_op jit(solution)/shard_map/ppermute | solution.py:619
  62.8 1.4 %collective-permute-done.11 = bf16[96,512]{1,0:T(8,128)(2,1)S(1)} collective-permute-done((bf16[96,512]{1,0:T(8,128)(2,1)S(1)}, bf16[96,512]{1,0:T(8,128)(2,1)S(1)}, u32[]{:S(2)}, u32[]{:S(2)}) %collective-permute-start.11) | collective-permute-done | bytes 98336 | tf_op jit(solution)/shard_map/ppermute | solution.py:619
  64.2 2.7 %collective-permute-start.12 = (bf16[96,512]{1,0:T(8,128)(2,1)S(1)}, bf16[96,512]{1,0:T(8,128)(2,1)S(1)}, u32[]{:S(2)}, u32[]{:S(2)}) collective-permute-start(bf16[96,512]{1,0:T(8,128)(2,1)S(1)} %add_convert_fusion.2), channel_id=1, source_target_pairs={{0,16},{4,20},{8,24},{12,28},{16,0},{20,4},{24,8},{28,12},{1,17},{... | collective-permute-start | bytes 294920 | tf_op jit(solution)/shard_map/ppermute | solution.py:619
  66.9 2.9 %collective-permute-done.12 = bf16[96,512]{1,0:T(8,128)(2,1)S(1)} collective-permute-done((bf16[96,512]{1,0:T(8,128)(2,1)S(1)}, bf16[96,512]{1,0:T(8,128)(2,1)S(1)}, u32[]{:S(2)}, u32[]{:S(2)}) %collective-permute-start.12) | collective-permute-done | bytes 98336 | tf_op jit(solution)/shard_map/ppermute | solution.py:619
  69.9 1.2 %collective-permute-start.13 = (bf16[96,512]{1,0:T(8,128)(2,1)S(1)}, bf16[96,512]{1,0:T(8,128)(2,1)S(1)}, u32[]{:S(2)}, u32[]{:S(2)}) collective-permute-start(bf16[96,512]{1,0:T(8,128)(2,1)S(1)} %add_convert_fusion.1.part), channel_id=1, source_target_pairs={{0,2},{1,3},{2,0},{3,1},{4,6},{5,7},{6,4},{7,5},{8,10},{9,11},{10,... | collective-permute-start | bytes 294920 | tf_op jit(solution)/shard_map/ppermute | solution.py:619
  71.0 0.7 maximum_bitcast_fusion.1
  71.7 2.8 %collective-permute-done.13.part_x = bf16[96,512]{1,0:T(8,128)(2,1)S(1)} collective-permute-done((bf16[96,512]{1,0:T(8,128)(2,1)S(1)}, bf16[96,512]{1,0:T(8,128)(2,1)S(1)}, u32[]{:S(2)}, u32[]{:S(2)}) %collective-permute-start.13) | collective-permute-done | bytes 98336 | tf_op jit(solution)/shard_map/ppermute | solution.py:619
  74.6 0.7 maximum_bitcast_fusion.2
  75.2 0.6 collective-permute-done.15.part_both
  75.9 1.0 %shard_map.316 = (f32[96,768]{1,0:T(8,128)}, f32[1,96]{1,0:T(1,128)}, f32[1,96]{1,0:T(1,128)}, f32[96,96]{1,0:T(8,128)}, f32[96,96]{1,0:T(8,128)}, /*index=5*/f3...) custom-call(bf16[96,512]{1,0:T(8,128)(2,1)S(1)} %add_convert_fusion.1.part, ...), custom_call_target="tpu_custom_call" | custom-call | bytes 2000000 | tf_op jit(solution)/shard_map/pallas_call | solution.py:66
  (56 shorter events, 0.3 us)
Async XLA Ops:
  0.6 4.5 %copy-start.12 = (s32[2,8]{1,0:T(2,128)S(1)}, s32[2,8]{1,0:T(2,128)}, u32[]{:S(2)}) copy-start(s32[2,8]{1,0:T(2,128)} %doc_lengths.1) | copy-start | bytes 196
  0.7 4.5 %copy-start = (bf16[768,768]{1,0:T(8,128)(2,1)S(1)}, bf16[768,768]{1,0:T(8,128)(2,1)}, u32[]{:S(2)}) copy-start(bf16[768,768]{1,0:T(8,128)(2,1)} %w_value.1) | copy-start | bytes 3538948
  0.7 4.5 %copy-start.10 = (bf16[768]{0:T(1024)(128)(2,1)S(1)}, bf16[768]{0:T(1024)(128)(2,1)}, u32[]{:S(2)}) copy-start(bf16[768]{0:T(1024)(128)(2,1)} %norm_in.1) | copy-start | bytes 4612
  0.7 4.5 %copy-start.11 = (bf16[768]{0:T(1024)(128)(2,1)S(1)}, bf16[768]{0:T(1024)(128)(2,1)}, u32[]{:S(2)}) copy-start(bf16[768]{0:T(1024)(128)(2,1)} %norm_mid.1) | copy-start | bytes 4612
  2.0 4.9 %copy-start.1 = (bf16[768,768]{1,0:T(8,128)(2,1)S(1)}, bf16[768,768]{1,0:T(8,128)(2,1)}, u32[]{:S(2)}) copy-start(bf16[768,768]{1,0:T(8,128)(2,1)} %w_query.3) | copy-start | bytes 3538948
  2.0 4.9 %collective-permute-start.1 = (bf16[2,256,768]{2,1,0:T(8,128)(2,1)S(1)}, bf16[2,256,768]{2,1,0:T(8,128)(2,1)}, u32[]{:S(2)}, u32[]{:S(2)}) collective-permute-start(bf16[2,256,768]{2,1,0:T(8,128)(2,1)S(1)} %bitcast.33), channel_id=1, source_target_pairs={{0,1},{1,0},{2,3},{3,2},{4,5},{5,4},{6,7},{7,6},{8,9},{9,8},{10,11... | collective-permute-start | bytes 2359304 | tf_op jit(solution)/shard_map/ppermute | solution.py:619
  2.6 12.3 %collective-permute-start = (bf16[256,768]{1,0:T(8,128)(2,1)S(1)}, bf16[256,768]{1,0:T(8,128)(2,1)S(1)}, u32[]{:S(2)}, u32[]{:S(2)}) collective-permute-start(bf16[256,768]{1,0:T(8,128)(2,1)S(1)} %dynamic-slice_bitcast_fusion), channel_id=1, source_target_pairs={{0,2},{1,3},{2,0},{3,1},{4,6},{5,7},{6,4},{7,5},{8,10},{9,11},{10,... | collective-permute-start | bytes 1179656 | tf_op jit(solution)/shard_map/ppermute | solution.py:619
  6.9 1.3 %copy-start.2 = (bf16[768,768]{1,0:T(8,128)(2,1)S(1)}, bf16[768,768]{1,0:T(8,128)(2,1)}, u32[]{:S(2)}) copy-start(bf16[768,768]{1,0:T(8,128)(2,1)} %w_key.3) | copy-start | bytes 3538948
  8.2 6.7 %copy-start.3 = (bf16[256,2,96]{0,2,1:T(8,128)(2,1)S(1)}, bf16[256,2,96]{0,2,1:T(8,128)(2,1)}, u32[]{:S(2)}) copy-start(bf16[256,2,96]{0,2,1:T(8,128)(2,1)} %param.23) | copy-start | bytes 294916
  8.2 6.7 %copy-start.4 = (bf16[256,2,96]{0,2,1:T(8,128)(2,1)S(1)}, bf16[256,2,96]{0,2,1:T(8,128)(2,1)}, u32[]{:S(2)}) copy-start(bf16[256,2,96]{0,2,1:T(8,128)(2,1)} %param.43) | copy-start | bytes 294916
  8.2 8.6 %copy-start.5 = (bf16[96,384]{1,0:T(8,128)(2,1)S(1)}, bf16[96,384]{1,0:T(8,128)(2,1)}, u32[]{:S(2)}) copy-start(bf16[96,384]{1,0:T(8,128)(2,1)} %s_inner.2) | copy-start | bytes 221188
  8.2 8.6 %copy-start.6 = (bf16[96,96]{1,0:T(8,128)(2,1)S(1)}, bf16[96,96]{1,0:T(8,128)(2,1)}, u32[]{:S(2)}) copy-start(bf16[96,96]{1,0:T(8,128)(2,1)} %s_out.2) | copy-start | bytes 55300
  8.2 8.6 %copy-start.7 = (bf16[96,96]{1,0:T(8,128)(2,1)S(1)}, bf16[96,96]{1,0:T(8,128)(2,1)}, u32[]{:S(2)}) copy-start(bf16[96,96]{1,0:T(8,128)(2,1)} %s_query.2) | copy-start | bytes 55300
  8.2 8.6 %copy-start.8 = (bf16[96,96]{1,0:T(8,128)(2,1)S(1)}, bf16[96,96]{1,0:T(8,128)(2,1)}, u32[]{:S(2)}) copy-start(bf16[96,96]{1,0:T(8,128)(2,1)} %s_key.2) | copy-start | bytes 55300
  8.2 8.6 %copy-start.9 = (bf16[96,96]{1,0:T(8,128)(2,1)S(1)}, bf16[96,96]{1,0:T(8,128)(2,1)}, u32[]{:S(2)}) copy-start(bf16[96,96]{1,0:T(8,128)(2,1)} %s_value.2) | copy-start | bytes 55300
  8.2 8.6 %copy-start.13 = (f32[96]{0:T(128)S(1)}, f32[96]{0:T(128)}, u32[]{:S(2)}) copy-start(f32[96]{0:T(128)} %gate) | copy-start | bytes 1156
  8.2 8.6 %copy-start.14 = (f32[96]{0:T(128)S(1)}, f32[96]{0:T(128)}, u32[]{:S(2)}) copy-start(f32[96]{0:T(128)} %gain_in) | copy-start | bytes 1156
  8.2 8.5 %copy-start.15 = (f32[96]{0:T(128)S(1)}, f32[96]{0:T(128)}, u32[]{:S(2)}) copy-start(f32[96]{0:T(128)} %gain_mid) | copy-start | bytes 1156
  14.9 2.3 %collective-permute-start.3 = (bf16[256,768]{1,0:T(8,128)(2,1)S(1)}, bf16[256,768]{1,0:T(8,128)(2,1)S(1)}, u32[]{:S(2)}, u32[]{:S(2)}) collective-permute-start(bf16[256,768]{1,0:T(8,128)(2,1)S(1)} %collective-permute-done.far), channel_id=1, source_target_pairs={{0,1},{1,0},{2,3},{3,2},{4,5},{5,4},{6,7},{7,6},{8,9},{9,8},{10,11... | collective-permute-start | bytes 1179656 | tf_op jit(solution)/shard_map/ppermute | solution.py:619
  14.9 9.6 %collective-permute-start.2 = (bf16[192,256]{1,0:T(8,128)(2,1)S(1)}, bf16[192,256]{1,0:T(8,128)(2,1)S(1)}, u32[]{:S(2)}, u32[]{:S(2)}) collective-permute-start(bf16[192,256]{1,0:T(8,128)(2,1)S(1)} %fusion.3), channel_id=1, source_target_pairs={{0,2},{1,3},{2,0},{3,1},{4,6},{5,7},{6,4},{7,5},{8,10},{9,11},{10,... | collective-permute-start | bytes 294920 | tf_op jit(solution)/shard_map/ppermute | solution.py:619
  16.8 7.7 %slice-start = ((s8[4718592]{0:T(1024)(128)(4,1)}), s8[4194304]{0:T(1024)(128)(4,1)S(1)}, s32[]{:S(2)}) async-start(s8[4718592]{0:T(1024)(128)(4,1)} %bitcast.40), calls=%async_computation | async-start | bytes 8388608
  16.8 7.7 %slice-start.2 = ((s8[4718592]{0:T(1024)(128)(4,1)}), s8[4194304]{0:T(1024)(128)(4,1)S(1)}, s32[]{:S(2)}) async-start(s8[4718592]{0:T(1024)(128)(4,1)} %bitcast.42), calls=%async_computation.2 | async-start | bytes 8388608
  17.1 7.4 %slice-start.1 = ((s8[4718592]{0:T(1024)(128)(4,1)}), s8[524288]{0:T(1024)(128)(4,1)S(1)}, s32[]{:S(2)}) async-start(s8[4718592]{0:T(1024)(128)(4,1)} %bitcast.40), calls=%async_computation.1 | async-start | bytes 1048576
  17.1 7.4 %slice-start.3 = ((s8[4718592]{0:T(1024)(128)(4,1)}), s8[524288]{0:T(1024)(128)(4,1)S(1)}, s32[]{:S(2)}) async-start(s8[4718592]{0:T(1024)(128)(4,1)} %bitcast.42), calls=%async_computation.3 | async-start | bytes 1048576
  17.2 7.4 %copy-start.16 = (bf16[768,768]{1,0:T(8,128)(2,1)S(1)}, bf16[768,768]{1,0:T(8,128)(2,1)}, u32[]{:S(2)}) copy-start(bf16[768,768]{1,0:T(8,128)(2,1)} %w_out.1) | copy-start | bytes 3538948
  17.2 7.4 %copy-start.17 = (bf16[768,96]{0,1:T(8,128)(2,1)S(1)}, bf16[768,96]{0,1:T(8,128)(2,1)}, u32[]{:S(2)}) copy-start(bf16[768,96]{0,1:T(8,128)(2,1)} %param.33) | copy-start | bytes 442372
  24.6 8.1 %copy-start.18 = (bf16[384,96]{0,1:T(8,128)(2,1)S(1)}, bf16[384,96]{0,1:T(8,128)(2,1)}, u32[]{:S(2)}) copy-start(bf16[384,96]{0,1:T(8,128)(2,1)} %param.42) | copy-start | bytes 221188
  31.3 1.4 %collective-permute-start.4 = (bf16[512,96]{1,0:T(8,128)(2,1)S(1)}, bf16[512,96]{1,0:T(8,128)(2,1)S(1)}, u32[]{:S(2)}, u32[]{:S(2)}) collective-permute-start(bf16[512,96]{1,0:T(8,128)(2,1)S(1)} %get-tuple-element.98.sn_own), channel_id=1, source_target_pairs={{0,1},{1,0},{2,3},{3,2},{4,5},{5,4},{6,7},{7,6},{8,9},{9,8},{10,11... | collective-permute-start | bytes 294920 | tf_op jit(solution)/shard_map/ppermute | solution.py:619
  31.5 16.0 %collective-permute-start.6 = (bf16[256,768]{1,0:T(8,128)(2,1)S(1)}, bf16[256,768]{1,0:T(8,128)(2,1)S(1)}, u32[]{:S(2)}, u32[]{:S(2)}) collective-permute-start(bf16[256,768]{1,0:T(8,128)(2,1)S(1)} %get-tuple-element.106.out_far), channel_id=1, source_target_pairs={{0,2},{1,3},{2,0},{3,1},{4,6},{5,7},{6,4},{7,5},{8,10},{9,11},{10,... | collective-permute-start | bytes 1179656 | tf_op jit(solution)/shard_map/ppermute | solution.py:619
  46.0 1.5 %collective-permute-start.5 = (bf16[192,512]{1,0:T(8,128)(2,1)S(1)}, bf16[192,512]{1,0:T(8,128)(2,1)S(1)}, u32[]{:S(2)}, u32[]{:S(2)}) collective-permute-start(bf16[192,512]{1,0:T(8,128)(2,1)S(1)} %get-tuple-element.105), channel_id=1, source_target_pairs={{0,1},{1,0},{2,3},{3,2},{4,5},{5,4},{6,7},{7,6},{8,9},{9,8},{10,11... | collective-permute-start | bytes 589832 | tf_op jit(solution)/shard_map/ppermute | solution.py:619
  48.2 1.5 %collective-permute-start.7 = (bf16[96,1024]{1,0:T(8,128)(2,1)S(1)}, bf16[96,1024]{1,0:T(8,128)(2,1)S(1)}, u32[]{:S(2)}, u32[]{:S(2)}) collective-permute-start(bf16[96,1024]{1,0:T(8,128)(2,1)S(1)} %get-tuple-element.118), channel_id=1, source_target_pairs={{0,1},{1,0},{2,3},{3,2},{4,5},{5,4},{6,7},{7,6},{8,9},{9,8},{10,11... | collective-permute-start | bytes 589832 | tf_op jit(solution)/shard_map/ppermute | solution.py:619
  49.8 5.0 %collective-permute-start.8 = (bf16[96,512]{1,0:T(8,128)(2,1)S(1)}, bf16[96,512]{1,0:T(8,128)(2,1)S(1)}, u32[]{:S(2)}, u32[]{:S(2)}) collective-permute-start(bf16[96,512]{1,0:T(8,128)(2,1)S(1)} %constant_dynamic-slice_fusion), channel_id=1, source_target_pairs={{0,2},{1,3},{2,0},{3,1},{4,6},{5,7},{6,4},{7,5},{8,10},{9,11},{10,... | collective-permute-start | bytes 294920 | tf_op jit(solution)/shard_map/ppermute | solution.py:619
  54.8 4.7 %collective-permute-start.10 = (bf16[96,512]{1,0:T(8,128)(2,1)S(1)}, bf16[96,512]{1,0:T(8,128)(2,1)S(1)}, u32[]{:S(2)}, u32[]{:S(2)}) collective-permute-start(bf16[96,512]{1,0:T(8,128)(2,1)S(1)} %add_convert_fusion.4), channel_id=1, source_target_pairs={{0,4},{4,0},{8,12},{12,8},{16,20},{20,16},{24,28},{28,24},{1,5},{5... | collective-permute-start | bytes 294920 | tf_op jit(solution)/shard_map/ppermute | solution.py:619
  58.2 4.6 %collective-permute-start.9 = (bf16[192,256]{1,0:T(8,128)(2,1)S(1)}, bf16[192,256]{1,0:T(8,128)(2,1)S(1)}, u32[]{:S(2)}, u32[]{:S(2)}) collective-permute-start(bf16[192,256]{1,0:T(8,128)(2,1)S(1)} %get-tuple-element.120), channel_id=1, source_target_pairs={{0,2},{1,3},{2,0},{3,1},{4,6},{5,7},{6,4},{7,5},{8,10},{9,11},{10,... | collective-permute-start | bytes 294920 | tf_op jit(solution)/shard_map/ppermute | solution.py:619
  59.5 4.7 %collective-permute-start.11 = (bf16[96,512]{1,0:T(8,128)(2,1)S(1)}, bf16[96,512]{1,0:T(8,128)(2,1)S(1)}, u32[]{:S(2)}, u32[]{:S(2)}) collective-permute-start(bf16[96,512]{1,0:T(8,128)(2,1)S(1)} %add_convert_fusion.3), channel_id=1, source_target_pairs={{0,8},{4,12},{8,0},{12,4},{16,24},{20,28},{24,16},{28,20},{1,9},{5... | collective-permute-start | bytes 294920 | tf_op jit(solution)/shard_map/ppermute | solution.py:619
  64.2 5.6 %collective-permute-start.12 = (bf16[96,512]{1,0:T(8,128)(2,1)S(1)}, bf16[96,512]{1,0:T(8,128)(2,1)S(1)}, u32[]{:S(2)}, u32[]{:S(2)}) collective-permute-start(bf16[96,512]{1,0:T(8,128)(2,1)S(1)} %add_convert_fusion.2), channel_id=1, source_target_pairs={{0,16},{4,20},{8,24},{12,28},{16,0},{20,4},{24,8},{28,12},{1,17},{... | collective-permute-start | bytes 294920 | tf_op jit(solution)/shard_map/ppermute | solution.py:619
  69.9 4.7 %collective-permute-start.13 = (bf16[96,512]{1,0:T(8,128)(2,1)S(1)}, bf16[96,512]{1,0:T(8,128)(2,1)S(1)}, u32[]{:S(2)}, u32[]{:S(2)}) collective-permute-start(bf16[96,512]{1,0:T(8,128)(2,1)S(1)} %add_convert_fusion.1.part), channel_id=1, source_target_pairs={{0,2},{1,3},{2,0},{3,1},{4,6},{5,7},{6,4},{7,5},{8,10},{9,11},{10,... | collective-permute-start | bytes 294920 | tf_op jit(solution)/shard_map/ppermute | solution.py:619
  71.7 3.5 %collective-permute-start.14 = (bf16[96,512]{1,0:T(8,128)(2,1)S(1)}, bf16[96,512]{1,0:T(8,128)(2,1)S(1)}, u32[]{:S(2)}, u32[]{:S(2)}) collective-permute-start(bf16[96,512]{1,0:T(8,128)(2,1)S(1)} %add_convert_fusion.1.part), channel_id=1, source_target_pairs={{0,1},{1,0},{2,3},{3,2},{4,5},{5,4},{6,7},{7,6},{8,9},{9,8},{10,11... | collective-permute-start | bytes 294920 | tf_op jit(solution)/shard_map/ppermute | solution.py:619
  74.6 1.3 %collective-permute-start.15 = (bf16[96,512]{1,0:T(8,128)(2,1)S(1)}, bf16[96,512]{1,0:T(8,128)(2,1)S(1)}, u32[]{:S(2)}, u32[]{:S(2)}) collective-permute-start(bf16[96,512]{1,0:T(8,128)(2,1)S(1)} %collective-permute-done.13.part_x), channel_id=1, source_target_pairs={{0,1},{1,0},{2,3},{3,2},{4,5},{5,4},{6,7},{7,6},{8,9},{9,8},{10,11... | collective-permute-start | bytes 294920 | tf_op jit(solution)/shard_map/ppermute | solution.py:619

commit v6 on v5

--- a/solution.py
+++ b/solution.py
@@ -330,13 +330,18 @@
     columns,
     key_doc,
     query_doc,
-    out_own,
-    out_far,
-    dquery,
     dkv_own,
     dkv_mate,
     dmid_t,
-    early,
+    attn_t,
+    inverse,
+    moments,
+    mid_t,
+    inner_t,
+    normed_t,
+    dinner_t,
+    dnormed_t,
+    dattn_t,
     weights,
     keys,
     key_t,
@@ -344,15 +349,11 @@
     query_t,
     query_s,
     query_h,
-    attn_t,
-    inverse,
     totals,
-    moments,
     back_rows,
     dkv_t,
 ):
     tokens, side = sn_own.shape
-    span = tokens // 2
     feature = side // SHEADS
     hidden = s_inner.shape[1]
     wide = 2 * side
@@ -422,35 +423,26 @@
     unit = mid * mid_scale
     normed = (unit * gain).astype(bf16)
     inner = nn(tall_t[side : side + hidden], normed)
-    act = gelu(inner).astype(bf16)
-    out = (mid + nn(s_outer_t[...], act)).astype(bf16)
-    out_own[...] = out[:, 0:span]
-    out_far[...] = out[:, span : 2 * span]
-
     dy_low = jnp.concatenate([cot[row], side_far[side : 2 * side]], axis=1)
-    dy = dy_low.astype(f32)
-    early[:, hidden : 2 * hidden] = nt(dy_low, act)
     dinner = (gelu_slope(inner) * tn(s_outer_t[...], dy_low)).astype(bf16)
-    early[:, 0:hidden] = nt(normed, dinner)
     dnormed = nn(s_inner[...], dinner)
-    grad_gain = jnp.sum(dnormed * unit, axis=1, keepdims=True)
     scaled = dnormed * gain
-    dmid = dy + mid_scale * (scaled - unit * jnp.mean(scaled * unit, axis=0, keepdims=True))
+    dmid = dy_low.astype(f32) + mid_scale * (
+        scaled - unit * jnp.mean(scaled * unit, axis=0, keepdims=True)
+    )
     dmid_t[...] = dmid
-    dmid_low = dmid.astype(bf16)
-    last = jnp.concatenate([nt(attn_low, dmid_low), jnp.zeros((side, 128 - side), f32)], axis=1)
-    early[:, 2 * hidden : 2 * hidden + 128] = jnp.where(
-        iota((side, 128), 1) == side, grad_gain, last
-    )
-    dattn = nn(s_out[...], dmid_low).astype(bf16).astype(f32)
+    dattn = nn(s_out[...], dmid.astype(bf16)).astype(bf16).astype(f32)
+    mid_t[...] = mid
+    inner_t[...] = inner
+    normed_t[...] = normed
+    dinner_t[...] = dinner
+    dnormed_t[...] = dnormed
+    dattn_t[...] = dattn
 
     for h in range(SHEADS):
         eight = slice(h * feature, (h + 1) * feature)
         invert = inverse[eight, :]
         term = jnp.sum(dattn[eight] * attn[eight], axis=0, keepdims=True)
-        moment = moments[h]
-        raw = inner_rows(dattn[eight], moment[2 * feature :]) - term * moment[0:feature]
-        dquery[eight, :] = raw * invert * scale
         query = query_t[2 * h * feature : (2 * h + 1) * feature].astype(f32)
         share = dattn[eight] * invert
         back_rows[h] = jnp.concatenate(
@@ -474,6 +466,54 @@
     lax.fori_loop(0, SHEADS // GROUP, back, 0)
     dkv_own[...] = dkv_t[:, 0:tokens]
     dkv_mate[...] = dkv_t[:, tokens : 2 * tokens].astype(bf16)
+
+
+def aside_body(
+    attn_t,
+    inverse,
+    moments,
+    mid_t,
+    inner_t,
+    normed_t,
+    dinner_t,
+    dnormed_t,
+    dattn_t,
+    dmid_t,
+    cot,
+    side_far,
+    s_outer_t,
+    out_own,
+    out_far,
+    dquery,
+    early,
+):
+    side, tokens = mid_t.shape
+    span = tokens // 2
+    feature = side // SHEADS
+    hidden = inner_t.shape[0]
+    row = lax.axis_index("blk") // (lax.axis_size("blk") // 2)
+    mid = mid_t[...]
+    act = gelu(inner_t[...]).astype(bf16)
+    out = (mid + nn(s_outer_t[...], act)).astype(bf16)
+    out_own[...] = out[:, 0:span]
+    out_far[...] = out[:, span : 2 * span]
+    dy_low = jnp.concatenate([cot[row], side_far[side : 2 * side]], axis=1)
+    early[:, 0:hidden] = nt(normed_t[...], dinner_t[...])
+    early[:, hidden : 2 * hidden] = nt(dy_low, act)
+    unit = mid * lax.rsqrt(jnp.mean(mid * mid, axis=0, keepdims=True) + EPS)
+    grad_gain = jnp.sum(dnormed_t[...] * unit, axis=1, keepdims=True)
+    last = nt(attn_t[...].astype(bf16), dmid_t[...].astype(bf16))
+    last = jnp.concatenate([last, jnp.zeros((side, 128 - side), f32)], axis=1)
+    early[:, 2 * hidden : 2 * hidden + 128] = jnp.where(
+        iota((side, 128), 1) == side, grad_gain, last
+    )
+    for h in range(SHEADS):
+        eight = slice(h * feature, (h + 1) * feature)
+        dattn = dattn_t[eight, :]
+        term = jnp.sum(dattn * attn_t[eight, :], axis=0, keepdims=True)
+        moment = moments[h]
+        raw = inner_rows(dattn, moment[2 * feature :]) - term * moment[0:feature]
+        dquery[eight, :] = raw * inverse[eight, :] * feature**-0.5
 
 
 def last_body(
@@ -539,31 +579,33 @@
     send[...] = pack[:, pl.ds(pl.multiple_of((1 - core) * size, 128), size)].astype(bf16)
 
 
-def spread_body(
-    part,
-    part_x,
-    part_core,
-    part_both,
-    grad_down,
-    grad_gate,
-    gain_in,
-    grad_query,
-    grad_key,
-    grad_value,
-    grad_out,
-    gain_mid,
-    grad_inner,
-    grad_outer,
-):
+def quarter_index():
+    return (lax.axis_index("blk") // 2) % 2 + 2 * (lax.axis_index("dp") % 2)
+
+
+def spread_body(*refs):
+    pieces, refs = refs[0:8], refs[8:]
+    (
+        grad_down,
+        grad_gate,
+        gain_in,
+        grad_query,
+        grad_key,
+        grad_value,
+        grad_out,
+        gain_mid,
+        grad_inner,
+        grad_outer,
+        pack,
+    ) = refs
     side, width = grad_down.shape
     hidden = grad_inner.shape[1]
-    place = lax.axis_index("blk")
-    core, chip = place % 2, place // 2
-    mine, cross, beside, both = (ref[...].astype(f32) for ref in (part, part_x, part_core, part_both))
-    near = [jnp.where(chip == 0, mine, cross), jnp.where(chip == 0, cross, mine)]
-    far = [jnp.where(chip == 0, beside, both), jnp.where(chip == 0, both, beside)]
-    pieces = [jnp.where(core == 0, a, b) for a, b in zip(near + far, far + near)]
-    whole = jnp.concatenate(pieces, axis=1)
+    size = pieces[0].shape[1]
+    core, quarter = lax.axis_index("blk") % 2, quarter_index()
+    for i, piece in enumerate(pieces):
+        at = ((core ^ (i // 4)) * 4 + (quarter ^ (i % 4))) * size
+        pack[:, pl.ds(pl.multiple_of(at, 128), size)] = piece[...].astype(f32)
+    whole = pack[...]
     grad_down[...] = whole[:, 0:width]
     at = width
     for target in (grad_query, grad_key, grad_value):
@@ -724,16 +766,21 @@
     )
     sn_mate = beside(sn_rows)
     out_back = across(out_far)
-    side_own, side_back, dquery, dkv_own, dkv_mate, dmid_t, early = kernel_call(
+    dkv_own, dkv_mate, dmid_t, *carried = kernel_call(
         side_body,
         [
-            ((side, span), bf16),
-            ((side, span), bf16),
-            ((side, tokens), f32),
             ((2 * side, tokens), f32),
             ((2 * side, tokens), bf16),
             ((side, tokens), f32),
-            ((side, 2 * sff + 128), f32),
+            ((side, tokens), f32),
+            ((side, tokens), f32),
+            ((SHEADS, feature * (feature + 2), tokens), f32),
+            ((side, tokens), f32),
+            ((sff, tokens), f32),
+            ((side, tokens), bf16),
+            ((sff, tokens), bf16),
+            ((side, tokens), f32),
+            ((side, tokens), f32),
         ],
         [
             sn_rows,
@@ -761,15 +808,24 @@
             pltpu.VMEM((2 * side, tokens), bf16),
             pltpu.VMEM((GROUP, 256, tokens), bf16),
             pltpu.VMEM((side, tokens), f32),
-            pltpu.VMEM((side, tokens), f32),
-            pltpu.VMEM((side, tokens), f32),
-            pltpu.VMEM((SHEADS, feature * (feature + 2), tokens), f32),
             pltpu.VMEM((SHEADS, feature * (2 * feature + 4), tokens), bf16),
             pltpu.VMEM((2 * side, 2 * tokens), f32),
         ],
         cost=(30 * 10**9, 3 * 10**6, 0),
     )
     dkv_back = beside(dkv_mate)
+    side_own, side_back, dquery, early = kernel_call(
+        aside_body,
+        [
+            ((side, span), bf16),
+            ((side, span), bf16),
+            ((side, tokens), f32),
+            ((side, 2 * sff + 128), f32),
+        ],
+        [*carried, dmid_t, cot, side_far, s_outer_t],
+        vmem=12,
+        cost=(10**9, 6 * 10**6, 0),
+    )
     dkv_back, out_back = lax.optimization_barrier((dkv_back, out_back))
     packed = width + 4 * 128 + 2 * sff
     grad_own, far, keep, send = kernel_call(
@@ -802,23 +858,32 @@
         cost=(10**9, 3 * 10**6, 0),
     )
 
-    def add(left, right):
-        return (left.astype(f32) + right.astype(f32)).astype(bf16)
-
-    quarter = packed // 4
-    chip = (place // 2) % 2
+    def add(*terms):
+        total = terms[0].astype(f32)
+        for term in terms[1:]:
+            total = total + term.astype(f32)
+        return total.astype(bf16)
+
+    quarter = packed // 8
+    mine = quarter_index()
+    devices = dp_size * blk_size
+
+    def between(value, chip):
+        mask = 2 * (chip % 2) + blk_size * (chip // 2)
+        return lax.ppermute(value, ("dp", "blk"), [(i, i ^ mask) for i in range(devices)])
+
+    def part(value, index):
+        return lax.dynamic_slice_in_dim(value, index * quarter, quarter, 1)
+
     total = add(keep, beside(send))
-    leaving = lax.dynamic_slice_in_dim(total, (1 - chip) * quarter, quarter, 1)
-    total = lax.dynamic_slice_in_dim(total, chip * quarter, quarter, 1)
-    total = add(total, swap(leaving, "blk", blk_size, 2))
+    total = add(part(total, mine), *[between(part(total, mine ^ chip), chip) for chip in (1, 2, 3)])
     total, far = lax.optimization_barrier((total, far))
-    hop = 1
+    hop = 2
     while hop < dp_size:
         total = add(total, swap(total, "dp", dp_size, hop))
         hop *= 2
-    total_x = swap(total, "blk", blk_size, 2)
-    total_core = beside(total)
-    total_both = beside(total_x)
+    pieces = [total] + [between(total, chip) for chip in (1, 2, 3)]
+    pieces += [beside(piece) for piece in pieces]
     vector = ((1, side), f32)
     square = ((side, side), f32)
     grads = kernel_call(
@@ -835,8 +900,9 @@
             ((side, sff), f32),
             ((side, sff), f32),
         ],
-        [total, total_x, total_core, total_both],
+        pieces,
         vmem=16,
+        scratch=[pltpu.VMEM((side, packed), f32)],
         cost=(0, 2 * 10**6, 0),
     )
     grads = [grad.reshape(side) if grad.shape[0] == 1 else grad for grad in grads]

time: 77 us -> 75.1 us (0.975)
  waiting for transfers between devices: 17.2 us -> 11.4 us
  starting transfers between devices: 16.2 us -> 20 us
    ppermute x16 -> x15, waiting for transfers between devices: 17.2 us -> 6.23 us  [swap(): return lax.ppermute(value, axis, [(i, i ^ hop) for i in range(size)])]
    ppermute x0 -> x6, starting transfers between devices: none -> 7.11 us  [between(): lax.ppermute(value, ('dp', 'blk'), [(i, i ^ mask) for i in range(devices)])]
    ppermute x0 -> x6, waiting for transfers between devices: none -> 5.21 us  [between(): lax.ppermute(value, ('dp', 'blk'), [(i, i ^ mask) for i in range(devices)])]
    ppermute x16 -> x15, starting transfers between devices: 16.2 us -> 12.8 us  [swap(): return lax.ppermute(value, axis, [(i, i ^ hop) for i in range(size)])]
    pallas_call x8 -> x9, Pallas kernels: 36.3 us -> 36.4 us  [kernel_call(): pl.pallas_call(body, out_shape=[jax.ShapeDtypeStruct(shape, kind) for sha...]
  transfers between devices with their start and end apart: 16 -> 21, of which waited for: 10 -> 10; matrix products, arithmetic and copies ran while one was open for 4% -> 4% of each run, Pallas kernels for 36% -> 38%
where the time goes in v6:
time: 75.1 us; the launch traced here: 74.9 us
  Pallas kernels  36.4 us (48%)
  starting transfers between devices  20 us (27%)
  waiting for transfers between devices  11.4 us (15%)
  local copies, waits for them, and re-layouts  4.44 us (6%)
  other arithmetic  1.63 us (2%)
  between operations  1.08 us (1%)
    pallas_call x9, Pallas kernels, kernel_call(): pl.pallas_call(body, out_shape=[jax.ShapeDtypeStruct(shape, kind) for sha...  36.4 us
    ppermute x15, starting transfers between devices, swap(): return lax.ppermute(value, axis, [(i, i ^ hop) for i in range(size)])  12.8 us
    ppermute x6, starting transfers between devices, between(): lax.ppermute(value, ('dp', 'blk'), [(i, i ^ mask) for i in range(devices)])  7.11 us
    ppermute x15, waiting for transfers between devices, swap(): return lax.ppermute(value, axis, [(i, i ^ hop) for i in range(size)])  6.23 us
    ppermute x6, waiting for transfers between devices, between(): lax.ppermute(value, ('dp', 'blk'), [(i, i ^ mask) for i in range(devices)])  5.21 us
    unnamed x48, local copies, waits for them, and re-layouts  4.39 us
  transfers between devices with their start and end apart: 21, of which 10 were waited for; matrix products, arithmetic and copies ran while one was open for 4% of the time, Pallas kernels for 38%

profile of v6, /device:TPU:0, one launch (start us, length us, event | category | flops | bytes accessed | tf_op | source)
XLA Modules:
  0.0 74.9 jit_solution(18372515426084393472)
XLA Ops:
  0.7 1.3 %copy.42 = bf16[256,2,768]{2,0,1:T(8,128)(2,1)S(1)} copy(bf16[256,2,768]{2,1,0:T(2,128)(2,1)} %param.22) | data formatting | bytes 1572864 | tf_op args[0]
  2.0 0.5 collective-permute-start.1
  2.6 2.6 %collective-permute-start = (bf16[256,768]{1,0:T(8,128)(2,1)S(1)}, bf16[256,768]{1,0:T(8,128)(2,1)S(1)}, u32[]{:S(2)}, u32[]{:S(2)}) collective-permute-start(bf16[256,768]{1,0:T(8,128)(2,1)S(1)} %dynamic-slice_bitcast_fusion), channel_id=1, source_target_pairs={{0,2},{1,3},{2,0},{3,1},{4,6},{5,7},{6,4},{7,5},{8,10},{9,11},{10,... | collective-permute-start | bytes 1179656 | tf_op jit(solution)/shard_map/ppermute | solution.py:661
  5.2 1.7 %shard_map.309 = (bf16[768,768]{1,0:T(8,128)(2,1)S(1)}, f32[2,768]{1,0:T(2,128)S(1)}, bf16[1024,128]{1,0:T(8,128)(2,1)S(1)}, bf16[512,128]{1,0:T(8,128)(2,1)S(1)...) custom-call(s32[2,8]{1,0:T(2,128)S(1)} %copy-done.13, bf16[768,768]{1,0:T(8,128)(2,1)S(1)} %copy-done, ...), custom_call_target="tpu_custom_call" | custom-call | flops 1000 | bytes 1000 | tf_op jit(solution)/shard_map/pallas_call | solution.py:66
  6.9 1.3 %copy-done.2 = bf16[768,768]{1,0:T(8,128)(2,1)S(1)} copy-done((bf16[768,768]{1,0:T(8,128)(2,1)S(1)}, bf16[768,768]{1,0:T(8,128)(2,1)}, u32[]{:S(2)}) %copy-start.2) | copy-done | bytes 1179672
  8.2 5.3 %shard_map.310 = (bf16[256,768]{1,0:T(8,128)(2,1)S(1)}, bf16[512,768]{1,0:T(8,128)(2,1)S(1)}, bf16[960,512]{1,0:T(8,128)(2,1)S(1)}, f32[6,144,256]{2,1,0:T(8,128)S(1)}) custom-call(bf16[2,256,768]{2,1,0:T(8,128)(2,1)S(1)} %bitcast.34, bf16[2,256,768]{2,1,0:T(8,128)(2,1)} %collective-permute-done.1.mate, f32[2,768]{1,0:T(2,128)S(1)} %get-tuple-element.82.gains, ...), custom_call_target="tpu_custom_call" | custom-call | flops 1000 | bytes 1000 | tf_op jit(solution)/shard_map/pallas_call | solution.py:66
  13.6 1.3 %collective-permute-done.far = bf16[256,768]{1,0:T(8,128)(2,1)S(1)} collective-permute-done((bf16[256,768]{1,0:T(8,128)(2,1)S(1)}, bf16[256,768]{1,0:T(8,128)(2,1)S(1)}, u32[]{:S(2)}, u32[]{:S(2)}) %collective-permute-start) | collective-permute-done | bytes 393248 | tf_op jit(solution)/shard_map/ppermute | solution.py:661
  14.9 1.8 %collective-permute-start.2 = (bf16[192,256]{1,0:T(8,128)(2,1)S(1)}, bf16[192,256]{1,0:T(8,128)(2,1)S(1)}, u32[]{:S(2)}, u32[]{:S(2)}) collective-permute-start(bf16[192,256]{1,0:T(8,128)(2,1)S(1)} %fusion.3), channel_id=1, source_target_pairs={{0,2},{1,3},{2,0},{3,1},{4,6},{5,7},{6,4},{7,5},{8,10},{9,11},{10,... | collective-permute-start | bytes 294920 | tf_op jit(solution)/shard_map/ppermute | solution.py:661
  16.8 0.0 slice-start
  16.8 0.0 slice-start.2
  16.8 0.3 shard_map.312
  17.1 0.0 slice-start.1
  17.1 0.0 slice-start.3
  17.2 7.3 %shard_map.311.attended = bf16[512,768]{1,0:T(8,128)(2,1)S(1)} custom-call(bf16[256,768]{1,0:T(8,128)(2,1)S(1)} %collective-permute-done.far, bf16[256,768]{1,0:T(8,128)(2,1)S(1)} %collective-permute-done.3.far_mate, f32[2,768]{1,0:T(2,128)S(1)} %get-tuple-element.82.gains, bf16[768,768]{1,0:T(8,128)(2,1)S(1)} %copy-done.1, bf16[768,768]{1,0:T(8,128)(2,1)S(1)} %copy-done.2, ...), custom_call_target="tpu_custom_call" | custom-call | flops 8000000000 | bytes 8000000 | tf_op jit(solution)/shard_map/pallas_call | solution.py:66
  24.6 6.6 %shard_map.313 = (bf16[256,768]{1,0:T(8,128)(2,1)S(1)}, bf16[256,768]{1,0:T(8,128)(2,1)S(1)}, bf16[512,96]{1,0:T(8,128)(2,1)S(1)}, bf16[96,512]{1,0:T(8,128)(2,1...) custom-call(bf16[2,256,768]{2,1,0:T(8,128)(2,1)S(1)} %bitcast.35, bf16[256,768]{1,0:T(8,128)(2,1)S(1)} %collective-permute-done.far, ...), custom_call_target="tpu_custom_call" | custom-call | flops 10000000000 | bytes 14000000 | tf_op jit(solution)/shard_map/pallas_call | solution.py:66
  31.1 0.3 collective-permute-start.4
  31.4 1.1 %collective-permute-start.6 = (bf16[256,768]{1,0:T(8,128)(2,1)S(1)}, bf16[256,768]{1,0:T(8,128)(2,1)S(1)}, u32[]{:S(2)}, u32[]{:S(2)}) collective-permute-start(bf16[256,768]{1,0:T(8,128)(2,1)S(1)} %get-tuple-element.115.out_far), channel_id=1, source_target_pairs={{0,2},{1,3},{2,0},{3,1},{4,6},{5,7},{6,4},{7,5},{8,10},{9,11},{10,... | collective-permute-start | bytes 1179656 | tf_op jit(solution)/shard_map/ppermute | solution.py:661
  32.5 0.0 collective-permute-done.4.sn_mate
  32.6 13.0 %shard_map.314 = (f32[192,512]{1,0:T(8,128)S(1)}, bf16[192,512]{1,0:T(8,128)(2,1)S(1)}, f32[96,512]{1,0:T(8,128)S(1)}, f32[96,512]{1,0:T(8,128)S(1)}, f32[96,512...) custom-call(bf16[512,96]{1,0:T(8,128)(2,1)S(1)} %get-tuple-element.1, ...), custom_call_target="tpu_custom_call" | custom-call | flops 30000001024 | bytes 3000000 | tf_op jit(solution)/shard_map/pallas_call | solution.py:66
  45.5 0.3 collective-permute-start.5
  45.8 0.6 shard_map.315
  46.4 0.6 collective-permute-done.5.dkv_back
  47.0 0.7 shard_map.316
  47.7 0.3 collective-permute-start.7
  48.0 1.2 %collective-permute-done.7 = bf16[96,1024]{1,0:T(8,128)(2,1)S(1)} collective-permute-done((bf16[96,1024]{1,0:T(8,128)(2,1)S(1)}, bf16[96,1024]{1,0:T(8,128)(2,1)S(1)}, u32[]{:S(2)}, u32[]{:S(2)}) %collective-permute-start.7) | collective-permute-done | bytes 196640 | tf_op jit(solution)/shard_map/ppermute | solution.py:661
  49.3 2.2 %collective-permute-start.10 = (bf16[96,256]{1,0:T(8,128)(2,1)S(1)}, bf16[96,256]{1,0:T(8,128)(2,1)S(1)}, u32[]{:S(2)}, u32[]{:S(2)}) collective-permute-start(bf16[96,256]{1,0:T(8,128)(2,1)S(1)} %get-tuple-element.184), channel_id=1, source_target_pairs={{0,6},{1,7},{2,4},{3,5},{4,2},{5,3},{6,0},{7,1},{8,14},{9,15},{10,... | collective-permute-start | bytes 147464 | tf_op jit(solution)/shard_map/ppermute | solution.py:873
  51.5 0.9 %collective-permute-start.8 = (bf16[96,256]{1,0:T(8,128)(2,1)S(1)}, bf16[96,256]{1,0:T(8,128)(2,1)S(1)}, u32[]{:S(2)}, u32[]{:S(2)}) collective-permute-start(bf16[96,256]{1,0:T(8,128)(2,1)S(1)} %get-tuple-element.183), channel_id=1, source_target_pairs={{0,2},{1,3},{2,0},{3,1},{4,6},{5,7},{6,4},{7,5},{8,10},{9,11},{10,... | collective-permute-start | bytes 147464 | tf_op jit(solution)/shard_map/ppermute | solution.py:873
  52.4 0.5 collective-permute-start.9
  52.9 2.0 %collective-permute-done.10 = bf16[96,256]{1,0:T(8,128)(2,1)S(1)} collective-permute-done((bf16[96,256]{1,0:T(8,128)(2,1)S(1)}, bf16[96,256]{1,0:T(8,128)(2,1)S(1)}, u32[]{:S(2)}, u32[]{:S(2)}) %collective-permute-start.10) | collective-permute-done | bytes 49184 | tf_op jit(solution)/shard_map/ppermute | solution.py:873
  54.8 0.8 %collective-permute-done.8 = bf16[96,256]{1,0:T(8,128)(2,1)S(1)} collective-permute-done((bf16[96,256]{1,0:T(8,128)(2,1)S(1)}, bf16[96,256]{1,0:T(8,128)(2,1)S(1)}, u32[]{:S(2)}, u32[]{:S(2)}) %collective-permute-start.8) | collective-permute-done | bytes 49184 | tf_op jit(solution)/shard_map/ppermute | solution.py:873
  55.6 0.9 %collective-permute-done.9 = bf16[96,256]{1,0:T(8,128)(2,1)S(1)} collective-permute-done((bf16[96,256]{1,0:T(8,128)(2,1)S(1)}, bf16[96,256]{1,0:T(8,128)(2,1)S(1)}, u32[]{:S(2)}, u32[]{:S(2)}) %collective-permute-start.9) | collective-permute-done | bytes 49184 | tf_op jit(solution)/shard_map/ppermute | solution.py:873
  56.5 1.6 %collective-permute-start.12 = (bf16[96,256]{1,0:T(8,128)(2,1)S(1)}, bf16[96,256]{1,0:T(8,128)(2,1)S(1)}, u32[]{:S(2)}, u32[]{:S(2)}) collective-permute-start(bf16[96,256]{1,0:T(8,128)(2,1)S(1)} %add_convert_fusion.3), channel_id=1, source_target_pairs={{0,8},{4,12},{8,0},{12,4},{16,24},{20,28},{24,16},{28,20},{1,9},{5... | collective-permute-start | bytes 147464 | tf_op jit(solution)/shard_map/ppermute | solution.py:661
  58.1 0.1 select_bitcast_fusion.1
  58.2 2.5 %collective-permute-done.12 = bf16[96,256]{1,0:T(8,128)(2,1)S(1)} collective-permute-done((bf16[96,256]{1,0:T(8,128)(2,1)S(1)}, bf16[96,256]{1,0:T(8,128)(2,1)S(1)}, u32[]{:S(2)}, u32[]{:S(2)}) %collective-permute-start.12) | collective-permute-done | bytes 49184 | tf_op jit(solution)/shard_map/ppermute | solution.py:661
  60.7 2.7 %collective-permute-start.13 = (bf16[96,256]{1,0:T(8,128)(2,1)S(1)}, bf16[96,256]{1,0:T(8,128)(2,1)S(1)}, u32[]{:S(2)}, u32[]{:S(2)}) collective-permute-start(bf16[96,256]{1,0:T(8,128)(2,1)S(1)} %add_convert_fusion.2), channel_id=1, source_target_pairs={{0,16},{4,20},{8,24},{12,28},{16,0},{20,4},{24,8},{28,12},{1,17},{... | collective-permute-start | bytes 147464 | tf_op jit(solution)/shard_map/ppermute | solution.py:661
  63.3 0.1 maximum_bitcast_fusion
  63.4 1.7 %copy.39 = bf16[256,2,768]{2,1,0:T(2,128)(2,1)} copy(bf16[256,2,768]{2,0,1:T(8,128)(2,1)S(1)} %maximum_bitcast_fusion) | data formatting | bytes 1572864
  65.1 1.2 %collective-permute-start.11 = (bf16[192,256]{1,0:T(8,128)(2,1)S(1)}, bf16[192,256]{1,0:T(8,128)(2,1)S(1)}, u32[]{:S(2)}, u32[]{:S(2)}) collective-permute-start(bf16[192,256]{1,0:T(8,128)(2,1)S(1)} %get-tuple-element.138), channel_id=1, source_target_pairs={{0,2},{1,3},{2,0},{3,1},{4,6},{5,7},{6,4},{7,5},{8,10},{9,11},{10,... | collective-permute-start | bytes 294920 | tf_op jit(solution)/shard_map/ppermute | solution.py:661
  66.3 0.9 %collective-permute-start.14 = (bf16[96,256]{1,0:T(8,128)(2,1)S(1)}, bf16[96,256]{1,0:T(8,128)(2,1)S(1)}, u32[]{:S(2)}, u32[]{:S(2)}) collective-permute-start(bf16[96,256]{1,0:T(8,128)(2,1)S(1)} %add_convert_fusion.1.refs_0_), channel_id=1, source_target_pairs={{0,2},{1,3},{2,0},{3,1},{4,6},{5,7},{6,4},{7,5},{8,10},{9,11},{10,... | collective-permute-start | bytes 147464 | tf_op jit(solution)/shard_map/ppermute | solution.py:873
  67.2 0.5 collective-permute-start.15
  67.7 2.1 %collective-permute-start.16 = (bf16[96,256]{1,0:T(8,128)(2,1)S(1)}, bf16[96,256]{1,0:T(8,128)(2,1)S(1)}, u32[]{:S(2)}, u32[]{:S(2)}) collective-permute-start(bf16[96,256]{1,0:T(8,128)(2,1)S(1)} %add_convert_fusion.1.refs_0_), channel_id=1, source_target_pairs={{0,6},{1,7},{2,4},{3,5},{4,2},{5,3},{6,0},{7,1},{8,14},{9,15},{10,... | collective-permute-start | bytes 147464 | tf_op jit(solution)/shard_map/ppermute | solution.py:873
  69.9 0.7 maximum_bitcast_fusion.1
  70.6 0.5 collective-permute-start.18
  71.1 0.2 collective-permute-done.15.refs_2_
  71.3 1.4 %collective-permute-done.16.refs_3_ = bf16[96,256]{1,0:T(8,128)(2,1)S(1)} collective-permute-done((bf16[96,256]{1,0:T(8,128)(2,1)S(1)}, bf16[96,256]{1,0:T(8,128)(2,1)S(1)}, u32[]{:S(2)}, u32[]{:S(2)}) %collective-permute-start.16) | collective-permute-done | bytes 49184 | tf_op jit(solution)/shard_map/ppermute | solution.py:873
  72.7 0.7 maximum_bitcast_fusion.2
  73.4 0.6 collective-permute-done.20.refs_7_
  73.9 1.0 %shard_map.317 = (f32[96,768]{1,0:T(8,128)}, f32[1,96]{1,0:T(1,128)}, f32[1,96]{1,0:T(1,128)}, f32[96,96]{1,0:T(8,128)}, f32[96,96]{1,0:T(8,128)}, /*index=5*/f3...) custom-call(bf16[96,256]{1,0:T(8,128)(2,1)S(1)} %add_convert_fusion.1.refs_0_, ...), custom_call_target="tpu_custom_call" | custom-call | bytes 2000000 | tf_op jit(solution)/shard_map/pallas_call | solution.py:66
  (66 shorter events, 0.4 us)
Async XLA Ops:
  0.6 4.5 %copy-start.13 = (s32[2,8]{1,0:T(2,128)S(1)}, s32[2,8]{1,0:T(2,128)}, u32[]{:S(2)}) copy-start(s32[2,8]{1,0:T(2,128)} %doc_lengths.1) | copy-start | bytes 196
  0.7 4.5 %copy-start.11 = (bf16[768]{0:T(1024)(128)(2,1)S(1)}, bf16[768]{0:T(1024)(128)(2,1)}, u32[]{:S(2)}) copy-start(bf16[768]{0:T(1024)(128)(2,1)} %norm_in.1) | copy-start | bytes 4612
  0.7 4.5 %copy-start = (bf16[768,768]{1,0:T(8,128)(2,1)S(1)}, bf16[768,768]{1,0:T(8,128)(2,1)}, u32[]{:S(2)}) copy-start(bf16[768,768]{1,0:T(8,128)(2,1)} %w_value.1) | copy-start | bytes 3538948
  0.7 4.5 %copy-start.12 = (bf16[768]{0:T(1024)(128)(2,1)S(1)}, bf16[768]{0:T(1024)(128)(2,1)}, u32[]{:S(2)}) copy-start(bf16[768]{0:T(1024)(128)(2,1)} %norm_mid.1) | copy-start | bytes 4612
  2.0 4.9 %copy-start.1 = (bf16[768,768]{1,0:T(8,128)(2,1)S(1)}, bf16[768,768]{1,0:T(8,128)(2,1)}, u32[]{:S(2)}) copy-start(bf16[768,768]{1,0:T(8,128)(2,1)} %w_query.3) | copy-start | bytes 3538948
  2.0 4.9 %collective-permute-start.1 = (bf16[2,256,768]{2,1,0:T(8,128)(2,1)S(1)}, bf16[2,256,768]{2,1,0:T(8,128)(2,1)}, u32[]{:S(2)}, u32[]{:S(2)}) collective-permute-start(bf16[2,256,768]{2,1,0:T(8,128)(2,1)S(1)} %bitcast.33), channel_id=1, source_target_pairs={{0,1},{1,0},{2,3},{3,2},{4,5},{5,4},{6,7},{7,6},{8,9},{9,8},{10,11... | collective-permute-start | bytes 2359304 | tf_op jit(solution)/shard_map/ppermute | solution.py:661
  2.6 12.3 %collective-permute-start = (bf16[256,768]{1,0:T(8,128)(2,1)S(1)}, bf16[256,768]{1,0:T(8,128)(2,1)S(1)}, u32[]{:S(2)}, u32[]{:S(2)}) collective-permute-start(bf16[256,768]{1,0:T(8,128)(2,1)S(1)} %dynamic-slice_bitcast_fusion), channel_id=1, source_target_pairs={{0,2},{1,3},{2,0},{3,1},{4,6},{5,7},{6,4},{7,5},{8,10},{9,11},{10,... | collective-permute-start | bytes 1179656 | tf_op jit(solution)/shard_map/ppermute | solution.py:661
  6.9 1.3 %copy-start.2 = (bf16[768,768]{1,0:T(8,128)(2,1)S(1)}, bf16[768,768]{1,0:T(8,128)(2,1)}, u32[]{:S(2)}) copy-start(bf16[768,768]{1,0:T(8,128)(2,1)} %w_key.3) | copy-start | bytes 3538948
  8.2 6.7 %copy-start.3 = (bf16[256,2,96]{0,2,1:T(8,128)(2,1)S(1)}, bf16[256,2,96]{0,2,1:T(8,128)(2,1)}, u32[]{:S(2)}) copy-start(bf16[256,2,96]{0,2,1:T(8,128)(2,1)} %param.43) | copy-start | bytes 294916
  8.2 6.7 %copy-start.4 = (bf16[256,2,96]{0,2,1:T(8,128)(2,1)S(1)}, bf16[256,2,96]{0,2,1:T(8,128)(2,1)}, u32[]{:S(2)}) copy-start(bf16[256,2,96]{0,2,1:T(8,128)(2,1)} %param.23) | copy-start | bytes 294916
  8.2 8.6 %copy-start.5 = (bf16[96,384]{1,0:T(8,128)(2,1)S(1)}, bf16[96,384]{1,0:T(8,128)(2,1)}, u32[]{:S(2)}) copy-start(bf16[96,384]{1,0:T(8,128)(2,1)} %s_inner.2) | copy-start | bytes 221188
  8.2 8.6 %copy-start.7 = (bf16[96,96]{1,0:T(8,128)(2,1)S(1)}, bf16[96,96]{1,0:T(8,128)(2,1)}, u32[]{:S(2)}) copy-start(bf16[96,96]{1,0:T(8,128)(2,1)} %s_out.2) | copy-start | bytes 55300
  8.2 8.6 %copy-start.8 = (bf16[96,96]{1,0:T(8,128)(2,1)S(1)}, bf16[96,96]{1,0:T(8,128)(2,1)}, u32[]{:S(2)}) copy-start(bf16[96,96]{1,0:T(8,128)(2,1)} %s_query.2) | copy-start | bytes 55300
  8.2 8.6 %copy-start.9 = (bf16[96,96]{1,0:T(8,128)(2,1)S(1)}, bf16[96,96]{1,0:T(8,128)(2,1)}, u32[]{:S(2)}) copy-start(bf16[96,96]{1,0:T(8,128)(2,1)} %s_key.2) | copy-start | bytes 55300
  8.2 8.6 %copy-start.10 = (bf16[96,96]{1,0:T(8,128)(2,1)S(1)}, bf16[96,96]{1,0:T(8,128)(2,1)}, u32[]{:S(2)}) copy-start(bf16[96,96]{1,0:T(8,128)(2,1)} %s_value.2) | copy-start | bytes 55300
  8.2 8.6 %copy-start.14 = (f32[96]{0:T(128)S(1)}, f32[96]{0:T(128)}, u32[]{:S(2)}) copy-start(f32[96]{0:T(128)} %gate) | copy-start | bytes 1156
  8.2 8.6 %copy-start.15 = (f32[96]{0:T(128)S(1)}, f32[96]{0:T(128)}, u32[]{:S(2)}) copy-start(f32[96]{0:T(128)} %gain_in) | copy-start | bytes 1156
  8.2 8.5 %copy-start.16 = (f32[96]{0:T(128)S(1)}, f32[96]{0:T(128)}, u32[]{:S(2)}) copy-start(f32[96]{0:T(128)} %gain_mid) | copy-start | bytes 1156
  14.9 2.3 %collective-permute-start.3 = (bf16[256,768]{1,0:T(8,128)(2,1)S(1)}, bf16[256,768]{1,0:T(8,128)(2,1)S(1)}, u32[]{:S(2)}, u32[]{:S(2)}) collective-permute-start(bf16[256,768]{1,0:T(8,128)(2,1)S(1)} %collective-permute-done.far), channel_id=1, source_target_pairs={{0,1},{1,0},{2,3},{3,2},{4,5},{5,4},{6,7},{7,6},{8,9},{9,8},{10,11... | collective-permute-start | bytes 1179656 | tf_op jit(solution)/shard_map/ppermute | solution.py:661
  14.9 9.5 %collective-permute-start.2 = (bf16[192,256]{1,0:T(8,128)(2,1)S(1)}, bf16[192,256]{1,0:T(8,128)(2,1)S(1)}, u32[]{:S(2)}, u32[]{:S(2)}) collective-permute-start(bf16[192,256]{1,0:T(8,128)(2,1)S(1)} %fusion.3), channel_id=1, source_target_pairs={{0,2},{1,3},{2,0},{3,1},{4,6},{5,7},{6,4},{7,5},{8,10},{9,11},{10,... | collective-permute-start | bytes 294920 | tf_op jit(solution)/shard_map/ppermute | solution.py:661
  16.8 7.7 %slice-start = ((s8[4718592]{0:T(1024)(128)(4,1)}), s8[4194304]{0:T(1024)(128)(4,1)S(1)}, s32[]{:S(2)}) async-start(s8[4718592]{0:T(1024)(128)(4,1)} %bitcast.43), calls=%async_computation | async-start | bytes 8388608
  16.8 7.7 %slice-start.2 = ((s8[4718592]{0:T(1024)(128)(4,1)}), s8[4194304]{0:T(1024)(128)(4,1)S(1)}, s32[]{:S(2)}) async-start(s8[4718592]{0:T(1024)(128)(4,1)} %bitcast.45), calls=%async_computation.2 | async-start | bytes 8388608
  17.1 7.4 %slice-start.1 = ((s8[4718592]{0:T(1024)(128)(4,1)}), s8[524288]{0:T(1024)(128)(4,1)S(1)}, s32[]{:S(2)}) async-start(s8[4718592]{0:T(1024)(128)(4,1)} %bitcast.43), calls=%async_computation.1 | async-start | bytes 1048576
  17.1 7.4 %slice-start.3 = ((s8[4718592]{0:T(1024)(128)(4,1)}), s8[524288]{0:T(1024)(128)(4,1)S(1)}, s32[]{:S(2)}) async-start(s8[4718592]{0:T(1024)(128)(4,1)} %bitcast.45), calls=%async_computation.3 | async-start | bytes 1048576
  17.2 7.4 %copy-start.17 = (bf16[768,768]{1,0:T(8,128)(2,1)S(1)}, bf16[768,768]{1,0:T(8,128)(2,1)}, u32[]{:S(2)}) copy-start(bf16[768,768]{1,0:T(8,128)(2,1)} %w_out.1) | copy-start | bytes 3538948
  17.2 7.4 %copy-start.18 = (bf16[768,96]{0,1:T(8,128)(2,1)S(1)}, bf16[768,96]{0,1:T(8,128)(2,1)}, u32[]{:S(2)}) copy-start(bf16[768,96]{0,1:T(8,128)(2,1)} %param.33) | copy-start | bytes 442372
  24.6 8.0 %copy-start.6 = (bf16[384,96]{0,1:T(8,128)(2,1)S(1)}, bf16[384,96]{0,1:T(8,128)(2,1)}, u32[]{:S(2)}) copy-start(bf16[384,96]{0,1:T(8,128)(2,1)} %param.42) | copy-start | bytes 221188
  31.1 1.4 %collective-permute-start.4 = (bf16[512,96]{1,0:T(8,128)(2,1)S(1)}, bf16[512,96]{1,0:T(8,128)(2,1)S(1)}, u32[]{:S(2)}, u32[]{:S(2)}) collective-permute-start(bf16[512,96]{1,0:T(8,128)(2,1)S(1)} %get-tuple-element.107.sn_own), channel_id=1, source_target_pairs={{0,1},{1,0},{2,3},{3,2},{4,5},{5,4},{6,7},{7,6},{8,9},{9,8},{10,11... | collective-permute-start | bytes 294920 | tf_op jit(solution)/shard_map/ppermute | solution.py:661
  31.4 15.6 %collective-permute-start.6 = (bf16[256,768]{1,0:T(8,128)(2,1)S(1)}, bf16[256,768]{1,0:T(8,128)(2,1)S(1)}, u32[]{:S(2)}, u32[]{:S(2)}) collective-permute-start(bf16[256,768]{1,0:T(8,128)(2,1)S(1)} %get-tuple-element.115.out_far), channel_id=1, source_target_pairs={{0,2},{1,3},{2,0},{3,1},{4,6},{5,7},{6,4},{7,5},{8,10},{9,11},{10,... | collective-permute-start | bytes 1179656 | tf_op jit(solution)/shard_map/ppermute | solution.py:661
  45.5 1.5 %collective-permute-start.5 = (bf16[192,512]{1,0:T(8,128)(2,1)S(1)}, bf16[192,512]{1,0:T(8,128)(2,1)S(1)}, u32[]{:S(2)}, u32[]{:S(2)}) collective-permute-start(bf16[192,512]{1,0:T(8,128)(2,1)S(1)} %get-tuple-element.114), channel_id=1, source_target_pairs={{0,1},{1,0},{2,3},{3,2},{4,5},{5,4},{6,7},{7,6},{8,9},{9,8},{10,11... | collective-permute-start | bytes 589832 | tf_op jit(solution)/shard_map/ppermute | solution.py:661
  47.7 1.5 %collective-permute-start.7 = (bf16[96,1024]{1,0:T(8,128)(2,1)S(1)}, bf16[96,1024]{1,0:T(8,128)(2,1)S(1)}, u32[]{:S(2)}, u32[]{:S(2)}) collective-permute-start(bf16[96,1024]{1,0:T(8,128)(2,1)S(1)} %get-tuple-element.136), channel_id=1, source_target_pairs={{0,1},{1,0},{2,3},{3,2},{4,5},{5,4},{6,7},{7,6},{8,9},{9,8},{10,11... | collective-permute-start | bytes 589832 | tf_op jit(solution)/shard_map/ppermute | solution.py:661
  49.3 5.5 %collective-permute-start.10 = (bf16[96,256]{1,0:T(8,128)(2,1)S(1)}, bf16[96,256]{1,0:T(8,128)(2,1)S(1)}, u32[]{:S(2)}, u32[]{:S(2)}) collective-permute-start(bf16[96,256]{1,0:T(8,128)(2,1)S(1)} %get-tuple-element.184), channel_id=1, source_target_pairs={{0,6},{1,7},{2,4},{3,5},{4,2},{5,3},{6,0},{7,1},{8,14},{9,15},{10,... | collective-permute-start | bytes 147464 | tf_op jit(solution)/shard_map/ppermute | solution.py:873
  51.5 4.1 %collective-permute-start.8 = (bf16[96,256]{1,0:T(8,128)(2,1)S(1)}, bf16[96,256]{1,0:T(8,128)(2,1)S(1)}, u32[]{:S(2)}, u32[]{:S(2)}) collective-permute-start(bf16[96,256]{1,0:T(8,128)(2,1)S(1)} %get-tuple-element.183), channel_id=1, source_target_pairs={{0,2},{1,3},{2,0},{3,1},{4,6},{5,7},{6,4},{7,5},{8,10},{9,11},{10,... | collective-permute-start | bytes 147464 | tf_op jit(solution)/shard_map/ppermute | solution.py:873
  52.4 4.1 %collective-permute-start.9 = (bf16[96,256]{1,0:T(8,128)(2,1)S(1)}, bf16[96,256]{1,0:T(8,128)(2,1)S(1)}, u32[]{:S(2)}, u32[]{:S(2)}) collective-permute-start(bf16[96,256]{1,0:T(8,128)(2,1)S(1)} %get-tuple-element.185), channel_id=1, source_target_pairs={{0,4},{1,5},{2,6},{3,7},{4,0},{5,1},{6,2},{7,3},{8,12},{9,13},{10,... | collective-permute-start | bytes 147464 | tf_op jit(solution)/shard_map/ppermute | solution.py:873
  56.5 4.2 %collective-permute-start.12 = (bf16[96,256]{1,0:T(8,128)(2,1)S(1)}, bf16[96,256]{1,0:T(8,128)(2,1)S(1)}, u32[]{:S(2)}, u32[]{:S(2)}) collective-permute-start(bf16[96,256]{1,0:T(8,128)(2,1)S(1)} %add_convert_fusion.3), channel_id=1, source_target_pairs={{0,8},{4,12},{8,0},{12,4},{16,24},{20,28},{24,16},{28,20},{1,9},{5... | collective-permute-start | bytes 147464 | tf_op jit(solution)/shard_map/ppermute | solution.py:661
  60.7 5.6 %collective-permute-start.13 = (bf16[96,256]{1,0:T(8,128)(2,1)S(1)}, bf16[96,256]{1,0:T(8,128)(2,1)S(1)}, u32[]{:S(2)}, u32[]{:S(2)}) collective-permute-start(bf16[96,256]{1,0:T(8,128)(2,1)S(1)} %add_convert_fusion.2), channel_id=1, source_target_pairs={{0,16},{4,20},{8,24},{12,28},{16,0},{20,4},{24,8},{28,12},{1,17},{... | collective-permute-start | bytes 147464 | tf_op jit(solution)/shard_map/ppermute | solution.py:661
  65.1 4.7 %collective-permute-start.11 = (bf16[192,256]{1,0:T(8,128)(2,1)S(1)}, bf16[192,256]{1,0:T(8,128)(2,1)S(1)}, u32[]{:S(2)}, u32[]{:S(2)}) collective-permute-start(bf16[192,256]{1,0:T(8,128)(2,1)S(1)} %get-tuple-element.138), channel_id=1, source_target_pairs={{0,2},{1,3},{2,0},{3,1},{4,6},{5,7},{6,4},{7,5},{8,10},{9,11},{10,... | collective-permute-start | bytes 294920 | tf_op jit(solution)/shard_map/ppermute | solution.py:661
  66.3 4.3 %collective-permute-start.14 = (bf16[96,256]{1,0:T(8,128)(2,1)S(1)}, bf16[96,256]{1,0:T(8,128)(2,1)S(1)}, u32[]{:S(2)}, u32[]{:S(2)}) collective-permute-start(bf16[96,256]{1,0:T(8,128)(2,1)S(1)} %add_convert_fusion.1.refs_0_), channel_id=1, source_target_pairs={{0,2},{1,3},{2,0},{3,1},{4,6},{5,7},{6,4},{7,5},{8,10},{9,11},{10,... | collective-permute-start | bytes 147464 | tf_op jit(solution)/shard_map/ppermute | solution.py:873
  67.2 4.1 %collective-permute-start.15 = (bf16[96,256]{1,0:T(8,128)(2,1)S(1)}, bf16[96,256]{1,0:T(8,128)(2,1)S(1)}, u32[]{:S(2)}, u32[]{:S(2)}) collective-permute-start(bf16[96,256]{1,0:T(8,128)(2,1)S(1)} %add_convert_fusion.1.refs_0_), channel_id=1, source_target_pairs={{0,4},{1,5},{2,6},{3,7},{4,0},{5,1},{6,2},{7,3},{8,12},{9,13},{10,... | collective-permute-start | bytes 147464 | tf_op jit(solution)/shard_map/ppermute | solution.py:873
  67.7 5.0 %collective-permute-start.16 = (bf16[96,256]{1,0:T(8,128)(2,1)S(1)}, bf16[96,256]{1,0:T(8,128)(2,1)S(1)}, u32[]{:S(2)}, u32[]{:S(2)}) collective-permute-start(bf16[96,256]{1,0:T(8,128)(2,1)S(1)} %add_convert_fusion.1.refs_0_), channel_id=1, source_target_pairs={{0,6},{1,7},{2,4},{3,5},{4,2},{5,3},{6,0},{7,1},{8,14},{9,15},{10,... | collective-permute-start | bytes 147464 | tf_op jit(solution)/shard_map/ppermute | solution.py:873
  69.8 3.5 %collective-permute-start.17 = (bf16[96,256]{1,0:T(8,128)(2,1)S(1)}, bf16[96,256]{1,0:T(8,128)(2,1)S(1)}, u32[]{:S(2)}, u32[]{:S(2)}) collective-permute-start(bf16[96,256]{1,0:T(8,128)(2,1)S(1)} %add_convert_fusion.1.refs_0_), channel_id=1, source_target_pairs={{0,1},{1,0},{2,3},{3,2},{4,5},{5,4},{6,7},{7,6},{8,9},{9,8},{10,11... | collective-permute-start | bytes 147464 | tf_op jit(solution)/shard_map/ppermute | solution.py:661
  70.6 2.8 %collective-permute-start.18 = (bf16[96,256]{1,0:T(8,128)(2,1)S(1)}, bf16[96,256]{1,0:T(8,128)(2,1)S(1)}, u32[]{:S(2)}, u32[]{:S(2)}) collective-permute-start(bf16[96,256]{1,0:T(8,128)(2,1)S(1)} %collective-permute-done.14.refs_1_), channel_id=1, source_target_pairs={{0,1},{1,0},{2,3},{3,2},{4,5},{5,4},{6,7},{7,6},{8,9},{9,8},{10,11... | collective-permute-start | bytes 147464 | tf_op jit(solution)/shard_map/ppermute | solution.py:661
  71.3 2.1 %collective-permute-start.19 = (bf16[96,256]{1,0:T(8,128)(2,1)S(1)}, bf16[96,256]{1,0:T(8,128)(2,1)S(1)}, u32[]{:S(2)}, u32[]{:S(2)}) collective-permute-start(bf16[96,256]{1,0:T(8,128)(2,1)S(1)} %collective-permute-done.15.refs_2_), channel_id=1, source_target_pairs={{0,1},{1,0},{2,3},{3,2},{4,5},{5,4},{6,7},{7,6},{8,9},{9,8},{10,11... | collective-permute-start | bytes 147464 | tf_op jit(solution)/shard_map/ppermute | solution.py:661
  72.7 1.2 %collective-permute-start.20 = (bf16[96,256]{1,0:T(8,128)(2,1)S(1)}, bf16[96,256]{1,0:T(8,128)(2,1)S(1)}, u32[]{:S(2)}, u32[]{:S(2)}) collective-permute-start(bf16[96,256]{1,0:T(8,128)(2,1)S(1)} %collective-permute-done.16.refs_3_), channel_id=1, source_target_pairs={{0,1},{1,0},{2,3},{3,2},{4,5},{5,4},{6,7},{7,6},{8,9},{9,8},{10,11... | collective-permute-start | bytes 147464 | tf_op jit(solution)/shard_map/ppermute | solution.py:661

commit v7 on v6

--- a/solution.py
+++ b/solution.py
@@ -9,12 +9,11 @@
 
 HEADS = 12
 SHEADS = 12
-GROUP = 6
 SPARE = 64
 EPS = 1e-06
 LOG2E = math.log2(math.e)
 FAR = 2.0**100
-LOW_TOTAL, HIGH_TOTAL = 2.0**-80, 2.0**100
+LOW_TOTAL, HIGH_TOTAL = 2.0**-60, 2.0**60
 
 f32, bf16, i32 = jnp.float32, jnp.bfloat16, jnp.int32
 
@@ -373,17 +372,17 @@
     high = scaled.astype(bf16).astype(f32)
     second = iota((wide, tokens), 0) % (2 * feature) >= feature
     query_s[...] = jnp.where(second, scaled - high, high).astype(bf16)
-    for i in range(GROUP):
+    for i in range(SHEADS):
         query_h[i] = jnp.zeros(query_h.shape[1:], bf16)
         query_h[i, wide : wide + 16] = query_doc[...]
 
     def head_rows(h, count):
         return pl.ds(pl.multiple_of(h * count, count), count)
 
-    def attend(shifted):
+    def attend(shifted, size):
         def group(j, carry):
-            for i in range(GROUP):
-                h = GROUP * j + i
+            for i in range(size):
+                h = size * j + i
                 rows, eight = head_rows(h, 16), head_rows(h, 8)
                 query_h[i, rows, :] = query_s[rows, :]
                 scores = nn(keys[...], query_h[i])
@@ -391,7 +390,7 @@
                 if shifted:
                     scores = scores - jnp.max(scores, axis=0, keepdims=True)
                 weight = jnp.exp2(scores).astype(bf16)
-                weights[h] = weight
+                weights[h] = weight.T
                 value, key = value_t[rows, :], key_t[rows, :]
                 products = outer_rows(value[0:feature].astype(f32), key[0:feature].astype(f32))
                 products = jnp.concatenate(two_parts(products), axis=0).astype(bf16)
@@ -407,13 +406,13 @@
                 )
             return carry
 
-        lax.fori_loop(0, SHEADS // GROUP, group, 0)
-
-    attend(False)
+        lax.fori_loop(0, SHEADS // size, group, 0)
+
+    attend(False, SHEADS)
 
     @pl.when(out_of_range(totals[...]))
     def _():
-        attend(True)
+        attend(True, 2)
 
     attn = attn_t[...]
     attn_low = attn.astype(bf16)
@@ -449,21 +448,17 @@
             two_parts(share) + two_parts(term * invert * query) + two_parts(outer_rows(share, query)), axis=0
         ).astype(bf16)
 
-    def back(j, carry):
-        for i in range(GROUP):
-            h = GROUP * j + i
-            summed = nt(back_rows[h], weights[h])
-            dkv_t[pl.ds(pl.multiple_of(side + h * feature, feature), feature), :] = (
-                summed[0:feature] + summed[feature : 2 * feature]
-            )
-            value = value_t[head_rows(h, 16), :][0:feature].astype(f32)
-            at = 4 * feature + feature * feature
-            raw = inner_rows(value, summed[4 * feature : at] + summed[at:])
-            raw = raw - (summed[2 * feature : 3 * feature] + summed[3 * feature : 4 * feature])
-            dkv_t[head_rows(h, feature), :] = raw * scale
-        return carry
-
-    lax.fori_loop(0, SHEADS // GROUP, back, 0)
+    for h in range(SHEADS):
+        eight = slice(h * feature, (h + 1) * feature)
+        summed = nn(back_rows[h], weights[h])
+        dkv_t[side + h * feature : side + (h + 1) * feature] = (
+            summed[0:feature] + summed[feature : 2 * feature]
+        )
+        value = value_t[2 * h * feature : (2 * h + 1) * feature].astype(f32)
+        at = 4 * feature + feature * feature
+        raw = inner_rows(value, summed[4 * feature : at] + summed[at:])
+        raw = raw - (summed[2 * feature : 3 * feature] + summed[3 * feature : 4 * feature])
+        dkv_t[eight] = raw * scale
     dkv_own[...] = dkv_t[:, 0:tokens]
     dkv_mate[...] = dkv_t[:, tokens : 2 * tokens].astype(bf16)
 
@@ -800,13 +795,13 @@
         ],
         vmem=36,
         scratch=[
-            pltpu.VMEM((SHEADS, 2 * tokens, tokens), bf16),
+            pltpu.VMEM((SHEADS, tokens, 2 * tokens), bf16),
             pltpu.VMEM((2 * tokens, 256), bf16),
             pltpu.VMEM((2 * side, 2 * tokens), bf16),
             pltpu.VMEM((2 * side, 2 * tokens), bf16),
             pltpu.VMEM((2 * side, tokens), bf16),
             pltpu.VMEM((2 * side, tokens), bf16),
-            pltpu.VMEM((GROUP, 256, tokens), bf16),
+            pltpu.VMEM((SHEADS, 256, tokens), bf16),
             pltpu.VMEM((side, tokens), f32),
             pltpu.VMEM((SHEADS, feature * (2 * feature + 4), tokens), bf16),
             pltpu.VMEM((2 * side, 2 * tokens), f32),

time: 75.1 us -> 72.3 us (0.963)
  Pallas kernels: 36.4 us -> 33.6 us
    pallas_call x9, Pallas kernels: 36.4 us -> 33.6 us  [kernel_call(): pl.pallas_call(body, out_shape=[jax.ShapeDtypeStruct(shape, kind) for sha...]
  transfers between devices with their start and end apart: 21 -> 21, of which waited for: 10 -> 10; matrix products, arithmetic and copies ran while one was open for 4% -> 5% of each run, Pallas kernels for 38% -> 35%
where the time goes in v7:
time: 72.3 us; the launch traced here: 72.1 us
  Pallas kernels  33.6 us (46%)
  starting transfers between devices  20 us (28%)
  waiting for transfers between devices  11.4 us (16%)
  local copies, waits for them, and re-layouts  4.44 us (6%)
  other arithmetic  1.63 us (2%)
  between operations  1.08 us (1%)
    pallas_call x9, Pallas kernels, kernel_call(): pl.pallas_call(body, out_shape=[jax.ShapeDtypeStruct(shape, kind) for sha...  33.6 us
    ppermute x15, starting transfers between devices, swap(): return lax.ppermute(value, axis, [(i, i ^ hop) for i in range(size)])  12.8 us
    ppermute x6, starting transfers between devices, between(): lax.ppermute(value, ('dp', 'blk'), [(i, i ^ mask) for i in range(devices)])  7.11 us
    ppermute x15, waiting for transfers between devices, swap(): return lax.ppermute(value, axis, [(i, i ^ hop) for i in range(size)])  6.23 us
    ppermute x6, waiting for transfers between devices, between(): lax.ppermute(value, ('dp', 'blk'), [(i, i ^ mask) for i in range(devices)])  5.21 us
    unnamed x48, local copies, waits for them, and re-layouts  4.39 us
  transfers between devices with their start and end apart: 21, of which 10 were waited for; matrix products, arithmetic and copies ran while one was open for 5% of the time, Pallas kernels for 35%

profile of v7, /device:TPU:0, one launch (start us, length us, event | category | flops | bytes accessed | tf_op | source)
XLA Modules:
  0.0 72.1 jit_solution(9680490466777756417)
XLA Ops:
  0.7 1.3 %copy.42 = bf16[256,2,768]{2,0,1:T(8,128)(2,1)S(1)} copy(bf16[256,2,768]{2,1,0:T(2,128)(2,1)} %param.22) | data formatting | bytes 1572864 | tf_op args[0]
  2.0 0.5 collective-permute-start.1
  2.6 2.6 %collective-permute-start = (bf16[256,768]{1,0:T(8,128)(2,1)S(1)}, bf16[256,768]{1,0:T(8,128)(2,1)S(1)}, u32[]{:S(2)}, u32[]{:S(2)}) collective-permute-start(bf16[256,768]{1,0:T(8,128)(2,1)S(1)} %dynamic-slice_bitcast_fusion), channel_id=1, source_target_pairs={{0,2},{1,3},{2,0},{3,1},{4,6},{5,7},{6,4},{7,5},{8,10},{9,11},{10,... | collective-permute-start | bytes 1179656 | tf_op jit(solution)/shard_map/ppermute | solution.py:656
  5.2 1.7 %shard_map.309 = (bf16[768,768]{1,0:T(8,128)(2,1)S(1)}, f32[2,768]{1,0:T(2,128)S(1)}, bf16[1024,128]{1,0:T(8,128)(2,1)S(1)}, bf16[512,128]{1,0:T(8,128)(2,1)S(1)...) custom-call(s32[2,8]{1,0:T(2,128)S(1)} %copy-done.13, bf16[768,768]{1,0:T(8,128)(2,1)S(1)} %copy-done, ...), custom_call_target="tpu_custom_call" | custom-call | flops 1000 | bytes 1000 | tf_op jit(solution)/shard_map/pallas_call | solution.py:65
  6.9 1.3 %copy-done.2 = bf16[768,768]{1,0:T(8,128)(2,1)S(1)} copy-done((bf16[768,768]{1,0:T(8,128)(2,1)S(1)}, bf16[768,768]{1,0:T(8,128)(2,1)}, u32[]{:S(2)}) %copy-start.2) | copy-done | bytes 1179672
  8.2 5.3 %shard_map.310 = (bf16[256,768]{1,0:T(8,128)(2,1)S(1)}, bf16[512,768]{1,0:T(8,128)(2,1)S(1)}, bf16[960,512]{1,0:T(8,128)(2,1)S(1)}, f32[6,144,256]{2,1,0:T(8,128)S(1)}) custom-call(bf16[2,256,768]{2,1,0:T(8,128)(2,1)S(1)} %bitcast.34, bf16[2,256,768]{2,1,0:T(8,128)(2,1)} %collective-permute-done.1.mate, f32[2,768]{1,0:T(2,128)S(1)} %get-tuple-element.82.gains, ...), custom_call_target="tpu_custom_call" | custom-call | flops 1000 | bytes 1000 | tf_op jit(solution)/shard_map/pallas_call | solution.py:65
  13.6 1.3 %collective-permute-done.far = bf16[256,768]{1,0:T(8,128)(2,1)S(1)} collective-permute-done((bf16[256,768]{1,0:T(8,128)(2,1)S(1)}, bf16[256,768]{1,0:T(8,128)(2,1)S(1)}, u32[]{:S(2)}, u32[]{:S(2)}) %collective-permute-start) | collective-permute-done | bytes 393248 | tf_op jit(solution)/shard_map/ppermute | solution.py:656
  14.9 1.8 %collective-permute-start.2 = (bf16[192,256]{1,0:T(8,128)(2,1)S(1)}, bf16[192,256]{1,0:T(8,128)(2,1)S(1)}, u32[]{:S(2)}, u32[]{:S(2)}) collective-permute-start(bf16[192,256]{1,0:T(8,128)(2,1)S(1)} %fusion.3), channel_id=1, source_target_pairs={{0,2},{1,3},{2,0},{3,1},{4,6},{5,7},{6,4},{7,5},{8,10},{9,11},{10,... | collective-permute-start | bytes 294920 | tf_op jit(solution)/shard_map/ppermute | solution.py:656
  16.8 0.0 slice-start
  16.8 0.0 slice-start.2
  16.8 0.3 shard_map.312
  17.1 0.0 slice-start.1
  17.1 0.0 slice-start.3
  17.2 7.3 %shard_map.311.attended = bf16[512,768]{1,0:T(8,128)(2,1)S(1)} custom-call(bf16[256,768]{1,0:T(8,128)(2,1)S(1)} %collective-permute-done.far, bf16[256,768]{1,0:T(8,128)(2,1)S(1)} %collective-permute-done.3.far_mate, f32[2,768]{1,0:T(2,128)S(1)} %get-tuple-element.82.gains, bf16[768,768]{1,0:T(8,128)(2,1)S(1)} %copy-done.1, bf16[768,768]{1,0:T(8,128)(2,1)S(1)} %copy-done.2, ...), custom_call_target="tpu_custom_call" | custom-call | flops 8000000000 | bytes 8000000 | tf_op jit(solution)/shard_map/pallas_call | solution.py:65
  24.6 6.6 %shard_map.313 = (bf16[256,768]{1,0:T(8,128)(2,1)S(1)}, bf16[256,768]{1,0:T(8,128)(2,1)S(1)}, bf16[512,96]{1,0:T(8,128)(2,1)S(1)}, bf16[96,512]{1,0:T(8,128)(2,1...) custom-call(bf16[2,256,768]{2,1,0:T(8,128)(2,1)S(1)} %bitcast.35, bf16[256,768]{1,0:T(8,128)(2,1)S(1)} %collective-permute-done.far, ...), custom_call_target="tpu_custom_call" | custom-call | flops 10000000000 | bytes 14000000 | tf_op jit(solution)/shard_map/pallas_call | solution.py:65
  31.1 0.3 collective-permute-start.4
  31.4 1.1 %collective-permute-start.6 = (bf16[256,768]{1,0:T(8,128)(2,1)S(1)}, bf16[256,768]{1,0:T(8,128)(2,1)S(1)}, u32[]{:S(2)}, u32[]{:S(2)}) collective-permute-start(bf16[256,768]{1,0:T(8,128)(2,1)S(1)} %get-tuple-element.115.out_far), channel_id=1, source_target_pairs={{0,2},{1,3},{2,0},{3,1},{4,6},{5,7},{6,4},{7,5},{8,10},{9,11},{10,... | collective-permute-start | bytes 1179656 | tf_op jit(solution)/shard_map/ppermute | solution.py:656
  32.5 0.0 collective-permute-done.4.sn_mate
  32.6 10.2 %shard_map.314 = (f32[192,512]{1,0:T(8,128)S(1)}, bf16[192,512]{1,0:T(8,128)(2,1)S(1)}, f32[96,512]{1,0:T(8,128)S(1)}, f32[96,512]{1,0:T(8,128)S(1)}, f32[96,512...) custom-call(bf16[512,96]{1,0:T(8,128)(2,1)S(1)} %get-tuple-element.1, ...), custom_call_target="tpu_custom_call" | custom-call | flops 30000001024 | bytes 3000000 | tf_op jit(solution)/shard_map/pallas_call | solution.py:65
  42.7 0.3 collective-permute-start.5
  43.0 0.6 shard_map.315
  43.7 0.6 collective-permute-done.5.dkv_back
  44.2 0.7 shard_map.316
  44.9 0.3 collective-permute-start.7
  45.2 1.2 %collective-permute-done.7 = bf16[96,1024]{1,0:T(8,128)(2,1)S(1)} collective-permute-done((bf16[96,1024]{1,0:T(8,128)(2,1)S(1)}, bf16[96,1024]{1,0:T(8,128)(2,1)S(1)}, u32[]{:S(2)}, u32[]{:S(2)}) %collective-permute-start.7) | collective-permute-done | bytes 196640 | tf_op jit(solution)/shard_map/ppermute | solution.py:656
  46.5 2.2 %collective-permute-start.10 = (bf16[96,256]{1,0:T(8,128)(2,1)S(1)}, bf16[96,256]{1,0:T(8,128)(2,1)S(1)}, u32[]{:S(2)}, u32[]{:S(2)}) collective-permute-start(bf16[96,256]{1,0:T(8,128)(2,1)S(1)} %get-tuple-element.184), channel_id=1, source_target_pairs={{0,6},{1,7},{2,4},{3,5},{4,2},{5,3},{6,0},{7,1},{8,14},{9,15},{10,... | collective-permute-start | bytes 147464 | tf_op jit(solution)/shard_map/ppermute | solution.py:868
  48.7 0.9 %collective-permute-start.8 = (bf16[96,256]{1,0:T(8,128)(2,1)S(1)}, bf16[96,256]{1,0:T(8,128)(2,1)S(1)}, u32[]{:S(2)}, u32[]{:S(2)}) collective-permute-start(bf16[96,256]{1,0:T(8,128)(2,1)S(1)} %get-tuple-element.183), channel_id=1, source_target_pairs={{0,2},{1,3},{2,0},{3,1},{4,6},{5,7},{6,4},{7,5},{8,10},{9,11},{10,... | collective-permute-start | bytes 147464 | tf_op jit(solution)/shard_map/ppermute | solution.py:868
  49.6 0.5 collective-permute-start.9
  50.1 2.0 %collective-permute-done.10 = bf16[96,256]{1,0:T(8,128)(2,1)S(1)} collective-permute-done((bf16[96,256]{1,0:T(8,128)(2,1)S(1)}, bf16[96,256]{1,0:T(8,128)(2,1)S(1)}, u32[]{:S(2)}, u32[]{:S(2)}) %collective-permute-start.10) | collective-permute-done | bytes 49184 | tf_op jit(solution)/shard_map/ppermute | solution.py:868
  52.1 0.8 %collective-permute-done.8 = bf16[96,256]{1,0:T(8,128)(2,1)S(1)} collective-permute-done((bf16[96,256]{1,0:T(8,128)(2,1)S(1)}, bf16[96,256]{1,0:T(8,128)(2,1)S(1)}, u32[]{:S(2)}, u32[]{:S(2)}) %collective-permute-start.8) | collective-permute-done | bytes 49184 | tf_op jit(solution)/shard_map/ppermute | solution.py:868
  52.8 0.9 %collective-permute-done.9 = bf16[96,256]{1,0:T(8,128)(2,1)S(1)} collective-permute-done((bf16[96,256]{1,0:T(8,128)(2,1)S(1)}, bf16[96,256]{1,0:T(8,128)(2,1)S(1)}, u32[]{:S(2)}, u32[]{:S(2)}) %collective-permute-start.9) | collective-permute-done | bytes 49184 | tf_op jit(solution)/shard_map/ppermute | solution.py:868
  53.7 1.6 %collective-permute-start.12 = (bf16[96,256]{1,0:T(8,128)(2,1)S(1)}, bf16[96,256]{1,0:T(8,128)(2,1)S(1)}, u32[]{:S(2)}, u32[]{:S(2)}) collective-permute-start(bf16[96,256]{1,0:T(8,128)(2,1)S(1)} %add_convert_fusion.3), channel_id=1, source_target_pairs={{0,8},{4,12},{8,0},{12,4},{16,24},{20,28},{24,16},{28,20},{1,9},{5... | collective-permute-start | bytes 147464 | tf_op jit(solution)/shard_map/ppermute | solution.py:656
  55.4 0.1 select_bitcast_fusion.1
  55.4 2.5 %collective-permute-done.12 = bf16[96,256]{1,0:T(8,128)(2,1)S(1)} collective-permute-done((bf16[96,256]{1,0:T(8,128)(2,1)S(1)}, bf16[96,256]{1,0:T(8,128)(2,1)S(1)}, u32[]{:S(2)}, u32[]{:S(2)}) %collective-permute-start.12) | collective-permute-done | bytes 49184 | tf_op jit(solution)/shard_map/ppermute | solution.py:656
  57.9 2.7 %collective-permute-start.13 = (bf16[96,256]{1,0:T(8,128)(2,1)S(1)}, bf16[96,256]{1,0:T(8,128)(2,1)S(1)}, u32[]{:S(2)}, u32[]{:S(2)}) collective-permute-start(bf16[96,256]{1,0:T(8,128)(2,1)S(1)} %add_convert_fusion.2), channel_id=1, source_target_pairs={{0,16},{4,20},{8,24},{12,28},{16,0},{20,4},{24,8},{28,12},{1,17},{... | collective-permute-start | bytes 147464 | tf_op jit(solution)/shard_map/ppermute | solution.py:656
  60.5 0.1 maximum_bitcast_fusion
  60.6 1.7 %copy.39 = bf16[256,2,768]{2,1,0:T(2,128)(2,1)} copy(bf16[256,2,768]{2,0,1:T(8,128)(2,1)S(1)} %maximum_bitcast_fusion) | data formatting | bytes 1572864
  62.3 1.2 %collective-permute-start.11 = (bf16[192,256]{1,0:T(8,128)(2,1)S(1)}, bf16[192,256]{1,0:T(8,128)(2,1)S(1)}, u32[]{:S(2)}, u32[]{:S(2)}) collective-permute-start(bf16[192,256]{1,0:T(8,128)(2,1)S(1)} %get-tuple-element.138), channel_id=1, source_target_pairs={{0,2},{1,3},{2,0},{3,1},{4,6},{5,7},{6,4},{7,5},{8,10},{9,11},{10,... | collective-permute-start | bytes 294920 | tf_op jit(solution)/shard_map/ppermute | solution.py:656
  63.5 0.9 %collective-permute-start.14 = (bf16[96,256]{1,0:T(8,128)(2,1)S(1)}, bf16[96,256]{1,0:T(8,128)(2,1)S(1)}, u32[]{:S(2)}, u32[]{:S(2)}) collective-permute-start(bf16[96,256]{1,0:T(8,128)(2,1)S(1)} %add_convert_fusion.1.refs_0_), channel_id=1, source_target_pairs={{0,2},{1,3},{2,0},{3,1},{4,6},{5,7},{6,4},{7,5},{8,10},{9,11},{10,... | collective-permute-start | bytes 147464 | tf_op jit(solution)/shard_map/ppermute | solution.py:868
  64.4 0.5 collective-permute-start.15
  64.9 2.1 %collective-permute-start.16 = (bf16[96,256]{1,0:T(8,128)(2,1)S(1)}, bf16[96,256]{1,0:T(8,128)(2,1)S(1)}, u32[]{:S(2)}, u32[]{:S(2)}) collective-permute-start(bf16[96,256]{1,0:T(8,128)(2,1)S(1)} %add_convert_fusion.1.refs_0_), channel_id=1, source_target_pairs={{0,6},{1,7},{2,4},{3,5},{4,2},{5,3},{6,0},{7,1},{8,14},{9,15},{10,... | collective-permute-start | bytes 147464 | tf_op jit(solution)/shard_map/ppermute | solution.py:868
  67.1 0.7 maximum_bitcast_fusion.1
  67.8 0.5 collective-permute-start.18
  68.3 0.2 collective-permute-done.15.refs_2_
  68.5 1.4 %collective-permute-done.16.refs_3_ = bf16[96,256]{1,0:T(8,128)(2,1)S(1)} collective-permute-done((bf16[96,256]{1,0:T(8,128)(2,1)S(1)}, bf16[96,256]{1,0:T(8,128)(2,1)S(1)}, u32[]{:S(2)}, u32[]{:S(2)}) %collective-permute-start.16) | collective-permute-done | bytes 49184 | tf_op jit(solution)/shard_map/ppermute | solution.py:868
  69.9 0.7 maximum_bitcast_fusion.2
  70.6 0.6 collective-permute-done.20.refs_7_
  71.2 1.0 %shard_map.317 = (f32[96,768]{1,0:T(8,128)}, f32[1,96]{1,0:T(1,128)}, f32[1,96]{1,0:T(1,128)}, f32[96,96]{1,0:T(8,128)}, f32[96,96]{1,0:T(8,128)}, /*index=5*/f3...) custom-call(bf16[96,256]{1,0:T(8,128)(2,1)S(1)} %add_convert_fusion.1.refs_0_, ...), custom_call_target="tpu_custom_call" | custom-call | bytes 2000000 | tf_op jit(solution)/shard_map/pallas_call | solution.py:65
  (66 shorter events, 0.4 us)
Async XLA Ops:
  0.6 4.5 %copy-start.13 = (s32[2,8]{1,0:T(2,128)S(1)}, s32[2,8]{1,0:T(2,128)}, u32[]{:S(2)}) copy-start(s32[2,8]{1,0:T(2,128)} %doc_lengths.1) | copy-start | bytes 196
  0.7 4.5 %copy-start.11 = (bf16[768]{0:T(1024)(128)(2,1)S(1)}, bf16[768]{0:T(1024)(128)(2,1)}, u32[]{:S(2)}) copy-start(bf16[768]{0:T(1024)(128)(2,1)} %norm_in.1) | copy-start | bytes 4612
  0.7 4.5 %copy-start = (bf16[768,768]{1,0:T(8,128)(2,1)S(1)}, bf16[768,768]{1,0:T(8,128)(2,1)}, u32[]{:S(2)}) copy-start(bf16[768,768]{1,0:T(8,128)(2,1)} %w_value.1) | copy-start | bytes 3538948
  0.7 4.5 %copy-start.12 = (bf16[768]{0:T(1024)(128)(2,1)S(1)}, bf16[768]{0:T(1024)(128)(2,1)}, u32[]{:S(2)}) copy-start(bf16[768]{0:T(1024)(128)(2,1)} %norm_mid.1) | copy-start | bytes 4612
  2.0 4.9 %copy-start.1 = (bf16[768,768]{1,0:T(8,128)(2,1)S(1)}, bf16[768,768]{1,0:T(8,128)(2,1)}, u32[]{:S(2)}) copy-start(bf16[768,768]{1,0:T(8,128)(2,1)} %w_query.3) | copy-start | bytes 3538948
  2.0 4.9 %collective-permute-start.1 = (bf16[2,256,768]{2,1,0:T(8,128)(2,1)S(1)}, bf16[2,256,768]{2,1,0:T(8,128)(2,1)}, u32[]{:S(2)}, u32[]{:S(2)}) collective-permute-start(bf16[2,256,768]{2,1,0:T(8,128)(2,1)S(1)} %bitcast.33), channel_id=1, source_target_pairs={{0,1},{1,0},{2,3},{3,2},{4,5},{5,4},{6,7},{7,6},{8,9},{9,8},{10,11... | collective-permute-start | bytes 2359304 | tf_op jit(solution)/shard_map/ppermute | solution.py:656
  2.6 12.3 %collective-permute-start = (bf16[256,768]{1,0:T(8,128)(2,1)S(1)}, bf16[256,768]{1,0:T(8,128)(2,1)S(1)}, u32[]{:S(2)}, u32[]{:S(2)}) collective-permute-start(bf16[256,768]{1,0:T(8,128)(2,1)S(1)} %dynamic-slice_bitcast_fusion), channel_id=1, source_target_pairs={{0,2},{1,3},{2,0},{3,1},{4,6},{5,7},{6,4},{7,5},{8,10},{9,11},{10,... | collective-permute-start | bytes 1179656 | tf_op jit(solution)/shard_map/ppermute | solution.py:656
  6.9 1.3 %copy-start.2 = (bf16[768,768]{1,0:T(8,128)(2,1)S(1)}, bf16[768,768]{1,0:T(8,128)(2,1)}, u32[]{:S(2)}) copy-start(bf16[768,768]{1,0:T(8,128)(2,1)} %w_key.3) | copy-start | bytes 3538948
  8.2 6.7 %copy-start.3 = (bf16[256,2,96]{0,2,1:T(8,128)(2,1)S(1)}, bf16[256,2,96]{0,2,1:T(8,128)(2,1)}, u32[]{:S(2)}) copy-start(bf16[256,2,96]{0,2,1:T(8,128)(2,1)} %param.43) | copy-start | bytes 294916
  8.2 6.7 %copy-start.4 = (bf16[256,2,96]{0,2,1:T(8,128)(2,1)S(1)}, bf16[256,2,96]{0,2,1:T(8,128)(2,1)}, u32[]{:S(2)}) copy-start(bf16[256,2,96]{0,2,1:T(8,128)(2,1)} %param.23) | copy-start | bytes 294916
  8.2 8.6 %copy-start.5 = (bf16[96,384]{1,0:T(8,128)(2,1)S(1)}, bf16[96,384]{1,0:T(8,128)(2,1)}, u32[]{:S(2)}) copy-start(bf16[96,384]{1,0:T(8,128)(2,1)} %s_inner.2) | copy-start | bytes 221188
  8.2 8.6 %copy-start.7 = (bf16[96,96]{1,0:T(8,128)(2,1)S(1)}, bf16[96,96]{1,0:T(8,128)(2,1)}, u32[]{:S(2)}) copy-start(bf16[96,96]{1,0:T(8,128)(2,1)} %s_out.2) | copy-start | bytes 55300
  8.2 8.6 %copy-start.8 = (bf16[96,96]{1,0:T(8,128)(2,1)S(1)}, bf16[96,96]{1,0:T(8,128)(2,1)}, u32[]{:S(2)}) copy-start(bf16[96,96]{1,0:T(8,128)(2,1)} %s_query.2) | copy-start | bytes 55300
  8.2 8.6 %copy-start.9 = (bf16[96,96]{1,0:T(8,128)(2,1)S(1)}, bf16[96,96]{1,0:T(8,128)(2,1)}, u32[]{:S(2)}) copy-start(bf16[96,96]{1,0:T(8,128)(2,1)} %s_key.2) | copy-start | bytes 55300
  8.2 8.6 %copy-start.10 = (bf16[96,96]{1,0:T(8,128)(2,1)S(1)}, bf16[96,96]{1,0:T(8,128)(2,1)}, u32[]{:S(2)}) copy-start(bf16[96,96]{1,0:T(8,128)(2,1)} %s_value.2) | copy-start | bytes 55300
  8.2 8.6 %copy-start.14 = (f32[96]{0:T(128)S(1)}, f32[96]{0:T(128)}, u32[]{:S(2)}) copy-start(f32[96]{0:T(128)} %gate) | copy-start | bytes 1156
  8.2 8.6 %copy-start.15 = (f32[96]{0:T(128)S(1)}, f32[96]{0:T(128)}, u32[]{:S(2)}) copy-start(f32[96]{0:T(128)} %gain_in) | copy-start | bytes 1156
  8.2 8.5 %copy-start.16 = (f32[96]{0:T(128)S(1)}, f32[96]{0:T(128)}, u32[]{:S(2)}) copy-start(f32[96]{0:T(128)} %gain_mid) | copy-start | bytes 1156
  14.9 2.3 %collective-permute-start.3 = (bf16[256,768]{1,0:T(8,128)(2,1)S(1)}, bf16[256,768]{1,0:T(8,128)(2,1)S(1)}, u32[]{:S(2)}, u32[]{:S(2)}) collective-permute-start(bf16[256,768]{1,0:T(8,128)(2,1)S(1)} %collective-permute-done.far), channel_id=1, source_target_pairs={{0,1},{1,0},{2,3},{3,2},{4,5},{5,4},{6,7},{7,6},{8,9},{9,8},{10,11... | collective-permute-start | bytes 1179656 | tf_op jit(solution)/shard_map/ppermute | solution.py:656
  14.9 9.5 %collective-permute-start.2 = (bf16[192,256]{1,0:T(8,128)(2,1)S(1)}, bf16[192,256]{1,0:T(8,128)(2,1)S(1)}, u32[]{:S(2)}, u32[]{:S(2)}) collective-permute-start(bf16[192,256]{1,0:T(8,128)(2,1)S(1)} %fusion.3), channel_id=1, source_target_pairs={{0,2},{1,3},{2,0},{3,1},{4,6},{5,7},{6,4},{7,5},{8,10},{9,11},{10,... | collective-permute-start | bytes 294920 | tf_op jit(solution)/shard_map/ppermute | solution.py:656
  16.8 7.7 %slice-start = ((s8[4718592]{0:T(1024)(128)(4,1)}), s8[4194304]{0:T(1024)(128)(4,1)S(1)}, s32[]{:S(2)}) async-start(s8[4718592]{0:T(1024)(128)(4,1)} %bitcast.43), calls=%async_computation | async-start | bytes 8388608
  16.8 7.7 %slice-start.2 = ((s8[4718592]{0:T(1024)(128)(4,1)}), s8[4194304]{0:T(1024)(128)(4,1)S(1)}, s32[]{:S(2)}) async-start(s8[4718592]{0:T(1024)(128)(4,1)} %bitcast.45), calls=%async_computation.2 | async-start | bytes 8388608
  17.1 7.4 %slice-start.1 = ((s8[4718592]{0:T(1024)(128)(4,1)}), s8[524288]{0:T(1024)(128)(4,1)S(1)}, s32[]{:S(2)}) async-start(s8[4718592]{0:T(1024)(128)(4,1)} %bitcast.43), calls=%async_computation.1 | async-start | bytes 1048576
  17.1 7.4 %slice-start.3 = ((s8[4718592]{0:T(1024)(128)(4,1)}), s8[524288]{0:T(1024)(128)(4,1)S(1)}, s32[]{:S(2)}) async-start(s8[4718592]{0:T(1024)(128)(4,1)} %bitcast.45), calls=%async_computation.3 | async-start | bytes 1048576
  17.2 7.4 %copy-start.17 = (bf16[768,768]{1,0:T(8,128)(2,1)S(1)}, bf16[768,768]{1,0:T(8,128)(2,1)}, u32[]{:S(2)}) copy-start(bf16[768,768]{1,0:T(8,128)(2,1)} %w_out.1) | copy-start | bytes 3538948
  17.2 7.4 %copy-start.18 = (bf16[768,96]{0,1:T(8,128)(2,1)S(1)}, bf16[768,96]{0,1:T(8,128)(2,1)}, u32[]{:S(2)}) copy-start(bf16[768,96]{0,1:T(8,128)(2,1)} %param.33) | copy-start | bytes 442372
  24.6 8.0 %copy-start.6 = (bf16[384,96]{0,1:T(8,128)(2,1)S(1)}, bf16[384,96]{0,1:T(8,128)(2,1)}, u32[]{:S(2)}) copy-start(bf16[384,96]{0,1:T(8,128)(2,1)} %param.42) | copy-start | bytes 221188
  31.1 1.4 %collective-permute-start.4 = (bf16[512,96]{1,0:T(8,128)(2,1)S(1)}, bf16[512,96]{1,0:T(8,128)(2,1)S(1)}, u32[]{:S(2)}, u32[]{:S(2)}) collective-permute-start(bf16[512,96]{1,0:T(8,128)(2,1)S(1)} %get-tuple-element.107.sn_own), channel_id=1, source_target_pairs={{0,1},{1,0},{2,3},{3,2},{4,5},{5,4},{6,7},{7,6},{8,9},{9,8},{10,11... | collective-permute-start | bytes 294920 | tf_op jit(solution)/shard_map/ppermute | solution.py:656
  31.4 12.8 %collective-permute-start.6 = (bf16[256,768]{1,0:T(8,128)(2,1)S(1)}, bf16[256,768]{1,0:T(8,128)(2,1)S(1)}, u32[]{:S(2)}, u32[]{:S(2)}) collective-permute-start(bf16[256,768]{1,0:T(8,128)(2,1)S(1)} %get-tuple-element.115.out_far), channel_id=1, source_target_pairs={{0,2},{1,3},{2,0},{3,1},{4,6},{5,7},{6,4},{7,5},{8,10},{9,11},{10,... | collective-permute-start | bytes 1179656 | tf_op jit(solution)/shard_map/ppermute | solution.py:656
  42.7 1.5 %collective-permute-start.5 = (bf16[192,512]{1,0:T(8,128)(2,1)S(1)}, bf16[192,512]{1,0:T(8,128)(2,1)S(1)}, u32[]{:S(2)}, u32[]{:S(2)}) collective-permute-start(bf16[192,512]{1,0:T(8,128)(2,1)S(1)} %get-tuple-element.114), channel_id=1, source_target_pairs={{0,1},{1,0},{2,3},{3,2},{4,5},{5,4},{6,7},{7,6},{8,9},{9,8},{10,11... | collective-permute-start | bytes 589832 | tf_op jit(solution)/shard_map/ppermute | solution.py:656
  44.9 1.5 %collective-permute-start.7 = (bf16[96,1024]{1,0:T(8,128)(2,1)S(1)}, bf16[96,1024]{1,0:T(8,128)(2,1)S(1)}, u32[]{:S(2)}, u32[]{:S(2)}) collective-permute-start(bf16[96,1024]{1,0:T(8,128)(2,1)S(1)} %get-tuple-element.136), channel_id=1, source_target_pairs={{0,1},{1,0},{2,3},{3,2},{4,5},{5,4},{6,7},{7,6},{8,9},{9,8},{10,11... | collective-permute-start | bytes 589832 | tf_op jit(solution)/shard_map/ppermute | solution.py:656
  46.5 5.5 %collective-permute-start.10 = (bf16[96,256]{1,0:T(8,128)(2,1)S(1)}, bf16[96,256]{1,0:T(8,128)(2,1)S(1)}, u32[]{:S(2)}, u32[]{:S(2)}) collective-permute-start(bf16[96,256]{1,0:T(8,128)(2,1)S(1)} %get-tuple-element.184), channel_id=1, source_target_pairs={{0,6},{1,7},{2,4},{3,5},{4,2},{5,3},{6,0},{7,1},{8,14},{9,15},{10,... | collective-permute-start | bytes 147464 | tf_op jit(solution)/shard_map/ppermute | solution.py:868
  48.7 4.1 %collective-permute-start.8 = (bf16[96,256]{1,0:T(8,128)(2,1)S(1)}, bf16[96,256]{1,0:T(8,128)(2,1)S(1)}, u32[]{:S(2)}, u32[]{:S(2)}) collective-permute-start(bf16[96,256]{1,0:T(8,128)(2,1)S(1)} %get-tuple-element.183), channel_id=1, source_target_pairs={{0,2},{1,3},{2,0},{3,1},{4,6},{5,7},{6,4},{7,5},{8,10},{9,11},{10,... | collective-permute-start | bytes 147464 | tf_op jit(solution)/shard_map/ppermute | solution.py:868
  49.6 4.1 %collective-permute-start.9 = (bf16[96,256]{1,0:T(8,128)(2,1)S(1)}, bf16[96,256]{1,0:T(8,128)(2,1)S(1)}, u32[]{:S(2)}, u32[]{:S(2)}) collective-permute-start(bf16[96,256]{1,0:T(8,128)(2,1)S(1)} %get-tuple-element.185), channel_id=1, source_target_pairs={{0,4},{1,5},{2,6},{3,7},{4,0},{5,1},{6,2},{7,3},{8,12},{9,13},{10,... | collective-permute-start | bytes 147464 | tf_op jit(solution)/shard_map/ppermute | solution.py:868
  53.7 4.2 %collective-permute-start.12 = (bf16[96,256]{1,0:T(8,128)(2,1)S(1)}, bf16[96,256]{1,0:T(8,128)(2,1)S(1)}, u32[]{:S(2)}, u32[]{:S(2)}) collective-permute-start(bf16[96,256]{1,0:T(8,128)(2,1)S(1)} %add_convert_fusion.3), channel_id=1, source_target_pairs={{0,8},{4,12},{8,0},{12,4},{16,24},{20,28},{24,16},{28,20},{1,9},{5... | collective-permute-start | bytes 147464 | tf_op jit(solution)/shard_map/ppermute | solution.py:656
  57.9 5.6 %collective-permute-start.13 = (bf16[96,256]{1,0:T(8,128)(2,1)S(1)}, bf16[96,256]{1,0:T(8,128)(2,1)S(1)}, u32[]{:S(2)}, u32[]{:S(2)}) collective-permute-start(bf16[96,256]{1,0:T(8,128)(2,1)S(1)} %add_convert_fusion.2), channel_id=1, source_target_pairs={{0,16},{4,20},{8,24},{12,28},{16,0},{20,4},{24,8},{28,12},{1,17},{... | collective-permute-start | bytes 147464 | tf_op jit(solution)/shard_map/ppermute | solution.py:656
  62.3 4.7 %collective-permute-start.11 = (bf16[192,256]{1,0:T(8,128)(2,1)S(1)}, bf16[192,256]{1,0:T(8,128)(2,1)S(1)}, u32[]{:S(2)}, u32[]{:S(2)}) collective-permute-start(bf16[192,256]{1,0:T(8,128)(2,1)S(1)} %get-tuple-element.138), channel_id=1, source_target_pairs={{0,2},{1,3},{2,0},{3,1},{4,6},{5,7},{6,4},{7,5},{8,10},{9,11},{10,... | collective-permute-start | bytes 294920 | tf_op jit(solution)/shard_map/ppermute | solution.py:656
  63.5 4.3 %collective-permute-start.14 = (bf16[96,256]{1,0:T(8,128)(2,1)S(1)}, bf16[96,256]{1,0:T(8,128)(2,1)S(1)}, u32[]{:S(2)}, u32[]{:S(2)}) collective-permute-start(bf16[96,256]{1,0:T(8,128)(2,1)S(1)} %add_convert_fusion.1.refs_0_), channel_id=1, source_target_pairs={{0,2},{1,3},{2,0},{3,1},{4,6},{5,7},{6,4},{7,5},{8,10},{9,11},{10,... | collective-permute-start | bytes 147464 | tf_op jit(solution)/shard_map/ppermute | solution.py:868
  64.4 4.1 %collective-permute-start.15 = (bf16[96,256]{1,0:T(8,128)(2,1)S(1)}, bf16[96,256]{1,0:T(8,128)(2,1)S(1)}, u32[]{:S(2)}, u32[]{:S(2)}) collective-permute-start(bf16[96,256]{1,0:T(8,128)(2,1)S(1)} %add_convert_fusion.1.refs_0_), channel_id=1, source_target_pairs={{0,4},{1,5},{2,6},{3,7},{4,0},{5,1},{6,2},{7,3},{8,12},{9,13},{10,... | collective-permute-start | bytes 147464 | tf_op jit(solution)/shard_map/ppermute | solution.py:868
  64.9 5.0 %collective-permute-start.16 = (bf16[96,256]{1,0:T(8,128)(2,1)S(1)}, bf16[96,256]{1,0:T(8,128)(2,1)S(1)}, u32[]{:S(2)}, u32[]{:S(2)}) collective-permute-start(bf16[96,256]{1,0:T(8,128)(2,1)S(1)} %add_convert_fusion.1.refs_0_), channel_id=1, source_target_pairs={{0,6},{1,7},{2,4},{3,5},{4,2},{5,3},{6,0},{7,1},{8,14},{9,15},{10,... | collective-permute-start | bytes 147464 | tf_op jit(solution)/shard_map/ppermute | solution.py:868
  67.0 3.5 %collective-permute-start.17 = (bf16[96,256]{1,0:T(8,128)(2,1)S(1)}, bf16[96,256]{1,0:T(8,128)(2,1)S(1)}, u32[]{:S(2)}, u32[]{:S(2)}) collective-permute-start(bf16[96,256]{1,0:T(8,128)(2,1)S(1)} %add_convert_fusion.1.refs_0_), channel_id=1, source_target_pairs={{0,1},{1,0},{2,3},{3,2},{4,5},{5,4},{6,7},{7,6},{8,9},{9,8},{10,11... | collective-permute-start | bytes 147464 | tf_op jit(solution)/shard_map/ppermute | solution.py:656
  67.8 2.8 %collective-permute-start.18 = (bf16[96,256]{1,0:T(8,128)(2,1)S(1)}, bf16[96,256]{1,0:T(8,128)(2,1)S(1)}, u32[]{:S(2)}, u32[]{:S(2)}) collective-permute-start(bf16[96,256]{1,0:T(8,128)(2,1)S(1)} %collective-permute-done.14.refs_1_), channel_id=1, source_target_pairs={{0,1},{1,0},{2,3},{3,2},{4,5},{5,4},{6,7},{7,6},{8,9},{9,8},{10,11... | collective-permute-start | bytes 147464 | tf_op jit(solution)/shard_map/ppermute | solution.py:656
  68.5 2.1 %collective-permute-start.19 = (bf16[96,256]{1,0:T(8,128)(2,1)S(1)}, bf16[96,256]{1,0:T(8,128)(2,1)S(1)}, u32[]{:S(2)}, u32[]{:S(2)}) collective-permute-start(bf16[96,256]{1,0:T(8,128)(2,1)S(1)} %collective-permute-done.15.refs_2_), channel_id=1, source_target_pairs={{0,1},{1,0},{2,3},{3,2},{4,5},{5,4},{6,7},{7,6},{8,9},{9,8},{10,11... | collective-permute-start | bytes 147464 | tf_op jit(solution)/shard_map/ppermute | solution.py:656
  69.9 1.2 %collective-permute-start.20 = (bf16[96,256]{1,0:T(8,128)(2,1)S(1)}, bf16[96,256]{1,0:T(8,128)(2,1)S(1)}, u32[]{:S(2)}, u32[]{:S(2)}) collective-permute-start(bf16[96,256]{1,0:T(8,128)(2,1)S(1)} %collective-permute-done.16.refs_3_), channel_id=1, source_target_pairs={{0,1},{1,0},{2,3},{3,2},{4,5},{5,4},{6,7},{7,6},{8,9},{9,8},{10,11... | collective-permute-start | bytes 147464 | tf_op jit(solution)/shard_map/ppermute | solution.py:656

commit v8 on v7

--- a/solution.py
+++ b/solution.py
@@ -9,7 +9,7 @@
 
 HEADS = 12
 SHEADS = 12
-SPARE = 64
+SPARE = 96
 EPS = 1e-06
 LOG2E = math.log2(math.e)
 FAR = 2.0**100
@@ -73,10 +73,8 @@
     )(*ins)
 
 
-def doubled(rows, columns, feature, transposed):
+def doubled(rows, columns, feature):
     wide, thin = iota((rows, columns), 0), iota((rows, columns), 1)
-    if not transposed:
-        wide, thin = thin, wide
     source = (wide // (2 * feature)) * feature + wide % feature
     return ones_where(source == thin)
 
@@ -108,13 +106,13 @@
 
 
 def side_weights_body(
-    s_query, s_key, s_value, s_out, s_inner, gate, gain_in, gain_mid, dup, dup_t, tall_t, columns, lines
+    s_query, s_key, s_value, s_out, s_inner, gate, gain_in, gain_mid, dup, dup_t, tall_t, columns, query_t, lines
 ):
     side, hidden = s_inner.shape
     feature = side // SHEADS
-    spread = doubled(side, dup.shape[1], feature, False)
-    dup[...] = nn(s_key[...], spread).astype(bf16)
-    spread_t = doubled(2 * side, side, feature, True)
+    dup[...] = nn(s_key[...], ones_where(iota(dup.shape, 0) == iota(dup.shape, 1))).astype(bf16)
+    query_t[...] = nt(eye(side), s_query[...]).astype(bf16)
+    spread_t = doubled(2 * side, side, feature)
     for i, weight in enumerate((s_query, s_key, s_value)):
         dup_t[2 * side * i : 2 * side * (i + 1)] = nt(spread_t, weight[...]).astype(bf16)
     tall_t[0:side] = nt(eye(side), s_out[...]).astype(bf16)
@@ -329,6 +327,7 @@
     columns,
     key_doc,
     query_doc,
+    thin_query,
     dkv_own,
     dkv_mate,
     dmid_t,
@@ -347,7 +346,6 @@
     value_t,
     query_t,
     query_s,
-    query_h,
     totals,
     back_rows,
     dkv_t,
@@ -360,21 +358,16 @@
     scale = feature**-0.5
 
     sn = jnp.concatenate([sn_own[...], sn_mate[...]], axis=0)
-    projected = nn(sn, dup[...]).astype(bf16)
-    keys[:, 0:128] = projected[:, 0:128]
-    keys[:, 128:256] = projected[:, 128:256] + key_doc[...]
+    keys[...] = nn(sn, dup[...]).astype(bf16) + key_doc[...]
     key_t[...] = nt(dup_t[wide : 2 * wide], sn).astype(bf16)
     second = iota((wide, 2 * tokens), 0) % (2 * feature) >= feature
     value_t[...] = jnp.where(second, 1.0, nt(dup_t[2 * wide : 3 * wide], sn)).astype(bf16)
     query = nt(dup_t[0:wide], sn_own[...]).astype(bf16)
     query_t[...] = query
-    scaled = query.astype(f32) * (scale * LOG2E)
-    high = scaled.astype(bf16).astype(f32)
-    second = iota((wide, tokens), 0) % (2 * feature) >= feature
-    query_s[...] = jnp.where(second, scaled - high, high).astype(bf16)
-    for i in range(SHEADS):
-        query_h[i] = jnp.zeros(query_h.shape[1:], bf16)
-        query_h[i, wide : wide + 16] = query_doc[...]
+    query_s[0:side] = nt(thin_query[...], sn_own[...]).astype(bf16)
+    query_s[side : side + 16] = query_doc[...]
+    query_s[side + 16 :] = jnp.zeros((128 - side - 16, tokens), bf16)
+    owner = iota((128, 1), 0) // feature
 
     def head_rows(h, count):
         return pl.ds(pl.multiple_of(h * count, count), count)
@@ -384,9 +377,8 @@
             for i in range(size):
                 h = size * j + i
                 rows, eight = head_rows(h, 16), head_rows(h, 8)
-                query_h[i, rows, :] = query_s[rows, :]
-                scores = nn(keys[...], query_h[i])
-                query_h[i, rows, :] = jnp.zeros((16, tokens), bf16)
+                mine = ones_where((owner == h) | (owner >= SHEADS))
+                scores = nn(keys[...], query_s[...] * mine) * (scale * LOG2E)
                 if shifted:
                     scores = scores - jnp.max(scores, axis=0, keepdims=True)
                 weight = jnp.exp2(scores).astype(bf16)
@@ -442,7 +434,7 @@
         eight = slice(h * feature, (h + 1) * feature)
         invert = inverse[eight, :]
         term = jnp.sum(dattn[eight] * attn[eight], axis=0, keepdims=True)
-        query = query_t[2 * h * feature : (2 * h + 1) * feature].astype(f32)
+        query = query_t[2 * h * feature : 2 * (h + 1) * feature].astype(f32)[0:feature]
         share = dattn[eight] * invert
         back_rows[h] = jnp.concatenate(
             two_parts(share) + two_parts(term * invert * query) + two_parts(outer_rows(share, query)), axis=0
@@ -454,7 +446,7 @@
         dkv_t[side + h * feature : side + (h + 1) * feature] = (
             summed[0:feature] + summed[feature : 2 * feature]
         )
-        value = value_t[2 * h * feature : (2 * h + 1) * feature].astype(f32)
+        value = value_t[2 * h * feature : 2 * (h + 1) * feature].astype(f32)[0:feature]
         at = 4 * feature + feature * feature
         raw = inner_rows(value, summed[4 * feature : at] + summed[at:])
         raw = raw - (summed[2 * feature : 3 * feature] + summed[3 * feature : 4 * feature])
@@ -706,13 +698,14 @@
     )
     small = (s_query, s_key, s_value, s_out, s_inner, gate, side_norm_in, side_norm_mid)
     hidden_far, small, *state_a = lax.optimization_barrier((hidden_far, small, *state_a))
-    dup, dup_t, tall_t, columns = kernel_call(
+    dup, dup_t, tall_t, columns, s_query_t = kernel_call(
         side_weights_body,
         [
-            ((side, 256), bf16),
+            ((side, 128), bf16),
             ((6 * side, side), bf16),
             ((side + sff, side), bf16),
             ((side, 128), f32),
+            ((side, side), bf16),
         ],
         small,
         vmem=8,
@@ -792,16 +785,16 @@
             columns,
             side_key_doc,
             side_query_doc,
+            s_query_t,
         ],
         vmem=36,
         scratch=[
             pltpu.VMEM((SHEADS, tokens, 2 * tokens), bf16),
-            pltpu.VMEM((2 * tokens, 256), bf16),
+            pltpu.VMEM((2 * tokens, 128), bf16),
             pltpu.VMEM((2 * side, 2 * tokens), bf16),
             pltpu.VMEM((2 * side, 2 * tokens), bf16),
             pltpu.VMEM((2 * side, tokens), bf16),
-            pltpu.VMEM((2 * side, tokens), bf16),
-            pltpu.VMEM((SHEADS, 256, tokens), bf16),
+            pltpu.VMEM((128, tokens), bf16),
             pltpu.VMEM((side, tokens), f32),
             pltpu.VMEM((SHEADS, feature * (2 * feature + 4), tokens), bf16),
             pltpu.VMEM((2 * side, 2 * tokens), f32),

time: 72.3 us -> 72.2 us (level)
  no operation moved by 1% of the time
where the time goes in v8:
time: 72.2 us; the launch traced here: 72 us
  Pallas kernels  33.5 us (46%)
  starting transfers between devices  19.9 us (28%)
  waiting for transfers between devices  11.5 us (16%)
  local copies, waits for them, and re-layouts  4.44 us (6%)
  other arithmetic  1.63 us (2%)
  between operations  1.08 us (1%)
    pallas_call x9, Pallas kernels, kernel_call(): pl.pallas_call(body, out_shape=[jax.ShapeDtypeStruct(shape, kind) for sha...  33.5 us
    ppermute x15, starting transfers between devices, swap(): return lax.ppermute(value, axis, [(i, i ^ hop) for i in range(size)])  12.8 us
    ppermute x6, starting transfers between devices, between(): lax.ppermute(value, ('dp', 'blk'), [(i, i ^ mask) for i in range(devices)])  7.11 us
    ppermute x15, waiting for transfers between devices, swap(): return lax.ppermute(value, axis, [(i, i ^ hop) for i in range(size)])  6.25 us
    ppermute x6, waiting for transfers between devices, between(): lax.ppermute(value, ('dp', 'blk'), [(i, i ^ mask) for i in range(devices)])  5.22 us
    unnamed x48, local copies, waits for them, and re-layouts  4.39 us
  transfers between devices with their start and end apart: 21, of which 10 were waited for; matrix products, arithmetic and copies ran while one was open for 5% of the time, Pallas kernels for 35%

profile of v8, /device:TPU:0, one launch (start us, length us, event | category | flops | bytes accessed | tf_op | source)
XLA Modules:
  0.0 72.0 jit_solution(13759323528838424332)
XLA Ops:
  0.7 1.3 %copy.42 = bf16[256,2,768]{2,0,1:T(8,128)(2,1)S(1)} copy(bf16[256,2,768]{2,1,0:T(2,128)(2,1)} %param.22) | data formatting | bytes 1572864 | tf_op args[0]
  2.0 0.5 collective-permute-start.1
  2.6 2.6 %collective-permute-start = (bf16[256,768]{1,0:T(8,128)(2,1)S(1)}, bf16[256,768]{1,0:T(8,128)(2,1)S(1)}, u32[]{:S(2)}, u32[]{:S(2)}) collective-permute-start(bf16[256,768]{1,0:T(8,128)(2,1)S(1)} %dynamic-slice_bitcast_fusion), channel_id=1, source_target_pairs={{0,2},{1,3},{2,0},{3,1},{4,6},{5,7},{6,4},{7,5},{8,10},{9,11},{10,... | collective-permute-start | bytes 1179656 | tf_op jit(solution)/shard_map/ppermute | solution.py:648
  5.2 1.7 %shard_map.309 = (bf16[768,768]{1,0:T(8,128)(2,1)S(1)}, f32[2,768]{1,0:T(2,128)S(1)}, bf16[1024,128]{1,0:T(8,128)(2,1)S(1)}, bf16[512,128]{1,0:T(8,128)(2,1)S(1)...) custom-call(s32[2,8]{1,0:T(2,128)S(1)} %copy-done.13, bf16[768,768]{1,0:T(8,128)(2,1)S(1)} %copy-done, ...), custom_call_target="tpu_custom_call" | custom-call | flops 1000 | bytes 1000 | tf_op jit(solution)/shard_map/pallas_call | solution.py:65
  6.9 1.3 %copy-done.2 = bf16[768,768]{1,0:T(8,128)(2,1)S(1)} copy-done((bf16[768,768]{1,0:T(8,128)(2,1)S(1)}, bf16[768,768]{1,0:T(8,128)(2,1)}, u32[]{:S(2)}) %copy-start.2) | copy-done | bytes 1179672
  8.2 5.3 %shard_map.310 = (bf16[256,768]{1,0:T(8,128)(2,1)S(1)}, bf16[512,768]{1,0:T(8,128)(2,1)S(1)}, bf16[960,512]{1,0:T(8,128)(2,1)S(1)}, f32[6,144,256]{2,1,0:T(8,128)S(1)}) custom-call(bf16[2,256,768]{2,1,0:T(8,128)(2,1)S(1)} %bitcast.34, bf16[2,256,768]{2,1,0:T(8,128)(2,1)} %collective-permute-done.1.mate, f32[2,768]{1,0:T(2,128)S(1)} %get-tuple-element.83.gains, ...), custom_call_target="tpu_custom_call" | custom-call | flops 1000 | bytes 1000 | tf_op jit(solution)/shard_map/pallas_call | solution.py:65
  13.6 1.3 %collective-permute-done.far = bf16[256,768]{1,0:T(8,128)(2,1)S(1)} collective-permute-done((bf16[256,768]{1,0:T(8,128)(2,1)S(1)}, bf16[256,768]{1,0:T(8,128)(2,1)S(1)}, u32[]{:S(2)}, u32[]{:S(2)}) %collective-permute-start) | collective-permute-done | bytes 393248 | tf_op jit(solution)/shard_map/ppermute | solution.py:648
  14.9 1.8 %collective-permute-start.2 = (bf16[192,256]{1,0:T(8,128)(2,1)S(1)}, bf16[192,256]{1,0:T(8,128)(2,1)S(1)}, u32[]{:S(2)}, u32[]{:S(2)}) collective-permute-start(bf16[192,256]{1,0:T(8,128)(2,1)S(1)} %fusion.3), channel_id=1, source_target_pairs={{0,2},{1,3},{2,0},{3,1},{4,6},{5,7},{6,4},{7,5},{8,10},{9,11},{10,... | collective-permute-start | bytes 294920 | tf_op jit(solution)/shard_map/ppermute | solution.py:648
  16.8 0.0 slice-start
  16.8 0.0 slice-start.2
  16.8 0.3 shard_map.312
  17.1 0.0 slice-start.1
  17.1 0.0 slice-start.3
  17.2 7.3 %shard_map.311.attended = bf16[512,768]{1,0:T(8,128)(2,1)S(1)} custom-call(bf16[256,768]{1,0:T(8,128)(2,1)S(1)} %collective-permute-done.far, bf16[256,768]{1,0:T(8,128)(2,1)S(1)} %collective-permute-done.3.far_mate, f32[2,768]{1,0:T(2,128)S(1)} %get-tuple-element.83.gains, bf16[768,768]{1,0:T(8,128)(2,1)S(1)} %copy-done.1, bf16[768,768]{1,0:T(8,128)(2,1)S(1)} %copy-done.2, ...), custom_call_target="tpu_custom_call" | custom-call | flops 8000000000 | bytes 8000000 | tf_op jit(solution)/shard_map/pallas_call | solution.py:65
  24.6 6.6 %shard_map.313 = (bf16[256,768]{1,0:T(8,128)(2,1)S(1)}, bf16[256,768]{1,0:T(8,128)(2,1)S(1)}, bf16[512,96]{1,0:T(8,128)(2,1)S(1)}, bf16[96,512]{1,0:T(8,128)(2,1...) custom-call(bf16[2,256,768]{2,1,0:T(8,128)(2,1)S(1)} %bitcast.35, bf16[256,768]{1,0:T(8,128)(2,1)S(1)} %collective-permute-done.far, ...), custom_call_target="tpu_custom_call" | custom-call | flops 10000000000 | bytes 14000000 | tf_op jit(solution)/shard_map/pallas_call | solution.py:65
  31.1 0.3 collective-permute-start.4
  31.4 1.1 %collective-permute-start.6 = (bf16[256,768]{1,0:T(8,128)(2,1)S(1)}, bf16[256,768]{1,0:T(8,128)(2,1)S(1)}, u32[]{:S(2)}, u32[]{:S(2)}) collective-permute-start(bf16[256,768]{1,0:T(8,128)(2,1)S(1)} %get-tuple-element.117.out_far), channel_id=1, source_target_pairs={{0,2},{1,3},{2,0},{3,1},{4,6},{5,7},{6,4},{7,5},{8,10},{9,11},{10,... | collective-permute-start | bytes 1179656 | tf_op jit(solution)/shard_map/ppermute | solution.py:648
  32.5 0.0 collective-permute-done.4.sn_mate
  32.6 10.1 %shard_map.314 = (f32[192,512]{1,0:T(8,128)S(1)}, bf16[192,512]{1,0:T(8,128)(2,1)S(1)}, f32[96,512]{1,0:T(8,128)S(1)}, f32[96,512]{1,0:T(8,128)S(1)}, f32[96,512...) custom-call(bf16[512,96]{1,0:T(8,128)(2,1)S(1)} %get-tuple-element.1, ...), custom_call_target="tpu_custom_call" | custom-call | flops 30000001024 | bytes 3000000 | tf_op jit(solution)/shard_map/pallas_call | solution.py:65
  42.7 0.3 collective-permute-start.5
  42.9 0.6 shard_map.315
  43.6 0.6 collective-permute-done.5.dkv_back
  44.2 0.7 shard_map.316
  44.9 0.3 collective-permute-start.7
  45.1 1.2 %collective-permute-done.7 = bf16[96,1024]{1,0:T(8,128)(2,1)S(1)} collective-permute-done((bf16[96,1024]{1,0:T(8,128)(2,1)S(1)}, bf16[96,1024]{1,0:T(8,128)(2,1)S(1)}, u32[]{:S(2)}, u32[]{:S(2)}) %collective-permute-start.7) | collective-permute-done | bytes 196640 | tf_op jit(solution)/shard_map/ppermute | solution.py:648
  46.5 2.2 %collective-permute-start.10 = (bf16[96,256]{1,0:T(8,128)(2,1)S(1)}, bf16[96,256]{1,0:T(8,128)(2,1)S(1)}, u32[]{:S(2)}, u32[]{:S(2)}) collective-permute-start(bf16[96,256]{1,0:T(8,128)(2,1)S(1)} %get-tuple-element.186), channel_id=1, source_target_pairs={{0,6},{1,7},{2,4},{3,5},{4,2},{5,3},{6,0},{7,1},{8,14},{9,15},{10,... | collective-permute-start | bytes 147464 | tf_op jit(solution)/shard_map/ppermute | solution.py:861
  48.6 0.9 %collective-permute-start.8 = (bf16[96,256]{1,0:T(8,128)(2,1)S(1)}, bf16[96,256]{1,0:T(8,128)(2,1)S(1)}, u32[]{:S(2)}, u32[]{:S(2)}) collective-permute-start(bf16[96,256]{1,0:T(8,128)(2,1)S(1)} %get-tuple-element.185), channel_id=1, source_target_pairs={{0,2},{1,3},{2,0},{3,1},{4,6},{5,7},{6,4},{7,5},{8,10},{9,11},{10,... | collective-permute-start | bytes 147464 | tf_op jit(solution)/shard_map/ppermute | solution.py:861
  49.5 0.5 collective-permute-start.9
  50.0 2.0 %collective-permute-done.10 = bf16[96,256]{1,0:T(8,128)(2,1)S(1)} collective-permute-done((bf16[96,256]{1,0:T(8,128)(2,1)S(1)}, bf16[96,256]{1,0:T(8,128)(2,1)S(1)}, u32[]{:S(2)}, u32[]{:S(2)}) %collective-permute-start.10) | collective-permute-done | bytes 49184 | tf_op jit(solution)/shard_map/ppermute | solution.py:861
  52.0 0.8 %collective-permute-done.8 = bf16[96,256]{1,0:T(8,128)(2,1)S(1)} collective-permute-done((bf16[96,256]{1,0:T(8,128)(2,1)S(1)}, bf16[96,256]{1,0:T(8,128)(2,1)S(1)}, u32[]{:S(2)}, u32[]{:S(2)}) %collective-permute-start.8) | collective-permute-done | bytes 49184 | tf_op jit(solution)/shard_map/ppermute | solution.py:861
  52.7 0.9 %collective-permute-done.9 = bf16[96,256]{1,0:T(8,128)(2,1)S(1)} collective-permute-done((bf16[96,256]{1,0:T(8,128)(2,1)S(1)}, bf16[96,256]{1,0:T(8,128)(2,1)S(1)}, u32[]{:S(2)}, u32[]{:S(2)}) %collective-permute-start.9) | collective-permute-done | bytes 49184 | tf_op jit(solution)/shard_map/ppermute | solution.py:861
  53.6 1.6 %collective-permute-start.12 = (bf16[96,256]{1,0:T(8,128)(2,1)S(1)}, bf16[96,256]{1,0:T(8,128)(2,1)S(1)}, u32[]{:S(2)}, u32[]{:S(2)}) collective-permute-start(bf16[96,256]{1,0:T(8,128)(2,1)S(1)} %add_convert_fusion.3), channel_id=1, source_target_pairs={{0,8},{4,12},{8,0},{12,4},{16,24},{20,28},{24,16},{28,20},{1,9},{5... | collective-permute-start | bytes 147464 | tf_op jit(solution)/shard_map/ppermute | solution.py:648
  55.3 0.1 select_bitcast_fusion.1
  55.3 2.5 %collective-permute-done.12 = bf16[96,256]{1,0:T(8,128)(2,1)S(1)} collective-permute-done((bf16[96,256]{1,0:T(8,128)(2,1)S(1)}, bf16[96,256]{1,0:T(8,128)(2,1)S(1)}, u32[]{:S(2)}, u32[]{:S(2)}) %collective-permute-start.12) | collective-permute-done | bytes 49184 | tf_op jit(solution)/shard_map/ppermute | solution.py:648
  57.8 2.6 %collective-permute-start.13 = (bf16[96,256]{1,0:T(8,128)(2,1)S(1)}, bf16[96,256]{1,0:T(8,128)(2,1)S(1)}, u32[]{:S(2)}, u32[]{:S(2)}) collective-permute-start(bf16[96,256]{1,0:T(8,128)(2,1)S(1)} %add_convert_fusion.2), channel_id=1, source_target_pairs={{0,16},{4,20},{8,24},{12,28},{16,0},{20,4},{24,8},{28,12},{1,17},{... | collective-permute-start | bytes 147464 | tf_op jit(solution)/shard_map/ppermute | solution.py:648
  60.5 0.1 maximum_bitcast_fusion
  60.5 1.7 %copy.39 = bf16[256,2,768]{2,1,0:T(2,128)(2,1)} copy(bf16[256,2,768]{2,0,1:T(8,128)(2,1)S(1)} %maximum_bitcast_fusion) | data formatting | bytes 1572864
  62.2 1.2 %collective-permute-start.11 = (bf16[192,256]{1,0:T(8,128)(2,1)S(1)}, bf16[192,256]{1,0:T(8,128)(2,1)S(1)}, u32[]{:S(2)}, u32[]{:S(2)}) collective-permute-start(bf16[192,256]{1,0:T(8,128)(2,1)S(1)} %get-tuple-element.140), channel_id=1, source_target_pairs={{0,2},{1,3},{2,0},{3,1},{4,6},{5,7},{6,4},{7,5},{8,10},{9,11},{10,... | collective-permute-start | bytes 294920 | tf_op jit(solution)/shard_map/ppermute | solution.py:648
  63.4 0.9 %collective-permute-start.14 = (bf16[96,256]{1,0:T(8,128)(2,1)S(1)}, bf16[96,256]{1,0:T(8,128)(2,1)S(1)}, u32[]{:S(2)}, u32[]{:S(2)}) collective-permute-start(bf16[96,256]{1,0:T(8,128)(2,1)S(1)} %add_convert_fusion.1.refs_0_), channel_id=1, source_target_pairs={{0,2},{1,3},{2,0},{3,1},{4,6},{5,7},{6,4},{7,5},{8,10},{9,11},{10,... | collective-permute-start | bytes 147464 | tf_op jit(solution)/shard_map/ppermute | solution.py:861
  64.3 0.5 collective-permute-start.15
  64.8 2.1 %collective-permute-start.16 = (bf16[96,256]{1,0:T(8,128)(2,1)S(1)}, bf16[96,256]{1,0:T(8,128)(2,1)S(1)}, u32[]{:S(2)}, u32[]{:S(2)}) collective-permute-start(bf16[96,256]{1,0:T(8,128)(2,1)S(1)} %add_convert_fusion.1.refs_0_), channel_id=1, source_target_pairs={{0,6},{1,7},{2,4},{3,5},{4,2},{5,3},{6,0},{7,1},{8,14},{9,15},{10,... | collective-permute-start | bytes 147464 | tf_op jit(solution)/shard_map/ppermute | solution.py:861
  67.0 0.7 maximum_bitcast_fusion.1
  67.7 0.5 collective-permute-start.18
  68.2 0.2 collective-permute-done.15.refs_2_
  68.4 1.4 %collective-permute-done.16.refs_3_ = bf16[96,256]{1,0:T(8,128)(2,1)S(1)} collective-permute-done((bf16[96,256]{1,0:T(8,128)(2,1)S(1)}, bf16[96,256]{1,0:T(8,128)(2,1)S(1)}, u32[]{:S(2)}, u32[]{:S(2)}) %collective-permute-start.16) | collective-permute-done | bytes 49184 | tf_op jit(solution)/shard_map/ppermute | solution.py:861
  69.8 0.7 maximum_bitcast_fusion.2
  70.5 0.6 collective-permute-done.20.refs_7_
  71.1 1.0 %shard_map.317 = (f32[96,768]{1,0:T(8,128)}, f32[1,96]{1,0:T(1,128)}, f32[1,96]{1,0:T(1,128)}, f32[96,96]{1,0:T(8,128)}, f32[96,96]{1,0:T(8,128)}, /*index=5*/f3...) custom-call(bf16[96,256]{1,0:T(8,128)(2,1)S(1)} %add_convert_fusion.1.refs_0_, ...), custom_call_target="tpu_custom_call" | custom-call | bytes 2000000 | tf_op jit(solution)/shard_map/pallas_call | solution.py:65
  (66 shorter events, 0.4 us)
Async XLA Ops:
  0.6 4.5 %copy-start.13 = (s32[2,8]{1,0:T(2,128)S(1)}, s32[2,8]{1,0:T(2,128)}, u32[]{:S(2)}) copy-start(s32[2,8]{1,0:T(2,128)} %doc_lengths.1) | copy-start | bytes 196
  0.7 4.5 %copy-start.11 = (bf16[768]{0:T(1024)(128)(2,1)S(1)}, bf16[768]{0:T(1024)(128)(2,1)}, u32[]{:S(2)}) copy-start(bf16[768]{0:T(1024)(128)(2,1)} %norm_in.1) | copy-start | bytes 4612
  0.7 4.5 %copy-start = (bf16[768,768]{1,0:T(8,128)(2,1)S(1)}, bf16[768,768]{1,0:T(8,128)(2,1)}, u32[]{:S(2)}) copy-start(bf16[768,768]{1,0:T(8,128)(2,1)} %w_value.1) | copy-start | bytes 3538948
  0.7 4.5 %copy-start.12 = (bf16[768]{0:T(1024)(128)(2,1)S(1)}, bf16[768]{0:T(1024)(128)(2,1)}, u32[]{:S(2)}) copy-start(bf16[768]{0:T(1024)(128)(2,1)} %norm_mid.1) | copy-start | bytes 4612
  2.0 4.9 %copy-start.1 = (bf16[768,768]{1,0:T(8,128)(2,1)S(1)}, bf16[768,768]{1,0:T(8,128)(2,1)}, u32[]{:S(2)}) copy-start(bf16[768,768]{1,0:T(8,128)(2,1)} %w_query.3) | copy-start | bytes 3538948
  2.0 4.9 %collective-permute-start.1 = (bf16[2,256,768]{2,1,0:T(8,128)(2,1)S(1)}, bf16[2,256,768]{2,1,0:T(8,128)(2,1)}, u32[]{:S(2)}, u32[]{:S(2)}) collective-permute-start(bf16[2,256,768]{2,1,0:T(8,128)(2,1)S(1)} %bitcast.33), channel_id=1, source_target_pairs={{0,1},{1,0},{2,3},{3,2},{4,5},{5,4},{6,7},{7,6},{8,9},{9,8},{10,11... | collective-permute-start | bytes 2359304 | tf_op jit(solution)/shard_map/ppermute | solution.py:648
  2.6 12.3 %collective-permute-start = (bf16[256,768]{1,0:T(8,128)(2,1)S(1)}, bf16[256,768]{1,0:T(8,128)(2,1)S(1)}, u32[]{:S(2)}, u32[]{:S(2)}) collective-permute-start(bf16[256,768]{1,0:T(8,128)(2,1)S(1)} %dynamic-slice_bitcast_fusion), channel_id=1, source_target_pairs={{0,2},{1,3},{2,0},{3,1},{4,6},{5,7},{6,4},{7,5},{8,10},{9,11},{10,... | collective-permute-start | bytes 1179656 | tf_op jit(solution)/shard_map/ppermute | solution.py:648
  6.9 1.3 %copy-start.2 = (bf16[768,768]{1,0:T(8,128)(2,1)S(1)}, bf16[768,768]{1,0:T(8,128)(2,1)}, u32[]{:S(2)}) copy-start(bf16[768,768]{1,0:T(8,128)(2,1)} %w_key.3) | copy-start | bytes 3538948
  8.2 6.7 %copy-start.3 = (bf16[256,2,96]{0,2,1:T(8,128)(2,1)S(1)}, bf16[256,2,96]{0,2,1:T(8,128)(2,1)}, u32[]{:S(2)}) copy-start(bf16[256,2,96]{0,2,1:T(8,128)(2,1)} %param.43) | copy-start | bytes 294916
  8.2 6.7 %copy-start.4 = (bf16[256,2,96]{0,2,1:T(8,128)(2,1)S(1)}, bf16[256,2,96]{0,2,1:T(8,128)(2,1)}, u32[]{:S(2)}) copy-start(bf16[256,2,96]{0,2,1:T(8,128)(2,1)} %param.23) | copy-start | bytes 294916
  8.2 8.6 %copy-start.5 = (bf16[96,384]{1,0:T(8,128)(2,1)S(1)}, bf16[96,384]{1,0:T(8,128)(2,1)}, u32[]{:S(2)}) copy-start(bf16[96,384]{1,0:T(8,128)(2,1)} %s_inner.2) | copy-start | bytes 221188
  8.2 8.6 %copy-start.7 = (bf16[96,96]{1,0:T(8,128)(2,1)S(1)}, bf16[96,96]{1,0:T(8,128)(2,1)}, u32[]{:S(2)}) copy-start(bf16[96,96]{1,0:T(8,128)(2,1)} %s_out.2) | copy-start | bytes 55300
  8.2 8.6 %copy-start.8 = (bf16[96,96]{1,0:T(8,128)(2,1)S(1)}, bf16[96,96]{1,0:T(8,128)(2,1)}, u32[]{:S(2)}) copy-start(bf16[96,96]{1,0:T(8,128)(2,1)} %s_query.2) | copy-start | bytes 55300
  8.2 8.6 %copy-start.9 = (bf16[96,96]{1,0:T(8,128)(2,1)S(1)}, bf16[96,96]{1,0:T(8,128)(2,1)}, u32[]{:S(2)}) copy-start(bf16[96,96]{1,0:T(8,128)(2,1)} %s_key.2) | copy-start | bytes 55300
  8.2 8.6 %copy-start.10 = (bf16[96,96]{1,0:T(8,128)(2,1)S(1)}, bf16[96,96]{1,0:T(8,128)(2,1)}, u32[]{:S(2)}) copy-start(bf16[96,96]{1,0:T(8,128)(2,1)} %s_value.2) | copy-start | bytes 55300
  8.2 8.6 %copy-start.14 = (f32[96]{0:T(128)S(1)}, f32[96]{0:T(128)}, u32[]{:S(2)}) copy-start(f32[96]{0:T(128)} %gate) | copy-start | bytes 1156
  8.2 8.6 %copy-start.15 = (f32[96]{0:T(128)S(1)}, f32[96]{0:T(128)}, u32[]{:S(2)}) copy-start(f32[96]{0:T(128)} %gain_in) | copy-start | bytes 1156
  8.2 8.5 %copy-start.16 = (f32[96]{0:T(128)S(1)}, f32[96]{0:T(128)}, u32[]{:S(2)}) copy-start(f32[96]{0:T(128)} %gain_mid) | copy-start | bytes 1156
  14.9 2.3 %collective-permute-start.3 = (bf16[256,768]{1,0:T(8,128)(2,1)S(1)}, bf16[256,768]{1,0:T(8,128)(2,1)S(1)}, u32[]{:S(2)}, u32[]{:S(2)}) collective-permute-start(bf16[256,768]{1,0:T(8,128)(2,1)S(1)} %collective-permute-done.far), channel_id=1, source_target_pairs={{0,1},{1,0},{2,3},{3,2},{4,5},{5,4},{6,7},{7,6},{8,9},{9,8},{10,11... | collective-permute-start | bytes 1179656 | tf_op jit(solution)/shard_map/ppermute | solution.py:648
  14.9 9.5 %collective-permute-start.2 = (bf16[192,256]{1,0:T(8,128)(2,1)S(1)}, bf16[192,256]{1,0:T(8,128)(2,1)S(1)}, u32[]{:S(2)}, u32[]{:S(2)}) collective-permute-start(bf16[192,256]{1,0:T(8,128)(2,1)S(1)} %fusion.3), channel_id=1, source_target_pairs={{0,2},{1,3},{2,0},{3,1},{4,6},{5,7},{6,4},{7,5},{8,10},{9,11},{10,... | collective-permute-start | bytes 294920 | tf_op jit(solution)/shard_map/ppermute | solution.py:648
  16.8 7.7 %slice-start = ((s8[4718592]{0:T(1024)(128)(4,1)}), s8[4194304]{0:T(1024)(128)(4,1)S(1)}, s32[]{:S(2)}) async-start(s8[4718592]{0:T(1024)(128)(4,1)} %bitcast.43), calls=%async_computation | async-start | bytes 8388608
  16.8 7.7 %slice-start.2 = ((s8[4718592]{0:T(1024)(128)(4,1)}), s8[4194304]{0:T(1024)(128)(4,1)S(1)}, s32[]{:S(2)}) async-start(s8[4718592]{0:T(1024)(128)(4,1)} %bitcast.45), calls=%async_computation.2 | async-start | bytes 8388608
  17.1 7.4 %slice-start.1 = ((s8[4718592]{0:T(1024)(128)(4,1)}), s8[524288]{0:T(1024)(128)(4,1)S(1)}, s32[]{:S(2)}) async-start(s8[4718592]{0:T(1024)(128)(4,1)} %bitcast.43), calls=%async_computation.1 | async-start | bytes 1048576
  17.1 7.4 %slice-start.3 = ((s8[4718592]{0:T(1024)(128)(4,1)}), s8[524288]{0:T(1024)(128)(4,1)S(1)}, s32[]{:S(2)}) async-start(s8[4718592]{0:T(1024)(128)(4,1)} %bitcast.45), calls=%async_computation.3 | async-start | bytes 1048576
  17.2 7.4 %copy-start.17 = (bf16[768,768]{1,0:T(8,128)(2,1)S(1)}, bf16[768,768]{1,0:T(8,128)(2,1)}, u32[]{:S(2)}) copy-start(bf16[768,768]{1,0:T(8,128)(2,1)} %w_out.1) | copy-start | bytes 3538948
  17.2 7.4 %copy-start.18 = (bf16[768,96]{0,1:T(8,128)(2,1)S(1)}, bf16[768,96]{0,1:T(8,128)(2,1)}, u32[]{:S(2)}) copy-start(bf16[768,96]{0,1:T(8,128)(2,1)} %param.33) | copy-start | bytes 442372
  24.6 8.0 %copy-start.6 = (bf16[384,96]{0,1:T(8,128)(2,1)S(1)}, bf16[384,96]{0,1:T(8,128)(2,1)}, u32[]{:S(2)}) copy-start(bf16[384,96]{0,1:T(8,128)(2,1)} %param.42) | copy-start | bytes 221188
  31.1 1.4 %collective-permute-start.4 = (bf16[512,96]{1,0:T(8,128)(2,1)S(1)}, bf16[512,96]{1,0:T(8,128)(2,1)S(1)}, u32[]{:S(2)}, u32[]{:S(2)}) collective-permute-start(bf16[512,96]{1,0:T(8,128)(2,1)S(1)} %get-tuple-element.108.sn_own), channel_id=1, source_target_pairs={{0,1},{1,0},{2,3},{3,2},{4,5},{5,4},{6,7},{7,6},{8,9},{9,8},{10,11... | collective-permute-start | bytes 294920 | tf_op jit(solution)/shard_map/ppermute | solution.py:648
  31.4 12.7 %collective-permute-start.6 = (bf16[256,768]{1,0:T(8,128)(2,1)S(1)}, bf16[256,768]{1,0:T(8,128)(2,1)S(1)}, u32[]{:S(2)}, u32[]{:S(2)}) collective-permute-start(bf16[256,768]{1,0:T(8,128)(2,1)S(1)} %get-tuple-element.117.out_far), channel_id=1, source_target_pairs={{0,2},{1,3},{2,0},{3,1},{4,6},{5,7},{6,4},{7,5},{8,10},{9,11},{10,... | collective-permute-start | bytes 1179656 | tf_op jit(solution)/shard_map/ppermute | solution.py:648
  42.7 1.5 %collective-permute-start.5 = (bf16[192,512]{1,0:T(8,128)(2,1)S(1)}, bf16[192,512]{1,0:T(8,128)(2,1)S(1)}, u32[]{:S(2)}, u32[]{:S(2)}) collective-permute-start(bf16[192,512]{1,0:T(8,128)(2,1)S(1)} %get-tuple-element.116), channel_id=1, source_target_pairs={{0,1},{1,0},{2,3},{3,2},{4,5},{5,4},{6,7},{7,6},{8,9},{9,8},{10,11... | collective-permute-start | bytes 589832 | tf_op jit(solution)/shard_map/ppermute | solution.py:648
  44.9 1.5 %collective-permute-start.7 = (bf16[96,1024]{1,0:T(8,128)(2,1)S(1)}, bf16[96,1024]{1,0:T(8,128)(2,1)S(1)}, u32[]{:S(2)}, u32[]{:S(2)}) collective-permute-start(bf16[96,1024]{1,0:T(8,128)(2,1)S(1)} %get-tuple-element.138), channel_id=1, source_target_pairs={{0,1},{1,0},{2,3},{3,2},{4,5},{5,4},{6,7},{7,6},{8,9},{9,8},{10,11... | collective-permute-start | bytes 589832 | tf_op jit(solution)/shard_map/ppermute | solution.py:648
  46.5 5.5 %collective-permute-start.10 = (bf16[96,256]{1,0:T(8,128)(2,1)S(1)}, bf16[96,256]{1,0:T(8,128)(2,1)S(1)}, u32[]{:S(2)}, u32[]{:S(2)}) collective-permute-start(bf16[96,256]{1,0:T(8,128)(2,1)S(1)} %get-tuple-element.186), channel_id=1, source_target_pairs={{0,6},{1,7},{2,4},{3,5},{4,2},{5,3},{6,0},{7,1},{8,14},{9,15},{10,... | collective-permute-start | bytes 147464 | tf_op jit(solution)/shard_map/ppermute | solution.py:861
  48.6 4.1 %collective-permute-start.8 = (bf16[96,256]{1,0:T(8,128)(2,1)S(1)}, bf16[96,256]{1,0:T(8,128)(2,1)S(1)}, u32[]{:S(2)}, u32[]{:S(2)}) collective-permute-start(bf16[96,256]{1,0:T(8,128)(2,1)S(1)} %get-tuple-element.185), channel_id=1, source_target_pairs={{0,2},{1,3},{2,0},{3,1},{4,6},{5,7},{6,4},{7,5},{8,10},{9,11},{10,... | collective-permute-start | bytes 147464 | tf_op jit(solution)/shard_map/ppermute | solution.py:861
  49.5 4.1 %collective-permute-start.9 = (bf16[96,256]{1,0:T(8,128)(2,1)S(1)}, bf16[96,256]{1,0:T(8,128)(2,1)S(1)}, u32[]{:S(2)}, u32[]{:S(2)}) collective-permute-start(bf16[96,256]{1,0:T(8,128)(2,1)S(1)} %get-tuple-element.187), channel_id=1, source_target_pairs={{0,4},{1,5},{2,6},{3,7},{4,0},{5,1},{6,2},{7,3},{8,12},{9,13},{10,... | collective-permute-start | bytes 147464 | tf_op jit(solution)/shard_map/ppermute | solution.py:861
  53.6 4.2 %collective-permute-start.12 = (bf16[96,256]{1,0:T(8,128)(2,1)S(1)}, bf16[96,256]{1,0:T(8,128)(2,1)S(1)}, u32[]{:S(2)}, u32[]{:S(2)}) collective-permute-start(bf16[96,256]{1,0:T(8,128)(2,1)S(1)} %add_convert_fusion.3), channel_id=1, source_target_pairs={{0,8},{4,12},{8,0},{12,4},{16,24},{20,28},{24,16},{28,20},{1,9},{5... | collective-permute-start | bytes 147464 | tf_op jit(solution)/shard_map/ppermute | solution.py:648
  57.8 5.6 %collective-permute-start.13 = (bf16[96,256]{1,0:T(8,128)(2,1)S(1)}, bf16[96,256]{1,0:T(8,128)(2,1)S(1)}, u32[]{:S(2)}, u32[]{:S(2)}) collective-permute-start(bf16[96,256]{1,0:T(8,128)(2,1)S(1)} %add_convert_fusion.2), channel_id=1, source_target_pairs={{0,16},{4,20},{8,24},{12,28},{16,0},{20,4},{24,8},{28,12},{1,17},{... | collective-permute-start | bytes 147464 | tf_op jit(solution)/shard_map/ppermute | solution.py:648
  62.2 4.7 %collective-permute-start.11 = (bf16[192,256]{1,0:T(8,128)(2,1)S(1)}, bf16[192,256]{1,0:T(8,128)(2,1)S(1)}, u32[]{:S(2)}, u32[]{:S(2)}) collective-permute-start(bf16[192,256]{1,0:T(8,128)(2,1)S(1)} %get-tuple-element.140), channel_id=1, source_target_pairs={{0,2},{1,3},{2,0},{3,1},{4,6},{5,7},{6,4},{7,5},{8,10},{9,11},{10,... | collective-permute-start | bytes 294920 | tf_op jit(solution)/shard_map/ppermute | solution.py:648
  63.4 4.3 %collective-permute-start.14 = (bf16[96,256]{1,0:T(8,128)(2,1)S(1)}, bf16[96,256]{1,0:T(8,128)(2,1)S(1)}, u32[]{:S(2)}, u32[]{:S(2)}) collective-permute-start(bf16[96,256]{1,0:T(8,128)(2,1)S(1)} %add_convert_fusion.1.refs_0_), channel_id=1, source_target_pairs={{0,2},{1,3},{2,0},{3,1},{4,6},{5,7},{6,4},{7,5},{8,10},{9,11},{10,... | collective-permute-start | bytes 147464 | tf_op jit(solution)/shard_map/ppermute | solution.py:861
  64.3 4.1 %collective-permute-start.15 = (bf16[96,256]{1,0:T(8,128)(2,1)S(1)}, bf16[96,256]{1,0:T(8,128)(2,1)S(1)}, u32[]{:S(2)}, u32[]{:S(2)}) collective-permute-start(bf16[96,256]{1,0:T(8,128)(2,1)S(1)} %add_convert_fusion.1.refs_0_), channel_id=1, source_target_pairs={{0,4},{1,5},{2,6},{3,7},{4,0},{5,1},{6,2},{7,3},{8,12},{9,13},{10,... | collective-permute-start | bytes 147464 | tf_op jit(solution)/shard_map/ppermute | solution.py:861
  64.8 5.0 %collective-permute-start.16 = (bf16[96,256]{1,0:T(8,128)(2,1)S(1)}, bf16[96,256]{1,0:T(8,128)(2,1)S(1)}, u32[]{:S(2)}, u32[]{:S(2)}) collective-permute-start(bf16[96,256]{1,0:T(8,128)(2,1)S(1)} %add_convert_fusion.1.refs_0_), channel_id=1, source_target_pairs={{0,6},{1,7},{2,4},{3,5},{4,2},{5,3},{6,0},{7,1},{8,14},{9,15},{10,... | collective-permute-start | bytes 147464 | tf_op jit(solution)/shard_map/ppermute | solution.py:861
  67.0 3.5 %collective-permute-start.17 = (bf16[96,256]{1,0:T(8,128)(2,1)S(1)}, bf16[96,256]{1,0:T(8,128)(2,1)S(1)}, u32[]{:S(2)}, u32[]{:S(2)}) collective-permute-start(bf16[96,256]{1,0:T(8,128)(2,1)S(1)} %add_convert_fusion.1.refs_0_), channel_id=1, source_target_pairs={{0,1},{1,0},{2,3},{3,2},{4,5},{5,4},{6,7},{7,6},{8,9},{9,8},{10,11... | collective-permute-start | bytes 147464 | tf_op jit(solution)/shard_map/ppermute | solution.py:648
  67.7 2.8 %collective-permute-start.18 = (bf16[96,256]{1,0:T(8,128)(2,1)S(1)}, bf16[96,256]{1,0:T(8,128)(2,1)S(1)}, u32[]{:S(2)}, u32[]{:S(2)}) collective-permute-start(bf16[96,256]{1,0:T(8,128)(2,1)S(1)} %collective-permute-done.14.refs_1_), channel_id=1, source_target_pairs={{0,1},{1,0},{2,3},{3,2},{4,5},{5,4},{6,7},{7,6},{8,9},{9,8},{10,11... | collective-permute-start | bytes 147464 | tf_op jit(solution)/shard_map/ppermute | solution.py:648
  68.4 2.1 %collective-permute-start.19 = (bf16[96,256]{1,0:T(8,128)(2,1)S(1)}, bf16[96,256]{1,0:T(8,128)(2,1)S(1)}, u32[]{:S(2)}, u32[]{:S(2)}) collective-permute-start(bf16[96,256]{1,0:T(8,128)(2,1)S(1)} %collective-permute-done.15.refs_2_), channel_id=1, source_target_pairs={{0,1},{1,0},{2,3},{3,2},{4,5},{5,4},{6,7},{7,6},{8,9},{9,8},{10,11... | collective-permute-start | bytes 147464 | tf_op jit(solution)/shard_map/ppermute | solution.py:648
  69.8 1.2 %collective-permute-start.20 = (bf16[96,256]{1,0:T(8,128)(2,1)S(1)}, bf16[96,256]{1,0:T(8,128)(2,1)S(1)}, u32[]{:S(2)}, u32[]{:S(2)}) collective-permute-start(bf16[96,256]{1,0:T(8,128)(2,1)S(1)} %collective-permute-done.16.refs_3_), channel_id=1, source_target_pairs={{0,1},{1,0},{2,3},{3,2},{4,5},{5,4},{6,7},{7,6},{8,9},{9,8},{10,11... | collective-permute-start | bytes 147464 | tf_op jit(solution)/shard_map/ppermute | solution.py:648

commit v9 on v8

--- a/solution.py
+++ b/solution.py
@@ -147,9 +147,9 @@
     side_query_doc[...] = (in_doc(doc_lengths, row, (own, far), span, (16, tokens), 1) * FAR).astype(bf16)
 
 
-def project(tokens, gain, w_query, w_key, value_t, scale, queries):
+def project(tokens, gain, w_query, w_key, value_t, queries):
     normed = norm_lanes(tokens.astype(f32), gain).astype(bf16)
-    query = (nn(normed[0:queries], w_query[...]) * scale).astype(bf16)
+    query = nn(normed[0:queries], w_query[...]).astype(bf16)
     return query, nn(normed, w_key[...]).astype(bf16), nt(value_t[...], normed).astype(bf16)
 
 
@@ -179,7 +179,7 @@
     masked = [jnp.concatenate([query * ones_where(lane == i), query_doc], axis=1) for i in range(2)]
     count = query.shape[0]
 
-    scores = nt(key, jnp.concatenate(masked, axis=0))
+    scores = nt(key, jnp.concatenate(masked, axis=0)) * (LOG2E * head**-0.5)
     if shifted:
         scores = scores - jnp.max(scores, axis=0, keepdims=True)
     both = nn(value, jnp.exp2(scores).astype(bf16))
@@ -192,7 +192,7 @@
     row = lax.axis_index("blk") // (lax.axis_size("blk") // 2)
     tokens = jnp.concatenate([own[row], mate[row]], axis=0)
     query[...], key[...], value_new = project(
-        tokens, gains[0:1], w_query, w_key, value_t, LOG2E * head**-0.5, span
+        tokens, gains[0:1], w_query, w_key, value_t, span
     )
     value[...] = padded(value_new, head)
 
@@ -232,7 +232,7 @@
     head = width // HEADS
     tokens = jnp.concatenate([far[...], far_mate[...]], axis=0)
     query[...], key[...], value_new = project(
-        tokens, gains[0:1], w_query, w_key, value_t, LOG2E * head**-0.5, span
+        tokens, gains[0:1], w_query, w_key, value_t, span
     )
     value[...] = padded(value_new, head)
     keys, values, queries = [key_a, key], [value_a, value], [query_a, query]

time: 72.2 us -> 72.2 us (level)
  no operation moved by 1% of the time
where the time goes in v9:
time: 72.2 us; the launch traced here: 72 us
  Pallas kernels  33.5 us (46%)
  starting transfers between devices  19.9 us (28%)
  waiting for transfers between devices  11.5 us (16%)
  local copies, waits for them, and re-layouts  4.44 us (6%)
  other arithmetic  1.63 us (2%)
  between operations  1.08 us (1%)
    pallas_call x9, Pallas kernels, kernel_call(): pl.pallas_call(body, out_shape=[jax.ShapeDtypeStruct(shape, kind) for sha...  33.5 us
    ppermute x15, starting transfers between devices, swap(): return lax.ppermute(value, axis, [(i, i ^ hop) for i in range(size)])  12.8 us
    ppermute x6, starting transfers between devices, between(): lax.ppermute(value, ('dp', 'blk'), [(i, i ^ mask) for i in range(devices)])  7.11 us
    ppermute x15, waiting for transfers between devices, swap(): return lax.ppermute(value, axis, [(i, i ^ hop) for i in range(size)])  6.25 us
    ppermute x6, waiting for transfers between devices, between(): lax.ppermute(value, ('dp', 'blk'), [(i, i ^ mask) for i in range(devices)])  5.21 us
    unnamed x48, local copies, waits for them, and re-layouts  4.39 us
  transfers between devices with their start and end apart: 21, of which 10 were waited for; matrix products, arithmetic and copies ran while one was open for 5% of the time, Pallas kernels for 35%

profile of v9, /device:TPU:0, one launch (start us, length us, event | category | flops | bytes accessed | tf_op | source)
XLA Modules:
  0.0 72.0 jit_solution(6223914685468678933)
XLA Ops:
  0.7 1.3 %copy.42 = bf16[256,2,768]{2,0,1:T(8,128)(2,1)S(1)} copy(bf16[256,2,768]{2,1,0:T(2,128)(2,1)} %param.22) | data formatting | bytes 1572864 | tf_op args[0]
  2.0 0.5 collective-permute-start.1
  2.6 2.6 %collective-permute-start = (bf16[256,768]{1,0:T(8,128)(2,1)S(1)}, bf16[256,768]{1,0:T(8,128)(2,1)S(1)}, u32[]{:S(2)}, u32[]{:S(2)}) collective-permute-start(bf16[256,768]{1,0:T(8,128)(2,1)S(1)} %dynamic-slice_bitcast_fusion), channel_id=1, source_target_pairs={{0,2},{1,3},{2,0},{3,1},{4,6},{5,7},{6,4},{7,5},{8,10},{9,11},{10,... | collective-permute-start | bytes 1179656 | tf_op jit(solution)/shard_map/ppermute | solution.py:648
  5.2 1.7 %shard_map.309 = (bf16[768,768]{1,0:T(8,128)(2,1)S(1)}, f32[2,768]{1,0:T(2,128)S(1)}, bf16[1024,128]{1,0:T(8,128)(2,1)S(1)}, bf16[512,128]{1,0:T(8,128)(2,1)S(1)...) custom-call(s32[2,8]{1,0:T(2,128)S(1)} %copy-done.13, bf16[768,768]{1,0:T(8,128)(2,1)S(1)} %copy-done, ...), custom_call_target="tpu_custom_call" | custom-call | flops 1000 | bytes 1000 | tf_op jit(solution)/shard_map/pallas_call | solution.py:65
  6.9 1.3 %copy-done.2 = bf16[768,768]{1,0:T(8,128)(2,1)S(1)} copy-done((bf16[768,768]{1,0:T(8,128)(2,1)S(1)}, bf16[768,768]{1,0:T(8,128)(2,1)}, u32[]{:S(2)}) %copy-start.2) | copy-done | bytes 1179672
  8.2 5.3 %shard_map.310 = (bf16[256,768]{1,0:T(8,128)(2,1)S(1)}, bf16[512,768]{1,0:T(8,128)(2,1)S(1)}, bf16[960,512]{1,0:T(8,128)(2,1)S(1)}, f32[6,144,256]{2,1,0:T(8,128)S(1)}) custom-call(bf16[2,256,768]{2,1,0:T(8,128)(2,1)S(1)} %bitcast.34, bf16[2,256,768]{2,1,0:T(8,128)(2,1)} %collective-permute-done.1.mate, f32[2,768]{1,0:T(2,128)S(1)} %get-tuple-element.83.gains, ...), custom_call_target="tpu_custom_call" | custom-call | flops 1000 | bytes 1000 | tf_op jit(solution)/shard_map/pallas_call | solution.py:65
  13.6 1.3 %collective-permute-done.far = bf16[256,768]{1,0:T(8,128)(2,1)S(1)} collective-permute-done((bf16[256,768]{1,0:T(8,128)(2,1)S(1)}, bf16[256,768]{1,0:T(8,128)(2,1)S(1)}, u32[]{:S(2)}, u32[]{:S(2)}) %collective-permute-start) | collective-permute-done | bytes 393248 | tf_op jit(solution)/shard_map/ppermute | solution.py:648
  14.9 1.8 %collective-permute-start.2 = (bf16[192,256]{1,0:T(8,128)(2,1)S(1)}, bf16[192,256]{1,0:T(8,128)(2,1)S(1)}, u32[]{:S(2)}, u32[]{:S(2)}) collective-permute-start(bf16[192,256]{1,0:T(8,128)(2,1)S(1)} %fusion.3), channel_id=1, source_target_pairs={{0,2},{1,3},{2,0},{3,1},{4,6},{5,7},{6,4},{7,5},{8,10},{9,11},{10,... | collective-permute-start | bytes 294920 | tf_op jit(solution)/shard_map/ppermute | solution.py:648
  16.8 0.0 slice-start
  16.8 0.0 slice-start.2
  16.8 0.3 shard_map.312
  17.1 0.0 slice-start.1
  17.1 0.0 slice-start.3
  17.2 7.3 %shard_map.311.attended = bf16[512,768]{1,0:T(8,128)(2,1)S(1)} custom-call(bf16[256,768]{1,0:T(8,128)(2,1)S(1)} %collective-permute-done.far, bf16[256,768]{1,0:T(8,128)(2,1)S(1)} %collective-permute-done.3.far_mate, f32[2,768]{1,0:T(2,128)S(1)} %get-tuple-element.83.gains, bf16[768,768]{1,0:T(8,128)(2,1)S(1)} %copy-done.1, bf16[768,768]{1,0:T(8,128)(2,1)S(1)} %copy-done.2, ...), custom_call_target="tpu_custom_call" | custom-call | flops 8000000000 | bytes 8000000 | tf_op jit(solution)/shard_map/pallas_call | solution.py:65
  24.6 6.6 %shard_map.313 = (bf16[256,768]{1,0:T(8,128)(2,1)S(1)}, bf16[256,768]{1,0:T(8,128)(2,1)S(1)}, bf16[512,96]{1,0:T(8,128)(2,1)S(1)}, bf16[96,512]{1,0:T(8,128)(2,1...) custom-call(bf16[2,256,768]{2,1,0:T(8,128)(2,1)S(1)} %bitcast.35, bf16[256,768]{1,0:T(8,128)(2,1)S(1)} %collective-permute-done.far, ...), custom_call_target="tpu_custom_call" | custom-call | flops 10000000000 | bytes 14000000 | tf_op jit(solution)/shard_map/pallas_call | solution.py:65
  31.1 0.3 collective-permute-start.4
  31.4 1.1 %collective-permute-start.6 = (bf16[256,768]{1,0:T(8,128)(2,1)S(1)}, bf16[256,768]{1,0:T(8,128)(2,1)S(1)}, u32[]{:S(2)}, u32[]{:S(2)}) collective-permute-start(bf16[256,768]{1,0:T(8,128)(2,1)S(1)} %get-tuple-element.117.out_far), channel_id=1, source_target_pairs={{0,2},{1,3},{2,0},{3,1},{4,6},{5,7},{6,4},{7,5},{8,10},{9,11},{10,... | collective-permute-start | bytes 1179656 | tf_op jit(solution)/shard_map/ppermute | solution.py:648
  32.5 0.0 collective-permute-done.4.sn_mate
  32.5 10.1 %shard_map.314 = (f32[192,512]{1,0:T(8,128)S(1)}, bf16[192,512]{1,0:T(8,128)(2,1)S(1)}, f32[96,512]{1,0:T(8,128)S(1)}, f32[96,512]{1,0:T(8,128)S(1)}, f32[96,512...) custom-call(bf16[512,96]{1,0:T(8,128)(2,1)S(1)} %get-tuple-element.1, ...), custom_call_target="tpu_custom_call" | custom-call | flops 30000001024 | bytes 3000000 | tf_op jit(solution)/shard_map/pallas_call | solution.py:65
  42.6 0.3 collective-permute-start.5
  42.9 0.6 shard_map.315
  43.6 0.6 collective-permute-done.5.dkv_back
  44.2 0.7 shard_map.316
  44.8 0.3 collective-permute-start.7
  45.1 1.2 %collective-permute-done.7 = bf16[96,1024]{1,0:T(8,128)(2,1)S(1)} collective-permute-done((bf16[96,1024]{1,0:T(8,128)(2,1)S(1)}, bf16[96,1024]{1,0:T(8,128)(2,1)S(1)}, u32[]{:S(2)}, u32[]{:S(2)}) %collective-permute-start.7) | collective-permute-done | bytes 196640 | tf_op jit(solution)/shard_map/ppermute | solution.py:648
  46.5 2.2 %collective-permute-start.10 = (bf16[96,256]{1,0:T(8,128)(2,1)S(1)}, bf16[96,256]{1,0:T(8,128)(2,1)S(1)}, u32[]{:S(2)}, u32[]{:S(2)}) collective-permute-start(bf16[96,256]{1,0:T(8,128)(2,1)S(1)} %get-tuple-element.186), channel_id=1, source_target_pairs={{0,6},{1,7},{2,4},{3,5},{4,2},{5,3},{6,0},{7,1},{8,14},{9,15},{10,... | collective-permute-start | bytes 147464 | tf_op jit(solution)/shard_map/ppermute | solution.py:861
  48.6 0.9 %collective-permute-start.8 = (bf16[96,256]{1,0:T(8,128)(2,1)S(1)}, bf16[96,256]{1,0:T(8,128)(2,1)S(1)}, u32[]{:S(2)}, u32[]{:S(2)}) collective-permute-start(bf16[96,256]{1,0:T(8,128)(2,1)S(1)} %get-tuple-element.185), channel_id=1, source_target_pairs={{0,2},{1,3},{2,0},{3,1},{4,6},{5,7},{6,4},{7,5},{8,10},{9,11},{10,... | collective-permute-start | bytes 147464 | tf_op jit(solution)/shard_map/ppermute | solution.py:861
  49.5 0.5 collective-permute-start.9
  50.0 2.0 %collective-permute-done.10 = bf16[96,256]{1,0:T(8,128)(2,1)S(1)} collective-permute-done((bf16[96,256]{1,0:T(8,128)(2,1)S(1)}, bf16[96,256]{1,0:T(8,128)(2,1)S(1)}, u32[]{:S(2)}, u32[]{:S(2)}) %collective-permute-start.10) | collective-permute-done | bytes 49184 | tf_op jit(solution)/shard_map/ppermute | solution.py:861
  52.0 0.7 %collective-permute-done.8 = bf16[96,256]{1,0:T(8,128)(2,1)S(1)} collective-permute-done((bf16[96,256]{1,0:T(8,128)(2,1)S(1)}, bf16[96,256]{1,0:T(8,128)(2,1)S(1)}, u32[]{:S(2)}, u32[]{:S(2)}) %collective-permute-start.8) | collective-permute-done | bytes 49184 | tf_op jit(solution)/shard_map/ppermute | solution.py:861
  52.7 0.9 %collective-permute-done.9 = bf16[96,256]{1,0:T(8,128)(2,1)S(1)} collective-permute-done((bf16[96,256]{1,0:T(8,128)(2,1)S(1)}, bf16[96,256]{1,0:T(8,128)(2,1)S(1)}, u32[]{:S(2)}, u32[]{:S(2)}) %collective-permute-start.9) | collective-permute-done | bytes 49184 | tf_op jit(solution)/shard_map/ppermute | solution.py:861
  53.6 1.6 %collective-permute-start.12 = (bf16[96,256]{1,0:T(8,128)(2,1)S(1)}, bf16[96,256]{1,0:T(8,128)(2,1)S(1)}, u32[]{:S(2)}, u32[]{:S(2)}) collective-permute-start(bf16[96,256]{1,0:T(8,128)(2,1)S(1)} %add_convert_fusion.3), channel_id=1, source_target_pairs={{0,8},{4,12},{8,0},{12,4},{16,24},{20,28},{24,16},{28,20},{1,9},{5... | collective-permute-start | bytes 147464 | tf_op jit(solution)/shard_map/ppermute | solution.py:648
  55.3 0.1 select_bitcast_fusion.1
  55.3 2.5 %collective-permute-done.12 = bf16[96,256]{1,0:T(8,128)(2,1)S(1)} collective-permute-done((bf16[96,256]{1,0:T(8,128)(2,1)S(1)}, bf16[96,256]{1,0:T(8,128)(2,1)S(1)}, u32[]{:S(2)}, u32[]{:S(2)}) %collective-permute-start.12) | collective-permute-done | bytes 49184 | tf_op jit(solution)/shard_map/ppermute | solution.py:648
  57.8 2.6 %collective-permute-start.13 = (bf16[96,256]{1,0:T(8,128)(2,1)S(1)}, bf16[96,256]{1,0:T(8,128)(2,1)S(1)}, u32[]{:S(2)}, u32[]{:S(2)}) collective-permute-start(bf16[96,256]{1,0:T(8,128)(2,1)S(1)} %add_convert_fusion.2), channel_id=1, source_target_pairs={{0,16},{4,20},{8,24},{12,28},{16,0},{20,4},{24,8},{28,12},{1,17},{... | collective-permute-start | bytes 147464 | tf_op jit(solution)/shard_map/ppermute | solution.py:648
  60.5 0.1 maximum_bitcast_fusion
  60.5 1.7 %copy.39 = bf16[256,2,768]{2,1,0:T(2,128)(2,1)} copy(bf16[256,2,768]{2,0,1:T(8,128)(2,1)S(1)} %maximum_bitcast_fusion) | data formatting | bytes 1572864
  62.2 1.2 %collective-permute-start.11 = (bf16[192,256]{1,0:T(8,128)(2,1)S(1)}, bf16[192,256]{1,0:T(8,128)(2,1)S(1)}, u32[]{:S(2)}, u32[]{:S(2)}) collective-permute-start(bf16[192,256]{1,0:T(8,128)(2,1)S(1)} %get-tuple-element.140), channel_id=1, source_target_pairs={{0,2},{1,3},{2,0},{3,1},{4,6},{5,7},{6,4},{7,5},{8,10},{9,11},{10,... | collective-permute-start | bytes 294920 | tf_op jit(solution)/shard_map/ppermute | solution.py:648
  63.4 0.9 %collective-permute-start.14 = (bf16[96,256]{1,0:T(8,128)(2,1)S(1)}, bf16[96,256]{1,0:T(8,128)(2,1)S(1)}, u32[]{:S(2)}, u32[]{:S(2)}) collective-permute-start(bf16[96,256]{1,0:T(8,128)(2,1)S(1)} %add_convert_fusion.1.refs_0_), channel_id=1, source_target_pairs={{0,2},{1,3},{2,0},{3,1},{4,6},{5,7},{6,4},{7,5},{8,10},{9,11},{10,... | collective-permute-start | bytes 147464 | tf_op jit(solution)/shard_map/ppermute | solution.py:861
  64.3 0.5 collective-permute-start.15
  64.8 2.1 %collective-permute-start.16 = (bf16[96,256]{1,0:T(8,128)(2,1)S(1)}, bf16[96,256]{1,0:T(8,128)(2,1)S(1)}, u32[]{:S(2)}, u32[]{:S(2)}) collective-permute-start(bf16[96,256]{1,0:T(8,128)(2,1)S(1)} %add_convert_fusion.1.refs_0_), channel_id=1, source_target_pairs={{0,6},{1,7},{2,4},{3,5},{4,2},{5,3},{6,0},{7,1},{8,14},{9,15},{10,... | collective-permute-start | bytes 147464 | tf_op jit(solution)/shard_map/ppermute | solution.py:861
  67.0 0.7 maximum_bitcast_fusion.1
  67.7 0.5 collective-permute-start.18
  68.2 0.2 collective-permute-done.15.refs_2_
  68.4 1.4 %collective-permute-done.16.refs_3_ = bf16[96,256]{1,0:T(8,128)(2,1)S(1)} collective-permute-done((bf16[96,256]{1,0:T(8,128)(2,1)S(1)}, bf16[96,256]{1,0:T(8,128)(2,1)S(1)}, u32[]{:S(2)}, u32[]{:S(2)}) %collective-permute-start.16) | collective-permute-done | bytes 49184 | tf_op jit(solution)/shard_map/ppermute | solution.py:861
  69.8 0.7 maximum_bitcast_fusion.2
  70.5 0.6 collective-permute-done.20.refs_7_
  71.1 1.0 %shard_map.317 = (f32[96,768]{1,0:T(8,128)}, f32[1,96]{1,0:T(1,128)}, f32[1,96]{1,0:T(1,128)}, f32[96,96]{1,0:T(8,128)}, f32[96,96]{1,0:T(8,128)}, /*index=5*/f3...) custom-call(bf16[96,256]{1,0:T(8,128)(2,1)S(1)} %add_convert_fusion.1.refs_0_, ...), custom_call_target="tpu_custom_call" | custom-call | bytes 2000000 | tf_op jit(solution)/shard_map/pallas_call | solution.py:65
  (66 shorter events, 0.4 us)
Async XLA Ops:
  0.6 4.5 %copy-start.13 = (s32[2,8]{1,0:T(2,128)S(1)}, s32[2,8]{1,0:T(2,128)}, u32[]{:S(2)}) copy-start(s32[2,8]{1,0:T(2,128)} %doc_lengths.1) | copy-start | bytes 196
  0.7 4.5 %copy-start.11 = (bf16[768]{0:T(1024)(128)(2,1)S(1)}, bf16[768]{0:T(1024)(128)(2,1)}, u32[]{:S(2)}) copy-start(bf16[768]{0:T(1024)(128)(2,1)} %norm_in.1) | copy-start | bytes 4612
  0.7 4.5 %copy-start = (bf16[768,768]{1,0:T(8,128)(2,1)S(1)}, bf16[768,768]{1,0:T(8,128)(2,1)}, u32[]{:S(2)}) copy-start(bf16[768,768]{1,0:T(8,128)(2,1)} %w_value.1) | copy-start | bytes 3538948
  0.7 4.5 %copy-start.12 = (bf16[768]{0:T(1024)(128)(2,1)S(1)}, bf16[768]{0:T(1024)(128)(2,1)}, u32[]{:S(2)}) copy-start(bf16[768]{0:T(1024)(128)(2,1)} %norm_mid.1) | copy-start | bytes 4612
  2.0 4.9 %copy-start.1 = (bf16[768,768]{1,0:T(8,128)(2,1)S(1)}, bf16[768,768]{1,0:T(8,128)(2,1)}, u32[]{:S(2)}) copy-start(bf16[768,768]{1,0:T(8,128)(2,1)} %w_query.3) | copy-start | bytes 3538948
  2.0 4.9 %collective-permute-start.1 = (bf16[2,256,768]{2,1,0:T(8,128)(2,1)S(1)}, bf16[2,256,768]{2,1,0:T(8,128)(2,1)}, u32[]{:S(2)}, u32[]{:S(2)}) collective-permute-start(bf16[2,256,768]{2,1,0:T(8,128)(2,1)S(1)} %bitcast.33), channel_id=1, source_target_pairs={{0,1},{1,0},{2,3},{3,2},{4,5},{5,4},{6,7},{7,6},{8,9},{9,8},{10,11... | collective-permute-start | bytes 2359304 | tf_op jit(solution)/shard_map/ppermute | solution.py:648
  2.6 12.3 %collective-permute-start = (bf16[256,768]{1,0:T(8,128)(2,1)S(1)}, bf16[256,768]{1,0:T(8,128)(2,1)S(1)}, u32[]{:S(2)}, u32[]{:S(2)}) collective-permute-start(bf16[256,768]{1,0:T(8,128)(2,1)S(1)} %dynamic-slice_bitcast_fusion), channel_id=1, source_target_pairs={{0,2},{1,3},{2,0},{3,1},{4,6},{5,7},{6,4},{7,5},{8,10},{9,11},{10,... | collective-permute-start | bytes 1179656 | tf_op jit(solution)/shard_map/ppermute | solution.py:648
  6.9 1.3 %copy-start.2 = (bf16[768,768]{1,0:T(8,128)(2,1)S(1)}, bf16[768,768]{1,0:T(8,128)(2,1)}, u32[]{:S(2)}) copy-start(bf16[768,768]{1,0:T(8,128)(2,1)} %w_key.3) | copy-start | bytes 3538948
  8.2 6.7 %copy-start.3 = (bf16[256,2,96]{0,2,1:T(8,128)(2,1)S(1)}, bf16[256,2,96]{0,2,1:T(8,128)(2,1)}, u32[]{:S(2)}) copy-start(bf16[256,2,96]{0,2,1:T(8,128)(2,1)} %param.43) | copy-start | bytes 294916
  8.2 6.7 %copy-start.4 = (bf16[256,2,96]{0,2,1:T(8,128)(2,1)S(1)}, bf16[256,2,96]{0,2,1:T(8,128)(2,1)}, u32[]{:S(2)}) copy-start(bf16[256,2,96]{0,2,1:T(8,128)(2,1)} %param.23) | copy-start | bytes 294916
  8.2 8.6 %copy-start.5 = (bf16[96,384]{1,0:T(8,128)(2,1)S(1)}, bf16[96,384]{1,0:T(8,128)(2,1)}, u32[]{:S(2)}) copy-start(bf16[96,384]{1,0:T(8,128)(2,1)} %s_inner.2) | copy-start | bytes 221188
  8.2 8.6 %copy-start.7 = (bf16[96,96]{1,0:T(8,128)(2,1)S(1)}, bf16[96,96]{1,0:T(8,128)(2,1)}, u32[]{:S(2)}) copy-start(bf16[96,96]{1,0:T(8,128)(2,1)} %s_out.2) | copy-start | bytes 55300
  8.2 8.6 %copy-start.8 = (bf16[96,96]{1,0:T(8,128)(2,1)S(1)}, bf16[96,96]{1,0:T(8,128)(2,1)}, u32[]{:S(2)}) copy-start(bf16[96,96]{1,0:T(8,128)(2,1)} %s_query.2) | copy-start | bytes 55300
  8.2 8.6 %copy-start.9 = (bf16[96,96]{1,0:T(8,128)(2,1)S(1)}, bf16[96,96]{1,0:T(8,128)(2,1)}, u32[]{:S(2)}) copy-start(bf16[96,96]{1,0:T(8,128)(2,1)} %s_key.2) | copy-start | bytes 55300
  8.2 8.6 %copy-start.10 = (bf16[96,96]{1,0:T(8,128)(2,1)S(1)}, bf16[96,96]{1,0:T(8,128)(2,1)}, u32[]{:S(2)}) copy-start(bf16[96,96]{1,0:T(8,128)(2,1)} %s_value.2) | copy-start | bytes 55300
  8.2 8.6 %copy-start.14 = (f32[96]{0:T(128)S(1)}, f32[96]{0:T(128)}, u32[]{:S(2)}) copy-start(f32[96]{0:T(128)} %gate) | copy-start | bytes 1156
  8.2 8.6 %copy-start.15 = (f32[96]{0:T(128)S(1)}, f32[96]{0:T(128)}, u32[]{:S(2)}) copy-start(f32[96]{0:T(128)} %gain_in) | copy-start | bytes 1156
  8.2 8.5 %copy-start.16 = (f32[96]{0:T(128)S(1)}, f32[96]{0:T(128)}, u32[]{:S(2)}) copy-start(f32[96]{0:T(128)} %gain_mid) | copy-start | bytes 1156
  14.9 2.3 %collective-permute-start.3 = (bf16[256,768]{1,0:T(8,128)(2,1)S(1)}, bf16[256,768]{1,0:T(8,128)(2,1)S(1)}, u32[]{:S(2)}, u32[]{:S(2)}) collective-permute-start(bf16[256,768]{1,0:T(8,128)(2,1)S(1)} %collective-permute-done.far), channel_id=1, source_target_pairs={{0,1},{1,0},{2,3},{3,2},{4,5},{5,4},{6,7},{7,6},{8,9},{9,8},{10,11... | collective-permute-start | bytes 1179656 | tf_op jit(solution)/shard_map/ppermute | solution.py:648
  14.9 9.5 %collective-permute-start.2 = (bf16[192,256]{1,0:T(8,128)(2,1)S(1)}, bf16[192,256]{1,0:T(8,128)(2,1)S(1)}, u32[]{:S(2)}, u32[]{:S(2)}) collective-permute-start(bf16[192,256]{1,0:T(8,128)(2,1)S(1)} %fusion.3), channel_id=1, source_target_pairs={{0,2},{1,3},{2,0},{3,1},{4,6},{5,7},{6,4},{7,5},{8,10},{9,11},{10,... | collective-permute-start | bytes 294920 | tf_op jit(solution)/shard_map/ppermute | solution.py:648
  16.8 7.7 %slice-start = ((s8[4718592]{0:T(1024)(128)(4,1)}), s8[4194304]{0:T(1024)(128)(4,1)S(1)}, s32[]{:S(2)}) async-start(s8[4718592]{0:T(1024)(128)(4,1)} %bitcast.43), calls=%async_computation | async-start | bytes 8388608
  16.8 7.7 %slice-start.2 = ((s8[4718592]{0:T(1024)(128)(4,1)}), s8[4194304]{0:T(1024)(128)(4,1)S(1)}, s32[]{:S(2)}) async-start(s8[4718592]{0:T(1024)(128)(4,1)} %bitcast.45), calls=%async_computation.2 | async-start | bytes 8388608
  17.1 7.4 %slice-start.1 = ((s8[4718592]{0:T(1024)(128)(4,1)}), s8[524288]{0:T(1024)(128)(4,1)S(1)}, s32[]{:S(2)}) async-start(s8[4718592]{0:T(1024)(128)(4,1)} %bitcast.43), calls=%async_computation.1 | async-start | bytes 1048576
  17.1 7.4 %slice-start.3 = ((s8[4718592]{0:T(1024)(128)(4,1)}), s8[524288]{0:T(1024)(128)(4,1)S(1)}, s32[]{:S(2)}) async-start(s8[4718592]{0:T(1024)(128)(4,1)} %bitcast.45), calls=%async_computation.3 | async-start | bytes 1048576
  17.2 7.4 %copy-start.17 = (bf16[768,768]{1,0:T(8,128)(2,1)S(1)}, bf16[768,768]{1,0:T(8,128)(2,1)}, u32[]{:S(2)}) copy-start(bf16[768,768]{1,0:T(8,128)(2,1)} %w_out.1) | copy-start | bytes 3538948
  17.2 7.3 %copy-start.18 = (bf16[768,96]{0,1:T(8,128)(2,1)S(1)}, bf16[768,96]{0,1:T(8,128)(2,1)}, u32[]{:S(2)}) copy-start(bf16[768,96]{0,1:T(8,128)(2,1)} %param.33) | copy-start | bytes 442372
  24.5 8.0 %copy-start.6 = (bf16[384,96]{0,1:T(8,128)(2,1)S(1)}, bf16[384,96]{0,1:T(8,128)(2,1)}, u32[]{:S(2)}) copy-start(bf16[384,96]{0,1:T(8,128)(2,1)} %param.42) | copy-start | bytes 221188
  31.1 1.4 %collective-permute-start.4 = (bf16[512,96]{1,0:T(8,128)(2,1)S(1)}, bf16[512,96]{1,0:T(8,128)(2,1)S(1)}, u32[]{:S(2)}, u32[]{:S(2)}) collective-permute-start(bf16[512,96]{1,0:T(8,128)(2,1)S(1)} %get-tuple-element.108.sn_own), channel_id=1, source_target_pairs={{0,1},{1,0},{2,3},{3,2},{4,5},{5,4},{6,7},{7,6},{8,9},{9,8},{10,11... | collective-permute-start | bytes 294920 | tf_op jit(solution)/shard_map/ppermute | solution.py:648
  31.4 12.7 %collective-permute-start.6 = (bf16[256,768]{1,0:T(8,128)(2,1)S(1)}, bf16[256,768]{1,0:T(8,128)(2,1)S(1)}, u32[]{:S(2)}, u32[]{:S(2)}) collective-permute-start(bf16[256,768]{1,0:T(8,128)(2,1)S(1)} %get-tuple-element.117.out_far), channel_id=1, source_target_pairs={{0,2},{1,3},{2,0},{3,1},{4,6},{5,7},{6,4},{7,5},{8,10},{9,11},{10,... | collective-permute-start | bytes 1179656 | tf_op jit(solution)/shard_map/ppermute | solution.py:648
  42.6 1.5 %collective-permute-start.5 = (bf16[192,512]{1,0:T(8,128)(2,1)S(1)}, bf16[192,512]{1,0:T(8,128)(2,1)S(1)}, u32[]{:S(2)}, u32[]{:S(2)}) collective-permute-start(bf16[192,512]{1,0:T(8,128)(2,1)S(1)} %get-tuple-element.116), channel_id=1, source_target_pairs={{0,1},{1,0},{2,3},{3,2},{4,5},{5,4},{6,7},{7,6},{8,9},{9,8},{10,11... | collective-permute-start | bytes 589832 | tf_op jit(solution)/shard_map/ppermute | solution.py:648
  44.8 1.5 %collective-permute-start.7 = (bf16[96,1024]{1,0:T(8,128)(2,1)S(1)}, bf16[96,1024]{1,0:T(8,128)(2,1)S(1)}, u32[]{:S(2)}, u32[]{:S(2)}) collective-permute-start(bf16[96,1024]{1,0:T(8,128)(2,1)S(1)} %get-tuple-element.138), channel_id=1, source_target_pairs={{0,1},{1,0},{2,3},{3,2},{4,5},{5,4},{6,7},{7,6},{8,9},{9,8},{10,11... | collective-permute-start | bytes 589832 | tf_op jit(solution)/shard_map/ppermute | solution.py:648
  46.5 5.5 %collective-permute-start.10 = (bf16[96,256]{1,0:T(8,128)(2,1)S(1)}, bf16[96,256]{1,0:T(8,128)(2,1)S(1)}, u32[]{:S(2)}, u32[]{:S(2)}) collective-permute-start(bf16[96,256]{1,0:T(8,128)(2,1)S(1)} %get-tuple-element.186), channel_id=1, source_target_pairs={{0,6},{1,7},{2,4},{3,5},{4,2},{5,3},{6,0},{7,1},{8,14},{9,15},{10,... | collective-permute-start | bytes 147464 | tf_op jit(solution)/shard_map/ppermute | solution.py:861
  48.6 4.1 %collective-permute-start.8 = (bf16[96,256]{1,0:T(8,128)(2,1)S(1)}, bf16[96,256]{1,0:T(8,128)(2,1)S(1)}, u32[]{:S(2)}, u32[]{:S(2)}) collective-permute-start(bf16[96,256]{1,0:T(8,128)(2,1)S(1)} %get-tuple-element.185), channel_id=1, source_target_pairs={{0,2},{1,3},{2,0},{3,1},{4,6},{5,7},{6,4},{7,5},{8,10},{9,11},{10,... | collective-permute-start | bytes 147464 | tf_op jit(solution)/shard_map/ppermute | solution.py:861
  49.5 4.1 %collective-permute-start.9 = (bf16[96,256]{1,0:T(8,128)(2,1)S(1)}, bf16[96,256]{1,0:T(8,128)(2,1)S(1)}, u32[]{:S(2)}, u32[]{:S(2)}) collective-permute-start(bf16[96,256]{1,0:T(8,128)(2,1)S(1)} %get-tuple-element.187), channel_id=1, source_target_pairs={{0,4},{1,5},{2,6},{3,7},{4,0},{5,1},{6,2},{7,3},{8,12},{9,13},{10,... | collective-permute-start | bytes 147464 | tf_op jit(solution)/shard_map/ppermute | solution.py:861
  53.6 4.2 %collective-permute-start.12 = (bf16[96,256]{1,0:T(8,128)(2,1)S(1)}, bf16[96,256]{1,0:T(8,128)(2,1)S(1)}, u32[]{:S(2)}, u32[]{:S(2)}) collective-permute-start(bf16[96,256]{1,0:T(8,128)(2,1)S(1)} %add_convert_fusion.3), channel_id=1, source_target_pairs={{0,8},{4,12},{8,0},{12,4},{16,24},{20,28},{24,16},{28,20},{1,9},{5... | collective-permute-start | bytes 147464 | tf_op jit(solution)/shard_map/ppermute | solution.py:648
  57.8 5.6 %collective-permute-start.13 = (bf16[96,256]{1,0:T(8,128)(2,1)S(1)}, bf16[96,256]{1,0:T(8,128)(2,1)S(1)}, u32[]{:S(2)}, u32[]{:S(2)}) collective-permute-start(bf16[96,256]{1,0:T(8,128)(2,1)S(1)} %add_convert_fusion.2), channel_id=1, source_target_pairs={{0,16},{4,20},{8,24},{12,28},{16,0},{20,4},{24,8},{28,12},{1,17},{... | collective-permute-start | bytes 147464 | tf_op jit(solution)/shard_map/ppermute | solution.py:648
  62.2 4.7 %collective-permute-start.11 = (bf16[192,256]{1,0:T(8,128)(2,1)S(1)}, bf16[192,256]{1,0:T(8,128)(2,1)S(1)}, u32[]{:S(2)}, u32[]{:S(2)}) collective-permute-start(bf16[192,256]{1,0:T(8,128)(2,1)S(1)} %get-tuple-element.140), channel_id=1, source_target_pairs={{0,2},{1,3},{2,0},{3,1},{4,6},{5,7},{6,4},{7,5},{8,10},{9,11},{10,... | collective-permute-start | bytes 294920 | tf_op jit(solution)/shard_map/ppermute | solution.py:648
  63.4 4.3 %collective-permute-start.14 = (bf16[96,256]{1,0:T(8,128)(2,1)S(1)}, bf16[96,256]{1,0:T(8,128)(2,1)S(1)}, u32[]{:S(2)}, u32[]{:S(2)}) collective-permute-start(bf16[96,256]{1,0:T(8,128)(2,1)S(1)} %add_convert_fusion.1.refs_0_), channel_id=1, source_target_pairs={{0,2},{1,3},{2,0},{3,1},{4,6},{5,7},{6,4},{7,5},{8,10},{9,11},{10,... | collective-permute-start | bytes 147464 | tf_op jit(solution)/shard_map/ppermute | solution.py:861
  64.3 4.1 %collective-permute-start.15 = (bf16[96,256]{1,0:T(8,128)(2,1)S(1)}, bf16[96,256]{1,0:T(8,128)(2,1)S(1)}, u32[]{:S(2)}, u32[]{:S(2)}) collective-permute-start(bf16[96,256]{1,0:T(8,128)(2,1)S(1)} %add_convert_fusion.1.refs_0_), channel_id=1, source_target_pairs={{0,4},{1,5},{2,6},{3,7},{4,0},{5,1},{6,2},{7,3},{8,12},{9,13},{10,... | collective-permute-start | bytes 147464 | tf_op jit(solution)/shard_map/ppermute | solution.py:861
  64.8 5.0 %collective-permute-start.16 = (bf16[96,256]{1,0:T(8,128)(2,1)S(1)}, bf16[96,256]{1,0:T(8,128)(2,1)S(1)}, u32[]{:S(2)}, u32[]{:S(2)}) collective-permute-start(bf16[96,256]{1,0:T(8,128)(2,1)S(1)} %add_convert_fusion.1.refs_0_), channel_id=1, source_target_pairs={{0,6},{1,7},{2,4},{3,5},{4,2},{5,3},{6,0},{7,1},{8,14},{9,15},{10,... | collective-permute-start | bytes 147464 | tf_op jit(solution)/shard_map/ppermute | solution.py:861
  67.0 3.5 %collective-permute-start.17 = (bf16[96,256]{1,0:T(8,128)(2,1)S(1)}, bf16[96,256]{1,0:T(8,128)(2,1)S(1)}, u32[]{:S(2)}, u32[]{:S(2)}) collective-permute-start(bf16[96,256]{1,0:T(8,128)(2,1)S(1)} %add_convert_fusion.1.refs_0_), channel_id=1, source_target_pairs={{0,1},{1,0},{2,3},{3,2},{4,5},{5,4},{6,7},{7,6},{8,9},{9,8},{10,11... | collective-permute-start | bytes 147464 | tf_op jit(solution)/shard_map/ppermute | solution.py:648
  67.7 2.8 %collective-permute-start.18 = (bf16[96,256]{1,0:T(8,128)(2,1)S(1)}, bf16[96,256]{1,0:T(8,128)(2,1)S(1)}, u32[]{:S(2)}, u32[]{:S(2)}) collective-permute-start(bf16[96,256]{1,0:T(8,128)(2,1)S(1)} %collective-permute-done.14.refs_1_), channel_id=1, source_target_pairs={{0,1},{1,0},{2,3},{3,2},{4,5},{5,4},{6,7},{7,6},{8,9},{9,8},{10,11... | collective-permute-start | bytes 147464 | tf_op jit(solution)/shard_map/ppermute | solution.py:648
  68.4 2.1 %collective-permute-start.19 = (bf16[96,256]{1,0:T(8,128)(2,1)S(1)}, bf16[96,256]{1,0:T(8,128)(2,1)S(1)}, u32[]{:S(2)}, u32[]{:S(2)}) collective-permute-start(bf16[96,256]{1,0:T(8,128)(2,1)S(1)} %collective-permute-done.15.refs_2_), channel_id=1, source_target_pairs={{0,1},{1,0},{2,3},{3,2},{4,5},{5,4},{6,7},{7,6},{8,9},{9,8},{10,11... | collective-permute-start | bytes 147464 | tf_op jit(solution)/shard_map/ppermute | solution.py:648
  69.8 1.2 %collective-permute-start.20 = (bf16[96,256]{1,0:T(8,128)(2,1)S(1)}, bf16[96,256]{1,0:T(8,128)(2,1)S(1)}, u32[]{:S(2)}, u32[]{:S(2)}) collective-permute-start(bf16[96,256]{1,0:T(8,128)(2,1)S(1)} %collective-permute-done.16.refs_3_), channel_id=1, source_target_pairs={{0,1},{1,0},{2,3},{3,2},{4,5},{5,4},{6,7},{7,6},{8,9},{9,8},{10,11... | collective-permute-start | bytes 147464 | tf_op jit(solution)/shard_map/ppermute | solution.py:648

commit v10 on v9

--- a/solution.py
+++ b/solution.py
@@ -124,21 +124,20 @@
 
 
 def prepare_body(
-    doc_lengths, w_value, norm_in, norm_mid, value_t, gains, key_doc, query_doc, side_key_doc, side_query_doc
+    doc_lengths, w_value, norm_in, norm_mid, value_t, gains, bias, side_key_doc, side_query_doc
 ):
     value_t[...] = nt(eye(w_value.shape[0]), w_value[...]).astype(bf16)
     for i, line in enumerate((norm_in, norm_mid)):
         gains[i : i + 1] = line[...].astype(f32).reshape(1, line.shape[0])
-    keys, tokens = key_doc.shape[0], query_doc.shape[0]
+    keys, tokens = bias.shape
     span = tokens // 2
     place, half = lax.axis_index("blk"), lax.axis_size("blk") // 2
     row = place // half
     own, mate = place * span, (place ^ 1) * span
     far, far_mate = (place ^ half) * span, (place ^ half ^ 1) * span
     found = in_doc(doc_lengths, row, (own, mate, far, far_mate), span, (keys, 128), 0)
-    key_doc[...] = (found - 1.0).astype(bf16)
     mine = jnp.concatenate([found[0:span], found[tokens : tokens + span]], axis=0)
-    query_doc[...] = (mine * FAR).astype(bf16)
+    bias[...] = nt((found - 1.0).astype(bf16), (mine * FAR).astype(bf16))
     mates = jnp.concatenate([found[span:tokens], found[tokens + span : keys]], axis=0)
     spare = SPARE
     low = iota((keys, 128), 1) < spare
@@ -165,28 +164,28 @@
     return pl.ds(pl.multiple_of(j * 128, 128), 128)
 
 
-def pair_sums(j, queries, query_doc, keys, key_doc, values, shifted=False):
+def pair_sums(j, queries, keys, values, bias, shifted=False):
     width = queries[0].shape[1]
     head = width // HEADS
     stride = values[0].shape[0] // HEADS
     lanes = pair_lanes(j)
     key = jnp.concatenate([ref[:, lanes] for ref in keys], axis=0)
-    key = jnp.concatenate([key, key_doc], axis=1)
     query = jnp.concatenate([ref[:, lanes] for ref in queries], axis=0)
     rows = pl.ds(pl.multiple_of(j * 2 * stride, 16), 2 * stride)
     value = jnp.concatenate([ref[rows, :] for ref in values], axis=1)
     lane = iota((1, 128), 1) // head
-    masked = [jnp.concatenate([query * ones_where(lane == i), query_doc], axis=1) for i in range(2)]
+    masked = [query * ones_where(lane == i) for i in range(2)]
     count = query.shape[0]
 
     scores = nt(key, jnp.concatenate(masked, axis=0)) * (LOG2E * head**-0.5)
+    scores = scores + jnp.concatenate([bias, bias], axis=1)
     if shifted:
         scores = scores - jnp.max(scores, axis=0, keepdims=True)
     both = nn(value, jnp.exp2(scores).astype(bf16))
     return [both[i * stride : i * stride + head + 8, i * count : (i + 1) * count] for i in range(2)]
 
 
-def first_body(own, mate, gains, w_query, w_key, value_t, key_doc, query_doc, query, key, value, part):
+def first_body(own, mate, gains, w_query, w_key, value_t, bias, query, key, value, part):
     _, span, width = own.shape
     head = width // HEADS
     row = lax.axis_index("blk") // (lax.axis_size("blk") // 2)
@@ -197,7 +196,7 @@
     value[...] = padded(value_new, head)
 
     def pair(j, carry):
-        sums = pair_sums(j, [query], query_doc[0:span], [key], key_doc[0 : 2 * span], [value])
+        sums = pair_sums(j, [query], [key], [value], bias[0 : 2 * span, 0:span])
         part[j] = jnp.concatenate(sums, axis=0)
         return carry
 
@@ -209,33 +208,39 @@
     return jnp.logical_not((lowest > LOW_TOTAL) & (highest < HIGH_TOTAL))
 
 
+def far_body(far, gains, w_query, w_key, w_value, query, key, value):
+    width = far.shape[1]
+    head = width // HEADS
+    normed = norm_lanes(far[...].astype(f32), gains[0:1]).astype(bf16)
+    query[...] = nn(normed, w_query[...]).astype(bf16)
+    key[...] = nn(normed, w_key[...]).astype(bf16)
+    value[...] = padded(nn(normed, w_value[...]).astype(bf16).T, head)
+
+
 def second_body(
-    far,
     far_mate,
     gains,
-    w_query,
     w_key,
-    value_t,
-    key_doc,
-    query_doc,
+    w_value,
+    bias,
     query_a,
     key_a,
     value_a,
     part_a,
+    query_b,
+    key_b,
+    value_b,
     attended,
-    query,
     key,
     value,
     totals,
 ):
-    span, width = far.shape
+    span, width = far_mate.shape
     head = width // HEADS
-    tokens = jnp.concatenate([far[...], far_mate[...]], axis=0)
-    query[...], key[...], value_new = project(
-        tokens, gains[0:1], w_query, w_key, value_t, span
-    )
-    value[...] = padded(value_new, head)
-    keys, values, queries = [key_a, key], [value_a, value], [query_a, query]
+    normed = norm_lanes(far_mate[...].astype(f32), gains[0:1]).astype(bf16)
+    key[...] = nn(normed, w_key[...]).astype(bf16)
+    value[...] = padded(nn(normed, w_value[...]).astype(bf16).T, head)
+    keys, values, queries = [key_a, key_b, key], [value_a, value_b, value], [query_a, query_b]
 
     def finish(j, sums):
         results = []
@@ -245,8 +250,8 @@
         attended[:, pair_lanes(j)] = jnp.concatenate(results, axis=0).T.astype(bf16)
 
     def pair(j, carry):
-        old = pair_sums(j, [query_a], query_doc[0:span], [key], key_doc[2 * span : 4 * span], [value])
-        new = pair_sums(j, [query], query_doc[span : 2 * span], keys, key_doc[...], values)
+        old = pair_sums(j, [query_a], keys[1:], values[1:], bias[2 * span : 4 * span, 0:span])
+        new = pair_sums(j, [query_b], keys, values, bias[:, span : 2 * span])
         sums = []
         for i in range(2):
             rows = slice(i * (head + 8), (i + 1) * (head + 8))
@@ -259,7 +264,7 @@
     @pl.when(out_of_range(totals[...]))
     def _():
         def again(j, carry):
-            finish(j, pair_sums(j, queries, query_doc[...], keys, key_doc[...], values, shifted=True))
+            finish(j, pair_sums(j, queries, keys, values, bias[...], shifted=True))
             return carry
 
         lax.fori_loop(0, HEADS // 2, again, 0)
@@ -662,13 +667,12 @@
     )
     down_w, s_outer_t = w_down.T, s_outer.T
 
-    value_t, gains, key_doc, query_doc, side_key_doc, side_query_doc = kernel_call(
+    value_t, gains, bias, side_key_doc, side_query_doc = kernel_call(
         prepare_body,
         [
             ((width, width), bf16),
             ((2, width), f32),
-            ((2 * tokens, 128), bf16),
-            ((tokens, 128), bf16),
+            ((2 * tokens, tokens), f32),
             ((2 * tokens, 128), bf16),
             ((16, tokens), bf16),
         ],
@@ -679,7 +683,7 @@
     )
     head = width // HEADS
     stride = head + 16
-    projections = (gains, w_query, w_key, value_t, key_doc, query_doc)
+    projections = (gains, w_query, w_key, value_t, bias)
 
     def state_of(queries, keys, columns):
         return [
@@ -712,15 +716,22 @@
         scratch=[pltpu.VMEM((128, 128), f32)],
         cost=(1000, 1000, 0),
     )
+    far_mate = beside(hidden_far)
+    state_b = kernel_call(
+        far_body,
+        state_of(span, span, span)[0:3],
+        [hidden_far, gains, w_query, w_key, w_value],
+        vmem=16,
+        cost=(5 * 10**9, 8 * 10**6, 0),
+    )
     (attended,) = kernel_call(
         second_body,
         [((tokens, width), bf16)],
-        [hidden_far, beside(hidden_far), *projections, *state_a],
-        vmem=30,
+        [far_mate, gains, w_key, w_value, bias, *state_a, *state_b],
+        vmem=26,
         scratch=[
             pltpu.VMEM((span, width), bf16),
-            pltpu.VMEM((tokens, width), bf16),
-            pltpu.VMEM((HEADS * stride, tokens), bf16),
+            pltpu.VMEM((HEADS * stride, span), bf16),
             pltpu.VMEM((HEADS * 8, tokens), f32),
         ],
         cost=(8 * 10**9, 8 * 10**6, 0),

time: 72.2 us -> 72.5 us (level)
  waiting for transfers between devices: 11.5 us -> 12.5 us
  starting transfers between devices: 19.9 us -> 19 us
    ppermute x15, starting transfers between devices: 12.8 us -> 11.8 us  [swap(): return lax.ppermute(value, axis, [(i, i ^ hop) for i in range(size)])]
    pallas_call x9 -> x10, Pallas kernels: 33.5 us -> 33.7 us  [kernel_call(): pl.pallas_call(body, out_shape=[jax.ShapeDtypeStruct(shape, kind) for sha...]
    unnamed x48 -> x50, local copies, waits for them, and re-layouts: 4.39 us -> 4.38 us
  transfers between devices with their start and end apart: 21 -> 21, of which waited for: 10 -> 10; matrix products, arithmetic and copies ran while one was open for 5% -> 4% of each run, Pallas kernels for 35% -> 35%
where the time goes in v10:
time: 72.5 us; the launch traced here: 72.3 us
  Pallas kernels  33.7 us (46%)
  starting transfers between devices  19 us (26%)
  waiting for transfers between devices  12.5 us (17%)
  local copies, waits for them, and re-layouts  4.44 us (6%)
  other arithmetic  1.62 us (2%)
  between operations  1.09 us (2%)
    pallas_call x10, Pallas kernels, kernel_call(): pl.pallas_call(body, out_shape=[jax.ShapeDtypeStruct(shape, kind) for sha...  33.7 us
    ppermute x15, starting transfers between devices, swap(): return lax.ppermute(value, axis, [(i, i ^ hop) for i in range(size)])  11.8 us
    ppermute x6, starting transfers between devices, between(): lax.ppermute(value, ('dp', 'blk'), [(i, i ^ mask) for i in range(devices)])  7.11 us
    ppermute x15, waiting for transfers between devices, swap(): return lax.ppermute(value, axis, [(i, i ^ hop) for i in range(size)])  6.65 us
    ppermute x6, waiting for transfers between devices, between(): lax.ppermute(value, ('dp', 'blk'), [(i, i ^ mask) for i in range(devices)])  5.81 us
    unnamed x50, local copies, waits for them, and re-layouts  4.38 us
  transfers between devices with their start and end apart: 21, of which 10 were waited for; matrix products, arithmetic and copies ran while one was open for 4% of the time, Pallas kernels for 35%

profile of v10, /device:TPU:0, one launch (start us, length us, event | category | flops | bytes accessed | tf_op | source)
XLA Modules:
  0.0 72.3 jit_solution(7056639656702214163)
XLA Ops:
  0.7 1.3 %copy.42 = bf16[256,2,768]{2,0,1:T(8,128)(2,1)S(1)} copy(bf16[256,2,768]{2,1,0:T(2,128)(2,1)} %param.22) | data formatting | bytes 1572864 | tf_op args[0]
  2.0 0.5 collective-permute-start.1
  2.6 2.6 %collective-permute-start = (bf16[256,768]{1,0:T(8,128)(2,1)S(1)}, bf16[256,768]{1,0:T(8,128)(2,1)S(1)}, u32[]{:S(2)}, u32[]{:S(2)}) collective-permute-start(bf16[256,768]{1,0:T(8,128)(2,1)S(1)} %dynamic-slice_bitcast_fusion), channel_id=1, source_target_pairs={{0,2},{1,3},{2,0},{3,1},{4,6},{5,7},{6,4},{7,5},{8,10},{9,11},{10,... | collective-permute-start | bytes 1179656 | tf_op jit(solution)/shard_map/ppermute | solution.py:653
  5.2 0.1 collective-permute-start.2
  5.3 1.9 %shard_map.309 = (bf16[768,768]{1,0:T(8,128)(2,1)S(1)}, f32[2,768]{1,0:T(2,128)S(1)}, f32[1024,512]{1,0:T(8,128)S(1)}, bf16[1024,128]{1,0:T(8,128)(2,1)S(1)}, bf16[16,512]{1,0:T(8,128)(2,1)S(1)}) custom-call(s32[2,8]{1,0:T(2,128)S(1)} %copy-done.14, bf16[768,768]{1,0:T(8,128)(2,1)S(1)} %copy-done, bf16[768]{0:T(1024)(128)(2,1)S(1)} %copy-done.12, ...), custom_call_target="tpu_custom_call" | custom-call | flops 1000 | bytes 1000 | tf_op jit(solution)/shard_map/pallas_call | solution.py:65
  7.3 1.3 %copy-done.2 = bf16[768,768]{1,0:T(8,128)(2,1)S(1)} copy-done((bf16[768,768]{1,0:T(8,128)(2,1)S(1)}, bf16[768,768]{1,0:T(8,128)(2,1)}, u32[]{:S(2)}) %copy-start.2) | copy-done | bytes 1179672
  8.6 5.1 %shard_map.310 = (bf16[256,768]{1,0:T(8,128)(2,1)S(1)}, bf16[512,768]{1,0:T(8,128)(2,1)S(1)}, bf16[960,512]{1,0:T(8,128)(2,1)S(1)}, f32[6,144,256]{2,1,0:T(8,128)S(1)}) custom-call(bf16[2,256,768]{2,1,0:T(8,128)(2,1)S(1)} %bitcast.34, bf16[2,256,768]{2,1,0:T(8,128)(2,1)} %collective-permute-done.1.mate, f32[2,768]{1,0:T(2,128)S(1)} %get-tuple-element.85.gains, ...), custom_call_target="tpu_custom_call" | custom-call | flops 1000 | bytes 1000 | tf_op jit(solution)/shard_map/pallas_call | solution.py:65
  13.7 1.5 %collective-permute-done.far = bf16[256,768]{1,0:T(8,128)(2,1)S(1)} collective-permute-done((bf16[256,768]{1,0:T(8,128)(2,1)S(1)}, bf16[256,768]{1,0:T(8,128)(2,1)S(1)}, u32[]{:S(2)}, u32[]{:S(2)}) %collective-permute-start) | collective-permute-done | bytes 393248 | tf_op jit(solution)/shard_map/ppermute | solution.py:653
  15.2 0.3 shard_map.313
  15.6 0.0 slice-start
  15.6 0.0 slice-start.2
  15.6 1.2 %shard_map.311 = (bf16[256,768]{1,0:T(8,128)(2,1)S(1)}, bf16[256,768]{1,0:T(8,128)(2,1)S(1)}, bf16[960,256]{1,0:T(8,128)(2,1)S(1)}) custom-call(bf16[256,768]{1,0:T(8,128)(2,1)S(1)} %collective-permute-done.far, f32[2,768]{1,0:T(2,128)S(1)} %get-tuple-element.85.gains, bf16[768,768]{1,0:T(8,128)(2,1)S(1)} %copy-done.1, bf16[768,768]{1,0:T(8,128)(2,1)S(1)} %copy-done.2, ...), custom_call_target="tpu_custom_call" | custom-call | flops 5000000000 | bytes 8000000 | tf_op jit(solution)/shard_map/pallas_call | solution.py:65
  16.8 0.0 collective-permute-done.3.far_mate
  16.9 6.1 %shard_map.312.attended = bf16[512,768]{1,0:T(8,128)(2,1)S(1)} custom-call(bf16[256,768]{1,0:T(8,128)(2,1)S(1)} %collective-permute-done.3.far_mate, f32[2,768]{1,0:T(2,128)S(1)} %get-tuple-element.85.gains, bf16[768,768]{1,0:T(8,128)(2,1)S(1)} %copy-done.3, bf16[768,768]{1,0:T(8,128)(2,1)S(1)} %copy-done, f32[1024,512]{1,0:T(8,128)S(1)} %get-tuple-element.87.bias, ...), custom_call_target="tpu_custom_call" | custom-call | flops 8000000000 | bytes 8000000 | tf_op jit(solution)/shard_map/pallas_call | solution.py:65
  23.1 6.7 %shard_map.314 = (bf16[256,768]{1,0:T(8,128)(2,1)S(1)}, bf16[256,768]{1,0:T(8,128)(2,1)S(1)}, bf16[512,96]{1,0:T(8,128)(2,1)S(1)}, bf16[96,512]{1,0:T(8,128)(2,1...) custom-call(bf16[2,256,768]{2,1,0:T(8,128)(2,1)S(1)} %bitcast.35, bf16[256,768]{1,0:T(8,128)(2,1)S(1)} %collective-permute-done.far, ...), custom_call_target="tpu_custom_call" | custom-call | flops 10000000000 | bytes 14000000 | tf_op jit(solution)/shard_map/pallas_call | solution.py:65
  29.8 0.6 collective-permute-start.4
  30.4 1.9 %collective-permute-start.6 = (bf16[256,768]{1,0:T(8,128)(2,1)S(1)}, bf16[256,768]{1,0:T(8,128)(2,1)S(1)}, u32[]{:S(2)}, u32[]{:S(2)}) collective-permute-start(bf16[256,768]{1,0:T(8,128)(2,1)S(1)} %get-tuple-element.121.out_far), channel_id=1, source_target_pairs={{0,2},{1,3},{2,0},{3,1},{4,6},{5,7},{6,4},{7,5},{8,10},{9,11},{10,... | collective-permute-start | bytes 1179656 | tf_op jit(solution)/shard_map/ppermute | solution.py:653
  32.3 10.1 %shard_map.315 = (f32[192,512]{1,0:T(8,128)S(1)}, bf16[192,512]{1,0:T(8,128)(2,1)S(1)}, f32[96,512]{1,0:T(8,128)S(1)}, f32[96,512]{1,0:T(8,128)S(1)}, f32[96,512...) custom-call(bf16[512,96]{1,0:T(8,128)(2,1)S(1)} %get-tuple-element.1, ...), custom_call_target="tpu_custom_call" | custom-call | flops 30000001024 | bytes 3000000 | tf_op jit(solution)/shard_map/pallas_call | solution.py:65
  42.4 0.1 collective-permute-start.5
  42.5 0.6 shard_map.316
  43.1 0.8 %collective-permute-done.5.dkv_back = bf16[192,512]{1,0:T(8,128)(2,1)S(1)} collective-permute-done((bf16[192,512]{1,0:T(8,128)(2,1)S(1)}, bf16[192,512]{1,0:T(8,128)(2,1)S(1)}, u32[]{:S(2)}, u32[]{:S(2)}) %collective-permute-start.5) | collective-permute-done | bytes 196640 | tf_op jit(solution)/shard_map/ppermute | solution.py:653
  43.9 0.7 shard_map.317
  44.6 0.2 collective-permute-start.7
  44.8 1.3 %collective-permute-done.7 = bf16[96,1024]{1,0:T(8,128)(2,1)S(1)} collective-permute-done((bf16[96,1024]{1,0:T(8,128)(2,1)S(1)}, bf16[96,1024]{1,0:T(8,128)(2,1)S(1)}, u32[]{:S(2)}, u32[]{:S(2)}) %collective-permute-start.7) | collective-permute-done | bytes 196640 | tf_op jit(solution)/shard_map/ppermute | solution.py:653
  46.2 2.0 %collective-permute-start.10 = (bf16[96,256]{1,0:T(8,128)(2,1)S(1)}, bf16[96,256]{1,0:T(8,128)(2,1)S(1)}, u32[]{:S(2)}, u32[]{:S(2)}) collective-permute-start(bf16[96,256]{1,0:T(8,128)(2,1)S(1)} %get-tuple-element.190), channel_id=1, source_target_pairs={{0,6},{1,7},{2,4},{3,5},{4,2},{5,3},{6,0},{7,1},{8,14},{9,15},{10,... | collective-permute-start | bytes 147464 | tf_op jit(solution)/shard_map/ppermute | solution.py:872
  48.2 0.5 collective-permute-start.9
  48.8 1.0 %collective-permute-start.8 = (bf16[96,256]{1,0:T(8,128)(2,1)S(1)}, bf16[96,256]{1,0:T(8,128)(2,1)S(1)}, u32[]{:S(2)}, u32[]{:S(2)}) collective-permute-start(bf16[96,256]{1,0:T(8,128)(2,1)S(1)} %get-tuple-element.189), channel_id=1, source_target_pairs={{0,2},{1,3},{2,0},{3,1},{4,6},{5,7},{6,4},{7,5},{8,10},{9,11},{10,... | collective-permute-start | bytes 147464 | tf_op jit(solution)/shard_map/ppermute | solution.py:872
  49.8 1.5 %collective-permute-done.10 = bf16[96,256]{1,0:T(8,128)(2,1)S(1)} collective-permute-done((bf16[96,256]{1,0:T(8,128)(2,1)S(1)}, bf16[96,256]{1,0:T(8,128)(2,1)S(1)}, u32[]{:S(2)}, u32[]{:S(2)}) %collective-permute-start.10) | collective-permute-done | bytes 49184 | tf_op jit(solution)/shard_map/ppermute | solution.py:872
  51.3 1.0 %collective-permute-done.9 = bf16[96,256]{1,0:T(8,128)(2,1)S(1)} collective-permute-done((bf16[96,256]{1,0:T(8,128)(2,1)S(1)}, bf16[96,256]{1,0:T(8,128)(2,1)S(1)}, u32[]{:S(2)}, u32[]{:S(2)}) %collective-permute-start.9) | collective-permute-done | bytes 49184 | tf_op jit(solution)/shard_map/ppermute | solution.py:872
  52.3 0.5 collective-permute-done.8
  52.9 1.6 %collective-permute-start.12 = (bf16[96,256]{1,0:T(8,128)(2,1)S(1)}, bf16[96,256]{1,0:T(8,128)(2,1)S(1)}, u32[]{:S(2)}, u32[]{:S(2)}) collective-permute-start(bf16[96,256]{1,0:T(8,128)(2,1)S(1)} %add_convert_fusion.3), channel_id=1, source_target_pairs={{0,8},{4,12},{8,0},{12,4},{16,24},{20,28},{24,16},{28,20},{1,9},{5... | collective-permute-start | bytes 147464 | tf_op jit(solution)/shard_map/ppermute | solution.py:653
  54.5 0.1 select_bitcast_fusion.1
  54.6 2.5 %collective-permute-done.12 = bf16[96,256]{1,0:T(8,128)(2,1)S(1)} collective-permute-done((bf16[96,256]{1,0:T(8,128)(2,1)S(1)}, bf16[96,256]{1,0:T(8,128)(2,1)S(1)}, u32[]{:S(2)}, u32[]{:S(2)}) %collective-permute-start.12) | collective-permute-done | bytes 49184 | tf_op jit(solution)/shard_map/ppermute | solution.py:653
  57.1 2.7 %collective-permute-start.13 = (bf16[96,256]{1,0:T(8,128)(2,1)S(1)}, bf16[96,256]{1,0:T(8,128)(2,1)S(1)}, u32[]{:S(2)}, u32[]{:S(2)}) collective-permute-start(bf16[96,256]{1,0:T(8,128)(2,1)S(1)} %add_convert_fusion.2), channel_id=1, source_target_pairs={{0,16},{4,20},{8,24},{12,28},{16,0},{20,4},{24,8},{28,12},{1,17},{... | collective-permute-start | bytes 147464 | tf_op jit(solution)/shard_map/ppermute | solution.py:653
  59.7 0.1 maximum_bitcast_fusion
  59.8 1.7 %copy.39 = bf16[256,2,768]{2,1,0:T(2,128)(2,1)} copy(bf16[256,2,768]{2,0,1:T(8,128)(2,1)S(1)} %maximum_bitcast_fusion) | data formatting | bytes 1572864
  61.5 1.0 %collective-permute-start.11 = (bf16[192,256]{1,0:T(8,128)(2,1)S(1)}, bf16[192,256]{1,0:T(8,128)(2,1)S(1)}, u32[]{:S(2)}, u32[]{:S(2)}) collective-permute-start(bf16[192,256]{1,0:T(8,128)(2,1)S(1)} %get-tuple-element.144), channel_id=1, source_target_pairs={{0,2},{1,3},{2,0},{3,1},{4,6},{5,7},{6,4},{7,5},{8,10},{9,11},{10,... | collective-permute-start | bytes 294920 | tf_op jit(solution)/shard_map/ppermute | solution.py:653
  62.5 1.1 %collective-permute-start.14 = (bf16[96,256]{1,0:T(8,128)(2,1)S(1)}, bf16[96,256]{1,0:T(8,128)(2,1)S(1)}, u32[]{:S(2)}, u32[]{:S(2)}) collective-permute-start(bf16[96,256]{1,0:T(8,128)(2,1)S(1)} %add_convert_fusion.1.refs_0_), channel_id=1, source_target_pairs={{0,2},{1,3},{2,0},{3,1},{4,6},{5,7},{6,4},{7,5},{8,10},{9,11},{10,... | collective-permute-start | bytes 147464 | tf_op jit(solution)/shard_map/ppermute | solution.py:872
  63.6 1.5 %collective-permute-start.15 = (bf16[96,256]{1,0:T(8,128)(2,1)S(1)}, bf16[96,256]{1,0:T(8,128)(2,1)S(1)}, u32[]{:S(2)}, u32[]{:S(2)}) collective-permute-start(bf16[96,256]{1,0:T(8,128)(2,1)S(1)} %add_convert_fusion.1.refs_0_), channel_id=1, source_target_pairs={{0,4},{1,5},{2,6},{3,7},{4,0},{5,1},{6,2},{7,3},{8,12},{9,13},{10,... | collective-permute-start | bytes 147464 | tf_op jit(solution)/shard_map/ppermute | solution.py:872
  65.1 1.0 %collective-permute-start.16 = (bf16[96,256]{1,0:T(8,128)(2,1)S(1)}, bf16[96,256]{1,0:T(8,128)(2,1)S(1)}, u32[]{:S(2)}, u32[]{:S(2)}) collective-permute-start(bf16[96,256]{1,0:T(8,128)(2,1)S(1)} %add_convert_fusion.1.refs_0_), channel_id=1, source_target_pairs={{0,6},{1,7},{2,4},{3,5},{4,2},{5,3},{6,0},{7,1},{8,14},{9,15},{10,... | collective-permute-start | bytes 147464 | tf_op jit(solution)/shard_map/ppermute | solution.py:872
  66.1 0.0 collective-permute-done.11
  66.1 0.7 maximum_bitcast_fusion.1
  66.8 0.5 collective-permute-start.18
  67.3 0.3 collective-permute-done.15.refs_2_
  67.7 2.4 %collective-permute-done.16.refs_3_ = bf16[96,256]{1,0:T(8,128)(2,1)S(1)} collective-permute-done((bf16[96,256]{1,0:T(8,128)(2,1)S(1)}, bf16[96,256]{1,0:T(8,128)(2,1)S(1)}, u32[]{:S(2)}, u32[]{:S(2)}) %collective-permute-start.16) | collective-permute-done | bytes 49184 | tf_op jit(solution)/shard_map/ppermute | solution.py:872
  70.1 0.7 maximum_bitcast_fusion.2
  70.8 0.6 collective-permute-done.20.refs_7_
  71.3 1.0 %shard_map.318 = (f32[96,768]{1,0:T(8,128)}, f32[1,96]{1,0:T(1,128)}, f32[1,96]{1,0:T(1,128)}, f32[96,96]{1,0:T(8,128)}, f32[96,96]{1,0:T(8,128)}, /*index=5*/f3...) custom-call(bf16[96,256]{1,0:T(8,128)(2,1)S(1)} %add_convert_fusion.1.refs_0_, ...), custom_call_target="tpu_custom_call" | custom-call | bytes 2000000 | tf_op jit(solution)/shard_map/pallas_call | solution.py:65
  (69 shorter events, 0.3 us)
Async XLA Ops:
  0.6 4.5 %copy-start.5 = (bf16[256,2,96]{0,2,1:T(8,128)(2,1)S(1)}, bf16[256,2,96]{0,2,1:T(8,128)(2,1)}, u32[]{:S(2)}) copy-start(bf16[256,2,96]{0,2,1:T(8,128)(2,1)} %param.23) | copy-start | bytes 294916
  0.7 4.5 %copy-start.4 = (bf16[256,2,96]{0,2,1:T(8,128)(2,1)S(1)}, bf16[256,2,96]{0,2,1:T(8,128)(2,1)}, u32[]{:S(2)}) copy-start(bf16[256,2,96]{0,2,1:T(8,128)(2,1)} %param.43) | copy-start | bytes 294916
  0.7 4.6 %copy-start.14 = (s32[2,8]{1,0:T(2,128)S(1)}, s32[2,8]{1,0:T(2,128)}, u32[]{:S(2)}) copy-start(s32[2,8]{1,0:T(2,128)} %doc_lengths.1) | copy-start | bytes 196
  0.7 4.6 %copy-start = (bf16[768,768]{1,0:T(8,128)(2,1)S(1)}, bf16[768,768]{1,0:T(8,128)(2,1)}, u32[]{:S(2)}) copy-start(bf16[768,768]{1,0:T(8,128)(2,1)} %w_value.5) | copy-start | bytes 3538948
  0.7 4.6 %copy-start.12 = (bf16[768]{0:T(1024)(128)(2,1)S(1)}, bf16[768]{0:T(1024)(128)(2,1)}, u32[]{:S(2)}) copy-start(bf16[768]{0:T(1024)(128)(2,1)} %norm_in.1) | copy-start | bytes 4612
  0.7 4.6 %copy-start.13 = (bf16[768]{0:T(1024)(128)(2,1)S(1)}, bf16[768]{0:T(1024)(128)(2,1)}, u32[]{:S(2)}) copy-start(bf16[768]{0:T(1024)(128)(2,1)} %norm_mid.1) | copy-start | bytes 4612
  2.0 5.3 %copy-start.1 = (bf16[768,768]{1,0:T(8,128)(2,1)S(1)}, bf16[768,768]{1,0:T(8,128)(2,1)}, u32[]{:S(2)}) copy-start(bf16[768,768]{1,0:T(8,128)(2,1)} %w_query.3) | copy-start | bytes 3538948
  2.0 5.2 %collective-permute-start.1 = (bf16[2,256,768]{2,1,0:T(8,128)(2,1)S(1)}, bf16[2,256,768]{2,1,0:T(8,128)(2,1)}, u32[]{:S(2)}, u32[]{:S(2)}) collective-permute-start(bf16[2,256,768]{2,1,0:T(8,128)(2,1)S(1)} %bitcast.33), channel_id=1, source_target_pairs={{0,1},{1,0},{2,3},{3,2},{4,5},{5,4},{6,7},{7,6},{8,9},{9,8},{10,11... | collective-permute-start | bytes 2359304 | tf_op jit(solution)/shard_map/ppermute | solution.py:653
  2.6 12.6 %collective-permute-start = (bf16[256,768]{1,0:T(8,128)(2,1)S(1)}, bf16[256,768]{1,0:T(8,128)(2,1)S(1)}, u32[]{:S(2)}, u32[]{:S(2)}) collective-permute-start(bf16[256,768]{1,0:T(8,128)(2,1)S(1)} %dynamic-slice_bitcast_fusion), channel_id=1, source_target_pairs={{0,2},{1,3},{2,0},{3,1},{4,6},{5,7},{6,4},{7,5},{8,10},{9,11},{10,... | collective-permute-start | bytes 1179656 | tf_op jit(solution)/shard_map/ppermute | solution.py:653
  5.2 17.8 %collective-permute-start.2 = (bf16[192,256]{1,0:T(8,128)(2,1)S(1)}, bf16[192,256]{1,0:T(8,128)(2,1)S(1)}, u32[]{:S(2)}, u32[]{:S(2)}) collective-permute-start(bf16[192,256]{1,0:T(8,128)(2,1)S(1)} %fusion.3), channel_id=1, source_target_pairs={{0,2},{1,3},{2,0},{3,1},{4,6},{5,7},{6,4},{7,5},{8,10},{9,11},{10,... | collective-permute-start | bytes 294920 | tf_op jit(solution)/shard_map/ppermute | solution.py:653
  7.3 1.3 %copy-start.2 = (bf16[768,768]{1,0:T(8,128)(2,1)S(1)}, bf16[768,768]{1,0:T(8,128)(2,1)}, u32[]{:S(2)}) copy-start(bf16[768,768]{1,0:T(8,128)(2,1)} %w_key.5) | copy-start | bytes 3538948
  8.6 6.6 %copy-start.6 = (bf16[96,384]{1,0:T(8,128)(2,1)S(1)}, bf16[96,384]{1,0:T(8,128)(2,1)}, u32[]{:S(2)}) copy-start(bf16[96,384]{1,0:T(8,128)(2,1)} %s_inner.2) | copy-start | bytes 221188
  8.6 6.6 %copy-start.8 = (bf16[96,96]{1,0:T(8,128)(2,1)S(1)}, bf16[96,96]{1,0:T(8,128)(2,1)}, u32[]{:S(2)}) copy-start(bf16[96,96]{1,0:T(8,128)(2,1)} %s_out.2) | copy-start | bytes 55300
  8.6 6.6 %copy-start.9 = (bf16[96,96]{1,0:T(8,128)(2,1)S(1)}, bf16[96,96]{1,0:T(8,128)(2,1)}, u32[]{:S(2)}) copy-start(bf16[96,96]{1,0:T(8,128)(2,1)} %s_query.2) | copy-start | bytes 55300
  8.6 6.6 %copy-start.10 = (bf16[96,96]{1,0:T(8,128)(2,1)S(1)}, bf16[96,96]{1,0:T(8,128)(2,1)}, u32[]{:S(2)}) copy-start(bf16[96,96]{1,0:T(8,128)(2,1)} %s_key.2) | copy-start | bytes 55300
  8.6 6.6 %copy-start.11 = (bf16[96,96]{1,0:T(8,128)(2,1)S(1)}, bf16[96,96]{1,0:T(8,128)(2,1)}, u32[]{:S(2)}) copy-start(bf16[96,96]{1,0:T(8,128)(2,1)} %s_value.2) | copy-start | bytes 55300
  8.6 6.6 %copy-start.15 = (f32[96]{0:T(128)S(1)}, f32[96]{0:T(128)}, u32[]{:S(2)}) copy-start(f32[96]{0:T(128)} %gate) | copy-start | bytes 1156
  8.6 6.6 %copy-start.16 = (f32[96]{0:T(128)S(1)}, f32[96]{0:T(128)}, u32[]{:S(2)}) copy-start(f32[96]{0:T(128)} %gain_in) | copy-start | bytes 1156
  8.6 6.6 %copy-start.17 = (f32[96]{0:T(128)S(1)}, f32[96]{0:T(128)}, u32[]{:S(2)}) copy-start(f32[96]{0:T(128)} %gain_mid) | copy-start | bytes 1156
  15.1 1.7 %collective-permute-start.3 = (bf16[256,768]{1,0:T(8,128)(2,1)S(1)}, bf16[256,768]{1,0:T(8,128)(2,1)S(1)}, u32[]{:S(2)}, u32[]{:S(2)}) collective-permute-start(bf16[256,768]{1,0:T(8,128)(2,1)S(1)} %collective-permute-done.far), channel_id=1, source_target_pairs={{0,1},{1,0},{2,3},{3,2},{4,5},{5,4},{6,7},{7,6},{8,9},{9,8},{10,11... | collective-permute-start | bytes 1179656 | tf_op jit(solution)/shard_map/ppermute | solution.py:653
  15.5 1.3 %copy-start.3 = (bf16[768,768]{1,0:T(8,128)(2,1)S(1)}, bf16[768,768]{1,0:T(8,128)(2,1)}, u32[]{:S(2)}) copy-start(bf16[768,768]{1,0:T(8,128)(2,1)} %w_key.5) | copy-start | bytes 3538948
  15.6 7.5 %slice-start = ((s8[4718592]{0:T(1024)(128)(4,1)}), s8[4194304]{0:T(1024)(128)(4,1)S(1)}, s32[]{:S(2)}) async-start(s8[4718592]{0:T(1024)(128)(4,1)} %bitcast.43), calls=%async_computation | async-start | bytes 8388608
  15.6 7.5 %slice-start.2 = ((s8[4718592]{0:T(1024)(128)(4,1)}), s8[4194304]{0:T(1024)(128)(4,1)S(1)}, s32[]{:S(2)}) async-start(s8[4718592]{0:T(1024)(128)(4,1)} %bitcast.45), calls=%async_computation.2 | async-start | bytes 8388608
  16.9 6.2 %slice-start.1 = ((s8[4718592]{0:T(1024)(128)(4,1)}), s8[524288]{0:T(1024)(128)(4,1)S(1)}, s32[]{:S(2)}) async-start(s8[4718592]{0:T(1024)(128)(4,1)} %bitcast.43), calls=%async_computation.1 | async-start | bytes 1048576
  16.9 6.2 %slice-start.3 = ((s8[4718592]{0:T(1024)(128)(4,1)}), s8[524288]{0:T(1024)(128)(4,1)S(1)}, s32[]{:S(2)}) async-start(s8[4718592]{0:T(1024)(128)(4,1)} %bitcast.45), calls=%async_computation.3 | async-start | bytes 1048576
  16.9 6.2 %copy-start.18 = (bf16[768,768]{1,0:T(8,128)(2,1)S(1)}, bf16[768,768]{1,0:T(8,128)(2,1)}, u32[]{:S(2)}) copy-start(bf16[768,768]{1,0:T(8,128)(2,1)} %w_out.1) | copy-start | bytes 3538948
  16.9 6.2 %copy-start.19 = (bf16[768,96]{0,1:T(8,128)(2,1)S(1)}, bf16[768,96]{0,1:T(8,128)(2,1)}, u32[]{:S(2)}) copy-start(bf16[768,96]{0,1:T(8,128)(2,1)} %param.33) | copy-start | bytes 442372
  23.1 9.2 %copy-start.7 = (bf16[384,96]{0,1:T(8,128)(2,1)S(1)}, bf16[384,96]{0,1:T(8,128)(2,1)}, u32[]{:S(2)}) copy-start(bf16[384,96]{0,1:T(8,128)(2,1)} %param.42) | copy-start | bytes 221188
  29.8 2.5 %collective-permute-start.4 = (bf16[512,96]{1,0:T(8,128)(2,1)S(1)}, bf16[512,96]{1,0:T(8,128)(2,1)S(1)}, u32[]{:S(2)}, u32[]{:S(2)}) collective-permute-start(bf16[512,96]{1,0:T(8,128)(2,1)S(1)} %get-tuple-element.112.sn_own), channel_id=1, source_target_pairs={{0,1},{1,0},{2,3},{3,2},{4,5},{5,4},{6,7},{7,6},{8,9},{9,8},{10,11... | collective-permute-start | bytes 294920 | tf_op jit(solution)/shard_map/ppermute | solution.py:653
  30.4 13.6 %collective-permute-start.6 = (bf16[256,768]{1,0:T(8,128)(2,1)S(1)}, bf16[256,768]{1,0:T(8,128)(2,1)S(1)}, u32[]{:S(2)}, u32[]{:S(2)}) collective-permute-start(bf16[256,768]{1,0:T(8,128)(2,1)S(1)} %get-tuple-element.121.out_far), channel_id=1, source_target_pairs={{0,2},{1,3},{2,0},{3,1},{4,6},{5,7},{6,4},{7,5},{8,10},{9,11},{10,... | collective-permute-start | bytes 1179656 | tf_op jit(solution)/shard_map/ppermute | solution.py:653
  42.4 1.5 %collective-permute-start.5 = (bf16[192,512]{1,0:T(8,128)(2,1)S(1)}, bf16[192,512]{1,0:T(8,128)(2,1)S(1)}, u32[]{:S(2)}, u32[]{:S(2)}) collective-permute-start(bf16[192,512]{1,0:T(8,128)(2,1)S(1)} %get-tuple-element.120), channel_id=1, source_target_pairs={{0,1},{1,0},{2,3},{3,2},{4,5},{5,4},{6,7},{7,6},{8,9},{9,8},{10,11... | collective-permute-start | bytes 589832 | tf_op jit(solution)/shard_map/ppermute | solution.py:653
  44.6 1.5 %collective-permute-start.7 = (bf16[96,1024]{1,0:T(8,128)(2,1)S(1)}, bf16[96,1024]{1,0:T(8,128)(2,1)S(1)}, u32[]{:S(2)}, u32[]{:S(2)}) collective-permute-start(bf16[96,1024]{1,0:T(8,128)(2,1)S(1)} %get-tuple-element.142), channel_id=1, source_target_pairs={{0,1},{1,0},{2,3},{3,2},{4,5},{5,4},{6,7},{7,6},{8,9},{9,8},{10,11... | collective-permute-start | bytes 589832 | tf_op jit(solution)/shard_map/ppermute | solution.py:653
  46.2 5.1 %collective-permute-start.10 = (bf16[96,256]{1,0:T(8,128)(2,1)S(1)}, bf16[96,256]{1,0:T(8,128)(2,1)S(1)}, u32[]{:S(2)}, u32[]{:S(2)}) collective-permute-start(bf16[96,256]{1,0:T(8,128)(2,1)S(1)} %get-tuple-element.190), channel_id=1, source_target_pairs={{0,6},{1,7},{2,4},{3,5},{4,2},{5,3},{6,0},{7,1},{8,14},{9,15},{10,... | collective-permute-start | bytes 147464 | tf_op jit(solution)/shard_map/ppermute | solution.py:872
  48.2 4.1 %collective-permute-start.9 = (bf16[96,256]{1,0:T(8,128)(2,1)S(1)}, bf16[96,256]{1,0:T(8,128)(2,1)S(1)}, u32[]{:S(2)}, u32[]{:S(2)}) collective-permute-start(bf16[96,256]{1,0:T(8,128)(2,1)S(1)} %get-tuple-element.191), channel_id=1, source_target_pairs={{0,4},{1,5},{2,6},{3,7},{4,0},{5,1},{6,2},{7,3},{8,12},{9,13},{10,... | collective-permute-start | bytes 147464 | tf_op jit(solution)/shard_map/ppermute | solution.py:872
  48.8 4.1 %collective-permute-start.8 = (bf16[96,256]{1,0:T(8,128)(2,1)S(1)}, bf16[96,256]{1,0:T(8,128)(2,1)S(1)}, u32[]{:S(2)}, u32[]{:S(2)}) collective-permute-start(bf16[96,256]{1,0:T(8,128)(2,1)S(1)} %get-tuple-element.189), channel_id=1, source_target_pairs={{0,2},{1,3},{2,0},{3,1},{4,6},{5,7},{6,4},{7,5},{8,10},{9,11},{10,... | collective-permute-start | bytes 147464 | tf_op jit(solution)/shard_map/ppermute | solution.py:872
  52.9 4.2 %collective-permute-start.12 = (bf16[96,256]{1,0:T(8,128)(2,1)S(1)}, bf16[96,256]{1,0:T(8,128)(2,1)S(1)}, u32[]{:S(2)}, u32[]{:S(2)}) collective-permute-start(bf16[96,256]{1,0:T(8,128)(2,1)S(1)} %add_convert_fusion.3), channel_id=1, source_target_pairs={{0,8},{4,12},{8,0},{12,4},{16,24},{20,28},{24,16},{28,20},{1,9},{5... | collective-permute-start | bytes 147464 | tf_op jit(solution)/shard_map/ppermute | solution.py:653
  57.1 5.5 %collective-permute-start.13 = (bf16[96,256]{1,0:T(8,128)(2,1)S(1)}, bf16[96,256]{1,0:T(8,128)(2,1)S(1)}, u32[]{:S(2)}, u32[]{:S(2)}) collective-permute-start(bf16[96,256]{1,0:T(8,128)(2,1)S(1)} %add_convert_fusion.2), channel_id=1, source_target_pairs={{0,16},{4,20},{8,24},{12,28},{16,0},{20,4},{24,8},{28,12},{1,17},{... | collective-permute-start | bytes 147464 | tf_op jit(solution)/shard_map/ppermute | solution.py:653
  61.5 4.6 %collective-permute-start.11 = (bf16[192,256]{1,0:T(8,128)(2,1)S(1)}, bf16[192,256]{1,0:T(8,128)(2,1)S(1)}, u32[]{:S(2)}, u32[]{:S(2)}) collective-permute-start(bf16[192,256]{1,0:T(8,128)(2,1)S(1)} %get-tuple-element.144), channel_id=1, source_target_pairs={{0,2},{1,3},{2,0},{3,1},{4,6},{5,7},{6,4},{7,5},{8,10},{9,11},{10,... | collective-permute-start | bytes 294920 | tf_op jit(solution)/shard_map/ppermute | solution.py:653
  62.5 4.3 %collective-permute-start.14 = (bf16[96,256]{1,0:T(8,128)(2,1)S(1)}, bf16[96,256]{1,0:T(8,128)(2,1)S(1)}, u32[]{:S(2)}, u32[]{:S(2)}) collective-permute-start(bf16[96,256]{1,0:T(8,128)(2,1)S(1)} %add_convert_fusion.1.refs_0_), channel_id=1, source_target_pairs={{0,2},{1,3},{2,0},{3,1},{4,6},{5,7},{6,4},{7,5},{8,10},{9,11},{10,... | collective-permute-start | bytes 147464 | tf_op jit(solution)/shard_map/ppermute | solution.py:872
  63.6 4.1 %collective-permute-start.15 = (bf16[96,256]{1,0:T(8,128)(2,1)S(1)}, bf16[96,256]{1,0:T(8,128)(2,1)S(1)}, u32[]{:S(2)}, u32[]{:S(2)}) collective-permute-start(bf16[96,256]{1,0:T(8,128)(2,1)S(1)} %add_convert_fusion.1.refs_0_), channel_id=1, source_target_pairs={{0,4},{1,5},{2,6},{3,7},{4,0},{5,1},{6,2},{7,3},{8,12},{9,13},{10,... | collective-permute-start | bytes 147464 | tf_op jit(solution)/shard_map/ppermute | solution.py:872
  65.1 5.0 %collective-permute-start.16 = (bf16[96,256]{1,0:T(8,128)(2,1)S(1)}, bf16[96,256]{1,0:T(8,128)(2,1)S(1)}, u32[]{:S(2)}, u32[]{:S(2)}) collective-permute-start(bf16[96,256]{1,0:T(8,128)(2,1)S(1)} %add_convert_fusion.1.refs_0_), channel_id=1, source_target_pairs={{0,6},{1,7},{2,4},{3,5},{4,2},{5,3},{6,0},{7,1},{8,14},{9,15},{10,... | collective-permute-start | bytes 147464 | tf_op jit(solution)/shard_map/ppermute | solution.py:872
  66.1 4.7 %collective-permute-start.17 = (bf16[96,256]{1,0:T(8,128)(2,1)S(1)}, bf16[96,256]{1,0:T(8,128)(2,1)S(1)}, u32[]{:S(2)}, u32[]{:S(2)}) collective-permute-start(bf16[96,256]{1,0:T(8,128)(2,1)S(1)} %add_convert_fusion.1.refs_0_), channel_id=1, source_target_pairs={{0,1},{1,0},{2,3},{3,2},{4,5},{5,4},{6,7},{7,6},{8,9},{9,8},{10,11... | collective-permute-start | bytes 147464 | tf_op jit(solution)/shard_map/ppermute | solution.py:653
  66.8 3.9 %collective-permute-start.18 = (bf16[96,256]{1,0:T(8,128)(2,1)S(1)}, bf16[96,256]{1,0:T(8,128)(2,1)S(1)}, u32[]{:S(2)}, u32[]{:S(2)}) collective-permute-start(bf16[96,256]{1,0:T(8,128)(2,1)S(1)} %collective-permute-done.14.refs_1_), channel_id=1, source_target_pairs={{0,1},{1,0},{2,3},{3,2},{4,5},{5,4},{6,7},{7,6},{8,9},{9,8},{10,11... | collective-permute-start | bytes 147464 | tf_op jit(solution)/shard_map/ppermute | solution.py:653
  67.7 3.1 %collective-permute-start.19 = (bf16[96,256]{1,0:T(8,128)(2,1)S(1)}, bf16[96,256]{1,0:T(8,128)(2,1)S(1)}, u32[]{:S(2)}, u32[]{:S(2)}) collective-permute-start(bf16[96,256]{1,0:T(8,128)(2,1)S(1)} %collective-permute-done.15.refs_2_), channel_id=1, source_target_pairs={{0,1},{1,0},{2,3},{3,2},{4,5},{5,4},{6,7},{7,6},{8,9},{9,8},{10,11... | collective-permute-start | bytes 147464 | tf_op jit(solution)/shard_map/ppermute | solution.py:653
  70.1 1.2 %collective-permute-start.20 = (bf16[96,256]{1,0:T(8,128)(2,1)S(1)}, bf16[96,256]{1,0:T(8,128)(2,1)S(1)}, u32[]{:S(2)}, u32[]{:S(2)}) collective-permute-start(bf16[96,256]{1,0:T(8,128)(2,1)S(1)} %collective-permute-done.16.refs_3_), channel_id=1, source_target_pairs={{0,1},{1,0},{2,3},{3,2},{4,5},{5,4},{6,7},{7,6},{8,9},{9,8},{10,11... | collective-permute-start | bytes 147464 | tf_op jit(solution)/shard_map/ppermute | solution.py:653

commit v11 on v9

--- a/solution.py
+++ b/solution.py
@@ -591,8 +591,8 @@
     core, quarter = lax.axis_index("blk") % 2, quarter_index()
     for i, piece in enumerate(pieces):
         at = ((core ^ (i // 4)) * 4 + (quarter ^ (i % 4))) * size
-        pack[:, pl.ds(pl.multiple_of(at, 128), size)] = piece[...].astype(f32)
-    whole = pack[...]
+        pack[:, pl.ds(pl.multiple_of(at, 128), size)] = piece[...]
+    whole = pack[...].astype(f32)
     grad_down[...] = whole[:, 0:width]
     at = width
     for target in (grad_query, grad_key, grad_value):
@@ -890,7 +890,7 @@
         ],
         pieces,
         vmem=16,
-        scratch=[pltpu.VMEM((side, packed), f32)],
+        scratch=[pltpu.VMEM((side, packed), bf16)],
         cost=(0, 2 * 10**6, 0),
     )
     grads = [grad.reshape(side) if grad.shape[0] == 1 else grad for grad in grads]

time: 72.2 us -> 72.2 us (level)
  no operation moved by 1% of the time
where the time goes in v11:
time: 72.2 us; the launch traced here: 72 us
  Pallas kernels  33.5 us (46%)
  starting transfers between devices  19.9 us (28%)
  waiting for transfers between devices  11.5 us (16%)
  local copies, waits for them, and re-layouts  4.44 us (6%)
  other arithmetic  1.63 us (2%)
  between operations  1.08 us (1%)
    pallas_call x9, Pallas kernels, kernel_call(): pl.pallas_call(body, out_shape=[jax.ShapeDtypeStruct(shape, kind) for sha...  33.5 us
    ppermute x15, starting transfers between devices, swap(): return lax.ppermute(value, axis, [(i, i ^ hop) for i in range(size)])  12.8 us
    ppermute x6, starting transfers between devices, between(): lax.ppermute(value, ('dp', 'blk'), [(i, i ^ mask) for i in range(devices)])  7.11 us
    ppermute x15, waiting for transfers between devices, swap(): return lax.ppermute(value, axis, [(i, i ^ hop) for i in range(size)])  6.25 us
    ppermute x6, waiting for transfers between devices, between(): lax.ppermute(value, ('dp', 'blk'), [(i, i ^ mask) for i in range(devices)])  5.21 us
    unnamed x48, local copies, waits for them, and re-layouts  4.39 us
  transfers between devices with their start and end apart: 21, of which 10 were waited for; matrix products, arithmetic and copies ran while one was open for 5% of the time, Pallas kernels for 35%

profile of v11, /device:TPU:0, one launch (start us, length us, event | category | flops | bytes accessed | tf_op | source)
XLA Modules:
  0.0 72.0 jit_solution(17936541289103934201)
XLA Ops:
  0.7 1.3 %copy.42 = bf16[256,2,768]{2,0,1:T(8,128)(2,1)S(1)} copy(bf16[256,2,768]{2,1,0:T(2,128)(2,1)} %param.22) | data formatting | bytes 1572864 | tf_op args[0]
  2.0 0.5 collective-permute-start.1
  2.6 2.6 %collective-permute-start = (bf16[256,768]{1,0:T(8,128)(2,1)S(1)}, bf16[256,768]{1,0:T(8,128)(2,1)S(1)}, u32[]{:S(2)}, u32[]{:S(2)}) collective-permute-start(bf16[256,768]{1,0:T(8,128)(2,1)S(1)} %dynamic-slice_bitcast_fusion), channel_id=1, source_target_pairs={{0,2},{1,3},{2,0},{3,1},{4,6},{5,7},{6,4},{7,5},{8,10},{9,11},{10,... | collective-permute-start | bytes 1179656 | tf_op jit(solution)/shard_map/ppermute | solution.py:648
  5.2 1.7 %shard_map.309 = (bf16[768,768]{1,0:T(8,128)(2,1)S(1)}, f32[2,768]{1,0:T(2,128)S(1)}, bf16[1024,128]{1,0:T(8,128)(2,1)S(1)}, bf16[512,128]{1,0:T(8,128)(2,1)S(1)...) custom-call(s32[2,8]{1,0:T(2,128)S(1)} %copy-done.13, bf16[768,768]{1,0:T(8,128)(2,1)S(1)} %copy-done, ...), custom_call_target="tpu_custom_call" | custom-call | flops 1000 | bytes 1000 | tf_op jit(solution)/shard_map/pallas_call | solution.py:65
  6.9 1.3 %copy-done.2 = bf16[768,768]{1,0:T(8,128)(2,1)S(1)} copy-done((bf16[768,768]{1,0:T(8,128)(2,1)S(1)}, bf16[768,768]{1,0:T(8,128)(2,1)}, u32[]{:S(2)}) %copy-start.2) | copy-done | bytes 1179672
  8.2 5.3 %shard_map.310 = (bf16[256,768]{1,0:T(8,128)(2,1)S(1)}, bf16[512,768]{1,0:T(8,128)(2,1)S(1)}, bf16[960,512]{1,0:T(8,128)(2,1)S(1)}, f32[6,144,256]{2,1,0:T(8,128)S(1)}) custom-call(bf16[2,256,768]{2,1,0:T(8,128)(2,1)S(1)} %bitcast.34, bf16[2,256,768]{2,1,0:T(8,128)(2,1)} %collective-permute-done.1.mate, f32[2,768]{1,0:T(2,128)S(1)} %get-tuple-element.83.gains, ...), custom_call_target="tpu_custom_call" | custom-call | flops 1000 | bytes 1000 | tf_op jit(solution)/shard_map/pallas_call | solution.py:65
  13.6 1.3 %collective-permute-done.far = bf16[256,768]{1,0:T(8,128)(2,1)S(1)} collective-permute-done((bf16[256,768]{1,0:T(8,128)(2,1)S(1)}, bf16[256,768]{1,0:T(8,128)(2,1)S(1)}, u32[]{:S(2)}, u32[]{:S(2)}) %collective-permute-start) | collective-permute-done | bytes 393248 | tf_op jit(solution)/shard_map/ppermute | solution.py:648
  14.9 1.8 %collective-permute-start.2 = (bf16[192,256]{1,0:T(8,128)(2,1)S(1)}, bf16[192,256]{1,0:T(8,128)(2,1)S(1)}, u32[]{:S(2)}, u32[]{:S(2)}) collective-permute-start(bf16[192,256]{1,0:T(8,128)(2,1)S(1)} %fusion.3), channel_id=1, source_target_pairs={{0,2},{1,3},{2,0},{3,1},{4,6},{5,7},{6,4},{7,5},{8,10},{9,11},{10,... | collective-permute-start | bytes 294920 | tf_op jit(solution)/shard_map/ppermute | solution.py:648
  16.8 0.0 slice-start
  16.8 0.0 slice-start.2
  16.8 0.3 shard_map.312
  17.1 0.0 slice-start.1
  17.1 0.0 slice-start.3
  17.2 7.3 %shard_map.311.attended = bf16[512,768]{1,0:T(8,128)(2,1)S(1)} custom-call(bf16[256,768]{1,0:T(8,128)(2,1)S(1)} %collective-permute-done.far, bf16[256,768]{1,0:T(8,128)(2,1)S(1)} %collective-permute-done.3.far_mate, f32[2,768]{1,0:T(2,128)S(1)} %get-tuple-element.83.gains, bf16[768,768]{1,0:T(8,128)(2,1)S(1)} %copy-done.1, bf16[768,768]{1,0:T(8,128)(2,1)S(1)} %copy-done.2, ...), custom_call_target="tpu_custom_call" | custom-call | flops 8000000000 | bytes 8000000 | tf_op jit(solution)/shard_map/pallas_call | solution.py:65
  24.6 6.6 %shard_map.313 = (bf16[256,768]{1,0:T(8,128)(2,1)S(1)}, bf16[256,768]{1,0:T(8,128)(2,1)S(1)}, bf16[512,96]{1,0:T(8,128)(2,1)S(1)}, bf16[96,512]{1,0:T(8,128)(2,1...) custom-call(bf16[2,256,768]{2,1,0:T(8,128)(2,1)S(1)} %bitcast.35, bf16[256,768]{1,0:T(8,128)(2,1)S(1)} %collective-permute-done.far, ...), custom_call_target="tpu_custom_call" | custom-call | flops 10000000000 | bytes 14000000 | tf_op jit(solution)/shard_map/pallas_call | solution.py:65
  31.1 0.3 collective-permute-start.4
  31.4 1.1 %collective-permute-start.6 = (bf16[256,768]{1,0:T(8,128)(2,1)S(1)}, bf16[256,768]{1,0:T(8,128)(2,1)S(1)}, u32[]{:S(2)}, u32[]{:S(2)}) collective-permute-start(bf16[256,768]{1,0:T(8,128)(2,1)S(1)} %get-tuple-element.117.out_far), channel_id=1, source_target_pairs={{0,2},{1,3},{2,0},{3,1},{4,6},{5,7},{6,4},{7,5},{8,10},{9,11},{10,... | collective-permute-start | bytes 1179656 | tf_op jit(solution)/shard_map/ppermute | solution.py:648
  32.5 0.0 collective-permute-done.4.sn_mate
  32.5 10.1 %shard_map.314 = (f32[192,512]{1,0:T(8,128)S(1)}, bf16[192,512]{1,0:T(8,128)(2,1)S(1)}, f32[96,512]{1,0:T(8,128)S(1)}, f32[96,512]{1,0:T(8,128)S(1)}, f32[96,512...) custom-call(bf16[512,96]{1,0:T(8,128)(2,1)S(1)} %get-tuple-element.1, ...), custom_call_target="tpu_custom_call" | custom-call | flops 30000001024 | bytes 3000000 | tf_op jit(solution)/shard_map/pallas_call | solution.py:65
  42.6 0.3 collective-permute-start.5
  42.9 0.6 shard_map.315
  43.6 0.6 collective-permute-done.5.dkv_back
  44.2 0.7 shard_map.316
  44.8 0.3 collective-permute-start.7
  45.1 1.2 %collective-permute-done.7 = bf16[96,1024]{1,0:T(8,128)(2,1)S(1)} collective-permute-done((bf16[96,1024]{1,0:T(8,128)(2,1)S(1)}, bf16[96,1024]{1,0:T(8,128)(2,1)S(1)}, u32[]{:S(2)}, u32[]{:S(2)}) %collective-permute-start.7) | collective-permute-done | bytes 196640 | tf_op jit(solution)/shard_map/ppermute | solution.py:648
  46.5 2.2 %collective-permute-start.10 = (bf16[96,256]{1,0:T(8,128)(2,1)S(1)}, bf16[96,256]{1,0:T(8,128)(2,1)S(1)}, u32[]{:S(2)}, u32[]{:S(2)}) collective-permute-start(bf16[96,256]{1,0:T(8,128)(2,1)S(1)} %get-tuple-element.186), channel_id=1, source_target_pairs={{0,6},{1,7},{2,4},{3,5},{4,2},{5,3},{6,0},{7,1},{8,14},{9,15},{10,... | collective-permute-start | bytes 147464 | tf_op jit(solution)/shard_map/ppermute | solution.py:861
  48.6 0.9 %collective-permute-start.8 = (bf16[96,256]{1,0:T(8,128)(2,1)S(1)}, bf16[96,256]{1,0:T(8,128)(2,1)S(1)}, u32[]{:S(2)}, u32[]{:S(2)}) collective-permute-start(bf16[96,256]{1,0:T(8,128)(2,1)S(1)} %get-tuple-element.185), channel_id=1, source_target_pairs={{0,2},{1,3},{2,0},{3,1},{4,6},{5,7},{6,4},{7,5},{8,10},{9,11},{10,... | collective-permute-start | bytes 147464 | tf_op jit(solution)/shard_map/ppermute | solution.py:861
  49.5 0.5 collective-permute-start.9
  50.0 2.0 %collective-permute-done.10 = bf16[96,256]{1,0:T(8,128)(2,1)S(1)} collective-permute-done((bf16[96,256]{1,0:T(8,128)(2,1)S(1)}, bf16[96,256]{1,0:T(8,128)(2,1)S(1)}, u32[]{:S(2)}, u32[]{:S(2)}) %collective-permute-start.10) | collective-permute-done | bytes 49184 | tf_op jit(solution)/shard_map/ppermute | solution.py:861
  52.0 0.7 %collective-permute-done.8 = bf16[96,256]{1,0:T(8,128)(2,1)S(1)} collective-permute-done((bf16[96,256]{1,0:T(8,128)(2,1)S(1)}, bf16[96,256]{1,0:T(8,128)(2,1)S(1)}, u32[]{:S(2)}, u32[]{:S(2)}) %collective-permute-start.8) | collective-permute-done | bytes 49184 | tf_op jit(solution)/shard_map/ppermute | solution.py:861
  52.7 0.9 %collective-permute-done.9 = bf16[96,256]{1,0:T(8,128)(2,1)S(1)} collective-permute-done((bf16[96,256]{1,0:T(8,128)(2,1)S(1)}, bf16[96,256]{1,0:T(8,128)(2,1)S(1)}, u32[]{:S(2)}, u32[]{:S(2)}) %collective-permute-start.9) | collective-permute-done | bytes 49184 | tf_op jit(solution)/shard_map/ppermute | solution.py:861
  53.6 1.6 %collective-permute-start.12 = (bf16[96,256]{1,0:T(8,128)(2,1)S(1)}, bf16[96,256]{1,0:T(8,128)(2,1)S(1)}, u32[]{:S(2)}, u32[]{:S(2)}) collective-permute-start(bf16[96,256]{1,0:T(8,128)(2,1)S(1)} %add_convert_fusion.3), channel_id=1, source_target_pairs={{0,8},{4,12},{8,0},{12,4},{16,24},{20,28},{24,16},{28,20},{1,9},{5... | collective-permute-start | bytes 147464 | tf_op jit(solution)/shard_map/ppermute | solution.py:648
  55.3 0.1 select_bitcast_fusion.1
  55.3 2.5 %collective-permute-done.12 = bf16[96,256]{1,0:T(8,128)(2,1)S(1)} collective-permute-done((bf16[96,256]{1,0:T(8,128)(2,1)S(1)}, bf16[96,256]{1,0:T(8,128)(2,1)S(1)}, u32[]{:S(2)}, u32[]{:S(2)}) %collective-permute-start.12) | collective-permute-done | bytes 49184 | tf_op jit(solution)/shard_map/ppermute | solution.py:648
  57.8 2.6 %collective-permute-start.13 = (bf16[96,256]{1,0:T(8,128)(2,1)S(1)}, bf16[96,256]{1,0:T(8,128)(2,1)S(1)}, u32[]{:S(2)}, u32[]{:S(2)}) collective-permute-start(bf16[96,256]{1,0:T(8,128)(2,1)S(1)} %add_convert_fusion.2), channel_id=1, source_target_pairs={{0,16},{4,20},{8,24},{12,28},{16,0},{20,4},{24,8},{28,12},{1,17},{... | collective-permute-start | bytes 147464 | tf_op jit(solution)/shard_map/ppermute | solution.py:648
  60.5 0.1 maximum_bitcast_fusion
  60.5 1.7 %copy.39 = bf16[256,2,768]{2,1,0:T(2,128)(2,1)} copy(bf16[256,2,768]{2,0,1:T(8,128)(2,1)S(1)} %maximum_bitcast_fusion) | data formatting | bytes 1572864
  62.2 1.2 %collective-permute-start.11 = (bf16[192,256]{1,0:T(8,128)(2,1)S(1)}, bf16[192,256]{1,0:T(8,128)(2,1)S(1)}, u32[]{:S(2)}, u32[]{:S(2)}) collective-permute-start(bf16[192,256]{1,0:T(8,128)(2,1)S(1)} %get-tuple-element.140), channel_id=1, source_target_pairs={{0,2},{1,3},{2,0},{3,1},{4,6},{5,7},{6,4},{7,5},{8,10},{9,11},{10,... | collective-permute-start | bytes 294920 | tf_op jit(solution)/shard_map/ppermute | solution.py:648
  63.4 0.9 %collective-permute-start.14 = (bf16[96,256]{1,0:T(8,128)(2,1)S(1)}, bf16[96,256]{1,0:T(8,128)(2,1)S(1)}, u32[]{:S(2)}, u32[]{:S(2)}) collective-permute-start(bf16[96,256]{1,0:T(8,128)(2,1)S(1)} %add_convert_fusion.1.refs_0_), channel_id=1, source_target_pairs={{0,2},{1,3},{2,0},{3,1},{4,6},{5,7},{6,4},{7,5},{8,10},{9,11},{10,... | collective-permute-start | bytes 147464 | tf_op jit(solution)/shard_map/ppermute | solution.py:861
  64.3 0.5 collective-permute-start.15
  64.8 2.1 %collective-permute-start.16 = (bf16[96,256]{1,0:T(8,128)(2,1)S(1)}, bf16[96,256]{1,0:T(8,128)(2,1)S(1)}, u32[]{:S(2)}, u32[]{:S(2)}) collective-permute-start(bf16[96,256]{1,0:T(8,128)(2,1)S(1)} %add_convert_fusion.1.refs_0_), channel_id=1, source_target_pairs={{0,6},{1,7},{2,4},{3,5},{4,2},{5,3},{6,0},{7,1},{8,14},{9,15},{10,... | collective-permute-start | bytes 147464 | tf_op jit(solution)/shard_map/ppermute | solution.py:861
  67.0 0.7 maximum_bitcast_fusion.1
  67.7 0.5 collective-permute-start.18
  68.2 0.2 collective-permute-done.15.refs_2_
  68.4 1.4 %collective-permute-done.16.refs_3_ = bf16[96,256]{1,0:T(8,128)(2,1)S(1)} collective-permute-done((bf16[96,256]{1,0:T(8,128)(2,1)S(1)}, bf16[96,256]{1,0:T(8,128)(2,1)S(1)}, u32[]{:S(2)}, u32[]{:S(2)}) %collective-permute-start.16) | collective-permute-done | bytes 49184 | tf_op jit(solution)/shard_map/ppermute | solution.py:861
  69.8 0.7 maximum_bitcast_fusion.2
  70.5 0.6 collective-permute-done.20.refs_7_
  71.1 0.9 %shard_map.317 = (f32[96,768]{1,0:T(8,128)}, f32[1,96]{1,0:T(1,128)}, f32[1,96]{1,0:T(1,128)}, f32[96,96]{1,0:T(8,128)}, f32[96,96]{1,0:T(8,128)}, /*index=5*/f3...) custom-call(bf16[96,256]{1,0:T(8,128)(2,1)S(1)} %add_convert_fusion.1.refs_0_, ...), custom_call_target="tpu_custom_call" | custom-call | bytes 2000000 | tf_op jit(solution)/shard_map/pallas_call | solution.py:65
  (66 shorter events, 0.4 us)
Async XLA Ops:
  0.6 4.5 %copy-start.13 = (s32[2,8]{1,0:T(2,128)S(1)}, s32[2,8]{1,0:T(2,128)}, u32[]{:S(2)}) copy-start(s32[2,8]{1,0:T(2,128)} %doc_lengths.1) | copy-start | bytes 196
  0.7 4.5 %copy-start.11 = (bf16[768]{0:T(1024)(128)(2,1)S(1)}, bf16[768]{0:T(1024)(128)(2,1)}, u32[]{:S(2)}) copy-start(bf16[768]{0:T(1024)(128)(2,1)} %norm_in.1) | copy-start | bytes 4612
  0.7 4.5 %copy-start = (bf16[768,768]{1,0:T(8,128)(2,1)S(1)}, bf16[768,768]{1,0:T(8,128)(2,1)}, u32[]{:S(2)}) copy-start(bf16[768,768]{1,0:T(8,128)(2,1)} %w_value.1) | copy-start | bytes 3538948
  0.7 4.5 %copy-start.12 = (bf16[768]{0:T(1024)(128)(2,1)S(1)}, bf16[768]{0:T(1024)(128)(2,1)}, u32[]{:S(2)}) copy-start(bf16[768]{0:T(1024)(128)(2,1)} %norm_mid.1) | copy-start | bytes 4612
  2.0 4.9 %copy-start.1 = (bf16[768,768]{1,0:T(8,128)(2,1)S(1)}, bf16[768,768]{1,0:T(8,128)(2,1)}, u32[]{:S(2)}) copy-start(bf16[768,768]{1,0:T(8,128)(2,1)} %w_query.3) | copy-start | bytes 3538948
  2.0 4.9 %collective-permute-start.1 = (bf16[2,256,768]{2,1,0:T(8,128)(2,1)S(1)}, bf16[2,256,768]{2,1,0:T(8,128)(2,1)}, u32[]{:S(2)}, u32[]{:S(2)}) collective-permute-start(bf16[2,256,768]{2,1,0:T(8,128)(2,1)S(1)} %bitcast.33), channel_id=1, source_target_pairs={{0,1},{1,0},{2,3},{3,2},{4,5},{5,4},{6,7},{7,6},{8,9},{9,8},{10,11... | collective-permute-start | bytes 2359304 | tf_op jit(solution)/shard_map/ppermute | solution.py:648
  2.6 12.3 %collective-permute-start = (bf16[256,768]{1,0:T(8,128)(2,1)S(1)}, bf16[256,768]{1,0:T(8,128)(2,1)S(1)}, u32[]{:S(2)}, u32[]{:S(2)}) collective-permute-start(bf16[256,768]{1,0:T(8,128)(2,1)S(1)} %dynamic-slice_bitcast_fusion), channel_id=1, source_target_pairs={{0,2},{1,3},{2,0},{3,1},{4,6},{5,7},{6,4},{7,5},{8,10},{9,11},{10,... | collective-permute-start | bytes 1179656 | tf_op jit(solution)/shard_map/ppermute | solution.py:648
  6.9 1.3 %copy-start.2 = (bf16[768,768]{1,0:T(8,128)(2,1)S(1)}, bf16[768,768]{1,0:T(8,128)(2,1)}, u32[]{:S(2)}) copy-start(bf16[768,768]{1,0:T(8,128)(2,1)} %w_key.3) | copy-start | bytes 3538948
  8.2 6.7 %copy-start.3 = (bf16[256,2,96]{0,2,1:T(8,128)(2,1)S(1)}, bf16[256,2,96]{0,2,1:T(8,128)(2,1)}, u32[]{:S(2)}) copy-start(bf16[256,2,96]{0,2,1:T(8,128)(2,1)} %param.43) | copy-start | bytes 294916
  8.2 6.7 %copy-start.4 = (bf16[256,2,96]{0,2,1:T(8,128)(2,1)S(1)}, bf16[256,2,96]{0,2,1:T(8,128)(2,1)}, u32[]{:S(2)}) copy-start(bf16[256,2,96]{0,2,1:T(8,128)(2,1)} %param.23) | copy-start | bytes 294916
  8.2 8.6 %copy-start.5 = (bf16[96,384]{1,0:T(8,128)(2,1)S(1)}, bf16[96,384]{1,0:T(8,128)(2,1)}, u32[]{:S(2)}) copy-start(bf16[96,384]{1,0:T(8,128)(2,1)} %s_inner.2) | copy-start | bytes 221188
  8.2 8.6 %copy-start.7 = (bf16[96,96]{1,0:T(8,128)(2,1)S(1)}, bf16[96,96]{1,0:T(8,128)(2,1)}, u32[]{:S(2)}) copy-start(bf16[96,96]{1,0:T(8,128)(2,1)} %s_out.2) | copy-start | bytes 55300
  8.2 8.6 %copy-start.8 = (bf16[96,96]{1,0:T(8,128)(2,1)S(1)}, bf16[96,96]{1,0:T(8,128)(2,1)}, u32[]{:S(2)}) copy-start(bf16[96,96]{1,0:T(8,128)(2,1)} %s_query.2) | copy-start | bytes 55300
  8.2 8.6 %copy-start.9 = (bf16[96,96]{1,0:T(8,128)(2,1)S(1)}, bf16[96,96]{1,0:T(8,128)(2,1)}, u32[]{:S(2)}) copy-start(bf16[96,96]{1,0:T(8,128)(2,1)} %s_key.2) | copy-start | bytes 55300
  8.2 8.6 %copy-start.10 = (bf16[96,96]{1,0:T(8,128)(2,1)S(1)}, bf16[96,96]{1,0:T(8,128)(2,1)}, u32[]{:S(2)}) copy-start(bf16[96,96]{1,0:T(8,128)(2,1)} %s_value.2) | copy-start | bytes 55300
  8.2 8.6 %copy-start.14 = (f32[96]{0:T(128)S(1)}, f32[96]{0:T(128)}, u32[]{:S(2)}) copy-start(f32[96]{0:T(128)} %gate) | copy-start | bytes 1156
  8.2 8.6 %copy-start.15 = (f32[96]{0:T(128)S(1)}, f32[96]{0:T(128)}, u32[]{:S(2)}) copy-start(f32[96]{0:T(128)} %gain_in) | copy-start | bytes 1156
  8.2 8.5 %copy-start.16 = (f32[96]{0:T(128)S(1)}, f32[96]{0:T(128)}, u32[]{:S(2)}) copy-start(f32[96]{0:T(128)} %gain_mid) | copy-start | bytes 1156
  14.9 2.3 %collective-permute-start.3 = (bf16[256,768]{1,0:T(8,128)(2,1)S(1)}, bf16[256,768]{1,0:T(8,128)(2,1)S(1)}, u32[]{:S(2)}, u32[]{:S(2)}) collective-permute-start(bf16[256,768]{1,0:T(8,128)(2,1)S(1)} %collective-permute-done.far), channel_id=1, source_target_pairs={{0,1},{1,0},{2,3},{3,2},{4,5},{5,4},{6,7},{7,6},{8,9},{9,8},{10,11... | collective-permute-start | bytes 1179656 | tf_op jit(solution)/shard_map/ppermute | solution.py:648
  14.9 9.5 %collective-permute-start.2 = (bf16[192,256]{1,0:T(8,128)(2,1)S(1)}, bf16[192,256]{1,0:T(8,128)(2,1)S(1)}, u32[]{:S(2)}, u32[]{:S(2)}) collective-permute-start(bf16[192,256]{1,0:T(8,128)(2,1)S(1)} %fusion.3), channel_id=1, source_target_pairs={{0,2},{1,3},{2,0},{3,1},{4,6},{5,7},{6,4},{7,5},{8,10},{9,11},{10,... | collective-permute-start | bytes 294920 | tf_op jit(solution)/shard_map/ppermute | solution.py:648
  16.8 7.7 %slice-start = ((s8[4718592]{0:T(1024)(128)(4,1)}), s8[4194304]{0:T(1024)(128)(4,1)S(1)}, s32[]{:S(2)}) async-start(s8[4718592]{0:T(1024)(128)(4,1)} %bitcast.43), calls=%async_computation | async-start | bytes 8388608
  16.8 7.7 %slice-start.2 = ((s8[4718592]{0:T(1024)(128)(4,1)}), s8[4194304]{0:T(1024)(128)(4,1)S(1)}, s32[]{:S(2)}) async-start(s8[4718592]{0:T(1024)(128)(4,1)} %bitcast.45), calls=%async_computation.2 | async-start | bytes 8388608
  17.1 7.4 %slice-start.1 = ((s8[4718592]{0:T(1024)(128)(4,1)}), s8[524288]{0:T(1024)(128)(4,1)S(1)}, s32[]{:S(2)}) async-start(s8[4718592]{0:T(1024)(128)(4,1)} %bitcast.43), calls=%async_computation.1 | async-start | bytes 1048576
  17.1 7.4 %slice-start.3 = ((s8[4718592]{0:T(1024)(128)(4,1)}), s8[524288]{0:T(1024)(128)(4,1)S(1)}, s32[]{:S(2)}) async-start(s8[4718592]{0:T(1024)(128)(4,1)} %bitcast.45), calls=%async_computation.3 | async-start | bytes 1048576
  17.2 7.4 %copy-start.17 = (bf16[768,768]{1,0:T(8,128)(2,1)S(1)}, bf16[768,768]{1,0:T(8,128)(2,1)}, u32[]{:S(2)}) copy-start(bf16[768,768]{1,0:T(8,128)(2,1)} %w_out.1) | copy-start | bytes 3538948
  17.2 7.3 %copy-start.18 = (bf16[768,96]{0,1:T(8,128)(2,1)S(1)}, bf16[768,96]{0,1:T(8,128)(2,1)}, u32[]{:S(2)}) copy-start(bf16[768,96]{0,1:T(8,128)(2,1)} %param.33) | copy-start | bytes 442372
  24.5 8.0 %copy-start.6 = (bf16[384,96]{0,1:T(8,128)(2,1)S(1)}, bf16[384,96]{0,1:T(8,128)(2,1)}, u32[]{:S(2)}) copy-start(bf16[384,96]{0,1:T(8,128)(2,1)} %param.42) | copy-start | bytes 221188
  31.1 1.4 %collective-permute-start.4 = (bf16[512,96]{1,0:T(8,128)(2,1)S(1)}, bf16[512,96]{1,0:T(8,128)(2,1)S(1)}, u32[]{:S(2)}, u32[]{:S(2)}) collective-permute-start(bf16[512,96]{1,0:T(8,128)(2,1)S(1)} %get-tuple-element.108.sn_own), channel_id=1, source_target_pairs={{0,1},{1,0},{2,3},{3,2},{4,5},{5,4},{6,7},{7,6},{8,9},{9,8},{10,11... | collective-permute-start | bytes 294920 | tf_op jit(solution)/shard_map/ppermute | solution.py:648
  31.4 12.7 %collective-permute-start.6 = (bf16[256,768]{1,0:T(8,128)(2,1)S(1)}, bf16[256,768]{1,0:T(8,128)(2,1)S(1)}, u32[]{:S(2)}, u32[]{:S(2)}) collective-permute-start(bf16[256,768]{1,0:T(8,128)(2,1)S(1)} %get-tuple-element.117.out_far), channel_id=1, source_target_pairs={{0,2},{1,3},{2,0},{3,1},{4,6},{5,7},{6,4},{7,5},{8,10},{9,11},{10,... | collective-permute-start | bytes 1179656 | tf_op jit(solution)/shard_map/ppermute | solution.py:648
  42.6 1.5 %collective-permute-start.5 = (bf16[192,512]{1,0:T(8,128)(2,1)S(1)}, bf16[192,512]{1,0:T(8,128)(2,1)S(1)}, u32[]{:S(2)}, u32[]{:S(2)}) collective-permute-start(bf16[192,512]{1,0:T(8,128)(2,1)S(1)} %get-tuple-element.116), channel_id=1, source_target_pairs={{0,1},{1,0},{2,3},{3,2},{4,5},{5,4},{6,7},{7,6},{8,9},{9,8},{10,11... | collective-permute-start | bytes 589832 | tf_op jit(solution)/shard_map/ppermute | solution.py:648
  44.8 1.5 %collective-permute-start.7 = (bf16[96,1024]{1,0:T(8,128)(2,1)S(1)}, bf16[96,1024]{1,0:T(8,128)(2,1)S(1)}, u32[]{:S(2)}, u32[]{:S(2)}) collective-permute-start(bf16[96,1024]{1,0:T(8,128)(2,1)S(1)} %get-tuple-element.138), channel_id=1, source_target_pairs={{0,1},{1,0},{2,3},{3,2},{4,5},{5,4},{6,7},{7,6},{8,9},{9,8},{10,11... | collective-permute-start | bytes 589832 | tf_op jit(solution)/shard_map/ppermute | solution.py:648
  46.5 5.5 %collective-permute-start.10 = (bf16[96,256]{1,0:T(8,128)(2,1)S(1)}, bf16[96,256]{1,0:T(8,128)(2,1)S(1)}, u32[]{:S(2)}, u32[]{:S(2)}) collective-permute-start(bf16[96,256]{1,0:T(8,128)(2,1)S(1)} %get-tuple-element.186), channel_id=1, source_target_pairs={{0,6},{1,7},{2,4},{3,5},{4,2},{5,3},{6,0},{7,1},{8,14},{9,15},{10,... | collective-permute-start | bytes 147464 | tf_op jit(solution)/shard_map/ppermute | solution.py:861
  48.6 4.1 %collective-permute-start.8 = (bf16[96,256]{1,0:T(8,128)(2,1)S(1)}, bf16[96,256]{1,0:T(8,128)(2,1)S(1)}, u32[]{:S(2)}, u32[]{:S(2)}) collective-permute-start(bf16[96,256]{1,0:T(8,128)(2,1)S(1)} %get-tuple-element.185), channel_id=1, source_target_pairs={{0,2},{1,3},{2,0},{3,1},{4,6},{5,7},{6,4},{7,5},{8,10},{9,11},{10,... | collective-permute-start | bytes 147464 | tf_op jit(solution)/shard_map/ppermute | solution.py:861
  49.5 4.1 %collective-permute-start.9 = (bf16[96,256]{1,0:T(8,128)(2,1)S(1)}, bf16[96,256]{1,0:T(8,128)(2,1)S(1)}, u32[]{:S(2)}, u32[]{:S(2)}) collective-permute-start(bf16[96,256]{1,0:T(8,128)(2,1)S(1)} %get-tuple-element.187), channel_id=1, source_target_pairs={{0,4},{1,5},{2,6},{3,7},{4,0},{5,1},{6,2},{7,3},{8,12},{9,13},{10,... | collective-permute-start | bytes 147464 | tf_op jit(solution)/shard_map/ppermute | solution.py:861
  53.6 4.2 %collective-permute-start.12 = (bf16[96,256]{1,0:T(8,128)(2,1)S(1)}, bf16[96,256]{1,0:T(8,128)(2,1)S(1)}, u32[]{:S(2)}, u32[]{:S(2)}) collective-permute-start(bf16[96,256]{1,0:T(8,128)(2,1)S(1)} %add_convert_fusion.3), channel_id=1, source_target_pairs={{0,8},{4,12},{8,0},{12,4},{16,24},{20,28},{24,16},{28,20},{1,9},{5... | collective-permute-start | bytes 147464 | tf_op jit(solution)/shard_map/ppermute | solution.py:648
  57.8 5.6 %collective-permute-start.13 = (bf16[96,256]{1,0:T(8,128)(2,1)S(1)}, bf16[96,256]{1,0:T(8,128)(2,1)S(1)}, u32[]{:S(2)}, u32[]{:S(2)}) collective-permute-start(bf16[96,256]{1,0:T(8,128)(2,1)S(1)} %add_convert_fusion.2), channel_id=1, source_target_pairs={{0,16},{4,20},{8,24},{12,28},{16,0},{20,4},{24,8},{28,12},{1,17},{... | collective-permute-start | bytes 147464 | tf_op jit(solution)/shard_map/ppermute | solution.py:648
  62.2 4.7 %collective-permute-start.11 = (bf16[192,256]{1,0:T(8,128)(2,1)S(1)}, bf16[192,256]{1,0:T(8,128)(2,1)S(1)}, u32[]{:S(2)}, u32[]{:S(2)}) collective-permute-start(bf16[192,256]{1,0:T(8,128)(2,1)S(1)} %get-tuple-element.140), channel_id=1, source_target_pairs={{0,2},{1,3},{2,0},{3,1},{4,6},{5,7},{6,4},{7,5},{8,10},{9,11},{10,... | collective-permute-start | bytes 294920 | tf_op jit(solution)/shard_map/ppermute | solution.py:648
  63.4 4.3 %collective-permute-start.14 = (bf16[96,256]{1,0:T(8,128)(2,1)S(1)}, bf16[96,256]{1,0:T(8,128)(2,1)S(1)}, u32[]{:S(2)}, u32[]{:S(2)}) collective-permute-start(bf16[96,256]{1,0:T(8,128)(2,1)S(1)} %add_convert_fusion.1.refs_0_), channel_id=1, source_target_pairs={{0,2},{1,3},{2,0},{3,1},{4,6},{5,7},{6,4},{7,5},{8,10},{9,11},{10,... | collective-permute-start | bytes 147464 | tf_op jit(solution)/shard_map/ppermute | solution.py:861
  64.3 4.1 %collective-permute-start.15 = (bf16[96,256]{1,0:T(8,128)(2,1)S(1)}, bf16[96,256]{1,0:T(8,128)(2,1)S(1)}, u32[]{:S(2)}, u32[]{:S(2)}) collective-permute-start(bf16[96,256]{1,0:T(8,128)(2,1)S(1)} %add_convert_fusion.1.refs_0_), channel_id=1, source_target_pairs={{0,4},{1,5},{2,6},{3,7},{4,0},{5,1},{6,2},{7,3},{8,12},{9,13},{10,... | collective-permute-start | bytes 147464 | tf_op jit(solution)/shard_map/ppermute | solution.py:861
  64.8 5.0 %collective-permute-start.16 = (bf16[96,256]{1,0:T(8,128)(2,1)S(1)}, bf16[96,256]{1,0:T(8,128)(2,1)S(1)}, u32[]{:S(2)}, u32[]{:S(2)}) collective-permute-start(bf16[96,256]{1,0:T(8,128)(2,1)S(1)} %add_convert_fusion.1.refs_0_), channel_id=1, source_target_pairs={{0,6},{1,7},{2,4},{3,5},{4,2},{5,3},{6,0},{7,1},{8,14},{9,15},{10,... | collective-permute-start | bytes 147464 | tf_op jit(solution)/shard_map/ppermute | solution.py:861
  67.0 3.5 %collective-permute-start.17 = (bf16[96,256]{1,0:T(8,128)(2,1)S(1)}, bf16[96,256]{1,0:T(8,128)(2,1)S(1)}, u32[]{:S(2)}, u32[]{:S(2)}) collective-permute-start(bf16[96,256]{1,0:T(8,128)(2,1)S(1)} %add_convert_fusion.1.refs_0_), channel_id=1, source_target_pairs={{0,1},{1,0},{2,3},{3,2},{4,5},{5,4},{6,7},{7,6},{8,9},{9,8},{10,11... | collective-permute-start | bytes 147464 | tf_op jit(solution)/shard_map/ppermute | solution.py:648
  67.7 2.8 %collective-permute-start.18 = (bf16[96,256]{1,0:T(8,128)(2,1)S(1)}, bf16[96,256]{1,0:T(8,128)(2,1)S(1)}, u32[]{:S(2)}, u32[]{:S(2)}) collective-permute-start(bf16[96,256]{1,0:T(8,128)(2,1)S(1)} %collective-permute-done.14.refs_1_), channel_id=1, source_target_pairs={{0,1},{1,0},{2,3},{3,2},{4,5},{5,4},{6,7},{7,6},{8,9},{9,8},{10,11... | collective-permute-start | bytes 147464 | tf_op jit(solution)/shard_map/ppermute | solution.py:648
  68.4 2.1 %collective-permute-start.19 = (bf16[96,256]{1,0:T(8,128)(2,1)S(1)}, bf16[96,256]{1,0:T(8,128)(2,1)S(1)}, u32[]{:S(2)}, u32[]{:S(2)}) collective-permute-start(bf16[96,256]{1,0:T(8,128)(2,1)S(1)} %collective-permute-done.15.refs_2_), channel_id=1, source_target_pairs={{0,1},{1,0},{2,3},{3,2},{4,5},{5,4},{6,7},{7,6},{8,9},{9,8},{10,11... | collective-permute-start | bytes 147464 | tf_op jit(solution)/shard_map/ppermute | solution.py:648
  69.8 1.2 %collective-permute-start.20 = (bf16[96,256]{1,0:T(8,128)(2,1)S(1)}, bf16[96,256]{1,0:T(8,128)(2,1)S(1)}, u32[]{:S(2)}, u32[]{:S(2)}) collective-permute-start(bf16[96,256]{1,0:T(8,128)(2,1)S(1)} %collective-permute-done.16.refs_3_), channel_id=1, source_target_pairs={{0,1},{1,0},{2,3},{3,2},{4,5},{5,4},{6,7},{7,6},{8,9},{9,8},{10,11... | collective-permute-start | bytes 147464 | tf_op jit(solution)/shard_map/ppermute | solution.py:648
